TPU v7x, 32 devices: a whole 2x2x4 slice. The times are simulated.
32 devices in a mesh: slab: 8 (over z, x), pencil: 4 (over y, core).
Axes of the slice: x: 2, y: 2, z: 4, core: 2. Of those that a mesh axis runs over, the one named last changes fastest.
Arguments:
- vorticity: float32 [3, 64, 128, 256], P(None, 'slab', 'pencil')
- velocity: float32 [3, 64, 128, 256], P(None, 'slab', 'pencil'), may hold values from -6 to 6
- viscosity: float32 [64, 128, 256], P('slab', 'pencil'), may hold values from 0.02 to 0.4
- tile_weights: float32 [1024, 3, 128], P(('slab', 'pencil')), may hold values from -6 to 6
- tile_cells: int32 [1024, 128], P(('slab', 'pencil')), may hold values from 0 to 65535
- tile_dest: int32 [1024, 1], P(('slab', 'pencil')), may hold values from 0 to 7; in each aligned block of 32 rows (0 to 31, 32 to 63, ...) at most 8 rows name the same one
- tile_count: int32 [32], P(('slab', 'pencil')), may hold values from 8 to 32, as said below
Outputs:
- vorticity_out: float32 [3, 64, 128, 256], P(None, 'slab', 'pencil')
- far_velocity: float32 [3, 8, 4, 16], P(None, 'slab', 'pencil')
Inputs may be any that keep to these rules, and one draw needn't show every extreme that they name: Tiles of device (s, p) go to device (tile_dest, p). Among the 32 tiles of one device, at most 8 name one slab, a bound that some block reaches. The live tiles of a device are its first tile_count ones; some device has all 32 live.
All inputs are finite; a program needn't handle non-finite values.
Results may differ from a plain program's by a relative error of at most 0.0003.
Values sent between devices are 32-bit elements; how exact they have to be, the bound alone decides.
No kernel may reach another device: no remote copies, remote signals or barrier semaphores. Data moves between devices by JAX's collectives and lax.ppermute only.
A program may use at most 128 MiB of HBM per device.

v0:
```python
import functools

import jax
import jax.numpy as jnp
from jax import lax
from jax.experimental import pallas as pl
from jax.experimental.pallas import tpu as pltpu
from jax.sharding import PartitionSpec as P

CB = 16
TIME_STEP = 0.1
LANES = 128
GROUP = 4
VMEM_LIMIT = 48 * 1024 * 1024

VMEM = pl.BlockSpec(memory_space=pltpu.VMEM)
ANY = pl.BlockSpec(memory_space=pl.ANY)
SMEM = pl.BlockSpec(memory_space=pltpu.SMEM)
FIRST_PARAMS = pltpu.CompilerParams(vmem_limit_bytes=60 * 1024 * 1024)
PARAMS = pltpu.CompilerParams(vmem_limit_bytes=VMEM_LIMIT)


def shaped(*shape):
    return jax.ShapeDtypeStruct(shape, jnp.float32)


def split(w):
    high = w.astype(jnp.bfloat16).astype(jnp.float32)
    return high, w - high


def tile_moments(cap, nz, packets, moments):
    n_slab = packets.shape[0] // cap
    ncl = nz // CB
    wide = cap * packets.shape[2]
    level = lax.broadcasted_iota(jnp.int32, (ncl, wide), 0)
    found = []
    for d in range(n_slab):
        block = jnp.concatenate([packets[d * cap + k] for k in range(cap)], axis=1)
        cell = block[3:4, :].astype(jnp.int32)
        spots = (level == cell % nz // CB).astype(jnp.float32).astype(jnp.bfloat16)
        high, low = split(block)
        left = jnp.concatenate([high, low], axis=0).astype(jnp.bfloat16)
        sums = lax.dot_general(left, spots, (((1,), (1,)), ((), ())), preferred_element_type=jnp.float32)
        found.append(sums[0:4] + sums[4:8])
    moments[...] = jnp.concatenate(found, axis=1)


def send_kernel(
    cap,
    vort,
    velo,
    visc,
    weights_in,
    cells_in,
    dest_in,
    count_in,
    xlo,
    xhi,
    ylo,
    yhi,
    sides,
    packets,
    moments,
    spin_rows,
    velo_rows,
    visc_rows,
    weights,
    cells,
    dest,
    count,
    filled,
    sems,
):
    cx, cy, nz = visc.shape
    copies = []

    def copy(source, target):
        copies.append(pltpu.make_async_copy(source, target, sems.at[len(copies)]))
        copies[-1].start()

    copy(weights_in, weights)
    copy(cells_in, cells)
    copy(dest_in, dest)
    copy(count_in, count)
    for k, at in ((0, 0), (1, cy - 8)):
        copy(vort.at[:, :, pl.ds(at, 8), :], spin_rows.at[k])
        copy(velo.at[:, :, pl.ds(at, 8), :], velo_rows.at[k])
        copy(visc.at[:, pl.ds(at, 8), :], visc_rows.at[k])
    for face, at in ((xlo, 0), (xhi, cx - 1)):
        copy(vort.at[:, at], face.at[0:3])
        copy(velo.at[:, at], face.at[3:6])
        copy(visc.at[at], face.at[6])

    packets[...] = jnp.zeros_like(packets)
    n_slab = packets.shape[0] // cap
    for d in range(n_slab):
        filled[d] = 0
    for k in range(4):
        copies[k].wait()

    def place(r, carry):
        d = dest[0, r]
        slot = filled[d]
        at = d * cap + slot
        for c in range(3):
            packets[at, c : c + 1, :] = weights[c, pl.ds(r, 1), :]
        packets[at, 3:4, :] = cells[pl.ds(r, 1), :].astype(jnp.float32)
        filled[d] = slot + 1
        return carry

    lax.fori_loop(0, count[0], place, 0)
    for d in range(n_slab):
        held = (filled[d] * (cx * cy * nz)).astype(jnp.float32)
        packets[d * cap, 3:4, :] = packets[d * cap, 3:4, :] + held
    tile_moments(cap, nz, packets, moments)
    sides[...] = jnp.zeros_like(sides)
    for k in range(4, 10):
        copies[k].wait()
    for k, face, at in ((0, ylo, 0), (1, yhi, 7)):
        for x in range(cx):
            for c in range(3):
                face[c, x : x + 1, :] = spin_rows[k, c, x, at : at + 1, :]
                face[3 + c, x : x + 1, :] = velo_rows[k, c, x, at : at + 1, :]
            face[6, x : x + 1, :] = visc_rows[k, x, at : at + 1, :]
    pencil = lax.axis_index("pencil")

    @pl.when(pencil < sides.shape[0] - 1)
    def _():
        sides[pencil + 1, 0:7] = yhi[...]

    @pl.when(pencil > 0)
    def _():
        sides[pencil - 1, 7:14] = ylo[...]

    for k in range(10, 16):
        copies[k].wait()


def to_send(vort, velo, visc, weights, cells, dest, count, n_slab, n_pencil, cap):
    _, cx, cy, nz = vort.shape
    return pl.pallas_call(
        functools.partial(send_kernel, cap),
        out_shape=(
            shaped(7, cy, nz),
            shaped(7, cy, nz),
            shaped(7, cx, nz),
            shaped(7, cx, nz),
            shaped(n_pencil, 14, cx, nz),
            shaped(n_slab * cap, 4, weights.shape[2]),
            shaped(4, n_slab * nz // CB),
        ),
        in_specs=[ANY] * 7,
        out_specs=(VMEM,) * 7,
        scratch_shapes=[
            pltpu.VMEM((2, 3, cx, 8, nz), jnp.float32),
            pltpu.VMEM((2, 3, cx, 8, nz), jnp.float32),
            pltpu.VMEM((2, cx, 8, nz), jnp.float32),
            pltpu.VMEM(weights.shape, jnp.float32),
            pltpu.VMEM(cells.shape, jnp.int32),
            pltpu.SMEM(dest.shape, jnp.int32),
            pltpu.SMEM(count.shape, jnp.int32),
            pltpu.SMEM((n_slab,), jnp.int32),
            pltpu.SemaphoreType.DMA((16,)),
        ],
        compiler_params=FIRST_PARAMS,
    )(vort, velo, visc, weights, cells, dest, count)


def ahead(a, axis):
    return pltpu.roll(a, a.shape[axis] - 1, axis)


def behind(a, axis):
    return pltpu.roll(a, 1, axis)


def interior_step(vort, velo, visc, out):
    cx, cy, nz = visc.shape
    row = lax.broadcasted_iota(jnp.int32, (cy, nz), 0)
    has_ahead = row < cy - 1
    has_behind = row > 0
    for x in range(cx):
        nu = visc[x]
        spin = [vort[c, x] for c in range(3)]
        mean_y = jnp.where(has_ahead, 0.5 * (nu + ahead(nu, 0)), 0.0)
        mean_z = 0.5 * (nu + ahead(nu, 1))
        if x < cx - 1:
            mean_next = 0.5 * (nu + visc[x + 1])
        if x > 0:
            mean_last = 0.5 * (nu + visc[x - 1])
        for c in range(3):
            w = spin[c]
            u = velo[c, x]
            flux_y = mean_y * (ahead(w, 0) - w)
            flux_z = mean_z * (ahead(w, 1) - w)
            change = (flux_y - behind(flux_y, 0)) + (flux_z - behind(flux_z, 1))
            slope_y = jnp.where(has_ahead, ahead(u, 0), 0.0) - jnp.where(has_behind, behind(u, 0), 0.0)
            slope_z = ahead(u, 1) - behind(u, 1)
            if x == 0:
                slope_x = velo[c, x + 1]
            elif x == cx - 1:
                slope_x = -velo[c, x - 1]
            else:
                slope_x = velo[c, x + 1] - velo[c, x - 1]
            stretch = 0.5 * (spin[0] * slope_x + spin[1] * slope_y + spin[2] * slope_z)
            if x < cx - 1:
                change = change + mean_next * (vort[c, x + 1] - w)
            if x > 0:
                change = change + mean_last * (vort[c, x - 1] - w)
            out[c, x] = w + TIME_STEP * (stretch + change)


def inner_kernel(vort, velo, visc, out, sums):
    interior_step(vort, velo, visc, out)
    for c in range(3):
        sums[c : c + 1, :] = jnp.sum(out[c].reshape(-1, out.shape[3]), axis=0, keepdims=True)


def inner(vort, velo, visc):
    return pl.pallas_call(
        inner_kernel,
        out_shape=(shaped(*vort.shape), shaped(3, vort.shape[3])),
        in_specs=[VMEM] * 3,
        out_specs=(VMEM,) * 2,
        compiler_params=PARAMS,
    )(vort, velo, visc)


def face_change(own, other, along, sign, c):
    stretch = (0.5 * sign) * own[along] * other[3 + c]
    diffuse = 0.5 * (own[6] + other[6]) * (other[c] - own[c])
    return TIME_STEP * (stretch + diffuse)


def edge_kernel(inside, sums, tiles, xlo, xhi, ylo, yhi, xlo_in, xhi_in, sides, out, load):
    _, cx, cy, nz = out.shape
    out[...] = inside[...]
    ylo_in, yhi_in = sides.at[0, 0:7], sides.at[0, 7:14]
    totals = []
    for c in range(3):
        total = sums[c : c + 1, :]
        for own, other, at, sign in ((xlo, xlo_in, 0, -1.0), (xhi, xhi_in, cx - 1, 1.0)):
            change = face_change(own, other, 0, sign, c)
            out[c, at] = out[c, at] + change
            total = total + jnp.sum(change, axis=0, keepdims=True)
        for own, other, at, sign in ((ylo, ylo_in, 0, -1.0), (yhi, yhi_in, cy - 1, 1.0)):
            change = face_change(own, other, 1, sign, c)
            for x in range(cx):
                out[c, x, at : at + 1, :] = out[c, x, at : at + 1, :] + change[x : x + 1, :]
            total = total + jnp.sum(change, axis=0, keepdims=True)
        totals.append(total)
    totals.append(jnp.zeros_like(totals[0]))
    shape = (nz, tiles.shape[1])
    level = lax.broadcasted_iota(jnp.int32, shape, 0) // CB
    lane = lax.broadcasted_iota(jnp.int32, shape, 1)
    own_slab = lax.axis_index("slab")
    pick = (lane == own_slab * (nz // CB) + level).astype(jnp.float32)
    moment = tiles[...] + jnp.dot(
        jnp.concatenate(totals, axis=0), pick, precision=lax.Precision.HIGHEST, preferred_element_type=jnp.float32
    )
    for k in range(load.shape[1] // 4):
        part = moment[:, k * LANES : (k + 1) * LANES]
        for j in range(load.shape[0]):
            load[j, 4 * k : 4 * k + 4, :] = part


def edges(inside, sums, tiles, faces, halos, n_all):
    return pl.pallas_call(
        edge_kernel,
        out_shape=(shaped(*inside.shape), shaped(n_all, 4 * tiles.shape[1] // LANES, LANES)),
        in_specs=[VMEM] * 10,
        out_specs=(VMEM,) * 2,
        compiler_params=PARAMS,
    )(inside, sums, tiles, *faces, *halos)


def far_kernel(cx, cy, ncl, n_pencil, load, out):
    n_all = load.shape[0]
    n_slab = n_all // n_pencil
    slab = lax.axis_index("slab")
    pencil = lax.axis_index("pencil")
    shape = (ncl, n_slab * ncl)
    target = lax.broadcasted_iota(jnp.int32, shape, 0)
    source = lax.broadcasted_iota(jnp.int32, shape, 1)
    sigma = jnp.float32(cx * n_slab // 4)
    rel_x = ((slab - source // ncl) * cx).astype(jnp.float32)
    rel_z = ((target - source % ncl) * CB).astype(jnp.float32)
    flat = rel_x * rel_x + rel_z * rel_z + sigma * sigma
    turned = [jnp.zeros(shape, jnp.float32) for _ in range(3)]
    for p in range(n_pencil):
        total = load[p]
        for s in range(1, n_slab):
            total = total + load[s * n_pencil + p]
        moment = jnp.concatenate([total[4 * k : 4 * k + 4] for k in range(load.shape[1] // 4)], axis=1)
        first, second, third = moment[0:1], moment[1:2], moment[2:3]
        rel_y = ((pencil - p) * cy).astype(jnp.float32)
        inverse = lax.rsqrt(flat + rel_y * rel_y)
        weight = inverse * inverse * inverse
        turned[0] = turned[0] + weight * (rel_z * second - rel_y * third)
        turned[1] = turned[1] + weight * (rel_x * third - rel_z * first)
        turned[2] = turned[2] + weight * (rel_y * first - rel_x * second)
    ones = jnp.ones((8, shape[1]), jnp.float32)
    for c in range(3):
        row = lax.dot_general(
            ones,
            turned[c],
            (((1,), (1,)), ((), ())),
            precision=lax.Precision.HIGHEST,
            preferred_element_type=jnp.float32,
        )
        out[c, 0] = row[0:1]


def far(load, cx, cy, ncl, n_pencil):
    return pl.pallas_call(
        functools.partial(far_kernel, cx, cy, ncl, n_pencil),
        out_shape=shaped(3, 1, 1, ncl),
        in_specs=[VMEM],
        out_specs=VMEM,
        compiler_params=PARAMS,
    )(load)


def deposit_kernel(cap, inside, load, out, acc, order):
    _, cx, cy, nz = out.shape
    rows = cx * cy // 2
    cells = 2 * rows * nz
    n_slab = load.shape[0] // cap
    wide = GROUP * load.shape[2]
    acc[...] = jnp.zeros_like(acc)
    listed = jnp.int32(0)
    for d in range(n_slab):
        first = d * cap
        held = jnp.max(load[first, 3:4, :]).astype(jnp.int32) // cells
        for k in range(cap):
            order[listed + k] = first + k
        listed = listed + held
    for k in range(GROUP):
        order[listed + k] = 0
    def numbers(length):
        shape = (length // 16, 16, wide)
        return (lax.broadcasted_iota(jnp.int32, shape, 0) * 16 + lax.broadcasted_iota(jnp.int32, shape, 1)).astype(
            jnp.float32
        ).astype(jnp.bfloat16)

    def spread(row):
        return jnp.broadcast_to(row, (16, wide)).astype(jnp.bfloat16)[None]

    row_numbers = numbers(rows)
    col_numbers = numbers(nz)
    place = lax.broadcasted_iota(jnp.int32, (1, wide), 1) // load.shape[2]
    zero = jnp.zeros((), jnp.bfloat16)
    one = jnp.ones((), jnp.bfloat16)

    def group(g, carry):
        tiles = [load[order[g * GROUP + k]] for k in range(GROUP)]
        block = jnp.concatenate(tiles, axis=1)
        live = place < listed - g * GROUP
        cell = block[3:4, :].astype(jnp.int32) % cells
        row = cell // nz
        half = row // rows
        at_row = row_numbers == spread(jnp.where(live, row % rows, -1).astype(jnp.float32))
        right = []
        for h in range(2):
            at_col = col_numbers == spread(jnp.where(half == h, cell % nz, -1).astype(jnp.float32))
            right.append(jnp.where(at_col, one, zero).reshape(nz, wide))
        left = []
        for piece in split(block):
            for c in range(3):
                left.append(jnp.where(at_row, spread(piece[c : c + 1, :]), zero).reshape(rows, wide))
        added = lax.dot_general(
            jnp.concatenate(left, axis=0),
            jnp.concatenate(right, axis=0),
            (((1,), (1,)), ((), ())),
            preferred_element_type=jnp.float32,
        )
        acc[...] += added[: 3 * rows] + added[3 * rows :]
        return carry

    lax.fori_loop(0, (listed + GROUP - 1) // GROUP, group, 0)
    for h in range(2):
        span = slice(h * (cx // 2), (h + 1) * (cx // 2))
        change = acc[:, h * nz : (h + 1) * nz].reshape(3, cx // 2, cy, nz)
        out[:, span] = inside[:, span] + change


def deposit(inside, load, cap):
    return pl.pallas_call(
        functools.partial(deposit_kernel, cap),
        out_shape=shaped(*inside.shape),
        in_specs=[VMEM] * 2,
        out_specs=VMEM,
        scratch_shapes=[
            pltpu.VMEM((3 * inside.shape[1] * inside.shape[2] // 2, 2 * inside.shape[3]), jnp.float32),
            pltpu.SMEM((load.shape[0] + max(cap, GROUP),), jnp.int32),
        ],
        compiler_params=PARAMS,
    )(inside, load)


def shift(array, axis, step):
    n = lax.axis_size(axis)
    pairs = [(i, i + step) for i in range(n) if 0 <= i + step < n]
    return lax.ppermute(array, axis, pairs)


def per_device(vorticity, velocity, viscosity, tile_weights, tile_cells, tile_dest, tile_count):
    _, cx, cy, nz = vorticity.shape
    ncl = nz // CB
    n_slab = lax.axis_size("slab")
    n_pencil = lax.axis_size("pencil")
    cap = 2 * tile_weights.shape[0] // n_slab
    weights = jnp.transpose(tile_weights, (1, 0, 2))
    xlo, xhi, ylo, yhi, sides, packets, tiles = to_send(
        vorticity, velocity, viscosity, weights, tile_cells, tile_dest.T, tile_count, n_slab, n_pencil, cap
    )
    sides_in = lax.psum_scatter(sides, "pencil", scatter_dimension=0, tiled=True)
    arrived = lax.all_to_all(packets, "slab", 0, 0, tiled=True)
    xlo_in = shift(xhi, "slab", 1)
    xhi_in = shift(xlo, "slab", -1)
    inside, sums = inner(vorticity, velocity, viscosity)
    advanced, load = edges(
        inside, sums, tiles, (xlo, xhi, ylo, yhi), (xlo_in, xhi_in, sides_in), n_slab * n_pencil
    )
    load = lax.all_to_all(load, ("slab", "pencil"), 0, 0, tiled=True)
    vorticity_out = deposit(advanced, arrived, cap)
    return (vorticity_out, far(load, cx, cy, ncl, n_pencil))


def solution(mesh):
    in_specs = (
        P(None, "slab", "pencil", None),
        P(None, "slab", "pencil", None),
        P("slab", "pencil", None),
        P(("slab", "pencil"), None, None),
        P(("slab", "pencil"), None),
        P(("slab", "pencil"), None),
        P(("slab", "pencil")),
    )
    out_specs = (P(None, "slab", "pencil", None), P(None, "slab", "pencil", None))
    return jax.shard_map(
        per_device, mesh=mesh, in_specs=in_specs, out_specs=out_specs, check_vma=False
    )
```

profile of v0, /device:TPU:0, one launch (start us, length us, event | category | flops | bytes accessed | tf_op | source)
XLA Modules:
  0.0 58.1 jit_solution(5427172324433570533)
XLA Ops:
  7.2 0.0 reduce-scatter.2.cloned.1.call-start
  7.9 0.0 copy-start
  7.9 0.0 copy-start.1
  7.9 2.9 %shard_map.87 = (f32[7,32,256]{2,1,0:T(8,128)}, f32[7,32,256]{2,1,0:T(8,128)}, f32[7,8,256]{2,1,0:T(8,128)}, f32[7,8,256]{2,1,0:T(8,128)}, f32[4,14,8,256]{3,2,1...) custom-call(f32[3,8,32,256]{3,2,1,0:T(8,128)} %vort.3, f32[3,8,32,256]{3,2,1,0:T(8,128)} %velo.3, ...), custom_call_target="tpu_custom_call" | custom-call | tf_op jit(solution)/shard_map/pallas_call | solution.py:142
  10.8 0.0 copy-start.2
  10.8 0.0 reduce-scatter.2.cloned.1.call-update
  10.9 0.9 %copy-done.3 = f32[7,32,256]{2,1,0:T(8,128)S(1)} copy-done((f32[7,32,256]{2,1,0:T(8,128)S(1)}, f32[7,32,256]{2,1,0:T(8,128)}, u32[]{:S(2)}) %copy-start.3) | copy-done | bytes 229400
  11.7 1.3 %collective-permute-start.1 = (f32[7,32,256]{2,1,0:T(8,128)S(1)}, f32[7,32,256]{2,1,0:T(8,128)S(1)}, u32[]{:S(2)}, u32[]{:S(2)}) collective-permute-start(f32[7,32,256]{2,1,0:T(8,128)S(1)} %copy-done.3), channel_id=1, source_target_pairs={{4,0},{8,4},{12,8},{16,12},{20,16},{24,20},{28,24},{5,1},{9,5},{13... | collective-permute-start | bytes 688136 | tf_op jit(solution)/shard_map/ppermute | solution.py:405
  13.0 6.2 %collective-permute-start = (f32[7,32,256]{2,1,0:T(8,128)S(1)}, f32[7,32,256]{2,1,0:T(8,128)}, u32[]{:S(2)}, u32[]{:S(2)}) collective-permute-start(f32[7,32,256]{2,1,0:T(8,128)S(1)} %copy-done.4), channel_id=1, source_target_pairs={{0,4},{4,8},{8,12},{12,16},{16,20},{20,24},{24,28},{1,5},{5,9},{9,... | collective-permute-start | bytes 688136 | tf_op jit(solution)/shard_map/ppermute | solution.py:405
  19.2 5.6 %all-to-all-start = ((f32[64,4,128]{2,1,0:T(4,128)}), f32[64,4,128]{2,1,0:T(4,128)S(1)}, u32[]{:S(2)}, u32[]{:S(2)}) async-start(f32[64,4,128]{2,1,0:T(4,128)} %get-tuple-element.22), calls=%async_computation.1 | async-start | bytes 262144 | tf_op jit(solution)/shard_map/all_to_all | solution.py:419
  24.8 2.4 %shard_map.86 = (f32[3,8,32,256]{3,2,1,0:T(8,128)S(1)}, f32[3,256]{1,0:T(4,128)S(1)}) custom-call(f32[3,8,32,256]{3,2,1,0:T(8,128)S(1)} %copy-done, f32[3,8,32,256]{3,2,1,0:T(8,128)S(1)} %copy-done.1, f32[8,32,256]{2,1,0:T(8,128)S(1)} %copy-done.2), custom_call_target="tpu_custom_call" | custom-call | tf_op jit(solution)/shard_map/pallas_call | solution.py:221
  27.2 0.6 copy-done.8
  27.8 0.0 collective-permute-done.1.xhi_in
  27.8 0.0 collective-permute-done.xlo_in
  27.8 7.2 %reduce-scatter.2.cloned.1.call-done.sides = f32[1,14,8,256]{3,2,1,0:T(8,128)} async-done(((f32[4,14,8,256]{3,2,1,0:T(8,128)}), f32[1,14,8,256]{3,2,1,0:T(8,128)}) %reduce-scatter.2.cloned.1.call-update) | async-done | bytes 114704 | tf_op jit(solution)/shard_map/reduce_scatter | solution.py:418
  35.0 0.0 copy-done.7
  35.0 0.7 %copy-done.9 = f32[3,256]{1,0:T(4,128)S(1)} copy-done((f32[3,256]{1,0:T(4,128)S(1)}, f32[3,256]{1,0:T(4,128)}, u32[]{:S(2)}) %copy-start.9) | copy-done | bytes 3096
  35.7 0.9 %copy-done.5 = f32[1,14,8,256]{3,2,1,0:T(8,128)S(1)} copy-done((f32[1,14,8,256]{3,2,1,0:T(8,128)S(1)}, f32[1,14,8,256]{3,2,1,0:T(8,128)}, u32[]{:S(2)}) %copy-start.5) | copy-done | bytes 114712
  36.6 1.9 %shard_map.88 = (f32[3,8,32,256]{3,2,1,0:T(8,128)S(1)}, f32[32,4,128]{2,1,0:T(4,128)}) custom-call(f32[3,8,32,256]{3,2,1,0:T(8,128)S(1)} %get-tuple-element.13.inside, f32[3,256]{1,0:T(4,128)S(1)} %copy-done.9, f32[4,128]{1,0:T(4,128)S(1)} %copy-done.10, f32[7,32,256]{2,1,0:T(8,128)S(1)} %copy-done.3, f32[7,32,256]{2,1,0:T(8,128)S(1)} %copy-done.4, ...), custom_call_target="tpu_custom_call" | custom-call | tf_op jit(solution)/shard_map/pallas_call | solution.py:269
  38.5 0.0 all-to-all-done.load
  38.5 4.6 %all-to-all-start.1 = ((f32[32,4,128]{2,1,0:T(4,128)}), f32[32,4,128]{2,1,0:T(4,128)S(1)}, u32[]{:S(2)}, u32[]{:S(2)}) async-start(f32[32,4,128]{2,1,0:T(4,128)} %get-tuple-element.23), calls=%async_computation.2 | async-start | bytes 131072 | tf_op jit(solution)/shard_map/all_to_all | solution.py:426
  43.1 3.1 %shard_map.89 = f32[3,8,32,256]{3,2,1,0:T(8,128)} custom-call(f32[3,8,32,256]{3,2,1,0:T(8,128)S(1)} %get-tuple-element.21.inside, f32[64,4,128]{2,1,0:T(4,128)S(1)} %all-to-all-done.load), custom_call_target="tpu_custom_call" | custom-call | tf_op jit(solution)/shard_map/pallas_call | solution.py:389
  46.2 4.3 %all-to-all-done.1.load = f32[32,4,128]{2,1,0:T(4,128)S(1)} async-done(((f32[32,4,128]{2,1,0:T(4,128)}), f32[32,4,128]{2,1,0:T(4,128)S(1)}, u32[]{:S(2)}, u32[]{:S(2)}) %all-to-all-start.1) | async-done | bytes 65568 | tf_op jit(solution)/shard_map/all_to_all | solution.py:426
  50.5 0.7 %shard_map.90 = f32[3,1,1,16]{3,2,1,0:T(1,128)} custom-call(f32[32,4,128]{2,1,0:T(4,128)S(1)} %all-to-all-done.1.load), custom_call_target="tpu_custom_call" | custom-call | tf_op jit(solution)/shard_map/pallas_call | solution.py:316
  (14 shorter events, 0.0 us)
Async XLA Ops:
  7.2 27.9 %reduce-scatter.2.cloned.1.call-start = ((), (), s32[]{:S(2)}) async-start(), calls=%async_computation.3 | async-start | bytes 573440 | tf_op jit(solution)/shard_map/reduce_scatter | solution.py:418
  7.9 16.9 %copy-start = (f32[3,8,32,256]{3,2,1,0:T(8,128)S(1)}, f32[3,8,32,256]{3,2,1,0:T(8,128)}, u32[]{:S(2)}) copy-start(f32[3,8,32,256]{3,2,1,0:T(8,128)} %vort.3) | copy-start | bytes 2359300
  7.9 16.9 %copy-start.1 = (f32[3,8,32,256]{3,2,1,0:T(8,128)S(1)}, f32[3,8,32,256]{3,2,1,0:T(8,128)}, u32[]{:S(2)}) copy-start(f32[3,8,32,256]{3,2,1,0:T(8,128)} %velo.3) | copy-start | bytes 2359300
  10.8 0.9 %copy-start.3 = (f32[7,32,256]{2,1,0:T(8,128)S(1)}, f32[7,32,256]{2,1,0:T(8,128)}, u32[]{:S(2)}) copy-start(f32[7,32,256]{2,1,0:T(8,128)} %get-tuple-element.16.xlo) | copy-start | bytes 688132
  10.8 2.2 %copy-start.4 = (f32[7,32,256]{2,1,0:T(8,128)S(1)}, f32[7,32,256]{2,1,0:T(8,128)}, u32[]{:S(2)}) copy-start(f32[7,32,256]{2,1,0:T(8,128)} %get-tuple-element.17.xhi) | copy-start | bytes 688132
  10.8 14.0 %copy-start.2 = (f32[8,32,256]{2,1,0:T(8,128)S(1)}, f32[8,32,256]{2,1,0:T(8,128)}, u32[]{:S(2)}) copy-start(f32[8,32,256]{2,1,0:T(8,128)} %visc.3) | copy-start | bytes 786436
  11.7 16.0 %collective-permute-start.1 = (f32[7,32,256]{2,1,0:T(8,128)S(1)}, f32[7,32,256]{2,1,0:T(8,128)S(1)}, u32[]{:S(2)}, u32[]{:S(2)}) collective-permute-start(f32[7,32,256]{2,1,0:T(8,128)S(1)} %copy-done.3), channel_id=1, source_target_pairs={{4,0},{8,4},{12,8},{16,12},{20,16},{24,20},{28,24},{5,1},{9,5},{13... | collective-permute-start | bytes 688136 | tf_op jit(solution)/shard_map/ppermute | solution.py:405
  13.0 14.7 %collective-permute-start = (f32[7,32,256]{2,1,0:T(8,128)S(1)}, f32[7,32,256]{2,1,0:T(8,128)}, u32[]{:S(2)}, u32[]{:S(2)}) collective-permute-start(f32[7,32,256]{2,1,0:T(8,128)S(1)} %copy-done.4), channel_id=1, source_target_pairs={{0,4},{4,8},{8,12},{12,16},{16,20},{20,24},{24,28},{1,5},{5,9},{9,... | collective-permute-start | bytes 688136 | tf_op jit(solution)/shard_map/ppermute | solution.py:405
  19.2 19.3 %all-to-all-start = ((f32[64,4,128]{2,1,0:T(4,128)}), f32[64,4,128]{2,1,0:T(4,128)S(1)}, u32[]{:S(2)}, u32[]{:S(2)}) async-start(f32[64,4,128]{2,1,0:T(4,128)} %get-tuple-element.22), calls=%async_computation.1 | async-start | bytes 262144 | tf_op jit(solution)/shard_map/all_to_all | solution.py:419
  24.8 10.2 %copy-start.6 = (f32[7,8,256]{2,1,0:T(8,128)S(1)}, f32[7,8,256]{2,1,0:T(8,128)}, u32[]{:S(2)}) copy-start(f32[7,8,256]{2,1,0:T(8,128)} %get-tuple-element.18.ylo) | copy-start | bytes 172036
  24.8 10.2 %copy-start.7 = (f32[7,8,256]{2,1,0:T(8,128)S(1)}, f32[7,8,256]{2,1,0:T(8,128)}, u32[]{:S(2)}) copy-start(f32[7,8,256]{2,1,0:T(8,128)} %get-tuple-element.19.yhi) | copy-start | bytes 172036
  27.2 0.6 %copy-start.8 = (f32[3,256]{1,0:T(4,128)}, f32[3,256]{1,0:T(4,128)S(1)}, u32[]{:S(2)}) copy-start(f32[3,256]{1,0:T(4,128)S(1)} %get-tuple-element.14.sums) | copy-start | bytes 9220
  35.0 0.7 %copy-start.9 = (f32[3,256]{1,0:T(4,128)S(1)}, f32[3,256]{1,0:T(4,128)}, u32[]{:S(2)}) copy-start(f32[3,256]{1,0:T(4,128)} %copy-done.8) | copy-start | bytes 9220
  35.0 0.7 %copy-start.10 = (f32[4,128]{1,0:T(4,128)S(1)}, f32[4,128]{1,0:T(4,128)}, u32[]{:S(2)}) copy-start(f32[4,128]{1,0:T(4,128)} %get-tuple-element.15.tiles) | copy-start | bytes 6148
  35.7 0.9 %copy-start.5 = (f32[1,14,8,256]{3,2,1,0:T(8,128)S(1)}, f32[1,14,8,256]{3,2,1,0:T(8,128)}, u32[]{:S(2)}) copy-start(f32[1,14,8,256]{3,2,1,0:T(8,128)} %reduce-scatter.2.cloned.1.call-done.sides) | copy-start | bytes 344068
  38.5 12.0 %all-to-all-start.1 = ((f32[32,4,128]{2,1,0:T(4,128)}), f32[32,4,128]{2,1,0:T(4,128)S(1)}, u32[]{:S(2)}, u32[]{:S(2)}) async-start(f32[32,4,128]{2,1,0:T(4,128)} %get-tuple-element.23), calls=%async_computation.2 | async-start | bytes 131072 | tf_op jit(solution)/shard_map/all_to_all | solution.py:426
Sparse Core Ops, SparseCore 0:
  11.1 23.8 reduce-scatter.1
where the time goes:
time: 58.9 us; the launch traced here: 58.1 us
  starting transfers between devices  17.7 us (30%)
  between operations  14.8 us (25%)
  waiting for transfers between devices  11.6 us (20%)
  Pallas kernels  11 us (19%)
  local copies, waits for them, and re-layouts  3.06 us (5%)
    ppermute x2, starting transfers between devices, shift(): return lax.ppermute(array, axis, pairs)  7.44 us
    reduce_scatter x1, waiting for transfers between devices, per_device(): lax.psum_scatter(sides, 'pencil', scatter_dimension=0, tiled=True)  7.25 us
    all_to_all x1, starting transfers between devices, per_device(): arrived = lax.all_to_all(packets, 'slab', 0, 0, tiled=True)  5.56 us
    all_to_all x1, starting transfers between devices, per_device(): load = lax.all_to_all(load, ('slab', 'pencil'), 0, 0, tiled=True)  4.61 us
    all_to_all x1, waiting for transfers between devices, per_device(): load = lax.all_to_all(load, ('slab', 'pencil'), 0, 0, tiled=True)  4.33 us
    pallas_call x1, Pallas kernels, deposit(): pl.pallas_call(functools.partial(deposit_kernel, cap), out_shape=shaped(*...  3.08 us
    unnamed x22, local copies, waits for them, and re-layouts  3.06 us
    pallas_call x1, Pallas kernels, to_send(): pl.pallas_call(functools.partial(send_kernel, cap), out_shape=(shaped(7,...  2.91 us
  transfers between devices with their start and end apart: 5, of which 2 were waited for; matrix products, arithmetic and copies ran while one was open for 0% of the time, Pallas kernels for 13%

commit v1 on v0

--- a/solution.py
+++ b/solution.py
@@ -127,11 +127,11 @@
 
     @pl.when(pencil < sides.shape[0] - 1)
     def _():
-        sides[pencil + 1, 0:7] = yhi[...]
+        sides[pencil + 1] = yhi[...]
 
     @pl.when(pencil > 0)
     def _():
-        sides[pencil - 1, 7:14] = ylo[...]
+        sides[pencil - 1] = ylo[...]
 
     for k in range(10, 16):
         copies[k].wait()
@@ -146,7 +146,7 @@
             shaped(7, cy, nz),
             shaped(7, cx, nz),
             shaped(7, cx, nz),
-            shaped(n_pencil, 14, cx, nz),
+            shaped(n_pencil, 7, cx, nz),
             shaped(n_slab * cap, 4, weights.shape[2]),
             shaped(4, n_slab * nz // CB),
         ),
@@ -236,7 +236,9 @@
 def edge_kernel(inside, sums, tiles, xlo, xhi, ylo, yhi, xlo_in, xhi_in, sides, out, load):
     _, cx, cy, nz = out.shape
     out[...] = inside[...]
-    ylo_in, yhi_in = sides.at[0, 0:7], sides.at[0, 7:14]
+    pencil = lax.axis_index("pencil")
+    ylo_in = sides.at[jnp.maximum(pencil - 1, 0)]
+    yhi_in = sides.at[jnp.minimum(pencil + 1, sides.shape[0] - 1)]
     totals = []
     for c in range(3):
         total = sums[c : c + 1, :]
@@ -322,13 +324,13 @@
     )(load)
 
 
-def deposit_kernel(cap, inside, load, out, acc, order):
+def deposit_kernel(cap, inside, load, out, order):
     _, cx, cy, nz = out.shape
-    rows = cx * cy // 2
-    cells = 2 * rows * nz
+    rows = cx * cy
+    cells = rows * nz
     n_slab = load.shape[0] // cap
     wide = GROUP * load.shape[2]
-    acc[...] = jnp.zeros_like(acc)
+    out[...] = inside[...]
     listed = jnp.int32(0)
     for d in range(n_slab):
         first = d * cap
@@ -338,51 +340,35 @@
         listed = listed + held
     for k in range(GROUP):
         order[listed + k] = 0
-    def numbers(length):
-        shape = (length // 16, 16, wide)
-        return (lax.broadcasted_iota(jnp.int32, shape, 0) * 16 + lax.broadcasted_iota(jnp.int32, shape, 1)).astype(
-            jnp.float32
-        ).astype(jnp.bfloat16)
-
-    def spread(row):
-        return jnp.broadcast_to(row, (16, wide)).astype(jnp.bfloat16)[None]
-
-    row_numbers = numbers(rows)
-    col_numbers = numbers(nz)
+    shape = (rows // 16, 16, wide)
+    row_numbers = lax.broadcasted_iota(jnp.int32, shape, 0) * 16 + lax.broadcasted_iota(jnp.int32, shape, 1)
+    row_numbers = row_numbers.astype(jnp.float32).astype(jnp.bfloat16)
+    col_numbers = lax.broadcasted_iota(jnp.int32, (wide, nz), 1).astype(jnp.float32).astype(jnp.bfloat16)
     place = lax.broadcasted_iota(jnp.int32, (1, wide), 1) // load.shape[2]
     zero = jnp.zeros((), jnp.bfloat16)
     one = jnp.ones((), jnp.bfloat16)
+
+    def spread(row):
+        return jnp.broadcast_to(row, (16, wide)).astype(jnp.bfloat16)[None]
 
     def group(g, carry):
         tiles = [load[order[g * GROUP + k]] for k in range(GROUP)]
         block = jnp.concatenate(tiles, axis=1)
         live = place < listed - g * GROUP
         cell = block[3:4, :].astype(jnp.int32) % cells
-        row = cell // nz
-        half = row // rows
-        at_row = row_numbers == spread(jnp.where(live, row % rows, -1).astype(jnp.float32))
-        right = []
-        for h in range(2):
-            at_col = col_numbers == spread(jnp.where(half == h, cell % nz, -1).astype(jnp.float32))
-            right.append(jnp.where(at_col, one, zero).reshape(nz, wide))
+        at_row = row_numbers == spread(jnp.where(live, cell // nz, -1).astype(jnp.float32))
+        columns = jnp.transpose(jnp.broadcast_to((cell % nz).astype(jnp.float32), (8, wide)))
+        columns = jnp.broadcast_to(columns[:, 0:1], (wide, nz)).astype(jnp.bfloat16)
+        right = jnp.where(col_numbers == columns, one, zero)
         left = []
         for piece in split(block):
             for c in range(3):
                 left.append(jnp.where(at_row, spread(piece[c : c + 1, :]), zero).reshape(rows, wide))
-        added = lax.dot_general(
-            jnp.concatenate(left, axis=0),
-            jnp.concatenate(right, axis=0),
-            (((1,), (1,)), ((), ())),
-            preferred_element_type=jnp.float32,
-        )
-        acc[...] += added[: 3 * rows] + added[3 * rows :]
+        added = jnp.dot(jnp.concatenate(left, axis=0), right, preferred_element_type=jnp.float32)
+        out[...] += (added[: 3 * rows] + added[3 * rows :]).reshape(out.shape)
         return carry
 
     lax.fori_loop(0, (listed + GROUP - 1) // GROUP, group, 0)
-    for h in range(2):
-        span = slice(h * (cx // 2), (h + 1) * (cx // 2))
-        change = acc[:, h * nz : (h + 1) * nz].reshape(3, cx // 2, cy, nz)
-        out[:, span] = inside[:, span] + change
 
 
 def deposit(inside, load, cap):
@@ -392,7 +378,6 @@
         in_specs=[VMEM] * 2,
         out_specs=VMEM,
         scratch_shapes=[
-            pltpu.VMEM((3 * inside.shape[1] * inside.shape[2] // 2, 2 * inside.shape[3]), jnp.float32),
             pltpu.SMEM((load.shape[0] + max(cap, GROUP),), jnp.int32),
         ],
         compiler_params=PARAMS,
@@ -415,10 +400,10 @@
     xlo, xhi, ylo, yhi, sides, packets, tiles = to_send(
         vorticity, velocity, viscosity, weights, tile_cells, tile_dest.T, tile_count, n_slab, n_pencil, cap
     )
-    sides_in = lax.psum_scatter(sides, "pencil", scatter_dimension=0, tiled=True)
     arrived = lax.all_to_all(packets, "slab", 0, 0, tiled=True)
     xlo_in = shift(xhi, "slab", 1)
     xhi_in = shift(xlo, "slab", -1)
+    sides_in = lax.all_to_all(sides, "pencil", 0, 0, tiled=True)
     inside, sums = inner(vorticity, velocity, viscosity)
     advanced, load = edges(
         inside, sums, tiles, (xlo, xhi, ylo, yhi), (xlo_in, xhi_in, sides_in), n_slab * n_pencil

time: 58.9 us -> 44.5 us (0.76)
  between operations: 14.8 us -> 1.42 us
  waiting for transfers between devices: 11.6 us -> 3.23 us
  Pallas kernels: 11 us -> 17.2 us
  starting transfers between devices: 17.7 us -> 21.2 us
  local copies, waits for them, and re-layouts: 3.06 us -> 0.69 us
    reduce_scatter x1 -> x0, waiting for transfers between devices: 7.25 us -> none  [per_device(): lax.psum_scatter(sides, 'pencil', scatter_dimension=0, tiled=True)]
    pallas_call x1, Pallas kernels: 3.08 us -> 10.2 us  [deposit(): pl.pallas_call(functools.partial(deposit_kernel, cap), out_shape=shaped(*...]
    all_to_all x0 -> x1, starting transfers between devices: none -> 4.33 us  [per_device(): sides_in = lax.all_to_all(sides, 'pencil', 0, 0, tiled=True)]
    all_to_all x1, waiting for transfers between devices: 4.33 us -> 0.01 us  [per_device(): load = lax.all_to_all(load, ('slab', 'pencil'), 0, 0, tiled=True)]
    unnamed x22 -> x16, local copies, waits for them, and re-layouts: 3.06 us -> 0.69 us
    ppermute x2, waiting for transfers between devices: 0.01 us -> 1.78 us  [shift(): return lax.ppermute(array, axis, pairs)]
    ppermute x2, starting transfers between devices: 7.44 us -> 5.94 us  [shift(): return lax.ppermute(array, axis, pairs)]
    all_to_all x1, waiting for transfers between devices: 0.01 us -> 1.45 us  [per_device(): arrived = lax.all_to_all(packets, 'slab', 0, 0, tiled=True)]
  transfers between devices with their start and end apart: 5 -> 5, of which waited for: 2 -> 2; matrix products, arithmetic and copies ran while one was open for 0% -> 0% of each run, Pallas kernels for 13% -> 31%
where the time goes in v1:
time: 44.5 us; the launch traced here: 43.7 us
  starting transfers between devices  21.2 us (48%)
  Pallas kernels  17.2 us (39%)
  waiting for transfers between devices  3.23 us (7%)
  between operations  1.42 us (3%)
  local copies, waits for them, and re-layouts  0.69 us (2%)
    pallas_call x1, Pallas kernels, deposit(): pl.pallas_call(functools.partial(deposit_kernel, cap), out_shape=shaped(*...  10.2 us
    all_to_all x1, starting transfers between devices, per_device(): arrived = lax.all_to_all(packets, 'slab', 0, 0, tiled=True)  6.16 us
    ppermute x2, starting transfers between devices, shift(): return lax.ppermute(array, axis, pairs)  5.94 us
    all_to_all x1, starting transfers between devices, per_device(): load = lax.all_to_all(load, ('slab', 'pencil'), 0, 0, tiled=True)  4.77 us
    all_to_all x1, starting transfers between devices, per_device(): sides_in = lax.all_to_all(sides, 'pencil', 0, 0, tiled=True)  4.33 us
    pallas_call x1, Pallas kernels, to_send(): pl.pallas_call(functools.partial(send_kernel, cap), out_shape=(shaped(7,...  2.85 us
    pallas_call x1, Pallas kernels, inner(): pl.pallas_call(inner_kernel, out_shape=(shaped(*vort.shape), shaped(3, vo...  2.36 us
    ppermute x2, waiting for transfers between devices, shift(): return lax.ppermute(array, axis, pairs)  1.78 us
  transfers between devices with their start and end apart: 5, of which 2 were waited for; matrix products, arithmetic and copies ran while one was open for 0% of the time, Pallas kernels for 31%

profile of v1, /device:TPU:0, one launch (start us, length us, event | category | flops | bytes accessed | tf_op | source)
XLA Modules:
  0.0 43.7 jit_solution(17270807717088942583)
XLA Ops:
  1.3 0.0 copy-start
  1.3 0.0 copy-start.1
  1.3 2.9 %shard_map.87 = (f32[7,32,256]{2,1,0:T(8,128)}, f32[7,32,256]{2,1,0:T(8,128)}, f32[7,8,256]{2,1,0:T(8,128)}, f32[7,8,256]{2,1,0:T(8,128)}, f32[4,7,8,256]{3,2,1,...) custom-call(f32[3,8,32,256]{3,2,1,0:T(8,128)} %vort.3, f32[3,8,32,256]{3,2,1,0:T(8,128)} %velo.3, ...), custom_call_target="tpu_custom_call" | custom-call | tf_op jit(solution)/shard_map/pallas_call | solution.py:142
  4.2 0.0 copy-start.2
  4.2 4.3 %all-to-all-start = ((f32[4,7,8,256]{3,2,1,0:T(8,128)}), f32[4,7,8,256]{3,2,1,0:T(8,128)S(1)}, u32[]{:S(2)}, u32[]{:S(2)}) async-start(f32[4,7,8,256]{3,2,1,0:T(8,128)} %get-tuple-element.20), calls=%async_computation | async-start | bytes 458752 | tf_op jit(solution)/shard_map/all_to_all | solution.py:406
  8.5 1.3 %collective-permute-start.1 = (f32[7,32,256]{2,1,0:T(8,128)}, f32[7,32,256]{2,1,0:T(8,128)S(1)}, u32[]{:S(2)}, u32[]{:S(2)}) collective-permute-start(f32[7,32,256]{2,1,0:T(8,128)} %get-tuple-element.16.xlo), channel_id=1, source_target_pairs={{4,0},{8,4},{12,8},{16,12},{20,16},{24,20},{28,24},{5,1},{9,5},{13... | collective-permute-start | bytes 688136 | tf_op jit(solution)/shard_map/ppermute | solution.py:390
  9.8 4.7 %collective-permute-start = (f32[7,32,256]{2,1,0:T(8,128)}, f32[7,32,256]{2,1,0:T(8,128)S(1)}, u32[]{:S(2)}, u32[]{:S(2)}) collective-permute-start(f32[7,32,256]{2,1,0:T(8,128)} %get-tuple-element.17.xhi), channel_id=1, source_target_pairs={{0,4},{4,8},{8,12},{12,16},{16,20},{20,24},{24,28},{1,5},{5,9},{9,... | collective-permute-start | bytes 688136 | tf_op jit(solution)/shard_map/ppermute | solution.py:390
  14.5 0.0 all-to-all-done.sides
  14.5 6.2 %all-to-all-start.1 = ((f32[64,4,128]{2,1,0:T(4,128)}), f32[64,4,128]{2,1,0:T(4,128)S(1)}, u32[]{:S(2)}, u32[]{:S(2)}) async-start(f32[64,4,128]{2,1,0:T(4,128)} %get-tuple-element.22), calls=%async_computation.1 | async-start | bytes 262144 | tf_op jit(solution)/shard_map/all_to_all | solution.py:403
  20.7 0.0 copy-start.3
  20.7 0.0 copy-start.4
  20.7 0.0 copy-start.5
  20.7 0.0 copy-start.6
  20.7 2.4 %shard_map.86 = (f32[3,8,32,256]{3,2,1,0:T(8,128)S(1)}, f32[3,256]{1,0:T(4,128)S(1)}) custom-call(f32[3,8,32,256]{3,2,1,0:T(8,128)S(1)} %copy-done, f32[3,8,32,256]{3,2,1,0:T(8,128)S(1)} %copy-done.1, f32[8,32,256]{2,1,0:T(8,128)S(1)} %copy-done.2), custom_call_target="tpu_custom_call" | custom-call | tf_op jit(solution)/shard_map/pallas_call | solution.py:221
  23.1 0.0 collective-permute-done.1.xhi_in
  23.1 1.8 %collective-permute-done.xlo_in = f32[7,32,256]{2,1,0:T(8,128)S(1)} collective-permute-done((f32[7,32,256]{2,1,0:T(8,128)}, f32[7,32,256]{2,1,0:T(8,128)S(1)}, u32[]{:S(2)}, u32[]{:S(2)}) %collective-permute-start) | collective-permute-done | bytes 229408 | tf_op jit(solution)/shard_map/ppermute | solution.py:390
  24.9 0.0 copy-done.6
  24.9 0.7 %copy-done.7 = f32[4,128]{1,0:T(4,128)S(1)} copy-done((f32[4,128]{1,0:T(4,128)S(1)}, f32[4,128]{1,0:T(4,128)}, u32[]{:S(2)}) %copy-start.7) | copy-done | bytes 2072
  25.5 1.0 %shard_map.88 = (f32[3,8,32,256]{3,2,1,0:T(8,128)S(1)}, f32[32,4,128]{2,1,0:T(4,128)}) custom-call(f32[3,8,32,256]{3,2,1,0:T(8,128)S(1)} %get-tuple-element.13.inside, f32[3,256]{1,0:T(4,128)S(1)} %get-tuple-element.14.sums, f32[4,128]{1,0:T(4,128)S(1)} %copy-done.7, f32[7,32,256]{2,1,0:T(8,128)S(1)} %copy-done.3, f32[7,32,256]{2,1,0:T(8,128)S(1)} %copy-done.4, ...), custom_call_target="tpu_custom_call" | custom-call | tf_op jit(solution)/shard_map/pallas_call | solution.py:271
  26.5 1.4 %all-to-all-done.1.load = f32[64,4,128]{2,1,0:T(4,128)S(1)} async-done(((f32[64,4,128]{2,1,0:T(4,128)}), f32[64,4,128]{2,1,0:T(4,128)S(1)}, u32[]{:S(2)}, u32[]{:S(2)}) %all-to-all-start.1) | async-done | bytes 131104 | tf_op jit(solution)/shard_map/all_to_all | solution.py:403
  28.0 4.8 %all-to-all-start.2 = ((f32[32,4,128]{2,1,0:T(4,128)}), f32[32,4,128]{2,1,0:T(4,128)S(1)}, u32[]{:S(2)}, u32[]{:S(2)}) async-start(f32[32,4,128]{2,1,0:T(4,128)} %get-tuple-element.23), calls=%async_computation.2 | async-start | bytes 131072 | tf_op jit(solution)/shard_map/all_to_all | solution.py:411
  32.7 10.2 %shard_map.89 = f32[3,8,32,256]{3,2,1,0:T(8,128)} custom-call(f32[3,8,32,256]{3,2,1,0:T(8,128)S(1)} %get-tuple-element.21.inside, f32[64,4,128]{2,1,0:T(4,128)S(1)} %all-to-all-done.1.load), custom_call_target="tpu_custom_call" | custom-call | tf_op jit(solution)/shard_map/pallas_call | solution.py:375
  43.0 0.0 all-to-all-done.2.load
  43.0 0.7 %shard_map.90 = f32[3,1,1,16]{3,2,1,0:T(1,128)} custom-call(f32[32,4,128]{2,1,0:T(4,128)S(1)} %all-to-all-done.2.load), custom_call_target="tpu_custom_call" | custom-call | tf_op jit(solution)/shard_map/pallas_call | solution.py:318
  (7 shorter events, 0.0 us)
Async XLA Ops:
  1.3 19.4 %copy-start = (f32[3,8,32,256]{3,2,1,0:T(8,128)S(1)}, f32[3,8,32,256]{3,2,1,0:T(8,128)}, u32[]{:S(2)}) copy-start(f32[3,8,32,256]{3,2,1,0:T(8,128)} %vort.3) | copy-start | bytes 2359300
  1.3 19.3 %copy-start.1 = (f32[3,8,32,256]{3,2,1,0:T(8,128)S(1)}, f32[3,8,32,256]{3,2,1,0:T(8,128)}, u32[]{:S(2)}) copy-start(f32[3,8,32,256]{3,2,1,0:T(8,128)} %velo.3) | copy-start | bytes 2359300
  4.2 16.5 %copy-start.2 = (f32[8,32,256]{2,1,0:T(8,128)S(1)}, f32[8,32,256]{2,1,0:T(8,128)}, u32[]{:S(2)}) copy-start(f32[8,32,256]{2,1,0:T(8,128)} %visc.3) | copy-start | bytes 786436
  4.2 10.3 %all-to-all-start = ((f32[4,7,8,256]{3,2,1,0:T(8,128)}), f32[4,7,8,256]{3,2,1,0:T(8,128)S(1)}, u32[]{:S(2)}, u32[]{:S(2)}) async-start(f32[4,7,8,256]{3,2,1,0:T(8,128)} %get-tuple-element.20), calls=%async_computation | async-start | bytes 458752 | tf_op jit(solution)/shard_map/all_to_all | solution.py:406
  8.5 14.6 %collective-permute-start.1 = (f32[7,32,256]{2,1,0:T(8,128)}, f32[7,32,256]{2,1,0:T(8,128)S(1)}, u32[]{:S(2)}, u32[]{:S(2)}) collective-permute-start(f32[7,32,256]{2,1,0:T(8,128)} %get-tuple-element.16.xlo), channel_id=1, source_target_pairs={{4,0},{8,4},{12,8},{16,12},{20,16},{24,20},{28,24},{5,1},{9,5},{13... | collective-permute-start | bytes 688136 | tf_op jit(solution)/shard_map/ppermute | solution.py:390
  9.8 15.1 %collective-permute-start = (f32[7,32,256]{2,1,0:T(8,128)}, f32[7,32,256]{2,1,0:T(8,128)S(1)}, u32[]{:S(2)}, u32[]{:S(2)}) collective-permute-start(f32[7,32,256]{2,1,0:T(8,128)} %get-tuple-element.17.xhi), channel_id=1, source_target_pairs={{0,4},{4,8},{8,12},{12,16},{16,20},{20,24},{24,28},{1,5},{5,9},{9,... | collective-permute-start | bytes 688136 | tf_op jit(solution)/shard_map/ppermute | solution.py:390
  14.5 13.5 %all-to-all-start.1 = ((f32[64,4,128]{2,1,0:T(4,128)}), f32[64,4,128]{2,1,0:T(4,128)S(1)}, u32[]{:S(2)}, u32[]{:S(2)}) async-start(f32[64,4,128]{2,1,0:T(4,128)} %get-tuple-element.22), calls=%async_computation.1 | async-start | bytes 262144 | tf_op jit(solution)/shard_map/all_to_all | solution.py:403
  20.7 4.2 %copy-start.3 = (f32[7,32,256]{2,1,0:T(8,128)S(1)}, f32[7,32,256]{2,1,0:T(8,128)}, u32[]{:S(2)}) copy-start(f32[7,32,256]{2,1,0:T(8,128)} %get-tuple-element.16.xlo) | copy-start | bytes 688132
  20.7 4.2 %copy-start.4 = (f32[7,32,256]{2,1,0:T(8,128)S(1)}, f32[7,32,256]{2,1,0:T(8,128)}, u32[]{:S(2)}) copy-start(f32[7,32,256]{2,1,0:T(8,128)} %get-tuple-element.17.xhi) | copy-start | bytes 688132
  20.7 4.2 %copy-start.5 = (f32[7,8,256]{2,1,0:T(8,128)S(1)}, f32[7,8,256]{2,1,0:T(8,128)}, u32[]{:S(2)}) copy-start(f32[7,8,256]{2,1,0:T(8,128)} %get-tuple-element.18.ylo) | copy-start | bytes 172036
  20.7 4.2 %copy-start.6 = (f32[7,8,256]{2,1,0:T(8,128)S(1)}, f32[7,8,256]{2,1,0:T(8,128)}, u32[]{:S(2)}) copy-start(f32[7,8,256]{2,1,0:T(8,128)} %get-tuple-element.19.yhi) | copy-start | bytes 172036
  24.9 0.7 %copy-start.7 = (f32[4,128]{1,0:T(4,128)S(1)}, f32[4,128]{1,0:T(4,128)}, u32[]{:S(2)}) copy-start(f32[4,128]{1,0:T(4,128)} %get-tuple-element.15.tiles) | copy-start | bytes 6148
  28.0 15.0 %all-to-all-start.2 = ((f32[32,4,128]{2,1,0:T(4,128)}), f32[32,4,128]{2,1,0:T(4,128)S(1)}, u32[]{:S(2)}, u32[]{:S(2)}) async-start(f32[32,4,128]{2,1,0:T(4,128)} %get-tuple-element.23), calls=%async_computation.2 | async-start | bytes 131072 | tf_op jit(solution)/shard_map/all_to_all | solution.py:411

commit v2 on v0

--- a/solution.py
+++ b/solution.py
@@ -10,7 +10,7 @@
 CB = 16
 TIME_STEP = 0.1
 LANES = 128
-GROUP = 4
+GROUP = 8
 VMEM_LIMIT = 48 * 1024 * 1024
 
 VMEM = pl.BlockSpec(memory_space=pltpu.VMEM)
@@ -46,6 +46,41 @@
     moments[...] = jnp.concatenate(found, axis=1)
 
 
+class Copies:
+    def __init__(self, sems):
+        self.sems = sems
+        self.made = []
+
+    def start(self, source, target):
+        self.made.append(pltpu.make_async_copy(source, target, self.sems.at[len(self.made)]))
+        self.made[-1].start()
+
+    def wait(self, first, last):
+        for k in range(first, last):
+            self.made[k].wait()
+
+
+def slab_kernel(vort, velo, visc, xlo, xhi, sems):
+    copies = Copies(sems)
+    for face, at in ((xlo, 0), (xhi, visc.shape[0] - 1)):
+        copies.start(vort.at[:, at], face.at[0:3])
+        copies.start(velo.at[:, at], face.at[3:6])
+        copies.start(visc.at[at], face.at[6])
+    copies.wait(0, 6)
+
+
+def slab_faces(vort, velo, visc):
+    _, _, cy, nz = vort.shape
+    return pl.pallas_call(
+        slab_kernel,
+        out_shape=(shaped(7, cy, nz), shaped(7, cy, nz)),
+        in_specs=[ANY] * 3,
+        out_specs=(VMEM,) * 2,
+        scratch_shapes=[pltpu.SemaphoreType.DMA((6,))],
+        compiler_params=FIRST_PARAMS,
+    )(vort, velo, visc)
+
+
 def send_kernel(
     cap,
     vort,
@@ -55,11 +90,9 @@
     cells_in,
     dest_in,
     count_in,
-    xlo,
-    xhi,
+    earlier,
     ylo,
     yhi,
-    sides,
     packets,
     moments,
     spin_rows,
@@ -73,31 +106,21 @@
     sems,
 ):
     cx, cy, nz = visc.shape
-    copies = []
-
-    def copy(source, target):
-        copies.append(pltpu.make_async_copy(source, target, sems.at[len(copies)]))
-        copies[-1].start()
-
-    copy(weights_in, weights)
-    copy(cells_in, cells)
-    copy(dest_in, dest)
-    copy(count_in, count)
+    copies = Copies(sems)
+    copies.start(weights_in, weights)
+    copies.start(cells_in, cells)
+    copies.start(dest_in, dest)
+    copies.start(count_in, count)
     for k, at in ((0, 0), (1, cy - 8)):
-        copy(vort.at[:, :, pl.ds(at, 8), :], spin_rows.at[k])
-        copy(velo.at[:, :, pl.ds(at, 8), :], velo_rows.at[k])
-        copy(visc.at[:, pl.ds(at, 8), :], visc_rows.at[k])
-    for face, at in ((xlo, 0), (xhi, cx - 1)):
-        copy(vort.at[:, at], face.at[0:3])
-        copy(velo.at[:, at], face.at[3:6])
-        copy(visc.at[at], face.at[6])
+        copies.start(vort.at[:, :, pl.ds(at, 8), :], spin_rows.at[k])
+        copies.start(velo.at[:, :, pl.ds(at, 8), :], velo_rows.at[k])
+        copies.start(visc.at[:, pl.ds(at, 8), :], visc_rows.at[k])
 
     packets[...] = jnp.zeros_like(packets)
     n_slab = packets.shape[0] // cap
     for d in range(n_slab):
         filled[d] = 0
-    for k in range(4):
-        copies[k].wait()
+    copies.wait(0, 4)
 
     def place(r, carry):
         d = dest[0, r]
@@ -114,44 +137,27 @@
         held = (filled[d] * (cx * cy * nz)).astype(jnp.float32)
         packets[d * cap, 3:4, :] = packets[d * cap, 3:4, :] + held
     tile_moments(cap, nz, packets, moments)
-    sides[...] = jnp.zeros_like(sides)
-    for k in range(4, 10):
-        copies[k].wait()
+    copies.wait(4, 10)
     for k, face, at in ((0, ylo, 0), (1, yhi, 7)):
         for x in range(cx):
             for c in range(3):
                 face[c, x : x + 1, :] = spin_rows[k, c, x, at : at + 1, :]
                 face[3 + c, x : x + 1, :] = velo_rows[k, c, x, at : at + 1, :]
             face[6, x : x + 1, :] = visc_rows[k, x, at : at + 1, :]
-    pencil = lax.axis_index("pencil")
-
-    @pl.when(pencil < sides.shape[0] - 1)
-    def _():
-        sides[pencil + 1, 0:7] = yhi[...]
-
-    @pl.when(pencil > 0)
-    def _():
-        sides[pencil - 1, 7:14] = ylo[...]
-
-    for k in range(10, 16):
-        copies[k].wait()
-
-
-def to_send(vort, velo, visc, weights, cells, dest, count, n_slab, n_pencil, cap):
+
+
+def to_send(vort, velo, visc, weights, cells, dest, count, earlier, n_slab, cap):
     _, cx, cy, nz = vort.shape
     return pl.pallas_call(
         functools.partial(send_kernel, cap),
         out_shape=(
-            shaped(7, cy, nz),
-            shaped(7, cy, nz),
             shaped(7, cx, nz),
             shaped(7, cx, nz),
-            shaped(n_pencil, 14, cx, nz),
             shaped(n_slab * cap, 4, weights.shape[2]),
             shaped(4, n_slab * nz // CB),
         ),
-        in_specs=[ANY] * 7,
-        out_specs=(VMEM,) * 7,
+        in_specs=[ANY] * 8,
+        out_specs=(VMEM,) * 4,
         scratch_shapes=[
             pltpu.VMEM((2, 3, cx, 8, nz), jnp.float32),
             pltpu.VMEM((2, 3, cx, 8, nz), jnp.float32),
@@ -161,10 +167,10 @@
             pltpu.SMEM(dest.shape, jnp.int32),
             pltpu.SMEM(count.shape, jnp.int32),
             pltpu.SMEM((n_slab,), jnp.int32),
-            pltpu.SemaphoreType.DMA((16,)),
+            pltpu.SemaphoreType.DMA((10,)),
         ],
         compiler_params=FIRST_PARAMS,
-    )(vort, velo, visc, weights, cells, dest, count)
+    )(vort, velo, visc, weights, cells, dest, count, earlier)
 
 
 def ahead(a, axis):
@@ -211,20 +217,35 @@
             out[c, x] = w + TIME_STEP * (stretch + change)
 
 
-def inner_kernel(vort, velo, visc, out, sums):
+def by_level(totals, width):
+    nz = totals[0].shape[1]
+    shape = (nz, width)
+    level = lax.broadcasted_iota(jnp.int32, shape, 0) // CB
+    lane = lax.broadcasted_iota(jnp.int32, shape, 1)
+    pick = (lane == lax.axis_index("slab") * (nz // CB) + level).astype(jnp.float32)
+    rows = jnp.concatenate(totals + [jnp.zeros_like(totals[0])], axis=0)
+    return jnp.dot(rows, pick, precision=lax.Precision.HIGHEST, preferred_element_type=jnp.float32)
+
+
+def inner_kernel(vort, velo, visc, tiles_in, out, moments, tiles, sem):
+    copy = pltpu.make_async_copy(tiles_in, tiles, sem)
+    copy.start()
     interior_step(vort, velo, visc, out)
-    for c in range(3):
-        sums[c : c + 1, :] = jnp.sum(out[c].reshape(-1, out.shape[3]), axis=0, keepdims=True)
-
-
-def inner(vort, velo, visc):
+    totals = [jnp.sum(out[c].reshape(-1, out.shape[3]), axis=0, keepdims=True) for c in range(3)]
+    own = by_level(totals, moments.shape[1])
+    copy.wait()
+    moments[...] = tiles[...] + own
+
+
+def inner(vort, velo, visc, tiles):
     return pl.pallas_call(
         inner_kernel,
-        out_shape=(shaped(*vort.shape), shaped(3, vort.shape[3])),
-        in_specs=[VMEM] * 3,
+        out_shape=(shaped(*vort.shape), shaped(*tiles.shape)),
+        in_specs=[VMEM] * 3 + [ANY],
         out_specs=(VMEM,) * 2,
+        scratch_shapes=[pltpu.VMEM(tiles.shape, jnp.float32), pltpu.SemaphoreType.DMA],
         compiler_params=PARAMS,
-    )(vort, velo, visc)
+    )(vort, velo, visc, tiles)
 
 
 def face_change(own, other, along, sign, c):
@@ -233,13 +254,12 @@
     return TIME_STEP * (stretch + diffuse)
 
 
-def edge_kernel(inside, sums, tiles, xlo, xhi, ylo, yhi, xlo_in, xhi_in, sides, out, load):
+def edge_kernel(inside, moments, xlo, xhi, ylo, yhi, xlo_in, xhi_in, ylo_in, yhi_in, out, load):
     _, cx, cy, nz = out.shape
     out[...] = inside[...]
-    ylo_in, yhi_in = sides.at[0, 0:7], sides.at[0, 7:14]
     totals = []
     for c in range(3):
-        total = sums[c : c + 1, :]
+        total = jnp.zeros((1, nz), jnp.float32)
         for own, other, at, sign in ((xlo, xlo_in, 0, -1.0), (xhi, xhi_in, cx - 1, 1.0)):
             change = face_change(own, other, 0, sign, c)
             out[c, at] = out[c, at] + change
@@ -250,29 +270,21 @@
                 out[c, x, at : at + 1, :] = out[c, x, at : at + 1, :] + change[x : x + 1, :]
             total = total + jnp.sum(change, axis=0, keepdims=True)
         totals.append(total)
-    totals.append(jnp.zeros_like(totals[0]))
-    shape = (nz, tiles.shape[1])
-    level = lax.broadcasted_iota(jnp.int32, shape, 0) // CB
-    lane = lax.broadcasted_iota(jnp.int32, shape, 1)
-    own_slab = lax.axis_index("slab")
-    pick = (lane == own_slab * (nz // CB) + level).astype(jnp.float32)
-    moment = tiles[...] + jnp.dot(
-        jnp.concatenate(totals, axis=0), pick, precision=lax.Precision.HIGHEST, preferred_element_type=jnp.float32
-    )
+    moment = moments[...] + by_level(totals, moments.shape[1])
     for k in range(load.shape[1] // 4):
         part = moment[:, k * LANES : (k + 1) * LANES]
         for j in range(load.shape[0]):
             load[j, 4 * k : 4 * k + 4, :] = part
 
 
-def edges(inside, sums, tiles, faces, halos, n_all):
+def edges(inside, moments, faces, halos, n_all):
     return pl.pallas_call(
         edge_kernel,
-        out_shape=(shaped(*inside.shape), shaped(n_all, 4 * tiles.shape[1] // LANES, LANES)),
+        out_shape=(shaped(*inside.shape), shaped(n_all, 4 * moments.shape[1] // LANES, LANES)),
         in_specs=[VMEM] * 10,
         out_specs=(VMEM,) * 2,
         compiler_params=PARAMS,
-    )(inside, sums, tiles, *faces, *halos)
+    )(inside, moments, *faces, *halos)
 
 
 def far_kernel(cx, cy, ncl, n_pencil, load, out):
@@ -412,16 +424,18 @@
     n_pencil = lax.axis_size("pencil")
     cap = 2 * tile_weights.shape[0] // n_slab
     weights = jnp.transpose(tile_weights, (1, 0, 2))
-    xlo, xhi, ylo, yhi, sides, packets, tiles = to_send(
-        vorticity, velocity, viscosity, weights, tile_cells, tile_dest.T, tile_count, n_slab, n_pencil, cap
+    xlo, xhi = slab_faces(vorticity, velocity, viscosity)
+    xhi_in = shift(xlo, "slab", -1)
+    xlo_in = shift(xhi, "slab", 1)
+    ylo, yhi, packets, tiles = to_send(
+        vorticity, velocity, viscosity, weights, tile_cells, tile_dest.T, tile_count, xhi, n_slab, cap
     )
-    sides_in = lax.psum_scatter(sides, "pencil", scatter_dimension=0, tiled=True)
     arrived = lax.all_to_all(packets, "slab", 0, 0, tiled=True)
-    xlo_in = shift(xhi, "slab", 1)
-    xhi_in = shift(xlo, "slab", -1)
-    inside, sums = inner(vorticity, velocity, viscosity)
+    ylo_in = shift(yhi, "pencil", 1)
+    yhi_in = shift(ylo, "pencil", -1)
+    inside, moments = inner(vorticity, velocity, viscosity, tiles)
     advanced, load = edges(
-        inside, sums, tiles, (xlo, xhi, ylo, yhi), (xlo_in, xhi_in, sides_in), n_slab * n_pencil
+        inside, moments, (xlo, xhi, ylo, yhi), (xlo_in, xhi_in, ylo_in, yhi_in), n_slab * n_pencil
     )
     load = lax.all_to_all(load, ("slab", "pencil"), 0, 0, tiled=True)
     vorticity_out = deposit(advanced, arrived, cap)

time: 58.9 us -> 42.3 us (0.72)
  between operations: 14.8 us -> 1.49 us
  waiting for transfers between devices: 11.6 us -> 4.16 us
  starting transfers between devices: 17.7 us -> 24.3 us
  local copies, waits for them, and re-layouts: 3.06 us -> 0.04 us
  Pallas kernels: 11 us -> 11.8 us
    reduce_scatter x1 -> x0, waiting for transfers between devices: 7.25 us -> none  [per_device(): lax.psum_scatter(sides, 'pencil', scatter_dimension=0, tiled=True)]
    ppermute x2 -> x4, starting transfers between devices: 7.44 us -> 11.1 us  [shift(): return lax.ppermute(array, axis, pairs)]
    unnamed x22 -> x16, local copies, waits for them, and re-layouts: 3.06 us -> 0.04 us
    all_to_all x1, starting transfers between devices: 4.61 us -> 7.08 us  [per_device(): load = lax.all_to_all(load, ('slab', 'pencil'), 0, 0, tiled=True)]
    pallas_call x1 -> x2, Pallas kernels: 2.36 us -> 4.2 us  [the longest x1 2.34 us: inner(): pl.pallas_call(inner_kernel, out_shape=(shaped(*vort.shape), shaped(*tile...]
    pallas_call x1, Pallas kernels: 1.92 us -> 0.98 us  [edges(): pl.pallas_call(edge_kernel, out_shape=(shaped(*inside.shape), shaped(n_al...]
    all_to_all x1, starting transfers between devices: 5.56 us -> 6.17 us  [per_device(): arrived = lax.all_to_all(packets, 'slab', 0, 0, tiled=True)]
  transfers between devices with their start and end apart: 5 -> 6, of which waited for: 2 -> 1; matrix products, arithmetic and copies ran while one was open for 0% -> 0% of each run, Pallas kernels for 13% -> 22%
where the time goes in v2:
time: 42.3 us; the launch traced here: 41.8 us
  starting transfers between devices  24.3 us (57%)
  Pallas kernels  11.8 us (28%)
  waiting for transfers between devices  4.16 us (10%)
  between operations  1.49 us (4%)
    ppermute x4, starting transfers between devices, shift(): return lax.ppermute(array, axis, pairs)  11.1 us
    all_to_all x1, starting transfers between devices, per_device(): load = lax.all_to_all(load, ('slab', 'pencil'), 0, 0, tiled=True)  7.08 us
    all_to_all x1, starting transfers between devices, per_device(): arrived = lax.all_to_all(packets, 'slab', 0, 0, tiled=True)  6.17 us
    all_to_all x1, waiting for transfers between devices, per_device(): load = lax.all_to_all(load, ('slab', 'pencil'), 0, 0, tiled=True)  4.15 us
    pallas_call x1, Pallas kernels, deposit(): pl.pallas_call(functools.partial(deposit_kernel, cap), out_shape=shaped(*...  3.26 us
    pallas_call x1, Pallas kernels, to_send(): pl.pallas_call(functools.partial(send_kernel, cap), out_shape=(shaped(7,...  2.59 us
    pallas_call x1, Pallas kernels, inner(): pl.pallas_call(inner_kernel, out_shape=(shaped(*vort.shape), shaped(*tile...  2.34 us
    pallas_call x1, Pallas kernels, slab_faces(): pl.pallas_call(slab_kernel, out_shape=(shaped(7, cy, nz), shaped(7, cy, n...  1.86 us
  transfers between devices with their start and end apart: 6, of which 1 were waited for; matrix products, arithmetic and copies ran while one was open for 0% of the time, Pallas kernels for 22%

profile of v2, /device:TPU:0, one launch (start us, length us, event | category | flops | bytes accessed | tf_op | source)
XLA Modules:
  0.0 41.8 jit_solution(5867166219787016305)
XLA Ops:
  0.6 1.9 %shard_map.86 = (f32[7,32,256]{2,1,0:T(8,128)}, f32[7,32,256]{2,1,0:T(8,128)}) custom-call(f32[3,8,32,256]{3,2,1,0:T(8,128)} %vort.5, f32[3,8,32,256]{3,2,1,0:T(8,128)} %velo.5, f32[8,32,256]{2,1,0:T(8,128)} %visc.5), custom_call_target="tpu_custom_call" | custom-call | tf_op jit(solution)/shard_map/pallas_call | solution.py:74
  2.5 1.3 %collective-permute-start.1 = (f32[7,32,256]{2,1,0:T(8,128)}, f32[7,32,256]{2,1,0:T(8,128)S(1)}, u32[]{:S(2)}, u32[]{:S(2)}) collective-permute-start(f32[7,32,256]{2,1,0:T(8,128)} %get-tuple-element.16.xlo), channel_id=1, source_target_pairs={{4,0},{8,4},{12,8},{16,12},{20,16},{24,20},{28,24},{5,1},{9,5},{13... | collective-permute-start | bytes 688136 | tf_op jit(solution)/shard_map/ppermute | solution.py:417
  3.8 5.5 %collective-permute-start = (f32[7,32,256]{2,1,0:T(8,128)}, f32[7,32,256]{2,1,0:T(8,128)S(1)}, u32[]{:S(2)}, u32[]{:S(2)}) collective-permute-start(f32[7,32,256]{2,1,0:T(8,128)} %get-tuple-element.12.earlier.xhi), channel_id=1, source_target_pairs={{0,4},{4,8},{8,12},{12,16},{16,20},{20,24},{24,28},{1,5},{5,9},{9,... | collective-permute-start | bytes 688136 | tf_op jit(solution)/shard_map/ppermute | solution.py:417
  9.9 0.0 copy-start
  9.9 0.0 copy-start.1
  10.0 2.6 %shard_map.87 = (f32[7,8,256]{2,1,0:T(8,128)}, f32[7,8,256]{2,1,0:T(8,128)}, f32[64,4,128]{2,1,0:T(4,128)}, f32[4,128]{1,0:T(4,128)}) custom-call(f32[3,8,32,256]{3,2,1,0:T(8,128)} %vort.5, f32[3,8,32,256]{3,2,1,0:T(8,128)} %velo.5, f32[8,32,256]{2,1,0:T(8,128)} %visc.5, f32[3,32,128]{2,1,0:T(8,128)} %bitcast.2, s32[32,128]{1,0:T(8,128)} %cells_in.1, ...), custom_call_target="tpu_custom_call" | custom-call | tf_op jit(solution)/shard_map/pallas_call | solution.py:151
  12.6 0.0 copy-start.2
  12.6 6.2 %all-to-all-start = ((f32[64,4,128]{2,1,0:T(4,128)}), f32[64,4,128]{2,1,0:T(4,128)S(1)}, u32[]{:S(2)}, u32[]{:S(2)}) async-start(f32[64,4,128]{2,1,0:T(4,128)} %get-tuple-element.20), calls=%async_computation | async-start | bytes 262144 | tf_op jit(solution)/shard_map/all_to_all | solution.py:433
  18.7 1.3 %collective-permute-start.3 = (f32[7,8,256]{2,1,0:T(8,128)}, f32[7,8,256]{2,1,0:T(8,128)S(1)}, u32[]{:S(2)}, u32[]{:S(2)}) collective-permute-start(f32[7,8,256]{2,1,0:T(8,128)} %get-tuple-element.17.ylo), channel_id=1, source_target_pairs={{1,0},{2,1},{3,2},{5,4},{6,5},{7,6},{9,8},{10,9},{11,10},{13,12},{... | collective-permute-start | bytes 172040 | tf_op jit(solution)/shard_map/ppermute | solution.py:417
  20.0 3.0 %collective-permute-start.2 = (f32[7,8,256]{2,1,0:T(8,128)}, f32[7,8,256]{2,1,0:T(8,128)S(1)}, u32[]{:S(2)}, u32[]{:S(2)}) collective-permute-start(f32[7,8,256]{2,1,0:T(8,128)} %get-tuple-element.18.yhi), channel_id=1, source_target_pairs={{0,1},{1,2},{2,3},{4,5},{5,6},{6,7},{8,9},{9,10},{10,11},{12,13},{... | collective-permute-start | bytes 172040 | tf_op jit(solution)/shard_map/ppermute | solution.py:417
  23.1 0.0 copy-done
  23.1 0.0 copy-done.1
  23.1 0.0 copy-start.4
  23.2 2.3 %shard_map.88 = (f32[3,8,32,256]{3,2,1,0:T(8,128)S(1)}, f32[4,128]{1,0:T(4,128)S(1)}) custom-call(f32[3,8,32,256]{3,2,1,0:T(8,128)S(1)} %copy-done, f32[3,8,32,256]{3,2,1,0:T(8,128)S(1)} %copy-done.1, f32[8,32,256]{2,1,0:T(8,128)S(1)} %copy-done.2, f32[4,128]{1,0:T(4,128)S(1)} %copy-done.7), custom_call_target="tpu_custom_call" | custom-call | tf_op jit(solution)/shard_map/pallas_call | solution.py:241
  25.5 0.0 collective-permute-done.3.yhi_in
  25.5 0.0 collective-permute-done.2.ylo_in
  25.5 0.0 collective-permute-done.1.xhi_in
  25.6 0.0 collective-permute-done.xlo_in
  25.6 1.0 %shard_map.89 = (f32[3,8,32,256]{3,2,1,0:T(8,128)S(1)}, f32[32,4,128]{2,1,0:T(4,128)}) custom-call(f32[3,8,32,256]{3,2,1,0:T(8,128)S(1)} %get-tuple-element.14.inside, f32[4,128]{1,0:T(4,128)S(1)} %get-tuple-element.15.moments, f32[7,32,256]{2,1,0:T(8,128)S(1)} %copy-done.4, f32[7,32,256]{2,1,0:T(8,128)S(1)} %copy-done.3, f32[7,8,256]{2,1,0:T(8,128)S(1)} %copy-done.5, ...), custom_call_target="tpu_custom_call" | custom-call | tf_op jit(solution)/shard_map/pallas_call | solution.py:281
  26.6 0.0 all-to-all-done.load
  26.6 7.1 %all-to-all-start.1 = ((f32[32,4,128]{2,1,0:T(4,128)}), f32[32,4,128]{2,1,0:T(4,128)S(1)}, u32[]{:S(2)}, u32[]{:S(2)}) async-start(f32[32,4,128]{2,1,0:T(4,128)} %get-tuple-element.21), calls=%async_computation.1 | async-start | bytes 131072 | tf_op jit(solution)/shard_map/all_to_all | solution.py:440
  33.7 3.3 %shard_map.90 = f32[3,8,32,256]{3,2,1,0:T(8,128)} custom-call(f32[3,8,32,256]{3,2,1,0:T(8,128)S(1)} %get-tuple-element.19.inside, f32[64,4,128]{2,1,0:T(4,128)S(1)} %all-to-all-done.load), custom_call_target="tpu_custom_call" | custom-call | tf_op jit(solution)/shard_map/pallas_call | solution.py:401
  36.9 4.1 %all-to-all-done.1.load = f32[32,4,128]{2,1,0:T(4,128)S(1)} async-done(((f32[32,4,128]{2,1,0:T(4,128)}), f32[32,4,128]{2,1,0:T(4,128)S(1)}, u32[]{:S(2)}, u32[]{:S(2)}) %all-to-all-start.1) | async-done | bytes 65568 | tf_op jit(solution)/shard_map/all_to_all | solution.py:440
  41.1 0.7 %shard_map.91 = f32[3,1,1,16]{3,2,1,0:T(1,128)} custom-call(f32[32,4,128]{2,1,0:T(4,128)S(1)} %all-to-all-done.1.load), custom_call_target="tpu_custom_call" | custom-call | tf_op jit(solution)/shard_map/pallas_call | solution.py:328
  (10 shorter events, 0.0 us)
Async XLA Ops:
  2.5 23.0 %collective-permute-start.1 = (f32[7,32,256]{2,1,0:T(8,128)}, f32[7,32,256]{2,1,0:T(8,128)S(1)}, u32[]{:S(2)}, u32[]{:S(2)}) collective-permute-start(f32[7,32,256]{2,1,0:T(8,128)} %get-tuple-element.16.xlo), channel_id=1, source_target_pairs={{4,0},{8,4},{12,8},{16,12},{20,16},{24,20},{28,24},{5,1},{9,5},{13... | collective-permute-start | bytes 688136 | tf_op jit(solution)/shard_map/ppermute | solution.py:417
  3.8 21.8 %collective-permute-start = (f32[7,32,256]{2,1,0:T(8,128)}, f32[7,32,256]{2,1,0:T(8,128)S(1)}, u32[]{:S(2)}, u32[]{:S(2)}) collective-permute-start(f32[7,32,256]{2,1,0:T(8,128)} %get-tuple-element.12.earlier.xhi), channel_id=1, source_target_pairs={{0,4},{4,8},{8,12},{12,16},{16,20},{20,24},{24,28},{1,5},{5,9},{9,... | collective-permute-start | bytes 688136 | tf_op jit(solution)/shard_map/ppermute | solution.py:417
  9.9 13.2 %copy-start = (f32[3,8,32,256]{3,2,1,0:T(8,128)S(1)}, f32[3,8,32,256]{3,2,1,0:T(8,128)}, u32[]{:S(2)}) copy-start(f32[3,8,32,256]{3,2,1,0:T(8,128)} %vort.5) | copy-start | bytes 2359300
  9.9 13.2 %copy-start.1 = (f32[3,8,32,256]{3,2,1,0:T(8,128)S(1)}, f32[3,8,32,256]{3,2,1,0:T(8,128)}, u32[]{:S(2)}) copy-start(f32[3,8,32,256]{3,2,1,0:T(8,128)} %velo.5) | copy-start | bytes 2359300
  12.6 10.5 %copy-start.2 = (f32[8,32,256]{2,1,0:T(8,128)S(1)}, f32[8,32,256]{2,1,0:T(8,128)}, u32[]{:S(2)}) copy-start(f32[8,32,256]{2,1,0:T(8,128)} %visc.5) | copy-start | bytes 786436
  12.6 14.0 %all-to-all-start = ((f32[64,4,128]{2,1,0:T(4,128)}), f32[64,4,128]{2,1,0:T(4,128)S(1)}, u32[]{:S(2)}, u32[]{:S(2)}) async-start(f32[64,4,128]{2,1,0:T(4,128)} %get-tuple-element.20), calls=%async_computation | async-start | bytes 262144 | tf_op jit(solution)/shard_map/all_to_all | solution.py:433
  18.7 4.4 %copy-start.7 = (f32[4,128]{1,0:T(4,128)S(1)}, f32[4,128]{1,0:T(4,128)}, u32[]{:S(2)}) copy-start(f32[4,128]{1,0:T(4,128)} %get-tuple-element.13.tiles_in) | copy-start | bytes 6148
  18.7 6.8 %collective-permute-start.3 = (f32[7,8,256]{2,1,0:T(8,128)}, f32[7,8,256]{2,1,0:T(8,128)S(1)}, u32[]{:S(2)}, u32[]{:S(2)}) collective-permute-start(f32[7,8,256]{2,1,0:T(8,128)} %get-tuple-element.17.ylo), channel_id=1, source_target_pairs={{1,0},{2,1},{3,2},{5,4},{6,5},{7,6},{9,8},{10,9},{11,10},{13,12},{... | collective-permute-start | bytes 172040 | tf_op jit(solution)/shard_map/ppermute | solution.py:417
  20.0 5.5 %collective-permute-start.2 = (f32[7,8,256]{2,1,0:T(8,128)}, f32[7,8,256]{2,1,0:T(8,128)S(1)}, u32[]{:S(2)}, u32[]{:S(2)}) collective-permute-start(f32[7,8,256]{2,1,0:T(8,128)} %get-tuple-element.18.yhi), channel_id=1, source_target_pairs={{0,1},{1,2},{2,3},{4,5},{5,6},{6,7},{8,9},{9,10},{10,11},{12,13},{... | collective-permute-start | bytes 172040 | tf_op jit(solution)/shard_map/ppermute | solution.py:417
  23.1 2.4 %copy-start.3 = (f32[7,32,256]{2,1,0:T(8,128)S(1)}, f32[7,32,256]{2,1,0:T(8,128)}, u32[]{:S(2)}) copy-start(f32[7,32,256]{2,1,0:T(8,128)} %get-tuple-element.12.earlier.xhi) | copy-start | bytes 688132
  23.1 2.4 %copy-start.4 = (f32[7,32,256]{2,1,0:T(8,128)S(1)}, f32[7,32,256]{2,1,0:T(8,128)}, u32[]{:S(2)}) copy-start(f32[7,32,256]{2,1,0:T(8,128)} %get-tuple-element.16.xlo) | copy-start | bytes 688132
  23.1 2.4 %copy-start.5 = (f32[7,8,256]{2,1,0:T(8,128)S(1)}, f32[7,8,256]{2,1,0:T(8,128)}, u32[]{:S(2)}) copy-start(f32[7,8,256]{2,1,0:T(8,128)} %get-tuple-element.17.ylo) | copy-start | bytes 172036
  23.2 2.4 %copy-start.6 = (f32[7,8,256]{2,1,0:T(8,128)S(1)}, f32[7,8,256]{2,1,0:T(8,128)}, u32[]{:S(2)}) copy-start(f32[7,8,256]{2,1,0:T(8,128)} %get-tuple-element.18.yhi) | copy-start | bytes 172036
  26.6 14.5 %all-to-all-start.1 = ((f32[32,4,128]{2,1,0:T(4,128)}), f32[32,4,128]{2,1,0:T(4,128)S(1)}, u32[]{:S(2)}, u32[]{:S(2)}) async-start(f32[32,4,128]{2,1,0:T(4,128)} %get-tuple-element.21), calls=%async_computation.1 | async-start | bytes 131072 | tf_op jit(solution)/shard_map/all_to_all | solution.py:440

commit v3 on v2

--- a/solution.py
+++ b/solution.py
@@ -11,7 +11,7 @@
 TIME_STEP = 0.1
 LANES = 128
 GROUP = 8
-VMEM_LIMIT = 48 * 1024 * 1024
+VMEM_LIMIT = 24 * 1024 * 1024
 
 VMEM = pl.BlockSpec(memory_space=pltpu.VMEM)
 ANY = pl.BlockSpec(memory_space=pl.ANY)
@@ -60,27 +60,6 @@
             self.made[k].wait()
 
 
-def slab_kernel(vort, velo, visc, xlo, xhi, sems):
-    copies = Copies(sems)
-    for face, at in ((xlo, 0), (xhi, visc.shape[0] - 1)):
-        copies.start(vort.at[:, at], face.at[0:3])
-        copies.start(velo.at[:, at], face.at[3:6])
-        copies.start(visc.at[at], face.at[6])
-    copies.wait(0, 6)
-
-
-def slab_faces(vort, velo, visc):
-    _, _, cy, nz = vort.shape
-    return pl.pallas_call(
-        slab_kernel,
-        out_shape=(shaped(7, cy, nz), shaped(7, cy, nz)),
-        in_specs=[ANY] * 3,
-        out_specs=(VMEM,) * 2,
-        scratch_shapes=[pltpu.SemaphoreType.DMA((6,))],
-        compiler_params=FIRST_PARAMS,
-    )(vort, velo, visc)
-
-
 def send_kernel(
     cap,
     vort,
@@ -90,7 +69,8 @@
     cells_in,
     dest_in,
     count_in,
-    earlier,
+    xlo,
+    xhi,
     ylo,
     yhi,
     packets,
@@ -115,6 +95,10 @@
         copies.start(vort.at[:, :, pl.ds(at, 8), :], spin_rows.at[k])
         copies.start(velo.at[:, :, pl.ds(at, 8), :], velo_rows.at[k])
         copies.start(visc.at[:, pl.ds(at, 8), :], visc_rows.at[k])
+    for face, at in ((xlo, 0), (xhi, cx - 1)):
+        copies.start(vort.at[:, at], face.at[0:3])
+        copies.start(velo.at[:, at], face.at[3:6])
+        copies.start(visc.at[at], face.at[6])
 
     packets[...] = jnp.zeros_like(packets)
     n_slab = packets.shape[0] // cap
@@ -144,20 +128,23 @@
                 face[c, x : x + 1, :] = spin_rows[k, c, x, at : at + 1, :]
                 face[3 + c, x : x + 1, :] = velo_rows[k, c, x, at : at + 1, :]
             face[6, x : x + 1, :] = visc_rows[k, x, at : at + 1, :]
-
-
-def to_send(vort, velo, visc, weights, cells, dest, count, earlier, n_slab, cap):
+    copies.wait(10, 16)
+
+
+def to_send(vort, velo, visc, weights, cells, dest, count, n_slab, cap):
     _, cx, cy, nz = vort.shape
     return pl.pallas_call(
         functools.partial(send_kernel, cap),
         out_shape=(
+            shaped(7, cy, nz),
+            shaped(7, cy, nz),
             shaped(7, cx, nz),
             shaped(7, cx, nz),
             shaped(n_slab * cap, 4, weights.shape[2]),
             shaped(4, n_slab * nz // CB),
         ),
-        in_specs=[ANY] * 8,
-        out_specs=(VMEM,) * 4,
+        in_specs=[ANY] * 7,
+        out_specs=(VMEM,) * 6,
         scratch_shapes=[
             pltpu.VMEM((2, 3, cx, 8, nz), jnp.float32),
             pltpu.VMEM((2, 3, cx, 8, nz), jnp.float32),
@@ -167,10 +154,10 @@
             pltpu.SMEM(dest.shape, jnp.int32),
             pltpu.SMEM(count.shape, jnp.int32),
             pltpu.SMEM((n_slab,), jnp.int32),
-            pltpu.SemaphoreType.DMA((10,)),
+            pltpu.SemaphoreType.DMA((16,)),
         ],
         compiler_params=FIRST_PARAMS,
-    )(vort, velo, visc, weights, cells, dest, count, earlier)
+    )(vort, velo, visc, weights, cells, dest, count)
 
 
 def ahead(a, axis):
@@ -424,15 +411,14 @@
     n_pencil = lax.axis_size("pencil")
     cap = 2 * tile_weights.shape[0] // n_slab
     weights = jnp.transpose(tile_weights, (1, 0, 2))
-    xlo, xhi = slab_faces(vorticity, velocity, viscosity)
+    xlo, xhi, ylo, yhi, packets, tiles = to_send(
+        vorticity, velocity, viscosity, weights, tile_cells, tile_dest.T, tile_count, n_slab, cap
+    )
     xhi_in = shift(xlo, "slab", -1)
     xlo_in = shift(xhi, "slab", 1)
-    ylo, yhi, packets, tiles = to_send(
-        vorticity, velocity, viscosity, weights, tile_cells, tile_dest.T, tile_count, xhi, n_slab, cap
-    )
     arrived = lax.all_to_all(packets, "slab", 0, 0, tiled=True)
+    yhi_in = shift(ylo, "pencil", -1)
     ylo_in = shift(yhi, "pencil", 1)
-    yhi_in = shift(ylo, "pencil", -1)
     inside, moments = inner(vorticity, velocity, viscosity, tiles)
     advanced, load = edges(
         inside, moments, (xlo, xhi, ylo, yhi), (xlo_in, xhi_in, ylo_in, yhi_in), n_slab * n_pencil

time: 42.3 us -> 40.7 us (0.962)
  Pallas kernels: 11.8 us -> 8.97 us
  waiting for transfers between devices: 4.16 us -> 5.21 us
    pallas_call x1 -> x0, Pallas kernels: 1.86 us -> none  [slab_faces(): pl.pallas_call(slab_kernel, out_shape=(shaped(7, cy, nz), shaped(7, cy, n...]
    all_to_all x1, waiting for transfers between devices: 4.15 us -> 5.19 us  [per_device(): load = lax.all_to_all(load, ('slab', 'pencil'), 0, 0, tiled=True)]
    pallas_call x1, Pallas kernels: 3.26 us -> 2.21 us  [deposit(): pl.pallas_call(functools.partial(deposit_kernel, cap), out_shape=shaped(*...]
  transfers between devices with their start and end apart: 6 -> 6, of which waited for: 1 -> 1; matrix products, arithmetic and copies ran while one was open for 0% -> 0% of each run, Pallas kernels for 22% -> 14%
where the time goes in v3:
time: 40.7 us; the launch traced here: 40.3 us
  starting transfers between devices  24.6 us (60%)
  Pallas kernels  8.97 us (22%)
  waiting for transfers between devices  5.21 us (13%)
  between operations  1.49 us (4%)
    ppermute x4, starting transfers between devices, shift(): return lax.ppermute(array, axis, pairs)  11.2 us
    all_to_all x1, starting transfers between devices, per_device(): load = lax.all_to_all(load, ('slab', 'pencil'), 0, 0, tiled=True)  7.04 us
    all_to_all x1, starting transfers between devices, per_device(): arrived = lax.all_to_all(packets, 'slab', 0, 0, tiled=True)  6.37 us
    all_to_all x1, waiting for transfers between devices, per_device(): load = lax.all_to_all(load, ('slab', 'pencil'), 0, 0, tiled=True)  5.19 us
    pallas_call x1, Pallas kernels, to_send(): pl.pallas_call(functools.partial(send_kernel, cap), out_shape=(shaped(7,...  2.67 us
    pallas_call x1, Pallas kernels, inner(): pl.pallas_call(inner_kernel, out_shape=(shaped(*vort.shape), shaped(*tile...  2.34 us
    pallas_call x1, Pallas kernels, deposit(): pl.pallas_call(functools.partial(deposit_kernel, cap), out_shape=shaped(*...  2.21 us
    pallas_call x1, Pallas kernels, edges(): pl.pallas_call(edge_kernel, out_shape=(shaped(*inside.shape), shaped(n_al...  0.99 us
  transfers between devices with their start and end apart: 6, of which 1 were waited for; matrix products, arithmetic and copies ran while one was open for 0% of the time, Pallas kernels for 14%

profile of v3, /device:TPU:0, one launch (start us, length us, event | category | flops | bytes accessed | tf_op | source)
XLA Modules:
  0.0 40.3 jit_solution(8405313562782262079)
XLA Ops:
  1.3 0.0 copy-start
  1.3 0.0 copy-start.1
  1.3 2.7 %shard_map.86 = (f32[7,32,256]{2,1,0:T(8,128)}, f32[7,32,256]{2,1,0:T(8,128)}, f32[7,8,256]{2,1,0:T(8,128)}, f32[7,8,256]{2,1,0:T(8,128)}, f32[64,4,128]{2,1,0:T(4,128)}, /*index=5*/f32[4,128]{1,0:T(4,128)}) custom-call(f32[3,8,32,256]{3,2,1,0:T(8,128)} %vort.3, f32[3,8,32,256]{3,2,1,0:T(8,128)} %velo.3, f32[8,32,256]{2,1,0:T(8,128)} %visc.3, ...), custom_call_target="tpu_custom_call" | custom-call | tf_op jit(solution)/shard_map/pallas_call | solution.py:136
  4.0 0.0 copy-start.2
  4.0 1.4 %collective-permute-start.1 = (f32[7,32,256]{2,1,0:T(8,128)}, f32[7,32,256]{2,1,0:T(8,128)S(1)}, u32[]{:S(2)}, u32[]{:S(2)}) collective-permute-start(f32[7,32,256]{2,1,0:T(8,128)} %get-tuple-element.15.xlo), channel_id=1, source_target_pairs={{4,0},{8,4},{12,8},{16,12},{20,16},{24,20},{28,24},{5,1},{9,5},{13... | collective-permute-start | bytes 688136 | tf_op jit(solution)/shard_map/ppermute | solution.py:404
  5.4 5.4 %collective-permute-start = (f32[7,32,256]{2,1,0:T(8,128)}, f32[7,32,256]{2,1,0:T(8,128)S(1)}, u32[]{:S(2)}, u32[]{:S(2)}) collective-permute-start(f32[7,32,256]{2,1,0:T(8,128)} %get-tuple-element.16.xhi), channel_id=1, source_target_pairs={{0,4},{4,8},{8,12},{12,16},{16,20},{20,24},{24,28},{1,5},{5,9},{9,... | collective-permute-start | bytes 688136 | tf_op jit(solution)/shard_map/ppermute | solution.py:404
  10.9 6.4 %all-to-all-start = ((f32[64,4,128]{2,1,0:T(4,128)}), f32[64,4,128]{2,1,0:T(4,128)S(1)}, u32[]{:S(2)}, u32[]{:S(2)}) async-start(f32[64,4,128]{2,1,0:T(4,128)} %get-tuple-element.20), calls=%async_computation | async-start | bytes 262144 | tf_op jit(solution)/shard_map/all_to_all | solution.py:419
  17.2 1.3 %collective-permute-start.3 = (f32[7,8,256]{2,1,0:T(8,128)}, f32[7,8,256]{2,1,0:T(8,128)S(1)}, u32[]{:S(2)}, u32[]{:S(2)}) collective-permute-start(f32[7,8,256]{2,1,0:T(8,128)} %get-tuple-element.17.ylo), channel_id=1, source_target_pairs={{1,0},{2,1},{3,2},{5,4},{6,5},{7,6},{9,8},{10,9},{11,10},{13,12},{... | collective-permute-start | bytes 172040 | tf_op jit(solution)/shard_map/ppermute | solution.py:404
  18.5 3.0 %collective-permute-start.2 = (f32[7,8,256]{2,1,0:T(8,128)}, f32[7,8,256]{2,1,0:T(8,128)S(1)}, u32[]{:S(2)}, u32[]{:S(2)}) collective-permute-start(f32[7,8,256]{2,1,0:T(8,128)} %get-tuple-element.18.yhi), channel_id=1, source_target_pairs={{0,1},{1,2},{2,3},{4,5},{5,6},{6,7},{8,9},{9,10},{10,11},{12,13},{... | collective-permute-start | bytes 172040 | tf_op jit(solution)/shard_map/ppermute | solution.py:404
  21.6 0.0 copy-start.3
  21.6 0.0 copy-start.4
  21.6 0.0 copy-start.5
  21.6 0.0 copy-start.6
  21.7 2.3 %shard_map.87 = (f32[3,8,32,256]{3,2,1,0:T(8,128)S(1)}, f32[4,128]{1,0:T(4,128)S(1)}) custom-call(f32[3,8,32,256]{3,2,1,0:T(8,128)S(1)} %copy-done, f32[3,8,32,256]{3,2,1,0:T(8,128)S(1)} %copy-done.1, f32[8,32,256]{2,1,0:T(8,128)S(1)} %copy-done.2, f32[4,128]{1,0:T(4,128)S(1)} %copy-done.7), custom_call_target="tpu_custom_call" | custom-call | tf_op jit(solution)/shard_map/pallas_call | solution.py:228
  24.0 0.0 collective-permute-done.3.yhi_in
  24.0 0.0 collective-permute-done.2.ylo_in
  24.0 0.0 collective-permute-done.1.xhi_in
  24.0 0.0 collective-permute-done.xlo_in
  24.1 1.0 %shard_map.88 = (f32[3,8,32,256]{3,2,1,0:T(8,128)S(1)}, f32[32,4,128]{2,1,0:T(4,128)}) custom-call(f32[3,8,32,256]{3,2,1,0:T(8,128)S(1)} %get-tuple-element.13.inside, f32[4,128]{1,0:T(4,128)S(1)} %get-tuple-element.14.moments, f32[7,32,256]{2,1,0:T(8,128)S(1)} %copy-done.3, f32[7,32,256]{2,1,0:T(8,128)S(1)} %copy-done.4, f32[7,8,256]{2,1,0:T(8,128)S(1)} %copy-done.5, ...), custom_call_target="tpu_custom_call" | custom-call | tf_op jit(solution)/shard_map/pallas_call | solution.py:268
  25.1 0.0 all-to-all-done.load
  25.1 7.0 %all-to-all-start.1 = ((f32[32,4,128]{2,1,0:T(4,128)}), f32[32,4,128]{2,1,0:T(4,128)S(1)}, u32[]{:S(2)}, u32[]{:S(2)}) async-start(f32[32,4,128]{2,1,0:T(4,128)} %get-tuple-element.21), calls=%async_computation.1 | async-start | bytes 131072 | tf_op jit(solution)/shard_map/all_to_all | solution.py:426
  32.1 2.2 %shard_map.89 = f32[3,8,32,256]{3,2,1,0:T(8,128)} custom-call(f32[3,8,32,256]{3,2,1,0:T(8,128)S(1)} %get-tuple-element.19.inside, f32[64,4,128]{2,1,0:T(4,128)S(1)} %all-to-all-done.load), custom_call_target="tpu_custom_call" | custom-call | tf_op jit(solution)/shard_map/pallas_call | solution.py:388
  34.3 5.2 %all-to-all-done.1.load = f32[32,4,128]{2,1,0:T(4,128)S(1)} async-done(((f32[32,4,128]{2,1,0:T(4,128)}), f32[32,4,128]{2,1,0:T(4,128)S(1)}, u32[]{:S(2)}, u32[]{:S(2)}) %all-to-all-start.1) | async-done | bytes 65568 | tf_op jit(solution)/shard_map/all_to_all | solution.py:426
  39.5 0.7 %shard_map.90 = f32[3,1,1,16]{3,2,1,0:T(1,128)} custom-call(f32[32,4,128]{2,1,0:T(4,128)S(1)} %all-to-all-done.1.load), custom_call_target="tpu_custom_call" | custom-call | tf_op jit(solution)/shard_map/pallas_call | solution.py:315
  (9 shorter events, 0.0 us)
Async XLA Ops:
  1.3 20.3 %copy-start = (f32[3,8,32,256]{3,2,1,0:T(8,128)S(1)}, f32[3,8,32,256]{3,2,1,0:T(8,128)}, u32[]{:S(2)}) copy-start(f32[3,8,32,256]{3,2,1,0:T(8,128)} %vort.3) | copy-start | bytes 2359300
  1.3 20.3 %copy-start.1 = (f32[3,8,32,256]{3,2,1,0:T(8,128)S(1)}, f32[3,8,32,256]{3,2,1,0:T(8,128)}, u32[]{:S(2)}) copy-start(f32[3,8,32,256]{3,2,1,0:T(8,128)} %velo.3) | copy-start | bytes 2359300
  4.0 17.6 %copy-start.2 = (f32[8,32,256]{2,1,0:T(8,128)S(1)}, f32[8,32,256]{2,1,0:T(8,128)}, u32[]{:S(2)}) copy-start(f32[8,32,256]{2,1,0:T(8,128)} %visc.3) | copy-start | bytes 786436
  4.0 20.0 %collective-permute-start.1 = (f32[7,32,256]{2,1,0:T(8,128)}, f32[7,32,256]{2,1,0:T(8,128)S(1)}, u32[]{:S(2)}, u32[]{:S(2)}) collective-permute-start(f32[7,32,256]{2,1,0:T(8,128)} %get-tuple-element.15.xlo), channel_id=1, source_target_pairs={{4,0},{8,4},{12,8},{16,12},{20,16},{24,20},{28,24},{5,1},{9,5},{13... | collective-permute-start | bytes 688136 | tf_op jit(solution)/shard_map/ppermute | solution.py:404
  5.4 18.6 %collective-permute-start = (f32[7,32,256]{2,1,0:T(8,128)}, f32[7,32,256]{2,1,0:T(8,128)S(1)}, u32[]{:S(2)}, u32[]{:S(2)}) collective-permute-start(f32[7,32,256]{2,1,0:T(8,128)} %get-tuple-element.16.xhi), channel_id=1, source_target_pairs={{0,4},{4,8},{8,12},{12,16},{16,20},{20,24},{24,28},{1,5},{5,9},{9,... | collective-permute-start | bytes 688136 | tf_op jit(solution)/shard_map/ppermute | solution.py:404
  10.9 14.2 %all-to-all-start = ((f32[64,4,128]{2,1,0:T(4,128)}), f32[64,4,128]{2,1,0:T(4,128)S(1)}, u32[]{:S(2)}, u32[]{:S(2)}) async-start(f32[64,4,128]{2,1,0:T(4,128)} %get-tuple-element.20), calls=%async_computation | async-start | bytes 262144 | tf_op jit(solution)/shard_map/all_to_all | solution.py:419
  17.2 4.4 %copy-start.7 = (f32[4,128]{1,0:T(4,128)S(1)}, f32[4,128]{1,0:T(4,128)}, u32[]{:S(2)}) copy-start(f32[4,128]{1,0:T(4,128)} %get-tuple-element.12.tiles_in) | copy-start | bytes 6148
  17.2 6.8 %collective-permute-start.3 = (f32[7,8,256]{2,1,0:T(8,128)}, f32[7,8,256]{2,1,0:T(8,128)S(1)}, u32[]{:S(2)}, u32[]{:S(2)}) collective-permute-start(f32[7,8,256]{2,1,0:T(8,128)} %get-tuple-element.17.ylo), channel_id=1, source_target_pairs={{1,0},{2,1},{3,2},{5,4},{6,5},{7,6},{9,8},{10,9},{11,10},{13,12},{... | collective-permute-start | bytes 172040 | tf_op jit(solution)/shard_map/ppermute | solution.py:404
  18.5 5.5 %collective-permute-start.2 = (f32[7,8,256]{2,1,0:T(8,128)}, f32[7,8,256]{2,1,0:T(8,128)S(1)}, u32[]{:S(2)}, u32[]{:S(2)}) collective-permute-start(f32[7,8,256]{2,1,0:T(8,128)} %get-tuple-element.18.yhi), channel_id=1, source_target_pairs={{0,1},{1,2},{2,3},{4,5},{5,6},{6,7},{8,9},{9,10},{10,11},{12,13},{... | collective-permute-start | bytes 172040 | tf_op jit(solution)/shard_map/ppermute | solution.py:404
  21.6 2.4 %copy-start.3 = (f32[7,32,256]{2,1,0:T(8,128)S(1)}, f32[7,32,256]{2,1,0:T(8,128)}, u32[]{:S(2)}) copy-start(f32[7,32,256]{2,1,0:T(8,128)} %get-tuple-element.15.xlo) | copy-start | bytes 688132
  21.6 2.4 %copy-start.4 = (f32[7,32,256]{2,1,0:T(8,128)S(1)}, f32[7,32,256]{2,1,0:T(8,128)}, u32[]{:S(2)}) copy-start(f32[7,32,256]{2,1,0:T(8,128)} %get-tuple-element.16.xhi) | copy-start | bytes 688132
  21.6 2.4 %copy-start.5 = (f32[7,8,256]{2,1,0:T(8,128)S(1)}, f32[7,8,256]{2,1,0:T(8,128)}, u32[]{:S(2)}) copy-start(f32[7,8,256]{2,1,0:T(8,128)} %get-tuple-element.17.ylo) | copy-start | bytes 172036
  21.6 2.4 %copy-start.6 = (f32[7,8,256]{2,1,0:T(8,128)S(1)}, f32[7,8,256]{2,1,0:T(8,128)}, u32[]{:S(2)}) copy-start(f32[7,8,256]{2,1,0:T(8,128)} %get-tuple-element.18.yhi) | copy-start | bytes 172036
  25.1 14.5 %all-to-all-start.1 = ((f32[32,4,128]{2,1,0:T(4,128)}), f32[32,4,128]{2,1,0:T(4,128)S(1)}, u32[]{:S(2)}, u32[]{:S(2)}) async-start(f32[32,4,128]{2,1,0:T(4,128)} %get-tuple-element.21), calls=%async_computation.1 | async-start | bytes 131072 | tf_op jit(solution)/shard_map/all_to_all | solution.py:426

commit v4 on v3

--- a/solution.py
+++ b/solution.py
@@ -69,15 +69,20 @@
     cells_in,
     dest_in,
     count_in,
+    xlo_out,
+    xhi_out,
+    swap_out,
+    other_out,
+    packets_out,
+    moments_out,
     xlo,
     xhi,
-    ylo,
-    yhi,
+    swap,
+    other,
     packets,
     moments,
-    spin_rows,
-    velo_rows,
-    visc_rows,
+    lows,
+    highs,
     weights,
     cells,
     dest,
@@ -91,14 +96,14 @@
     copies.start(cells_in, cells)
     copies.start(dest_in, dest)
     copies.start(count_in, count)
-    for k, at in ((0, 0), (1, cy - 8)):
-        copies.start(vort.at[:, :, pl.ds(at, 8), :], spin_rows.at[k])
-        copies.start(velo.at[:, :, pl.ds(at, 8), :], velo_rows.at[k])
-        copies.start(visc.at[:, pl.ds(at, 8), :], visc_rows.at[k])
     for face, at in ((xlo, 0), (xhi, cx - 1)):
         copies.start(vort.at[:, at], face.at[0:3])
         copies.start(velo.at[:, at], face.at[3:6])
         copies.start(visc.at[at], face.at[6])
+    for rows, at in ((lows, 0), (highs, cy - 8)):
+        copies.start(vort.at[:, :, pl.ds(at, 8), :], rows.at[0:3])
+        copies.start(velo.at[:, :, pl.ds(at, 8), :], rows.at[3:6])
+        copies.start(visc.at[:, pl.ds(at, 8), :], rows.at[6])
 
     packets[...] = jnp.zeros_like(packets)
     n_slab = packets.shape[0] // cap
@@ -120,41 +125,50 @@
     for d in range(n_slab):
         held = (filled[d] * (cx * cy * nz)).astype(jnp.float32)
         packets[d * cap, 3:4, :] = packets[d * cap, 3:4, :] + held
+    copies.start(packets, packets_out)
+    copies.wait(4, 10)
+    copies.start(xlo, xlo_out)
+    copies.start(xhi, xhi_out)
+    copies.wait(10, 16)
+    even = lax.axis_index("pencil") % 2 == 0
+    for k in range(7):
+        for x in range(cx):
+            low = lows[k, x, 0:1, :]
+            high = highs[k, x, 7:8, :]
+            swap[k, x : x + 1, :] = jnp.where(even, high, low)
+            other[k, x : x + 1, :] = jnp.where(even, low, high)
+    copies.start(swap, swap_out)
+    copies.start(other, other_out)
     tile_moments(cap, nz, packets, moments)
-    copies.wait(4, 10)
-    for k, face, at in ((0, ylo, 0), (1, yhi, 7)):
-        for x in range(cx):
-            for c in range(3):
-                face[c, x : x + 1, :] = spin_rows[k, c, x, at : at + 1, :]
-                face[3 + c, x : x + 1, :] = velo_rows[k, c, x, at : at + 1, :]
-            face[6, x : x + 1, :] = visc_rows[k, x, at : at + 1, :]
-    copies.wait(10, 16)
+    copies.start(moments, moments_out)
+    copies.wait(16, 22)
 
 
 def to_send(vort, velo, visc, weights, cells, dest, count, n_slab, cap):
     _, cx, cy, nz = vort.shape
+    made = (
+        shaped(7, cy, nz),
+        shaped(7, cy, nz),
+        shaped(7, cx, nz),
+        shaped(7, cx, nz),
+        shaped(n_slab * cap, 4, weights.shape[2]),
+        shaped(4, n_slab * nz // CB),
+    )
     return pl.pallas_call(
         functools.partial(send_kernel, cap),
-        out_shape=(
-            shaped(7, cy, nz),
-            shaped(7, cy, nz),
-            shaped(7, cx, nz),
-            shaped(7, cx, nz),
-            shaped(n_slab * cap, 4, weights.shape[2]),
-            shaped(4, n_slab * nz // CB),
-        ),
+        out_shape=made,
         in_specs=[ANY] * 7,
-        out_specs=(VMEM,) * 6,
-        scratch_shapes=[
-            pltpu.VMEM((2, 3, cx, 8, nz), jnp.float32),
-            pltpu.VMEM((2, 3, cx, 8, nz), jnp.float32),
-            pltpu.VMEM((2, cx, 8, nz), jnp.float32),
+        out_specs=(ANY,) * 6,
+        scratch_shapes=[pltpu.VMEM(one.shape, jnp.float32) for one in made]
+        + [
+            pltpu.VMEM((7, cx, 8, nz), jnp.float32),
+            pltpu.VMEM((7, cx, 8, nz), jnp.float32),
             pltpu.VMEM(weights.shape, jnp.float32),
             pltpu.VMEM(cells.shape, jnp.int32),
             pltpu.SMEM(dest.shape, jnp.int32),
             pltpu.SMEM(count.shape, jnp.int32),
             pltpu.SMEM((n_slab,), jnp.int32),
-            pltpu.SemaphoreType.DMA((16,)),
+            pltpu.SemaphoreType.DMA((22,)),
         ],
         compiler_params=FIRST_PARAMS,
     )(vort, velo, visc, weights, cells, dest, count)
@@ -170,38 +184,44 @@
 
 def interior_step(vort, velo, visc, out):
     cx, cy, nz = visc.shape
-    row = lax.broadcasted_iota(jnp.int32, (cy, nz), 0)
-    has_ahead = row < cy - 1
-    has_behind = row > 0
+    has_ahead = lax.broadcasted_iota(jnp.int32, (cy, nz), 0) < cy - 1
+    totals = [jnp.zeros((8, nz), jnp.float32) for _ in range(3)]
+    flux_x = [None] * 3
     for x in range(cx):
         nu = visc[x]
         spin = [vort[c, x] for c in range(3)]
         mean_y = jnp.where(has_ahead, 0.5 * (nu + ahead(nu, 0)), 0.0)
         mean_z = 0.5 * (nu + ahead(nu, 1))
+        half_y = 0.5 * spin[1]
+        half_z = 0.5 * spin[2]
+        next_y = jnp.where(has_ahead, ahead(half_y, 0), 0.0)
+        next_z = ahead(half_z, 1)
+        half_y = jnp.where(has_ahead, half_y, 0.0)
+        half_x = 0.5 * spin[0]
         if x < cx - 1:
-            mean_next = 0.5 * (nu + visc[x + 1])
-        if x > 0:
-            mean_last = 0.5 * (nu + visc[x - 1])
+            mean_x = 0.5 * (nu + visc[x + 1])
         for c in range(3):
             w = spin[c]
             u = velo[c, x]
             flux_y = mean_y * (ahead(w, 0) - w)
             flux_z = mean_z * (ahead(w, 1) - w)
-            change = (flux_y - behind(flux_y, 0)) + (flux_z - behind(flux_z, 1))
-            slope_y = jnp.where(has_ahead, ahead(u, 0), 0.0) - jnp.where(has_behind, behind(u, 0), 0.0)
-            slope_z = ahead(u, 1) - behind(u, 1)
+            change = flux_y + half_y * ahead(u, 0) - behind(flux_y + next_y * u, 0)
+            change = change + (flux_z + half_z * ahead(u, 1) - behind(flux_z + next_z * u, 1))
             if x == 0:
-                slope_x = velo[c, x + 1]
+                change = change + half_x * velo[c, x + 1]
             elif x == cx - 1:
-                slope_x = -velo[c, x - 1]
+                change = change - half_x * velo[c, x - 1]
             else:
-                slope_x = velo[c, x + 1] - velo[c, x - 1]
-            stretch = 0.5 * (spin[0] * slope_x + spin[1] * slope_y + spin[2] * slope_z)
+                change = change + half_x * (velo[c, x + 1] - velo[c, x - 1])
+            if x > 0:
+                change = change - flux_x[c]
             if x < cx - 1:
-                change = change + mean_next * (vort[c, x + 1] - w)
-            if x > 0:
-                change = change + mean_last * (vort[c, x - 1] - w)
-            out[c, x] = w + TIME_STEP * (stretch + change)
+                flux_x[c] = mean_x * (vort[c, x + 1] - w)
+                change = change + flux_x[c]
+            new = w + TIME_STEP * change
+            out[c, x] = new
+            totals[c] = totals[c] + jnp.sum(new.reshape(cy // 8, 8, nz), axis=0)
+    return [jnp.sum(total, axis=0, keepdims=True) for total in totals]
 
 
 def by_level(totals, width):
@@ -217,9 +237,7 @@
 def inner_kernel(vort, velo, visc, tiles_in, out, moments, tiles, sem):
     copy = pltpu.make_async_copy(tiles_in, tiles, sem)
     copy.start()
-    interior_step(vort, velo, visc, out)
-    totals = [jnp.sum(out[c].reshape(-1, out.shape[3]), axis=0, keepdims=True) for c in range(3)]
-    own = by_level(totals, moments.shape[1])
+    own = by_level(interior_step(vort, velo, visc, out), moments.shape[1])
     copy.wait()
     moments[...] = tiles[...] + own
 
@@ -241,35 +259,52 @@
     return TIME_STEP * (stretch + diffuse)
 
 
-def edge_kernel(inside, moments, xlo, xhi, ylo, yhi, xlo_in, xhi_in, ylo_in, yhi_in, out, load):
+def edge_kernel(
+    inside, moments, xlo, xhi, swap, other, xlo_in, xhi_in, swap_in, other_in, out, load_out, load, side_change, sem
+):
     _, cx, cy, nz = out.shape
-    out[...] = inside[...]
+    even = lax.axis_index("pencil") % 2 == 0
+    low, low_in = jnp.where(even, other[...], swap[...]), jnp.where(even, other_in[...], swap_in[...])
+    high, high_in = jnp.where(even, swap[...], other[...]), jnp.where(even, swap_in[...], other_in[...])
     totals = []
     for c in range(3):
-        total = jnp.zeros((1, nz), jnp.float32)
-        for own, other, at, sign in ((xlo, xlo_in, 0, -1.0), (xhi, xhi_in, cx - 1, 1.0)):
-            change = face_change(own, other, 0, sign, c)
-            out[c, at] = out[c, at] + change
-            total = total + jnp.sum(change, axis=0, keepdims=True)
-        for own, other, at, sign in ((ylo, ylo_in, 0, -1.0), (yhi, yhi_in, cy - 1, 1.0)):
-            change = face_change(own, other, 1, sign, c)
-            for x in range(cx):
-                out[c, x, at : at + 1, :] = out[c, x, at : at + 1, :] + change[x : x + 1, :]
-            total = total + jnp.sum(change, axis=0, keepdims=True)
-        totals.append(total)
+        total = jnp.zeros((8, nz), jnp.float32)
+        for own, came, at, sign in ((xlo, xlo_in, 0, -1.0), (xhi, xhi_in, cx - 1, 1.0)):
+            change = face_change(own, came, 0, sign, c)
+            out[c, at] = inside[c, at] + change
+            total = total + jnp.sum(change.reshape(cy // 8, 8, nz), axis=0)
+        for k, own, came, sign in ((0, low, low_in, -1.0), (1, high, high_in, 1.0)):
+            change = face_change(own, came, 1, sign, c)
+            side_change[k, c] = change
+            total = total + change
+        totals.append(jnp.sum(total, axis=0, keepdims=True))
     moment = moments[...] + by_level(totals, moments.shape[1])
     for k in range(load.shape[1] // 4):
         part = moment[:, k * LANES : (k + 1) * LANES]
-        for j in range(load.shape[0]):
-            load[j, 4 * k : 4 * k + 4, :] = part
+        load[:, 4 * k : 4 * k + 4, :] = jnp.broadcast_to(part[None], (load.shape[0], 4, LANES))
+    copy = pltpu.make_async_copy(load, load_out, sem)
+    copy.start()
+    for c in range(3):
+        out[c, 1 : cx - 1] = inside[c, 1 : cx - 1]
+        for k, at in ((0, 0), (1, cy - 1)):
+            for x in range(cx):
+                out[c, x, at : at + 1, :] = out[c, x, at : at + 1, :] + side_change[k, c, x : x + 1, :]
+    copy.wait()
 
 
 def edges(inside, moments, faces, halos, n_all):
+    _, cx, _, nz = inside.shape
+    load = shaped(n_all, 4 * moments.shape[1] // LANES, LANES)
     return pl.pallas_call(
         edge_kernel,
-        out_shape=(shaped(*inside.shape), shaped(n_all, 4 * moments.shape[1] // LANES, LANES)),
+        out_shape=(shaped(*inside.shape), load),
         in_specs=[VMEM] * 10,
-        out_specs=(VMEM,) * 2,
+        out_specs=(VMEM, ANY),
+        scratch_shapes=[
+            pltpu.VMEM(load.shape, jnp.float32),
+            pltpu.VMEM((2, 3, cx, nz), jnp.float32),
+            pltpu.SemaphoreType.DMA,
+        ],
         compiler_params=PARAMS,
     )(inside, moments, *faces, *halos)
 
@@ -404,6 +439,11 @@
     return lax.ppermute(array, axis, pairs)
 
 
+def swapped(array, axis, first):
+    up = [(i, i + 1) for i in range(first, lax.axis_size(axis) - 1, 2)]
+    return lax.ppermute(array, axis, up + [(j, i) for i, j in up])
+
+
 def per_device(vorticity, velocity, viscosity, tile_weights, tile_cells, tile_dest, tile_count):
     _, cx, cy, nz = vorticity.shape
     ncl = nz // CB
@@ -411,18 +451,20 @@
     n_pencil = lax.axis_size("pencil")
     cap = 2 * tile_weights.shape[0] // n_slab
     weights = jnp.transpose(tile_weights, (1, 0, 2))
-    xlo, xhi, ylo, yhi, packets, tiles = to_send(
-        vorticity, velocity, viscosity, weights, tile_cells, tile_dest.T, tile_count, n_slab, cap
+    count = tile_count
+    *faces, packets, tiles = to_send(
+        vorticity, velocity, viscosity, weights, tile_cells, tile_dest.T, count, n_slab, cap
     )
-    xhi_in = shift(xlo, "slab", -1)
-    xlo_in = shift(xhi, "slab", 1)
+    xlo, xhi, swap, other = faces
+    halos = (
+        shift(xhi, "slab", 1),
+        shift(xlo, "slab", -1),
+        swapped(swap, "pencil", 0),
+        swapped(other, "pencil", 1),
+    )
     arrived = lax.all_to_all(packets, "slab", 0, 0, tiled=True)
-    yhi_in = shift(ylo, "pencil", -1)
-    ylo_in = shift(yhi, "pencil", 1)
     inside, moments = inner(vorticity, velocity, viscosity, tiles)
-    advanced, load = edges(
-        inside, moments, (xlo, xhi, ylo, yhi), (xlo_in, xhi_in, ylo_in, yhi_in), n_slab * n_pencil
-    )
+    advanced, load = edges(inside, moments, faces, halos, n_slab * n_pencil)
     load = lax.all_to_all(load, ("slab", "pencil"), 0, 0, tiled=True)
     vorticity_out = deposit(advanced, arrived, cap)
     return (vorticity_out, far(load, cx, cy, ncl, n_pencil))

time: 40.7 us -> 38.6 us (0.948)
  starting transfers between devices: 24.6 us -> 19.3 us
  Pallas kernels: 8.97 us -> 12 us
    ppermute x4 -> x2, starting transfers between devices: 11.2 us -> 6.9 us  [shift(): return lax.ppermute(array, axis, pairs)]
    all_to_all x1, waiting for transfers between devices: 5.19 us -> 2.08 us  [per_device(): load = lax.all_to_all(load, ('slab', 'pencil'), 0, 0, tiled=True)]
    pallas_call x1, Pallas kernels: 2.21 us -> 5.33 us  [deposit(): pl.pallas_call(functools.partial(deposit_kernel, cap), out_shape=shaped(*...]
    all_to_all x1, waiting for transfers between devices: 0.01 us -> 2.78 us  [per_device(): arrived = lax.all_to_all(packets, 'slab', 0, 0, tiled=True)]
    all_to_all x1, starting transfers between devices: 7.04 us -> 5.46 us  [per_device(): load = lax.all_to_all(load, ('slab', 'pencil'), 0, 0, tiled=True)]
    ppermute x0 -> x2, starting transfers between devices: none -> 0.73 us  [swapped(): return lax.ppermute(array, axis, up + [(j, i) for i, j in up])]
    ppermute x4 -> x2, waiting for transfers between devices: 0.01 us -> 0.61 us  [shift(): return lax.ppermute(array, axis, pairs)]
  transfers between devices with their start and end apart: 6 -> 6, of which waited for: 1 -> 3; matrix products, arithmetic and copies ran while one was open for 0% -> 0% of each run, Pallas kernels for 14% -> 22%
where the time goes in v4:
time: 38.6 us; the launch traced here: 38.3 us
  starting transfers between devices  19.3 us (50%)
  Pallas kernels  12 us (31%)
  waiting for transfers between devices  5.47 us (14%)
  between operations  1.46 us (4%)
    ppermute x2, starting transfers between devices, shift(): return lax.ppermute(array, axis, pairs)  6.9 us
    all_to_all x1, starting transfers between devices, per_device(): arrived = lax.all_to_all(packets, 'slab', 0, 0, tiled=True)  6.22 us
    all_to_all x1, starting transfers between devices, per_device(): load = lax.all_to_all(load, ('slab', 'pencil'), 0, 0, tiled=True)  5.46 us
    pallas_call x1, Pallas kernels, deposit(): pl.pallas_call(functools.partial(deposit_kernel, cap), out_shape=shaped(*...  5.33 us
    pallas_call x1, Pallas kernels, to_send(): pl.pallas_call(functools.partial(send_kernel, cap), out_shape=made, in_sp...  2.83 us
    all_to_all x1, waiting for transfers between devices, per_device(): arrived = lax.all_to_all(packets, 'slab', 0, 0, tiled=True)  2.78 us
    all_to_all x1, waiting for transfers between devices, per_device(): load = lax.all_to_all(load, ('slab', 'pencil'), 0, 0, tiled=True)  2.08 us
    pallas_call x1, Pallas kernels, inner(): pl.pallas_call(inner_kernel, out_shape=(shaped(*vort.shape), shaped(*tile...  2.07 us
  transfers between devices with their start and end apart: 6, of which 3 were waited for; matrix products, arithmetic and copies ran while one was open for 0% of the time, Pallas kernels for 22%

profile of v4, /device:TPU:0, one launch (start us, length us, event | category | flops | bytes accessed | tf_op | source)
XLA Modules:
  0.0 38.3 jit_solution(3245100296079707778)
XLA Ops:
  1.3 0.0 copy-start
  1.3 0.0 copy-start.1
  1.3 2.8 %shard_map.86 = (f32[7,32,256]{2,1,0:T(8,128)}, f32[7,32,256]{2,1,0:T(8,128)}, f32[7,8,256]{2,1,0:T(8,128)}, f32[7,8,256]{2,1,0:T(8,128)}, f32[64,4,128]{2,1,0:T(4,128)}, /*index=5*/f32[4,128]{1,0:T(4,128)}) custom-call(f32[3,8,32,256]{3,2,1,0:T(8,128)} %vort.3, f32[3,8,32,256]{3,2,1,0:T(8,128)} %velo.3, f32[8,32,256]{2,1,0:T(8,128)} %visc.3, ...), custom_call_target="tpu_custom_call" | custom-call | tf_op jit(solution)/shard_map/pallas_call | solution.py:157
  4.1 0.0 copy-start.2
  4.1 1.4 %collective-permute-start.1 = (f32[7,32,256]{2,1,0:T(8,128)}, f32[7,32,256]{2,1,0:T(8,128)S(1)}, u32[]{:S(2)}, u32[]{:S(2)}) collective-permute-start(f32[7,32,256]{2,1,0:T(8,128)} %get-tuple-element.15.xlo), channel_id=1, source_target_pairs={{4,0},{8,4},{12,8},{16,12},{20,16},{24,20},{28,24},{5,1},{9,5},{13... | collective-permute-start | bytes 688136 | tf_op jit(solution)/shard_map/ppermute | solution.py:439
  5.6 5.5 %collective-permute-start = (f32[7,32,256]{2,1,0:T(8,128)}, f32[7,32,256]{2,1,0:T(8,128)S(1)}, u32[]{:S(2)}, u32[]{:S(2)}) collective-permute-start(f32[7,32,256]{2,1,0:T(8,128)} %get-tuple-element.16.xhi), channel_id=1, source_target_pairs={{0,4},{4,8},{8,12},{12,16},{16,20},{20,24},{24,28},{1,5},{5,9},{9,... | collective-permute-start | bytes 688136 | tf_op jit(solution)/shard_map/ppermute | solution.py:439
  11.1 6.2 %all-to-all-start = ((f32[64,4,128]{2,1,0:T(4,128)}), f32[64,4,128]{2,1,0:T(4,128)S(1)}, u32[]{:S(2)}, u32[]{:S(2)}) async-start(f32[64,4,128]{2,1,0:T(4,128)} %get-tuple-element.20), calls=%async_computation | async-start | bytes 262144 | tf_op jit(solution)/shard_map/all_to_all | solution.py:465
  17.3 0.1 collective-permute-start.2
  17.4 0.7 %collective-permute-start.3 = (f32[7,8,256]{2,1,0:T(8,128)}, f32[7,8,256]{2,1,0:T(8,128)S(1)}, u32[]{:S(2)}, u32[]{:S(2)}) collective-permute-start(f32[7,8,256]{2,1,0:T(8,128)} %get-tuple-element.18.other), channel_id=1, source_target_pairs={{1,2},{2,1},{5,6},{6,5},{9,10},{10,9},{13,14},{14,13},{17,18},{18,... | collective-permute-start | bytes 172040 | tf_op jit(solution)/shard_map/ppermute | solution.py:444
  18.0 0.0 copy-done
  18.1 0.0 copy-start.3
  18.1 2.1 %shard_map.87 = (f32[3,8,32,256]{3,2,1,0:T(8,128)S(1)}, f32[4,128]{1,0:T(4,128)S(1)}) custom-call(f32[3,8,32,256]{3,2,1,0:T(8,128)S(1)} %copy-done, f32[3,8,32,256]{3,2,1,0:T(8,128)S(1)} %copy-done.1, f32[8,32,256]{2,1,0:T(8,128)S(1)} %copy-done.2, f32[4,128]{1,0:T(4,128)S(1)} %copy-done.7), custom_call_target="tpu_custom_call" | custom-call | tf_op jit(solution)/shard_map/pallas_call | solution.py:246
  20.2 0.0 collective-permute-done.2.swap_in
  20.2 0.0 collective-permute-done.3.other_in
  20.2 0.0 collective-permute-done.1.xhi_in
  20.2 0.6 %collective-permute-done.xlo_in = f32[7,32,256]{2,1,0:T(8,128)S(1)} collective-permute-done((f32[7,32,256]{2,1,0:T(8,128)}, f32[7,32,256]{2,1,0:T(8,128)S(1)}, u32[]{:S(2)}, u32[]{:S(2)}) %collective-permute-start) | collective-permute-done | bytes 229408 | tf_op jit(solution)/shard_map/ppermute | solution.py:439
  20.8 0.0 copy-done.3
  20.8 0.0 copy-done.5
  20.8 1.0 %shard_map.88 = (f32[3,8,32,256]{3,2,1,0:T(8,128)S(1)}, f32[32,4,128]{2,1,0:T(4,128)}) custom-call(f32[3,8,32,256]{3,2,1,0:T(8,128)S(1)} %get-tuple-element.13.inside, f32[4,128]{1,0:T(4,128)S(1)} %get-tuple-element.14.moments, f32[7,32,256]{2,1,0:T(8,128)S(1)} %copy-done.3, f32[7,32,256]{2,1,0:T(8,128)S(1)} %copy-done.4, f32[7,8,256]{2,1,0:T(8,128)S(1)} %copy-done.5, ...), custom_call_target="tpu_custom_call" | custom-call | tf_op jit(solution)/shard_map/pallas_call | solution.py:298
  21.8 2.8 %all-to-all-done.load = f32[64,4,128]{2,1,0:T(4,128)S(1)} async-done(((f32[64,4,128]{2,1,0:T(4,128)}), f32[64,4,128]{2,1,0:T(4,128)S(1)}, u32[]{:S(2)}, u32[]{:S(2)}) %all-to-all-start) | async-done | bytes 131104 | tf_op jit(solution)/shard_map/all_to_all | solution.py:465
  24.6 5.5 %all-to-all-start.1 = ((f32[32,4,128]{2,1,0:T(4,128)}), f32[32,4,128]{2,1,0:T(4,128)S(1)}, u32[]{:S(2)}, u32[]{:S(2)}) async-start(f32[32,4,128]{2,1,0:T(4,128)} %get-tuple-element.21), calls=%async_computation.1 | async-start | bytes 131072 | tf_op jit(solution)/shard_map/all_to_all | solution.py:468
  30.1 5.3 %shard_map.89 = f32[3,8,32,256]{3,2,1,0:T(8,128)} custom-call(f32[3,8,32,256]{3,2,1,0:T(8,128)S(1)} %get-tuple-element.19.inside, f32[64,4,128]{2,1,0:T(4,128)S(1)} %all-to-all-done.load), custom_call_target="tpu_custom_call" | custom-call | tf_op jit(solution)/shard_map/pallas_call | solution.py:423
  35.4 2.1 %all-to-all-done.1.load = f32[32,4,128]{2,1,0:T(4,128)S(1)} async-done(((f32[32,4,128]{2,1,0:T(4,128)}), f32[32,4,128]{2,1,0:T(4,128)S(1)}, u32[]{:S(2)}, u32[]{:S(2)}) %all-to-all-start.1) | async-done | bytes 65568 | tf_op jit(solution)/shard_map/all_to_all | solution.py:468
  37.5 0.7 %shard_map.90 = f32[3,1,1,16]{3,2,1,0:T(1,128)} custom-call(f32[32,4,128]{2,1,0:T(4,128)S(1)} %all-to-all-done.1.load), custom_call_target="tpu_custom_call" | custom-call | tf_op jit(solution)/shard_map/pallas_call | solution.py:350
  (9 shorter events, 0.0 us)
Async XLA Ops:
  1.3 16.8 %copy-start = (f32[3,8,32,256]{3,2,1,0:T(8,128)S(1)}, f32[3,8,32,256]{3,2,1,0:T(8,128)}, u32[]{:S(2)}) copy-start(f32[3,8,32,256]{3,2,1,0:T(8,128)} %vort.3) | copy-start | bytes 2359300
  1.3 16.8 %copy-start.1 = (f32[3,8,32,256]{3,2,1,0:T(8,128)S(1)}, f32[3,8,32,256]{3,2,1,0:T(8,128)}, u32[]{:S(2)}) copy-start(f32[3,8,32,256]{3,2,1,0:T(8,128)} %velo.3) | copy-start | bytes 2359300
  4.1 13.9 %copy-start.2 = (f32[8,32,256]{2,1,0:T(8,128)S(1)}, f32[8,32,256]{2,1,0:T(8,128)}, u32[]{:S(2)}) copy-start(f32[8,32,256]{2,1,0:T(8,128)} %visc.3) | copy-start | bytes 786436
  4.1 16.1 %collective-permute-start.1 = (f32[7,32,256]{2,1,0:T(8,128)}, f32[7,32,256]{2,1,0:T(8,128)S(1)}, u32[]{:S(2)}, u32[]{:S(2)}) collective-permute-start(f32[7,32,256]{2,1,0:T(8,128)} %get-tuple-element.15.xlo), channel_id=1, source_target_pairs={{4,0},{8,4},{12,8},{16,12},{20,16},{24,20},{28,24},{5,1},{9,5},{13... | collective-permute-start | bytes 688136 | tf_op jit(solution)/shard_map/ppermute | solution.py:439
  5.6 15.3 %collective-permute-start = (f32[7,32,256]{2,1,0:T(8,128)}, f32[7,32,256]{2,1,0:T(8,128)S(1)}, u32[]{:S(2)}, u32[]{:S(2)}) collective-permute-start(f32[7,32,256]{2,1,0:T(8,128)} %get-tuple-element.16.xhi), channel_id=1, source_target_pairs={{0,4},{4,8},{8,12},{12,16},{16,20},{20,24},{24,28},{1,5},{5,9},{9,... | collective-permute-start | bytes 688136 | tf_op jit(solution)/shard_map/ppermute | solution.py:439
  11.1 13.6 %all-to-all-start = ((f32[64,4,128]{2,1,0:T(4,128)}), f32[64,4,128]{2,1,0:T(4,128)S(1)}, u32[]{:S(2)}, u32[]{:S(2)}) async-start(f32[64,4,128]{2,1,0:T(4,128)} %get-tuple-element.20), calls=%async_computation | async-start | bytes 262144 | tf_op jit(solution)/shard_map/all_to_all | solution.py:465
  17.3 0.8 %copy-start.7 = (f32[4,128]{1,0:T(4,128)S(1)}, f32[4,128]{1,0:T(4,128)}, u32[]{:S(2)}) copy-start(f32[4,128]{1,0:T(4,128)} %get-tuple-element.12.tiles_in) | copy-start | bytes 6148
  17.3 2.9 %collective-permute-start.2 = (f32[7,8,256]{2,1,0:T(8,128)}, f32[7,8,256]{2,1,0:T(8,128)S(1)}, u32[]{:S(2)}, u32[]{:S(2)}) collective-permute-start(f32[7,8,256]{2,1,0:T(8,128)} %get-tuple-element.17.swap), channel_id=1, source_target_pairs={{0,1},{2,3},{1,0},{3,2},{4,5},{6,7},{5,4},{7,6},{8,9},{10,11},{9,8... | collective-permute-start | bytes 172040 | tf_op jit(solution)/shard_map/ppermute | solution.py:444
  17.4 2.8 %collective-permute-start.3 = (f32[7,8,256]{2,1,0:T(8,128)}, f32[7,8,256]{2,1,0:T(8,128)S(1)}, u32[]{:S(2)}, u32[]{:S(2)}) collective-permute-start(f32[7,8,256]{2,1,0:T(8,128)} %get-tuple-element.18.other), channel_id=1, source_target_pairs={{1,2},{2,1},{5,6},{6,5},{9,10},{10,9},{13,14},{14,13},{17,18},{18,... | collective-permute-start | bytes 172040 | tf_op jit(solution)/shard_map/ppermute | solution.py:444
  18.1 2.8 %copy-start.3 = (f32[7,32,256]{2,1,0:T(8,128)S(1)}, f32[7,32,256]{2,1,0:T(8,128)}, u32[]{:S(2)}) copy-start(f32[7,32,256]{2,1,0:T(8,128)} %get-tuple-element.15.xlo) | copy-start | bytes 688132
  18.1 2.8 %copy-start.4 = (f32[7,32,256]{2,1,0:T(8,128)S(1)}, f32[7,32,256]{2,1,0:T(8,128)}, u32[]{:S(2)}) copy-start(f32[7,32,256]{2,1,0:T(8,128)} %get-tuple-element.16.xhi) | copy-start | bytes 688132
  18.1 2.7 %copy-start.5 = (f32[7,8,256]{2,1,0:T(8,128)S(1)}, f32[7,8,256]{2,1,0:T(8,128)}, u32[]{:S(2)}) copy-start(f32[7,8,256]{2,1,0:T(8,128)} %get-tuple-element.17.swap) | copy-start | bytes 172036
  18.1 2.7 %copy-start.6 = (f32[7,8,256]{2,1,0:T(8,128)S(1)}, f32[7,8,256]{2,1,0:T(8,128)}, u32[]{:S(2)}) copy-start(f32[7,8,256]{2,1,0:T(8,128)} %get-tuple-element.18.other) | copy-start | bytes 172036
  24.6 12.9 %all-to-all-start.1 = ((f32[32,4,128]{2,1,0:T(4,128)}), f32[32,4,128]{2,1,0:T(4,128)S(1)}, u32[]{:S(2)}, u32[]{:S(2)}) async-start(f32[32,4,128]{2,1,0:T(4,128)} %get-tuple-element.21), calls=%async_computation.1 | async-start | bytes 131072 | tf_op jit(solution)/shard_map/all_to_all | solution.py:468

commit v5 on v4

--- a/solution.py
+++ b/solution.py
@@ -10,6 +10,7 @@
 CB = 16
 TIME_STEP = 0.1
 LANES = 128
+SIDES = ("slab", "slab", "pencil", "pencil")
 GROUP = 8
 VMEM_LIMIT = 24 * 1024 * 1024
 
@@ -69,14 +70,14 @@
     cells_in,
     dest_in,
     count_in,
-    xlo_out,
-    xhi_out,
+    near_out,
+    far_out,
     swap_out,
     other_out,
     packets_out,
     moments_out,
-    xlo,
-    xhi,
+    near,
+    far,
     swap,
     other,
     packets,
@@ -96,7 +97,8 @@
     copies.start(cells_in, cells)
     copies.start(dest_in, dest)
     copies.start(count_in, count)
-    for face, at in ((xlo, 0), (xhi, cx - 1)):
+    even = lax.axis_index("slab") % 2 == 0
+    for face, at in ((near, jnp.where(even, cx - 1, 0)), (far, jnp.where(even, 0, cx - 1))):
         copies.start(vort.at[:, at], face.at[0:3])
         copies.start(velo.at[:, at], face.at[3:6])
         copies.start(visc.at[at], face.at[6])
@@ -127,8 +129,8 @@
         packets[d * cap, 3:4, :] = packets[d * cap, 3:4, :] + held
     copies.start(packets, packets_out)
     copies.wait(4, 10)
-    copies.start(xlo, xlo_out)
-    copies.start(xhi, xhi_out)
+    copies.start(near, near_out)
+    copies.start(far, far_out)
     copies.wait(10, 16)
     even = lax.axis_index("pencil") % 2 == 0
     for k in range(7):
@@ -260,16 +262,19 @@
 
 
 def edge_kernel(
-    inside, moments, xlo, xhi, swap, other, xlo_in, xhi_in, swap_in, other_in, out, load_out, load, side_change, sem
+    inside, moments, near, far, swap, other, near_in, far_in, swap_in, other_in, out, load_out, load, side_change, sem
 ):
     _, cx, cy, nz = out.shape
     even = lax.axis_index("pencil") % 2 == 0
     low, low_in = jnp.where(even, other[...], swap[...]), jnp.where(even, other_in[...], swap_in[...])
     high, high_in = jnp.where(even, swap[...], other[...]), jnp.where(even, swap_in[...], other_in[...])
+    even = lax.axis_index("slab") % 2 == 0
+    near_at, far_at = jnp.where(even, cx - 1, 0), jnp.where(even, 0, cx - 1)
+    near_sign = jnp.where(even, 1.0, -1.0)
     totals = []
     for c in range(3):
         total = jnp.zeros((8, nz), jnp.float32)
-        for own, came, at, sign in ((xlo, xlo_in, 0, -1.0), (xhi, xhi_in, cx - 1, 1.0)):
+        for own, came, at, sign in ((near, near_in, near_at, near_sign), (far, far_in, far_at, -near_sign)):
             change = face_change(own, came, 0, sign, c)
             out[c, at] = inside[c, at] + change
             total = total + jnp.sum(change.reshape(cy // 8, 8, nz), axis=0)
@@ -433,12 +438,6 @@
     )(inside, load)
 
 
-def shift(array, axis, step):
-    n = lax.axis_size(axis)
-    pairs = [(i, i + step) for i in range(n) if 0 <= i + step < n]
-    return lax.ppermute(array, axis, pairs)
-
-
 def swapped(array, axis, first):
     up = [(i, i + 1) for i in range(first, lax.axis_size(axis) - 1, 2)]
     return lax.ppermute(array, axis, up + [(j, i) for i, j in up])
@@ -455,13 +454,7 @@
     *faces, packets, tiles = to_send(
         vorticity, velocity, viscosity, weights, tile_cells, tile_dest.T, count, n_slab, cap
     )
-    xlo, xhi, swap, other = faces
-    halos = (
-        shift(xhi, "slab", 1),
-        shift(xlo, "slab", -1),
-        swapped(swap, "pencil", 0),
-        swapped(other, "pencil", 1),
-    )
+    halos = [swapped(face, axis, k % 2) for k, (face, axis) in enumerate(zip(faces, SIDES))]
     arrived = lax.all_to_all(packets, "slab", 0, 0, tiled=True)
     inside, moments = inner(vorticity, velocity, viscosity, tiles)
     advanced, load = edges(inside, moments, faces, halos, n_slab * n_pencil)

time: 38.6 us -> 36.7 us (0.951)
  Pallas kernels: 12 us -> 9.89 us
  waiting for transfers between devices: 5.47 us -> 7.51 us
  starting transfers between devices: 19.3 us -> 17.5 us
    ppermute x2 -> x0, starting transfers between devices: 6.9 us -> none  [shift(): return lax.ppermute(array, axis, pairs)]
    ppermute x2 -> x4, starting transfers between devices: 0.73 us -> 4.4 us  [swapped(): return lax.ppermute(array, axis, up + [(j, i) for i, j in up])]
    all_to_all x1, waiting for transfers between devices: 2.08 us -> 4.15 us  [per_device(): load = lax.all_to_all(load, ('slab', 'pencil'), 0, 0, tiled=True)]
    pallas_call x1, Pallas kernels: 5.33 us -> 3.25 us  [deposit(): pl.pallas_call(functools.partial(deposit_kernel, cap), out_shape=shaped(*...]
    all_to_all x1, starting transfers between devices: 6.22 us -> 7.59 us  [per_device(): arrived = lax.all_to_all(packets, 'slab', 0, 0, tiled=True)]
    ppermute x2 -> x0, waiting for transfers between devices: 0.61 us -> none  [shift(): return lax.ppermute(array, axis, pairs)]
    all_to_all x1, waiting for transfers between devices: 2.78 us -> 3.35 us  [per_device(): arrived = lax.all_to_all(packets, 'slab', 0, 0, tiled=True)]
  transfers between devices with their start and end apart: 6 -> 6, of which waited for: 3 -> 2; matrix products, arithmetic and copies ran while one was open for 0% -> 0% of each run, Pallas kernels for 22% -> 17%
where the time goes in v5:
time: 36.7 us; the launch traced here: 36.4 us
  starting transfers between devices  17.5 us (48%)
  Pallas kernels  9.89 us (27%)
  waiting for transfers between devices  7.51 us (20%)
  between operations  1.49 us (4%)
    all_to_all x1, starting transfers between devices, per_device(): arrived = lax.all_to_all(packets, 'slab', 0, 0, tiled=True)  7.59 us
    all_to_all x1, starting transfers between devices, per_device(): load = lax.all_to_all(load, ('slab', 'pencil'), 0, 0, tiled=True)  5.46 us
    ppermute x4, starting transfers between devices, swapped(): return lax.ppermute(array, axis, up + [(j, i) for i, j in up])  4.4 us
    all_to_all x1, waiting for transfers between devices, per_device(): load = lax.all_to_all(load, ('slab', 'pencil'), 0, 0, tiled=True)  4.15 us
    all_to_all x1, waiting for transfers between devices, per_device(): arrived = lax.all_to_all(packets, 'slab', 0, 0, tiled=True)  3.35 us
    pallas_call x1, Pallas kernels, deposit(): pl.pallas_call(functools.partial(deposit_kernel, cap), out_shape=shaped(*...  3.25 us
    pallas_call x1, Pallas kernels, to_send(): pl.pallas_call(functools.partial(send_kernel, cap), out_shape=made, in_sp...  2.83 us
    pallas_call x1, Pallas kernels, inner(): pl.pallas_call(inner_kernel, out_shape=(shaped(*vort.shape), shaped(*tile...  2.07 us
  transfers between devices with their start and end apart: 6, of which 2 were waited for; matrix products, arithmetic and copies ran while one was open for 0% of the time, Pallas kernels for 17%

profile of v5, /device:TPU:0, one launch (start us, length us, event | category | flops | bytes accessed | tf_op | source)
XLA Modules:
  0.0 36.4 jit_solution(17547762266481348053)
XLA Ops:
  1.3 0.0 copy-start
  1.3 2.8 %shard_map.86 = (f32[7,32,256]{2,1,0:T(8,128)}, f32[7,32,256]{2,1,0:T(8,128)}, f32[7,8,256]{2,1,0:T(8,128)}, f32[7,8,256]{2,1,0:T(8,128)}, f32[64,4,128]{2,1,0:T(4,128)}, /*index=5*/f32[4,128]{1,0:T(4,128)}) custom-call(f32[3,8,32,256]{3,2,1,0:T(8,128)} %vort.3, f32[3,8,32,256]{3,2,1,0:T(8,128)} %velo.3, f32[8,32,256]{2,1,0:T(8,128)} %visc.3, ...), custom_call_target="tpu_custom_call" | custom-call | tf_op jit(solution)/shard_map/pallas_call | solution.py:159
  4.1 0.0 copy-start.2
  4.1 3.0 %collective-permute-start = (f32[7,32,256]{2,1,0:T(8,128)}, f32[7,32,256]{2,1,0:T(8,128)S(1)}, u32[]{:S(2)}, u32[]{:S(2)}) collective-permute-start(f32[7,32,256]{2,1,0:T(8,128)} %get-tuple-element.15.near), channel_id=1, source_target_pairs={{0,4},{8,12},{16,20},{24,28},{4,0},{12,8},{20,16},{28,24},{1,5},{9... | collective-permute-start | bytes 688136 | tf_op jit(solution)/shard_map/ppermute | solution.py:443
  7.2 0.7 %collective-permute-start.1 = (f32[7,32,256]{2,1,0:T(8,128)}, f32[7,32,256]{2,1,0:T(8,128)S(1)}, u32[]{:S(2)}, u32[]{:S(2)}) collective-permute-start(f32[7,32,256]{2,1,0:T(8,128)} %get-tuple-element.16.far), channel_id=1, source_target_pairs={{4,8},{12,16},{20,24},{8,4},{16,12},{24,20},{5,9},{13,17},{21,25},... | collective-permute-start | bytes 688136 | tf_op jit(solution)/shard_map/ppermute | solution.py:443
  7.8 7.6 %all-to-all-start = ((f32[64,4,128]{2,1,0:T(4,128)}), f32[64,4,128]{2,1,0:T(4,128)S(1)}, u32[]{:S(2)}, u32[]{:S(2)}) async-start(f32[64,4,128]{2,1,0:T(4,128)} %get-tuple-element.20), calls=%async_computation | async-start | bytes 262144 | tf_op jit(solution)/shard_map/all_to_all | solution.py:458
  15.4 0.1 collective-permute-start.2
  15.5 0.7 %collective-permute-start.3 = (f32[7,8,256]{2,1,0:T(8,128)}, f32[7,8,256]{2,1,0:T(8,128)S(1)}, u32[]{:S(2)}, u32[]{:S(2)}) collective-permute-start(f32[7,8,256]{2,1,0:T(8,128)} %get-tuple-element.18.other), channel_id=1, source_target_pairs={{1,2},{2,1},{5,6},{6,5},{9,10},{10,9},{13,14},{14,13},{17,18},{18,... | collective-permute-start | bytes 172040 | tf_op jit(solution)/shard_map/ppermute | solution.py:443
  16.2 0.0 copy-start.3
  16.2 2.1 %shard_map.87 = (f32[3,8,32,256]{3,2,1,0:T(8,128)S(1)}, f32[4,128]{1,0:T(4,128)S(1)}) custom-call(f32[3,8,32,256]{3,2,1,0:T(8,128)S(1)} %copy-done, f32[3,8,32,256]{3,2,1,0:T(8,128)S(1)} %copy-done.1, f32[8,32,256]{2,1,0:T(8,128)S(1)} %copy-done.2, f32[4,128]{1,0:T(4,128)S(1)} %copy-done.7), custom_call_target="tpu_custom_call" | custom-call | tf_op jit(solution)/shard_map/pallas_call | solution.py:248
  18.3 0.0 collective-permute-done.2.swap_in
  18.3 0.0 collective-permute-done.3.other_in
  18.3 0.0 collective-permute-done.near_in
  18.4 0.0 collective-permute-done.1.far_in
  18.4 0.0 copy-done.3
  18.4 0.0 copy-done.4
  18.4 0.0 copy-done.5
  18.4 0.0 copy-done.6
  18.4 1.0 %shard_map.88 = (f32[3,8,32,256]{3,2,1,0:T(8,128)S(1)}, f32[32,4,128]{2,1,0:T(4,128)}) custom-call(f32[3,8,32,256]{3,2,1,0:T(8,128)S(1)} %get-tuple-element.13.inside, f32[4,128]{1,0:T(4,128)S(1)} %get-tuple-element.14.moments, f32[7,32,256]{2,1,0:T(8,128)S(1)} %copy-done.3, f32[7,32,256]{2,1,0:T(8,128)S(1)} %copy-done.4, f32[7,8,256]{2,1,0:T(8,128)S(1)} %copy-done.5, ...), custom_call_target="tpu_custom_call" | custom-call | tf_op jit(solution)/shard_map/pallas_call | solution.py:303
  19.4 3.4 %all-to-all-done.load = f32[64,4,128]{2,1,0:T(4,128)S(1)} async-done(((f32[64,4,128]{2,1,0:T(4,128)}), f32[64,4,128]{2,1,0:T(4,128)S(1)}, u32[]{:S(2)}, u32[]{:S(2)}) %all-to-all-start) | async-done | bytes 131104 | tf_op jit(solution)/shard_map/all_to_all | solution.py:458
  22.8 5.5 %all-to-all-start.1 = ((f32[32,4,128]{2,1,0:T(4,128)}), f32[32,4,128]{2,1,0:T(4,128)S(1)}, u32[]{:S(2)}, u32[]{:S(2)}) async-start(f32[32,4,128]{2,1,0:T(4,128)} %get-tuple-element.21), calls=%async_computation.1 | async-start | bytes 131072 | tf_op jit(solution)/shard_map/all_to_all | solution.py:461
  28.2 3.3 %shard_map.89 = f32[3,8,32,256]{3,2,1,0:T(8,128)} custom-call(f32[3,8,32,256]{3,2,1,0:T(8,128)S(1)} %get-tuple-element.19.inside, f32[64,4,128]{2,1,0:T(4,128)S(1)} %all-to-all-done.load), custom_call_target="tpu_custom_call" | custom-call | tf_op jit(solution)/shard_map/pallas_call | solution.py:428
  31.5 4.2 %all-to-all-done.1.load = f32[32,4,128]{2,1,0:T(4,128)S(1)} async-done(((f32[32,4,128]{2,1,0:T(4,128)}), f32[32,4,128]{2,1,0:T(4,128)S(1)}, u32[]{:S(2)}, u32[]{:S(2)}) %all-to-all-start.1) | async-done | bytes 65568 | tf_op jit(solution)/shard_map/all_to_all | solution.py:461
  35.6 0.7 %shard_map.90 = f32[3,1,1,16]{3,2,1,0:T(1,128)} custom-call(f32[32,4,128]{2,1,0:T(4,128)S(1)} %all-to-all-done.1.load), custom_call_target="tpu_custom_call" | custom-call | tf_op jit(solution)/shard_map/pallas_call | solution.py:355
  (9 shorter events, 0.0 us)
Async XLA Ops:
  1.3 14.9 %copy-start = (f32[3,8,32,256]{3,2,1,0:T(8,128)S(1)}, f32[3,8,32,256]{3,2,1,0:T(8,128)}, u32[]{:S(2)}) copy-start(f32[3,8,32,256]{3,2,1,0:T(8,128)} %vort.3) | copy-start | bytes 2359300
  1.3 14.9 %copy-start.1 = (f32[3,8,32,256]{3,2,1,0:T(8,128)S(1)}, f32[3,8,32,256]{3,2,1,0:T(8,128)}, u32[]{:S(2)}) copy-start(f32[3,8,32,256]{3,2,1,0:T(8,128)} %velo.3) | copy-start | bytes 2359300
  4.1 12.1 %copy-start.2 = (f32[8,32,256]{2,1,0:T(8,128)S(1)}, f32[8,32,256]{2,1,0:T(8,128)}, u32[]{:S(2)}) copy-start(f32[8,32,256]{2,1,0:T(8,128)} %visc.3) | copy-start | bytes 786436
  4.1 14.2 %collective-permute-start = (f32[7,32,256]{2,1,0:T(8,128)}, f32[7,32,256]{2,1,0:T(8,128)S(1)}, u32[]{:S(2)}, u32[]{:S(2)}) collective-permute-start(f32[7,32,256]{2,1,0:T(8,128)} %get-tuple-element.15.near), channel_id=1, source_target_pairs={{0,4},{8,12},{16,20},{24,28},{4,0},{12,8},{20,16},{28,24},{1,5},{9... | collective-permute-start | bytes 688136 | tf_op jit(solution)/shard_map/ppermute | solution.py:443
  7.2 11.2 %collective-permute-start.1 = (f32[7,32,256]{2,1,0:T(8,128)}, f32[7,32,256]{2,1,0:T(8,128)S(1)}, u32[]{:S(2)}, u32[]{:S(2)}) collective-permute-start(f32[7,32,256]{2,1,0:T(8,128)} %get-tuple-element.16.far), channel_id=1, source_target_pairs={{4,8},{12,16},{20,24},{8,4},{16,12},{24,20},{5,9},{13,17},{21,25},... | collective-permute-start | bytes 688136 | tf_op jit(solution)/shard_map/ppermute | solution.py:443
  7.8 14.9 %all-to-all-start = ((f32[64,4,128]{2,1,0:T(4,128)}), f32[64,4,128]{2,1,0:T(4,128)S(1)}, u32[]{:S(2)}, u32[]{:S(2)}) async-start(f32[64,4,128]{2,1,0:T(4,128)} %get-tuple-element.20), calls=%async_computation | async-start | bytes 262144 | tf_op jit(solution)/shard_map/all_to_all | solution.py:458
  15.4 0.8 %copy-start.7 = (f32[4,128]{1,0:T(4,128)S(1)}, f32[4,128]{1,0:T(4,128)}, u32[]{:S(2)}) copy-start(f32[4,128]{1,0:T(4,128)} %get-tuple-element.12.tiles_in) | copy-start | bytes 6148
  15.4 2.9 %collective-permute-start.2 = (f32[7,8,256]{2,1,0:T(8,128)}, f32[7,8,256]{2,1,0:T(8,128)S(1)}, u32[]{:S(2)}, u32[]{:S(2)}) collective-permute-start(f32[7,8,256]{2,1,0:T(8,128)} %get-tuple-element.17.swap), channel_id=1, source_target_pairs={{0,1},{2,3},{1,0},{3,2},{4,5},{6,7},{5,4},{7,6},{8,9},{10,11},{9,8... | collective-permute-start | bytes 172040 | tf_op jit(solution)/shard_map/ppermute | solution.py:443
  15.5 2.8 %collective-permute-start.3 = (f32[7,8,256]{2,1,0:T(8,128)}, f32[7,8,256]{2,1,0:T(8,128)S(1)}, u32[]{:S(2)}, u32[]{:S(2)}) collective-permute-start(f32[7,8,256]{2,1,0:T(8,128)} %get-tuple-element.18.other), channel_id=1, source_target_pairs={{1,2},{2,1},{5,6},{6,5},{9,10},{10,9},{13,14},{14,13},{17,18},{18,... | collective-permute-start | bytes 172040 | tf_op jit(solution)/shard_map/ppermute | solution.py:443
  16.2 2.2 %copy-start.3 = (f32[7,32,256]{2,1,0:T(8,128)S(1)}, f32[7,32,256]{2,1,0:T(8,128)}, u32[]{:S(2)}) copy-start(f32[7,32,256]{2,1,0:T(8,128)} %get-tuple-element.15.near) | copy-start | bytes 688132
  16.2 2.2 %copy-start.4 = (f32[7,32,256]{2,1,0:T(8,128)S(1)}, f32[7,32,256]{2,1,0:T(8,128)}, u32[]{:S(2)}) copy-start(f32[7,32,256]{2,1,0:T(8,128)} %get-tuple-element.16.far) | copy-start | bytes 688132
  16.2 2.2 %copy-start.5 = (f32[7,8,256]{2,1,0:T(8,128)S(1)}, f32[7,8,256]{2,1,0:T(8,128)}, u32[]{:S(2)}) copy-start(f32[7,8,256]{2,1,0:T(8,128)} %get-tuple-element.17.swap) | copy-start | bytes 172036
  16.2 2.2 %copy-start.6 = (f32[7,8,256]{2,1,0:T(8,128)S(1)}, f32[7,8,256]{2,1,0:T(8,128)}, u32[]{:S(2)}) copy-start(f32[7,8,256]{2,1,0:T(8,128)} %get-tuple-element.18.other) | copy-start | bytes 172036
  22.8 12.9 %all-to-all-start.1 = ((f32[32,4,128]{2,1,0:T(4,128)}), f32[32,4,128]{2,1,0:T(4,128)S(1)}, u32[]{:S(2)}, u32[]{:S(2)}) async-start(f32[32,4,128]{2,1,0:T(4,128)} %get-tuple-element.21), calls=%async_computation.1 | async-start | bytes 131072 | tf_op jit(solution)/shard_map/all_to_all | solution.py:461

commit v6 on v5

--- a/solution.py
+++ b/solution.py
@@ -28,6 +28,32 @@
 def split(w):
     high = w.astype(jnp.bfloat16).astype(jnp.float32)
     return high, w - high
+
+
+def pack_tiles(cap, cells_dev, weights, cells, dest, count, packets):
+    slots = packets.shape[0]
+    tiles = cells.shape[0]
+    names = dest[...]
+    live = (lax.broadcasted_iota(jnp.int32, (1, tiles), 1) < count[0]).astype(jnp.float32)
+    same = (lax.broadcasted_iota(jnp.int32, (slots // cap, tiles), 0) == names).astype(jnp.float32)
+    shape = (tiles, tiles)
+    earlier = lax.broadcasted_iota(jnp.int32, shape, 0) < lax.broadcasted_iota(jnp.int32, shape, 1)
+    before = jnp.dot(same, earlier.astype(jnp.float32), preferred_element_type=jnp.float32)
+    rank = jnp.sum(same * before, axis=0, keepdims=True).astype(jnp.int32)
+    slot = lax.broadcasted_iota(jnp.int32, (slots, tiles), 0)
+    placed = (slot == names * cap + rank).astype(jnp.float32) * live
+    held = jnp.sum((slot == names * cap).astype(jnp.float32) * live, axis=1, keepdims=True)
+    rows = [weights[0], weights[1], weights[2], cells[...].astype(jnp.float32)]
+    found = jnp.dot(
+        placed,
+        jnp.concatenate(rows, axis=1),
+        precision=lax.Precision.HIGHEST,
+        preferred_element_type=jnp.float32,
+    )
+    length = cells.shape[1]
+    for c in range(3):
+        packets[:, c, :] = found[:, c * length : (c + 1) * length]
+    packets[:, 3, :] = found[:, 3 * length :] + held * cells_dev
 
 
 def tile_moments(cap, nz, packets, moments):
@@ -88,7 +114,6 @@
     cells,
     dest,
     count,
-    filled,
     sems,
 ):
     cx, cy, nz = visc.shape
@@ -107,26 +132,8 @@
         copies.start(velo.at[:, :, pl.ds(at, 8), :], rows.at[3:6])
         copies.start(visc.at[:, pl.ds(at, 8), :], rows.at[6])
 
-    packets[...] = jnp.zeros_like(packets)
-    n_slab = packets.shape[0] // cap
-    for d in range(n_slab):
-        filled[d] = 0
     copies.wait(0, 4)
-
-    def place(r, carry):
-        d = dest[0, r]
-        slot = filled[d]
-        at = d * cap + slot
-        for c in range(3):
-            packets[at, c : c + 1, :] = weights[c, pl.ds(r, 1), :]
-        packets[at, 3:4, :] = cells[pl.ds(r, 1), :].astype(jnp.float32)
-        filled[d] = slot + 1
-        return carry
-
-    lax.fori_loop(0, count[0], place, 0)
-    for d in range(n_slab):
-        held = (filled[d] * (cx * cy * nz)).astype(jnp.float32)
-        packets[d * cap, 3:4, :] = packets[d * cap, 3:4, :] + held
+    pack_tiles(cap, cx * cy * nz, weights, cells, dest, count, packets)
     copies.start(packets, packets_out)
     copies.wait(4, 10)
     copies.start(near, near_out)
@@ -167,9 +174,8 @@
             pltpu.VMEM((7, cx, 8, nz), jnp.float32),
             pltpu.VMEM(weights.shape, jnp.float32),
             pltpu.VMEM(cells.shape, jnp.int32),
-            pltpu.SMEM(dest.shape, jnp.int32),
+            pltpu.VMEM(dest.shape, jnp.int32),
             pltpu.SMEM(count.shape, jnp.int32),
-            pltpu.SMEM((n_slab,), jnp.int32),
             pltpu.SemaphoreType.DMA((22,)),
         ],
         compiler_params=FIRST_PARAMS,

time: 36.7 us -> 36.7 us (level)
  no operation moved by 1% of the time
where the time goes in v6:
time: 36.7 us; the launch traced here: 36.4 us
  starting transfers between devices  17.5 us (48%)
  Pallas kernels  9.92 us (27%)
  waiting for transfers between devices  7.51 us (20%)
  between operations  1.49 us (4%)
    all_to_all x1, starting transfers between devices, per_device(): arrived = lax.all_to_all(packets, 'slab', 0, 0, tiled=True)  7.59 us
    all_to_all x1, starting transfers between devices, per_device(): load = lax.all_to_all(load, ('slab', 'pencil'), 0, 0, tiled=True)  5.46 us
    ppermute x4, starting transfers between devices, swapped(): return lax.ppermute(array, axis, up + [(j, i) for i, j in up])  4.4 us
    all_to_all x1, waiting for transfers between devices, per_device(): load = lax.all_to_all(load, ('slab', 'pencil'), 0, 0, tiled=True)  4.15 us
    all_to_all x1, waiting for transfers between devices, per_device(): arrived = lax.all_to_all(packets, 'slab', 0, 0, tiled=True)  3.35 us
    pallas_call x1, Pallas kernels, deposit(): pl.pallas_call(functools.partial(deposit_kernel, cap), out_shape=shaped(*...  3.26 us
    pallas_call x1, Pallas kernels, to_send(): pl.pallas_call(functools.partial(send_kernel, cap), out_shape=made, in_sp...  2.85 us
    pallas_call x1, Pallas kernels, inner(): pl.pallas_call(inner_kernel, out_shape=(shaped(*vort.shape), shaped(*tile...  2.07 us
  transfers between devices with their start and end apart: 6, of which 2 were waited for; matrix products, arithmetic and copies ran while one was open for 0% of the time, Pallas kernels for 17%

profile of v6, /device:TPU:0, one launch (start us, length us, event | category | flops | bytes accessed | tf_op | source)
XLA Modules:
  0.0 36.4 jit_solution(11819260158782455001)
XLA Ops:
  1.3 0.0 copy-start
  1.3 0.0 copy-start.1
  1.3 2.8 %shard_map.86 = (f32[7,32,256]{2,1,0:T(8,128)}, f32[7,32,256]{2,1,0:T(8,128)}, f32[7,8,256]{2,1,0:T(8,128)}, f32[7,8,256]{2,1,0:T(8,128)}, f32[64,4,128]{2,1,0:T(4,128)}, /*index=5*/f32[4,128]{1,0:T(4,128)}) custom-call(f32[3,8,32,256]{3,2,1,0:T(8,128)} %vort.3, f32[3,8,32,256]{3,2,1,0:T(8,128)} %velo.3, f32[8,32,256]{2,1,0:T(8,128)} %visc.3, ...), custom_call_target="tpu_custom_call" | custom-call | tf_op jit(solution)/shard_map/pallas_call | solution.py:166
  4.2 0.0 copy-start.2
  4.2 3.0 %collective-permute-start = (f32[7,32,256]{2,1,0:T(8,128)}, f32[7,32,256]{2,1,0:T(8,128)S(1)}, u32[]{:S(2)}, u32[]{:S(2)}) collective-permute-start(f32[7,32,256]{2,1,0:T(8,128)} %get-tuple-element.15.near), channel_id=1, source_target_pairs={{0,4},{8,12},{16,20},{24,28},{4,0},{12,8},{20,16},{28,24},{1,5},{9... | collective-permute-start | bytes 688136 | tf_op jit(solution)/shard_map/ppermute | solution.py:449
  7.2 0.7 %collective-permute-start.1 = (f32[7,32,256]{2,1,0:T(8,128)}, f32[7,32,256]{2,1,0:T(8,128)S(1)}, u32[]{:S(2)}, u32[]{:S(2)}) collective-permute-start(f32[7,32,256]{2,1,0:T(8,128)} %get-tuple-element.16.far), channel_id=1, source_target_pairs={{4,8},{12,16},{20,24},{8,4},{16,12},{24,20},{5,9},{13,17},{21,25},... | collective-permute-start | bytes 688136 | tf_op jit(solution)/shard_map/ppermute | solution.py:449
  7.8 7.6 %all-to-all-start = ((f32[64,4,128]{2,1,0:T(4,128)}), f32[64,4,128]{2,1,0:T(4,128)S(1)}, u32[]{:S(2)}, u32[]{:S(2)}) async-start(f32[64,4,128]{2,1,0:T(4,128)} %get-tuple-element.20), calls=%async_computation | async-start | bytes 262144 | tf_op jit(solution)/shard_map/all_to_all | solution.py:464
  15.4 0.1 collective-permute-start.2
  15.5 0.7 %collective-permute-start.3 = (f32[7,8,256]{2,1,0:T(8,128)}, f32[7,8,256]{2,1,0:T(8,128)S(1)}, u32[]{:S(2)}, u32[]{:S(2)}) collective-permute-start(f32[7,8,256]{2,1,0:T(8,128)} %get-tuple-element.18.other), channel_id=1, source_target_pairs={{1,2},{2,1},{5,6},{6,5},{9,10},{10,9},{13,14},{14,13},{17,18},{18,... | collective-permute-start | bytes 172040 | tf_op jit(solution)/shard_map/ppermute | solution.py:449
  16.2 0.0 copy-start.3
  16.2 0.0 copy-start.4
  16.2 0.0 copy-start.5
  16.3 0.0 copy-start.6
  16.3 2.1 %shard_map.87 = (f32[3,8,32,256]{3,2,1,0:T(8,128)S(1)}, f32[4,128]{1,0:T(4,128)S(1)}) custom-call(f32[3,8,32,256]{3,2,1,0:T(8,128)S(1)} %copy-done, f32[3,8,32,256]{3,2,1,0:T(8,128)S(1)} %copy-done.1, f32[8,32,256]{2,1,0:T(8,128)S(1)} %copy-done.2, f32[4,128]{1,0:T(4,128)S(1)} %copy-done.7), custom_call_target="tpu_custom_call" | custom-call | tf_op jit(solution)/shard_map/pallas_call | solution.py:254
  18.3 0.0 collective-permute-done.2.swap_in
  18.4 0.0 collective-permute-done.3.other_in
  18.4 0.0 collective-permute-done.near_in
  18.4 0.0 collective-permute-done.1.far_in
  18.4 1.0 %shard_map.88 = (f32[3,8,32,256]{3,2,1,0:T(8,128)S(1)}, f32[32,4,128]{2,1,0:T(4,128)}) custom-call(f32[3,8,32,256]{3,2,1,0:T(8,128)S(1)} %get-tuple-element.13.inside, f32[4,128]{1,0:T(4,128)S(1)} %get-tuple-element.14.moments, f32[7,32,256]{2,1,0:T(8,128)S(1)} %copy-done.3, f32[7,32,256]{2,1,0:T(8,128)S(1)} %copy-done.4, f32[7,8,256]{2,1,0:T(8,128)S(1)} %copy-done.5, ...), custom_call_target="tpu_custom_call" | custom-call | tf_op jit(solution)/shard_map/pallas_call | solution.py:309
  19.4 3.4 %all-to-all-done.load = f32[64,4,128]{2,1,0:T(4,128)S(1)} async-done(((f32[64,4,128]{2,1,0:T(4,128)}), f32[64,4,128]{2,1,0:T(4,128)S(1)}, u32[]{:S(2)}, u32[]{:S(2)}) %all-to-all-start) | async-done | bytes 131104 | tf_op jit(solution)/shard_map/all_to_all | solution.py:464
  22.8 5.5 %all-to-all-start.1 = ((f32[32,4,128]{2,1,0:T(4,128)}), f32[32,4,128]{2,1,0:T(4,128)S(1)}, u32[]{:S(2)}, u32[]{:S(2)}) async-start(f32[32,4,128]{2,1,0:T(4,128)} %get-tuple-element.21), calls=%async_computation.1 | async-start | bytes 131072 | tf_op jit(solution)/shard_map/all_to_all | solution.py:467
  28.2 3.3 %shard_map.89 = f32[3,8,32,256]{3,2,1,0:T(8,128)} custom-call(f32[3,8,32,256]{3,2,1,0:T(8,128)S(1)} %get-tuple-element.19.inside, f32[64,4,128]{2,1,0:T(4,128)S(1)} %all-to-all-done.load), custom_call_target="tpu_custom_call" | custom-call | tf_op jit(solution)/shard_map/pallas_call | solution.py:434
  31.5 4.1 %all-to-all-done.1.load = f32[32,4,128]{2,1,0:T(4,128)S(1)} async-done(((f32[32,4,128]{2,1,0:T(4,128)}), f32[32,4,128]{2,1,0:T(4,128)S(1)}, u32[]{:S(2)}, u32[]{:S(2)}) %all-to-all-start.1) | async-done | bytes 65568 | tf_op jit(solution)/shard_map/all_to_all | solution.py:467
  35.7 0.7 %shard_map.90 = f32[3,1,1,16]{3,2,1,0:T(1,128)} custom-call(f32[32,4,128]{2,1,0:T(4,128)S(1)} %all-to-all-done.1.load), custom_call_target="tpu_custom_call" | custom-call | tf_op jit(solution)/shard_map/pallas_call | solution.py:361
  (9 shorter events, 0.0 us)
Async XLA Ops:
  1.3 14.9 %copy-start = (f32[3,8,32,256]{3,2,1,0:T(8,128)S(1)}, f32[3,8,32,256]{3,2,1,0:T(8,128)}, u32[]{:S(2)}) copy-start(f32[3,8,32,256]{3,2,1,0:T(8,128)} %vort.3) | copy-start | bytes 2359300
  1.3 14.9 %copy-start.1 = (f32[3,8,32,256]{3,2,1,0:T(8,128)S(1)}, f32[3,8,32,256]{3,2,1,0:T(8,128)}, u32[]{:S(2)}) copy-start(f32[3,8,32,256]{3,2,1,0:T(8,128)} %velo.3) | copy-start | bytes 2359300
  4.2 12.1 %copy-start.2 = (f32[8,32,256]{2,1,0:T(8,128)S(1)}, f32[8,32,256]{2,1,0:T(8,128)}, u32[]{:S(2)}) copy-start(f32[8,32,256]{2,1,0:T(8,128)} %visc.3) | copy-start | bytes 786436
  4.2 14.2 %collective-permute-start = (f32[7,32,256]{2,1,0:T(8,128)}, f32[7,32,256]{2,1,0:T(8,128)S(1)}, u32[]{:S(2)}, u32[]{:S(2)}) collective-permute-start(f32[7,32,256]{2,1,0:T(8,128)} %get-tuple-element.15.near), channel_id=1, source_target_pairs={{0,4},{8,12},{16,20},{24,28},{4,0},{12,8},{20,16},{28,24},{1,5},{9... | collective-permute-start | bytes 688136 | tf_op jit(solution)/shard_map/ppermute | solution.py:449
  7.2 11.2 %collective-permute-start.1 = (f32[7,32,256]{2,1,0:T(8,128)}, f32[7,32,256]{2,1,0:T(8,128)S(1)}, u32[]{:S(2)}, u32[]{:S(2)}) collective-permute-start(f32[7,32,256]{2,1,0:T(8,128)} %get-tuple-element.16.far), channel_id=1, source_target_pairs={{4,8},{12,16},{20,24},{8,4},{16,12},{24,20},{5,9},{13,17},{21,25},... | collective-permute-start | bytes 688136 | tf_op jit(solution)/shard_map/ppermute | solution.py:449
  7.8 14.9 %all-to-all-start = ((f32[64,4,128]{2,1,0:T(4,128)}), f32[64,4,128]{2,1,0:T(4,128)S(1)}, u32[]{:S(2)}, u32[]{:S(2)}) async-start(f32[64,4,128]{2,1,0:T(4,128)} %get-tuple-element.20), calls=%async_computation | async-start | bytes 262144 | tf_op jit(solution)/shard_map/all_to_all | solution.py:464
  15.4 0.8 %copy-start.7 = (f32[4,128]{1,0:T(4,128)S(1)}, f32[4,128]{1,0:T(4,128)}, u32[]{:S(2)}) copy-start(f32[4,128]{1,0:T(4,128)} %get-tuple-element.12.tiles_in) | copy-start | bytes 6148
  15.4 2.9 %collective-permute-start.2 = (f32[7,8,256]{2,1,0:T(8,128)}, f32[7,8,256]{2,1,0:T(8,128)S(1)}, u32[]{:S(2)}, u32[]{:S(2)}) collective-permute-start(f32[7,8,256]{2,1,0:T(8,128)} %get-tuple-element.17.swap), channel_id=1, source_target_pairs={{0,1},{2,3},{1,0},{3,2},{4,5},{6,7},{5,4},{7,6},{8,9},{10,11},{9,8... | collective-permute-start | bytes 172040 | tf_op jit(solution)/shard_map/ppermute | solution.py:449
  15.5 2.8 %collective-permute-start.3 = (f32[7,8,256]{2,1,0:T(8,128)}, f32[7,8,256]{2,1,0:T(8,128)S(1)}, u32[]{:S(2)}, u32[]{:S(2)}) collective-permute-start(f32[7,8,256]{2,1,0:T(8,128)} %get-tuple-element.18.other), channel_id=1, source_target_pairs={{1,2},{2,1},{5,6},{6,5},{9,10},{10,9},{13,14},{14,13},{17,18},{18,... | collective-permute-start | bytes 172040 | tf_op jit(solution)/shard_map/ppermute | solution.py:449
  16.2 2.2 %copy-start.3 = (f32[7,32,256]{2,1,0:T(8,128)S(1)}, f32[7,32,256]{2,1,0:T(8,128)}, u32[]{:S(2)}) copy-start(f32[7,32,256]{2,1,0:T(8,128)} %get-tuple-element.15.near) | copy-start | bytes 688132
  16.2 2.2 %copy-start.4 = (f32[7,32,256]{2,1,0:T(8,128)S(1)}, f32[7,32,256]{2,1,0:T(8,128)}, u32[]{:S(2)}) copy-start(f32[7,32,256]{2,1,0:T(8,128)} %get-tuple-element.16.far) | copy-start | bytes 688132
  16.2 2.2 %copy-start.5 = (f32[7,8,256]{2,1,0:T(8,128)S(1)}, f32[7,8,256]{2,1,0:T(8,128)}, u32[]{:S(2)}) copy-start(f32[7,8,256]{2,1,0:T(8,128)} %get-tuple-element.17.swap) | copy-start | bytes 172036
  16.3 2.2 %copy-start.6 = (f32[7,8,256]{2,1,0:T(8,128)S(1)}, f32[7,8,256]{2,1,0:T(8,128)}, u32[]{:S(2)}) copy-start(f32[7,8,256]{2,1,0:T(8,128)} %get-tuple-element.18.other) | copy-start | bytes 172036
  22.8 12.9 %all-to-all-start.1 = ((f32[32,4,128]{2,1,0:T(4,128)}), f32[32,4,128]{2,1,0:T(4,128)S(1)}, u32[]{:S(2)}, u32[]{:S(2)}) async-start(f32[32,4,128]{2,1,0:T(4,128)} %get-tuple-element.21), calls=%async_computation.1 | async-start | bytes 131072 | tf_op jit(solution)/shard_map/all_to_all | solution.py:467

commit v7 on v6

--- a/solution.py
+++ b/solution.py
@@ -108,8 +108,6 @@
     other,
     packets,
     moments,
-    lows,
-    highs,
     weights,
     cells,
     dest,
@@ -127,11 +125,11 @@
         copies.start(vort.at[:, at], face.at[0:3])
         copies.start(velo.at[:, at], face.at[3:6])
         copies.start(visc.at[at], face.at[6])
-    for rows, at in ((lows, 0), (highs, cy - 8)):
-        copies.start(vort.at[:, :, pl.ds(at, 8), :], rows.at[0:3])
-        copies.start(velo.at[:, :, pl.ds(at, 8), :], rows.at[3:6])
-        copies.start(visc.at[:, pl.ds(at, 8), :], rows.at[6])
-
+    even = lax.axis_index("pencil") % 2 == 0
+    for face, at in ((swap, jnp.where(even, cy - 1, 0)), (other, jnp.where(even, 0, cy - 1))):
+        copies.start(vort.at[:, :, at], face.at[0:3])
+        copies.start(velo.at[:, :, at], face.at[3:6])
+        copies.start(visc.at[:, at], face.at[6])
     copies.wait(0, 4)
     pack_tiles(cap, cx * cy * nz, weights, cells, dest, count, packets)
     copies.start(packets, packets_out)
@@ -139,13 +137,6 @@
     copies.start(near, near_out)
     copies.start(far, far_out)
     copies.wait(10, 16)
-    even = lax.axis_index("pencil") % 2 == 0
-    for k in range(7):
-        for x in range(cx):
-            low = lows[k, x, 0:1, :]
-            high = highs[k, x, 7:8, :]
-            swap[k, x : x + 1, :] = jnp.where(even, high, low)
-            other[k, x : x + 1, :] = jnp.where(even, low, high)
     copies.start(swap, swap_out)
     copies.start(other, other_out)
     tile_moments(cap, nz, packets, moments)
@@ -170,8 +161,6 @@
         out_specs=(ANY,) * 6,
         scratch_shapes=[pltpu.VMEM(one.shape, jnp.float32) for one in made]
         + [
-            pltpu.VMEM((7, cx, 8, nz), jnp.float32),
-            pltpu.VMEM((7, cx, 8, nz), jnp.float32),
             pltpu.VMEM(weights.shape, jnp.float32),
             pltpu.VMEM(cells.shape, jnp.int32),
             pltpu.VMEM(dest.shape, jnp.int32),

time: 36.7 us -> 36.7 us (level)
  no operation moved by 1% of the time
where the time goes in v7:
time: 36.7 us; the launch traced here: 36.3 us
  starting transfers between devices  17.5 us (48%)
  Pallas kernels  9.77 us (27%)
  waiting for transfers between devices  7.51 us (20%)
  between operations  1.49 us (4%)
    all_to_all x1, starting transfers between devices, per_device(): arrived = lax.all_to_all(packets, 'slab', 0, 0, tiled=True)  7.59 us
    all_to_all x1, starting transfers between devices, per_device(): load = lax.all_to_all(load, ('slab', 'pencil'), 0, 0, tiled=True)  5.46 us
    ppermute x4, starting transfers between devices, swapped(): return lax.ppermute(array, axis, up + [(j, i) for i, j in up])  4.4 us
    all_to_all x1, waiting for transfers between devices, per_device(): load = lax.all_to_all(load, ('slab', 'pencil'), 0, 0, tiled=True)  4.15 us
    all_to_all x1, waiting for transfers between devices, per_device(): arrived = lax.all_to_all(packets, 'slab', 0, 0, tiled=True)  3.35 us
    pallas_call x1, Pallas kernels, deposit(): pl.pallas_call(functools.partial(deposit_kernel, cap), out_shape=shaped(*...  3.26 us
    pallas_call x1, Pallas kernels, to_send(): pl.pallas_call(functools.partial(send_kernel, cap), out_shape=made, in_sp...  2.71 us
    pallas_call x1, Pallas kernels, inner(): pl.pallas_call(inner_kernel, out_shape=(shaped(*vort.shape), shaped(*tile...  2.07 us
  transfers between devices with their start and end apart: 6, of which 2 were waited for; matrix products, arithmetic and copies ran while one was open for 0% of the time, Pallas kernels for 17%

profile of v7, /device:TPU:0, one launch (start us, length us, event | category | flops | bytes accessed | tf_op | source)
XLA Modules:
  0.0 36.3 jit_solution(9087998826935561223)
XLA Ops:
  1.3 0.0 copy-start
  1.3 2.7 %shard_map.86 = (f32[7,32,256]{2,1,0:T(8,128)}, f32[7,32,256]{2,1,0:T(8,128)}, f32[7,8,256]{2,1,0:T(8,128)}, f32[7,8,256]{2,1,0:T(8,128)}, f32[64,4,128]{2,1,0:T(4,128)}, /*index=5*/f32[4,128]{1,0:T(4,128)}) custom-call(f32[3,8,32,256]{3,2,1,0:T(8,128)} %vort.3, f32[3,8,32,256]{3,2,1,0:T(8,128)} %velo.3, f32[8,32,256]{2,1,0:T(8,128)} %visc.3, ...), custom_call_target="tpu_custom_call" | custom-call | tf_op jit(solution)/shard_map/pallas_call | solution.py:157
  4.0 0.0 copy-start.2
  4.0 3.0 %collective-permute-start = (f32[7,32,256]{2,1,0:T(8,128)}, f32[7,32,256]{2,1,0:T(8,128)S(1)}, u32[]{:S(2)}, u32[]{:S(2)}) collective-permute-start(f32[7,32,256]{2,1,0:T(8,128)} %get-tuple-element.15.near), channel_id=1, source_target_pairs={{0,4},{8,12},{16,20},{24,28},{4,0},{12,8},{20,16},{28,24},{1,5},{9... | collective-permute-start | bytes 688136 | tf_op jit(solution)/shard_map/ppermute | solution.py:438
  7.0 0.7 %collective-permute-start.1 = (f32[7,32,256]{2,1,0:T(8,128)}, f32[7,32,256]{2,1,0:T(8,128)S(1)}, u32[]{:S(2)}, u32[]{:S(2)}) collective-permute-start(f32[7,32,256]{2,1,0:T(8,128)} %get-tuple-element.16.far), channel_id=1, source_target_pairs={{4,8},{12,16},{20,24},{8,4},{16,12},{24,20},{5,9},{13,17},{21,25},... | collective-permute-start | bytes 688136 | tf_op jit(solution)/shard_map/ppermute | solution.py:438
  7.7 7.6 %all-to-all-start = ((f32[64,4,128]{2,1,0:T(4,128)}), f32[64,4,128]{2,1,0:T(4,128)S(1)}, u32[]{:S(2)}, u32[]{:S(2)}) async-start(f32[64,4,128]{2,1,0:T(4,128)} %get-tuple-element.20), calls=%async_computation | async-start | bytes 262144 | tf_op jit(solution)/shard_map/all_to_all | solution.py:453
  15.3 0.1 collective-permute-start.2
  15.4 0.7 %collective-permute-start.3 = (f32[7,8,256]{2,1,0:T(8,128)}, f32[7,8,256]{2,1,0:T(8,128)S(1)}, u32[]{:S(2)}, u32[]{:S(2)}) collective-permute-start(f32[7,8,256]{2,1,0:T(8,128)} %get-tuple-element.18.other), channel_id=1, source_target_pairs={{1,2},{2,1},{5,6},{6,5},{9,10},{10,9},{13,14},{14,13},{17,18},{18,... | collective-permute-start | bytes 172040 | tf_op jit(solution)/shard_map/ppermute | solution.py:438
  16.0 0.0 copy-done
  16.1 0.0 copy-done.1
  16.1 0.0 copy-done.2
  16.1 0.0 copy-done.7
  16.1 0.0 copy-start.3
  16.1 2.1 %shard_map.87 = (f32[3,8,32,256]{3,2,1,0:T(8,128)S(1)}, f32[4,128]{1,0:T(4,128)S(1)}) custom-call(f32[3,8,32,256]{3,2,1,0:T(8,128)S(1)} %copy-done, f32[3,8,32,256]{3,2,1,0:T(8,128)S(1)} %copy-done.1, f32[8,32,256]{2,1,0:T(8,128)S(1)} %copy-done.2, f32[4,128]{1,0:T(4,128)S(1)} %copy-done.7), custom_call_target="tpu_custom_call" | custom-call | tf_op jit(solution)/shard_map/pallas_call | solution.py:243
  18.2 0.0 collective-permute-done.2.swap_in
  18.2 0.0 collective-permute-done.3.other_in
  18.2 0.0 collective-permute-done.near_in
  18.2 0.0 collective-permute-done.1.far_in
  18.3 1.0 %shard_map.88 = (f32[3,8,32,256]{3,2,1,0:T(8,128)S(1)}, f32[32,4,128]{2,1,0:T(4,128)}) custom-call(f32[3,8,32,256]{3,2,1,0:T(8,128)S(1)} %get-tuple-element.13.inside, f32[4,128]{1,0:T(4,128)S(1)} %get-tuple-element.14.moments, f32[7,32,256]{2,1,0:T(8,128)S(1)} %copy-done.3, f32[7,32,256]{2,1,0:T(8,128)S(1)} %copy-done.4, f32[7,8,256]{2,1,0:T(8,128)S(1)} %copy-done.5, ...), custom_call_target="tpu_custom_call" | custom-call | tf_op jit(solution)/shard_map/pallas_call | solution.py:298
  19.3 3.4 %all-to-all-done.load = f32[64,4,128]{2,1,0:T(4,128)S(1)} async-done(((f32[64,4,128]{2,1,0:T(4,128)}), f32[64,4,128]{2,1,0:T(4,128)S(1)}, u32[]{:S(2)}, u32[]{:S(2)}) %all-to-all-start) | async-done | bytes 131104 | tf_op jit(solution)/shard_map/all_to_all | solution.py:453
  22.6 5.5 %all-to-all-start.1 = ((f32[32,4,128]{2,1,0:T(4,128)}), f32[32,4,128]{2,1,0:T(4,128)S(1)}, u32[]{:S(2)}, u32[]{:S(2)}) async-start(f32[32,4,128]{2,1,0:T(4,128)} %get-tuple-element.21), calls=%async_computation.1 | async-start | bytes 131072 | tf_op jit(solution)/shard_map/all_to_all | solution.py:456
  28.1 3.3 %shard_map.89 = f32[3,8,32,256]{3,2,1,0:T(8,128)} custom-call(f32[3,8,32,256]{3,2,1,0:T(8,128)S(1)} %get-tuple-element.19.inside, f32[64,4,128]{2,1,0:T(4,128)S(1)} %all-to-all-done.load), custom_call_target="tpu_custom_call" | custom-call | tf_op jit(solution)/shard_map/pallas_call | solution.py:423
  31.4 4.1 %all-to-all-done.1.load = f32[32,4,128]{2,1,0:T(4,128)S(1)} async-done(((f32[32,4,128]{2,1,0:T(4,128)}), f32[32,4,128]{2,1,0:T(4,128)S(1)}, u32[]{:S(2)}, u32[]{:S(2)}) %all-to-all-start.1) | async-done | bytes 65568 | tf_op jit(solution)/shard_map/all_to_all | solution.py:456
  35.5 0.7 %shard_map.90 = f32[3,1,1,16]{3,2,1,0:T(1,128)} custom-call(f32[32,4,128]{2,1,0:T(4,128)S(1)} %all-to-all-done.1.load), custom_call_target="tpu_custom_call" | custom-call | tf_op jit(solution)/shard_map/pallas_call | solution.py:350
  (9 shorter events, 0.0 us)
Async XLA Ops:
  1.3 14.8 %copy-start = (f32[3,8,32,256]{3,2,1,0:T(8,128)S(1)}, f32[3,8,32,256]{3,2,1,0:T(8,128)}, u32[]{:S(2)}) copy-start(f32[3,8,32,256]{3,2,1,0:T(8,128)} %vort.3) | copy-start | bytes 2359300
  1.3 14.8 %copy-start.1 = (f32[3,8,32,256]{3,2,1,0:T(8,128)S(1)}, f32[3,8,32,256]{3,2,1,0:T(8,128)}, u32[]{:S(2)}) copy-start(f32[3,8,32,256]{3,2,1,0:T(8,128)} %velo.3) | copy-start | bytes 2359300
  4.0 12.1 %copy-start.2 = (f32[8,32,256]{2,1,0:T(8,128)S(1)}, f32[8,32,256]{2,1,0:T(8,128)}, u32[]{:S(2)}) copy-start(f32[8,32,256]{2,1,0:T(8,128)} %visc.3) | copy-start | bytes 786436
  4.0 14.2 %collective-permute-start = (f32[7,32,256]{2,1,0:T(8,128)}, f32[7,32,256]{2,1,0:T(8,128)S(1)}, u32[]{:S(2)}, u32[]{:S(2)}) collective-permute-start(f32[7,32,256]{2,1,0:T(8,128)} %get-tuple-element.15.near), channel_id=1, source_target_pairs={{0,4},{8,12},{16,20},{24,28},{4,0},{12,8},{20,16},{28,24},{1,5},{9... | collective-permute-start | bytes 688136 | tf_op jit(solution)/shard_map/ppermute | solution.py:438
  7.0 11.2 %collective-permute-start.1 = (f32[7,32,256]{2,1,0:T(8,128)}, f32[7,32,256]{2,1,0:T(8,128)S(1)}, u32[]{:S(2)}, u32[]{:S(2)}) collective-permute-start(f32[7,32,256]{2,1,0:T(8,128)} %get-tuple-element.16.far), channel_id=1, source_target_pairs={{4,8},{12,16},{20,24},{8,4},{16,12},{24,20},{5,9},{13,17},{21,25},... | collective-permute-start | bytes 688136 | tf_op jit(solution)/shard_map/ppermute | solution.py:438
  7.7 14.9 %all-to-all-start = ((f32[64,4,128]{2,1,0:T(4,128)}), f32[64,4,128]{2,1,0:T(4,128)S(1)}, u32[]{:S(2)}, u32[]{:S(2)}) async-start(f32[64,4,128]{2,1,0:T(4,128)} %get-tuple-element.20), calls=%async_computation | async-start | bytes 262144 | tf_op jit(solution)/shard_map/all_to_all | solution.py:453
  15.3 0.8 %copy-start.7 = (f32[4,128]{1,0:T(4,128)S(1)}, f32[4,128]{1,0:T(4,128)}, u32[]{:S(2)}) copy-start(f32[4,128]{1,0:T(4,128)} %get-tuple-element.12.tiles_in) | copy-start | bytes 6148
  15.3 2.9 %collective-permute-start.2 = (f32[7,8,256]{2,1,0:T(8,128)}, f32[7,8,256]{2,1,0:T(8,128)S(1)}, u32[]{:S(2)}, u32[]{:S(2)}) collective-permute-start(f32[7,8,256]{2,1,0:T(8,128)} %get-tuple-element.17.swap), channel_id=1, source_target_pairs={{0,1},{2,3},{1,0},{3,2},{4,5},{6,7},{5,4},{7,6},{8,9},{10,11},{9,8... | collective-permute-start | bytes 172040 | tf_op jit(solution)/shard_map/ppermute | solution.py:438
  15.4 2.8 %collective-permute-start.3 = (f32[7,8,256]{2,1,0:T(8,128)}, f32[7,8,256]{2,1,0:T(8,128)S(1)}, u32[]{:S(2)}, u32[]{:S(2)}) collective-permute-start(f32[7,8,256]{2,1,0:T(8,128)} %get-tuple-element.18.other), channel_id=1, source_target_pairs={{1,2},{2,1},{5,6},{6,5},{9,10},{10,9},{13,14},{14,13},{17,18},{18,... | collective-permute-start | bytes 172040 | tf_op jit(solution)/shard_map/ppermute | solution.py:438
  16.1 2.2 %copy-start.3 = (f32[7,32,256]{2,1,0:T(8,128)S(1)}, f32[7,32,256]{2,1,0:T(8,128)}, u32[]{:S(2)}) copy-start(f32[7,32,256]{2,1,0:T(8,128)} %get-tuple-element.15.near) | copy-start | bytes 688132
  16.1 2.2 %copy-start.4 = (f32[7,32,256]{2,1,0:T(8,128)S(1)}, f32[7,32,256]{2,1,0:T(8,128)}, u32[]{:S(2)}) copy-start(f32[7,32,256]{2,1,0:T(8,128)} %get-tuple-element.16.far) | copy-start | bytes 688132
  16.1 2.2 %copy-start.5 = (f32[7,8,256]{2,1,0:T(8,128)S(1)}, f32[7,8,256]{2,1,0:T(8,128)}, u32[]{:S(2)}) copy-start(f32[7,8,256]{2,1,0:T(8,128)} %get-tuple-element.17.swap) | copy-start | bytes 172036
  16.1 2.2 %copy-start.6 = (f32[7,8,256]{2,1,0:T(8,128)S(1)}, f32[7,8,256]{2,1,0:T(8,128)}, u32[]{:S(2)}) copy-start(f32[7,8,256]{2,1,0:T(8,128)} %get-tuple-element.18.other) | copy-start | bytes 172036
  22.6 12.9 %all-to-all-start.1 = ((f32[32,4,128]{2,1,0:T(4,128)}), f32[32,4,128]{2,1,0:T(4,128)S(1)}, u32[]{:S(2)}, u32[]{:S(2)}) async-start(f32[32,4,128]{2,1,0:T(4,128)} %get-tuple-element.21), calls=%async_computation.1 | async-start | bytes 131072 | tf_op jit(solution)/shard_map/all_to_all | solution.py:456

commit v8 on v7

--- a/solution.py
+++ b/solution.py
@@ -11,7 +11,7 @@
 TIME_STEP = 0.1
 LANES = 128
 SIDES = ("slab", "slab", "pencil", "pencil")
-GROUP = 8
+GROUP = 16
 VMEM_LIMIT = 24 * 1024 * 1024
 
 VMEM = pl.BlockSpec(memory_space=pltpu.VMEM)
@@ -96,16 +96,16 @@
     cells_in,
     dest_in,
     count_in,
+    far_out,
     near_out,
-    far_out,
+    other_out,
     swap_out,
-    other_out,
     packets_out,
     moments_out,
+    far,
     near,
-    far,
+    other,
     swap,
-    other,
     packets,
     moments,
     weights,
@@ -116,29 +116,30 @@
 ):
     cx, cy, nz = visc.shape
     copies = Copies(sems)
+    even = lax.axis_index("slab") % 2 == 0
+    for face, at in ((far, jnp.where(even, 0, cx - 1)), (near, jnp.where(even, cx - 1, 0))):
+        copies.start(vort.at[:, at], face.at[0:3])
+        copies.start(velo.at[:, at], face.at[3:6])
+        copies.start(visc.at[at], face.at[6])
     copies.start(weights_in, weights)
     copies.start(cells_in, cells)
     copies.start(dest_in, dest)
     copies.start(count_in, count)
-    even = lax.axis_index("slab") % 2 == 0
-    for face, at in ((near, jnp.where(even, cx - 1, 0)), (far, jnp.where(even, 0, cx - 1))):
-        copies.start(vort.at[:, at], face.at[0:3])
-        copies.start(velo.at[:, at], face.at[3:6])
-        copies.start(visc.at[at], face.at[6])
     even = lax.axis_index("pencil") % 2 == 0
-    for face, at in ((swap, jnp.where(even, cy - 1, 0)), (other, jnp.where(even, 0, cy - 1))):
+    for face, at in ((other, jnp.where(even, 0, cy - 1)), (swap, jnp.where(even, cy - 1, 0))):
         copies.start(vort.at[:, :, at], face.at[0:3])
         copies.start(velo.at[:, :, at], face.at[3:6])
         copies.start(visc.at[:, at], face.at[6])
-    copies.wait(0, 4)
+    copies.wait(0, 3)
+    copies.start(far, far_out)
+    copies.wait(3, 6)
+    copies.start(near, near_out)
+    copies.wait(6, 10)
     pack_tiles(cap, cx * cy * nz, weights, cells, dest, count, packets)
     copies.start(packets, packets_out)
-    copies.wait(4, 10)
-    copies.start(near, near_out)
-    copies.start(far, far_out)
     copies.wait(10, 16)
+    copies.start(other, other_out)
     copies.start(swap, swap_out)
-    copies.start(other, other_out)
     tile_moments(cap, nz, packets, moments)
     copies.start(moments, moments_out)
     copies.wait(16, 22)
@@ -257,7 +258,7 @@
 
 
 def edge_kernel(
-    inside, moments, near, far, swap, other, near_in, far_in, swap_in, other_in, out, load_out, load, side_change, sem
+    inside, moments, far, near, other, swap, far_in, near_in, other_in, swap_in, out, load_out, load, side_change, sem
 ):
     _, cx, cy, nz = out.shape
     even = lax.axis_index("pencil") % 2 == 0
@@ -356,63 +357,71 @@
     )(load)
 
 
+def deposit_step(group, first, listed, load, order, acc, shape):
+    cx, cy, nz = shape
+    rows = cx * cy // 2
+    wide = group * load.shape[2]
+
+    def numbers(length):
+        shape = (length // 16, 16, wide)
+        return (lax.broadcasted_iota(jnp.int32, shape, 0) * 16 + lax.broadcasted_iota(jnp.int32, shape, 1)).astype(
+            jnp.float32
+        ).astype(jnp.bfloat16)
+
+    def spread(row):
+        return jnp.broadcast_to(row, (16, wide)).astype(jnp.bfloat16)[None]
+
+    zero = jnp.zeros((), jnp.bfloat16)
+    one = jnp.ones((), jnp.bfloat16)
+    block = jnp.concatenate([load[order[first + k]] for k in range(group)], axis=1)
+    live = lax.broadcasted_iota(jnp.int32, (1, wide), 1) // load.shape[2] < listed - first
+    cell = block[3:4, :].astype(jnp.int32) % (cx * cy * nz)
+    row = cell // nz
+    half = row // rows
+    at_row = numbers(rows) == spread(jnp.where(live, row % rows, -1).astype(jnp.float32))
+    right = []
+    for h in range(2):
+        at_col = numbers(nz) == spread(jnp.where(half == h, cell % nz, -1).astype(jnp.float32))
+        right.append(jnp.where(at_col, one, zero).reshape(nz, wide))
+    left = []
+    for piece in split(block):
+        for c in range(3):
+            left.append(jnp.where(at_row, spread(piece[c : c + 1, :]), zero).reshape(rows, wide))
+    added = lax.dot_general(
+        jnp.concatenate(left, axis=0),
+        jnp.concatenate(right, axis=0),
+        (((1,), (1,)), ((), ())),
+        preferred_element_type=jnp.float32,
+    )
+    acc[...] += added[: 3 * rows] + added[3 * rows :]
+
+
 def deposit_kernel(cap, inside, load, out, acc, order):
     _, cx, cy, nz = out.shape
-    rows = cx * cy // 2
-    cells = 2 * rows * nz
-    n_slab = load.shape[0] // cap
-    wide = GROUP * load.shape[2]
+    shape = (cx, cy, nz)
     acc[...] = jnp.zeros_like(acc)
     listed = jnp.int32(0)
-    for d in range(n_slab):
+    for d in range(load.shape[0] // cap):
         first = d * cap
-        held = jnp.max(load[first, 3:4, :]).astype(jnp.int32) // cells
+        held = jnp.max(load[first, 3:4, :]).astype(jnp.int32) // (cx * cy * nz)
         for k in range(cap):
             order[listed + k] = first + k
         listed = listed + held
     for k in range(GROUP):
         order[listed + k] = 0
-    def numbers(length):
-        shape = (length // 16, 16, wide)
-        return (lax.broadcasted_iota(jnp.int32, shape, 0) * 16 + lax.broadcasted_iota(jnp.int32, shape, 1)).astype(
-            jnp.float32
-        ).astype(jnp.bfloat16)
-
-    def spread(row):
-        return jnp.broadcast_to(row, (16, wide)).astype(jnp.bfloat16)[None]
-
-    row_numbers = numbers(rows)
-    col_numbers = numbers(nz)
-    place = lax.broadcasted_iota(jnp.int32, (1, wide), 1) // load.shape[2]
-    zero = jnp.zeros((), jnp.bfloat16)
-    one = jnp.ones((), jnp.bfloat16)
-
-    def group(g, carry):
-        tiles = [load[order[g * GROUP + k]] for k in range(GROUP)]
-        block = jnp.concatenate(tiles, axis=1)
-        live = place < listed - g * GROUP
-        cell = block[3:4, :].astype(jnp.int32) % cells
-        row = cell // nz
-        half = row // rows
-        at_row = row_numbers == spread(jnp.where(live, row % rows, -1).astype(jnp.float32))
-        right = []
-        for h in range(2):
-            at_col = col_numbers == spread(jnp.where(half == h, cell % nz, -1).astype(jnp.float32))
-            right.append(jnp.where(at_col, one, zero).reshape(nz, wide))
-        left = []
-        for piece in split(block):
-            for c in range(3):
-                left.append(jnp.where(at_row, spread(piece[c : c + 1, :]), zero).reshape(rows, wide))
-        added = lax.dot_general(
-            jnp.concatenate(left, axis=0),
-            jnp.concatenate(right, axis=0),
-            (((1,), (1,)), ((), ())),
-            preferred_element_type=jnp.float32,
-        )
-        acc[...] += added[: 3 * rows] + added[3 * rows :]
+    rest = listed % GROUP
+    whole = listed // GROUP + (rest > GROUP // 2).astype(jnp.int32)
+
+    def step(g, carry):
+        deposit_step(GROUP, g * GROUP, listed, load, order, acc, shape)
         return carry
 
-    lax.fori_loop(0, (listed + GROUP - 1) // GROUP, group, 0)
+    lax.fori_loop(0, whole, step, 0)
+
+    @pl.when((rest > 0) & (rest <= GROUP // 2))
+    def _():
+        deposit_step(GROUP // 2, whole * GROUP, listed, load, order, acc, shape)
+
     for h in range(2):
         span = slice(h * (cx // 2), (h + 1) * (cx // 2))
         change = acc[:, h * nz : (h + 1) * nz].reshape(3, cx // 2, cy, nz)
@@ -449,7 +458,7 @@
     *faces, packets, tiles = to_send(
         vorticity, velocity, viscosity, weights, tile_cells, tile_dest.T, count, n_slab, cap
     )
-    halos = [swapped(face, axis, k % 2) for k, (face, axis) in enumerate(zip(faces, SIDES))]
+    halos = [swapped(face, axis, 1 - k % 2) for k, (face, axis) in enumerate(zip(faces, SIDES))]
     arrived = lax.all_to_all(packets, "slab", 0, 0, tiled=True)
     inside, moments = inner(vorticity, velocity, viscosity, tiles)
     advanced, load = edges(inside, moments, faces, halos, n_slab * n_pencil)

time: 36.7 us -> 37 us (level)
  waiting for transfers between devices: 7.51 us -> 3.9 us
  starting transfers between devices: 17.5 us -> 20.5 us
  Pallas kernels: 9.77 us -> 10.8 us
    ppermute x4, starting transfers between devices: 4.4 us -> 10.2 us  [swapped(): return lax.ppermute(array, axis, up + [(j, i) for i, j in up])]
    all_to_all x1, starting transfers between devices: 7.59 us -> 4.68 us  [per_device(): arrived = lax.all_to_all(packets, 'slab', 0, 0, tiled=True)]
    all_to_all x1, waiting for transfers between devices: 3.35 us -> 0.51 us  [per_device(): arrived = lax.all_to_all(packets, 'slab', 0, 0, tiled=True)]
    all_to_all x1, waiting for transfers between devices: 4.15 us -> 3.35 us  [per_device(): load = lax.all_to_all(load, ('slab', 'pencil'), 0, 0, tiled=True)]
    pallas_call x1, Pallas kernels: 3.26 us -> 4.06 us  [deposit(): pl.pallas_call(functools.partial(deposit_kernel, cap), out_shape=shaped(*...]
  transfers between devices with their start and end apart: 6 -> 6, of which waited for: 2 -> 2; matrix products, arithmetic and copies ran while one was open for 0% -> 0% of each run, Pallas kernels for 17% -> 19%
where the time goes in v8:
time: 37 us; the launch traced here: 36.7 us
  starting transfers between devices  20.5 us (55%)
  Pallas kernels  10.8 us (29%)
  waiting for transfers between devices  3.9 us (11%)
  between operations  1.42 us (4%)
    ppermute x4, starting transfers between devices, swapped(): return lax.ppermute(array, axis, up + [(j, i) for i, j in up])  10.2 us
    all_to_all x1, starting transfers between devices, per_device(): load = lax.all_to_all(load, ('slab', 'pencil'), 0, 0, tiled=True)  5.59 us
    all_to_all x1, starting transfers between devices, per_device(): arrived = lax.all_to_all(packets, 'slab', 0, 0, tiled=True)  4.68 us
    pallas_call x1, Pallas kernels, deposit(): pl.pallas_call(functools.partial(deposit_kernel, cap), out_shape=shaped(*...  4.06 us
    all_to_all x1, waiting for transfers between devices, per_device(): load = lax.all_to_all(load, ('slab', 'pencil'), 0, 0, tiled=True)  3.35 us
    pallas_call x1, Pallas kernels, to_send(): pl.pallas_call(functools.partial(send_kernel, cap), out_shape=made, in_sp...  2.97 us
    pallas_call x1, Pallas kernels, inner(): pl.pallas_call(inner_kernel, out_shape=(shaped(*vort.shape), shaped(*tile...  2.07 us
    pallas_call x1, Pallas kernels, edges(): pl.pallas_call(edge_kernel, out_shape=(shaped(*inside.shape), load), in_s...  0.99 us
  transfers between devices with their start and end apart: 6, of which 2 were waited for; matrix products, arithmetic and copies ran while one was open for 0% of the time, Pallas kernels for 19%

profile of v8, /device:TPU:0, one launch (start us, length us, event | category | flops | bytes accessed | tf_op | source)
XLA Modules:
  0.0 36.7 jit_solution(8937868315438731687)
XLA Ops:
  1.3 0.0 copy-start
  1.3 0.0 copy-start.1
  1.3 3.0 %shard_map.86 = (f32[7,32,256]{2,1,0:T(8,128)}, f32[7,32,256]{2,1,0:T(8,128)}, f32[7,8,256]{2,1,0:T(8,128)}, f32[7,8,256]{2,1,0:T(8,128)}, f32[64,4,128]{2,1,0:T(4,128)}, /*index=5*/f32[4,128]{1,0:T(4,128)}) custom-call(f32[3,8,32,256]{3,2,1,0:T(8,128)} %vort.3, f32[3,8,32,256]{3,2,1,0:T(8,128)} %velo.3, f32[8,32,256]{2,1,0:T(8,128)} %visc.3, ...), custom_call_target="tpu_custom_call" | custom-call | tf_op jit(solution)/shard_map/pallas_call | solution.py:158
  4.3 0.0 copy-start.2
  4.3 0.8 %collective-permute-start = (f32[7,32,256]{2,1,0:T(8,128)}, f32[7,32,256]{2,1,0:T(8,128)S(1)}, u32[]{:S(2)}, u32[]{:S(2)}) collective-permute-start(f32[7,32,256]{2,1,0:T(8,128)} %get-tuple-element.15.far), channel_id=1, source_target_pairs={{4,8},{12,16},{20,24},{8,4},{16,12},{24,20},{5,9},{13,17},{21,25},... | collective-permute-start | bytes 688136 | tf_op jit(solution)/shard_map/ppermute | solution.py:447
  5.1 5.8 %collective-permute-start.1 = (f32[7,32,256]{2,1,0:T(8,128)}, f32[7,32,256]{2,1,0:T(8,128)S(1)}, u32[]{:S(2)}, u32[]{:S(2)}) collective-permute-start(f32[7,32,256]{2,1,0:T(8,128)} %get-tuple-element.16.near), channel_id=1, source_target_pairs={{0,4},{8,12},{16,20},{24,28},{4,0},{12,8},{20,16},{28,24},{1,5},{9... | collective-permute-start | bytes 688136 | tf_op jit(solution)/shard_map/ppermute | solution.py:447
  10.9 4.7 %all-to-all-start = ((f32[64,4,128]{2,1,0:T(4,128)}), f32[64,4,128]{2,1,0:T(4,128)S(1)}, u32[]{:S(2)}, u32[]{:S(2)}) async-start(f32[64,4,128]{2,1,0:T(4,128)} %get-tuple-element.20), calls=%async_computation | async-start | bytes 262144 | tf_op jit(solution)/shard_map/all_to_all | solution.py:462
  15.6 0.7 %collective-permute-start.2 = (f32[7,8,256]{2,1,0:T(8,128)}, f32[7,8,256]{2,1,0:T(8,128)S(1)}, u32[]{:S(2)}, u32[]{:S(2)}) collective-permute-start(f32[7,8,256]{2,1,0:T(8,128)} %get-tuple-element.17.other), channel_id=1, source_target_pairs={{1,2},{2,1},{5,6},{6,5},{9,10},{10,9},{13,14},{14,13},{17,18},{18,... | collective-permute-start | bytes 172040 | tf_op jit(solution)/shard_map/ppermute | solution.py:447
  16.2 2.9 %collective-permute-start.3 = (f32[7,8,256]{2,1,0:T(8,128)}, f32[7,8,256]{2,1,0:T(8,128)S(1)}, u32[]{:S(2)}, u32[]{:S(2)}) collective-permute-start(f32[7,8,256]{2,1,0:T(8,128)} %get-tuple-element.18.swap), channel_id=1, source_target_pairs={{0,1},{2,3},{1,0},{3,2},{4,5},{6,7},{5,4},{7,6},{8,9},{10,11},{9,8... | collective-permute-start | bytes 172040 | tf_op jit(solution)/shard_map/ppermute | solution.py:447
  19.2 0.0 copy-done
  19.2 0.0 copy-done.1
  19.2 0.0 copy-start.3
  19.2 2.1 %shard_map.87 = (f32[3,8,32,256]{3,2,1,0:T(8,128)S(1)}, f32[4,128]{1,0:T(4,128)S(1)}) custom-call(f32[3,8,32,256]{3,2,1,0:T(8,128)S(1)} %copy-done, f32[3,8,32,256]{3,2,1,0:T(8,128)S(1)} %copy-done.1, f32[8,32,256]{2,1,0:T(8,128)S(1)} %copy-done.2, f32[4,128]{1,0:T(4,128)S(1)} %copy-done.7), custom_call_target="tpu_custom_call" | custom-call | tf_op jit(solution)/shard_map/pallas_call | solution.py:244
  21.3 0.0 collective-permute-done.2.other_in
  21.3 0.0 collective-permute-done.3.swap_in
  21.3 0.0 collective-permute-done.far_in
  21.4 0.0 collective-permute-done.1.near_in
  21.4 0.0 copy-done.6
  21.4 1.0 %shard_map.88 = (f32[3,8,32,256]{3,2,1,0:T(8,128)S(1)}, f32[32,4,128]{2,1,0:T(4,128)}) custom-call(f32[3,8,32,256]{3,2,1,0:T(8,128)S(1)} %get-tuple-element.13.inside, f32[4,128]{1,0:T(4,128)S(1)} %get-tuple-element.14.moments, f32[7,32,256]{2,1,0:T(8,128)S(1)} %copy-done.3, f32[7,32,256]{2,1,0:T(8,128)S(1)} %copy-done.4, f32[7,8,256]{2,1,0:T(8,128)S(1)} %copy-done.5, ...), custom_call_target="tpu_custom_call" | custom-call | tf_op jit(solution)/shard_map/pallas_call | solution.py:299
  22.4 0.5 %all-to-all-done.load = f32[64,4,128]{2,1,0:T(4,128)S(1)} async-done(((f32[64,4,128]{2,1,0:T(4,128)}), f32[64,4,128]{2,1,0:T(4,128)S(1)}, u32[]{:S(2)}, u32[]{:S(2)}) %all-to-all-start) | async-done | bytes 131104 | tf_op jit(solution)/shard_map/all_to_all | solution.py:462
  22.9 5.6 %all-to-all-start.1 = ((f32[32,4,128]{2,1,0:T(4,128)}), f32[32,4,128]{2,1,0:T(4,128)S(1)}, u32[]{:S(2)}, u32[]{:S(2)}) async-start(f32[32,4,128]{2,1,0:T(4,128)} %get-tuple-element.21), calls=%async_computation.1 | async-start | bytes 131072 | tf_op jit(solution)/shard_map/all_to_all | solution.py:465
  28.5 4.1 %shard_map.89 = f32[3,8,32,256]{3,2,1,0:T(8,128)} custom-call(f32[3,8,32,256]{3,2,1,0:T(8,128)S(1)} %get-tuple-element.19.inside, f32[64,4,128]{2,1,0:T(4,128)S(1)} %all-to-all-done.load), custom_call_target="tpu_custom_call" | custom-call | tf_op jit(solution)/shard_map/pallas_call | solution.py:432
  32.6 3.3 %all-to-all-done.1.load = f32[32,4,128]{2,1,0:T(4,128)S(1)} async-done(((f32[32,4,128]{2,1,0:T(4,128)}), f32[32,4,128]{2,1,0:T(4,128)S(1)}, u32[]{:S(2)}, u32[]{:S(2)}) %all-to-all-start.1) | async-done | bytes 65568 | tf_op jit(solution)/shard_map/all_to_all | solution.py:465
  35.9 0.7 %shard_map.90 = f32[3,1,1,16]{3,2,1,0:T(1,128)} custom-call(f32[32,4,128]{2,1,0:T(4,128)S(1)} %all-to-all-done.1.load), custom_call_target="tpu_custom_call" | custom-call | tf_op jit(solution)/shard_map/pallas_call | solution.py:351
  (9 shorter events, 0.0 us)
Async XLA Ops:
  1.3 17.9 %copy-start = (f32[3,8,32,256]{3,2,1,0:T(8,128)S(1)}, f32[3,8,32,256]{3,2,1,0:T(8,128)}, u32[]{:S(2)}) copy-start(f32[3,8,32,256]{3,2,1,0:T(8,128)} %vort.3) | copy-start | bytes 2359300
  1.3 17.9 %copy-start.1 = (f32[3,8,32,256]{3,2,1,0:T(8,128)S(1)}, f32[3,8,32,256]{3,2,1,0:T(8,128)}, u32[]{:S(2)}) copy-start(f32[3,8,32,256]{3,2,1,0:T(8,128)} %velo.3) | copy-start | bytes 2359300
  4.3 14.9 %copy-start.2 = (f32[8,32,256]{2,1,0:T(8,128)S(1)}, f32[8,32,256]{2,1,0:T(8,128)}, u32[]{:S(2)}) copy-start(f32[8,32,256]{2,1,0:T(8,128)} %visc.3) | copy-start | bytes 786436
  4.3 17.1 %collective-permute-start = (f32[7,32,256]{2,1,0:T(8,128)}, f32[7,32,256]{2,1,0:T(8,128)S(1)}, u32[]{:S(2)}, u32[]{:S(2)}) collective-permute-start(f32[7,32,256]{2,1,0:T(8,128)} %get-tuple-element.15.far), channel_id=1, source_target_pairs={{4,8},{12,16},{20,24},{8,4},{16,12},{24,20},{5,9},{13,17},{21,25},... | collective-permute-start | bytes 688136 | tf_op jit(solution)/shard_map/ppermute | solution.py:447
  5.1 16.3 %collective-permute-start.1 = (f32[7,32,256]{2,1,0:T(8,128)}, f32[7,32,256]{2,1,0:T(8,128)S(1)}, u32[]{:S(2)}, u32[]{:S(2)}) collective-permute-start(f32[7,32,256]{2,1,0:T(8,128)} %get-tuple-element.16.near), channel_id=1, source_target_pairs={{0,4},{8,12},{16,20},{24,28},{4,0},{12,8},{20,16},{28,24},{1,5},{9... | collective-permute-start | bytes 688136 | tf_op jit(solution)/shard_map/ppermute | solution.py:447
  10.9 12.0 %all-to-all-start = ((f32[64,4,128]{2,1,0:T(4,128)}), f32[64,4,128]{2,1,0:T(4,128)S(1)}, u32[]{:S(2)}, u32[]{:S(2)}) async-start(f32[64,4,128]{2,1,0:T(4,128)} %get-tuple-element.20), calls=%async_computation | async-start | bytes 262144 | tf_op jit(solution)/shard_map/all_to_all | solution.py:462
  15.6 3.6 %copy-start.7 = (f32[4,128]{1,0:T(4,128)S(1)}, f32[4,128]{1,0:T(4,128)}, u32[]{:S(2)}) copy-start(f32[4,128]{1,0:T(4,128)} %get-tuple-element.12.tiles_in) | copy-start | bytes 6148
  15.6 5.8 %collective-permute-start.2 = (f32[7,8,256]{2,1,0:T(8,128)}, f32[7,8,256]{2,1,0:T(8,128)S(1)}, u32[]{:S(2)}, u32[]{:S(2)}) collective-permute-start(f32[7,8,256]{2,1,0:T(8,128)} %get-tuple-element.17.other), channel_id=1, source_target_pairs={{1,2},{2,1},{5,6},{6,5},{9,10},{10,9},{13,14},{14,13},{17,18},{18,... | collective-permute-start | bytes 172040 | tf_op jit(solution)/shard_map/ppermute | solution.py:447
  16.2 5.1 %collective-permute-start.3 = (f32[7,8,256]{2,1,0:T(8,128)}, f32[7,8,256]{2,1,0:T(8,128)S(1)}, u32[]{:S(2)}, u32[]{:S(2)}) collective-permute-start(f32[7,8,256]{2,1,0:T(8,128)} %get-tuple-element.18.swap), channel_id=1, source_target_pairs={{0,1},{2,3},{1,0},{3,2},{4,5},{6,7},{5,4},{7,6},{8,9},{10,11},{9,8... | collective-permute-start | bytes 172040 | tf_op jit(solution)/shard_map/ppermute | solution.py:447
  19.2 2.2 %copy-start.3 = (f32[7,32,256]{2,1,0:T(8,128)S(1)}, f32[7,32,256]{2,1,0:T(8,128)}, u32[]{:S(2)}) copy-start(f32[7,32,256]{2,1,0:T(8,128)} %get-tuple-element.15.far) | copy-start | bytes 688132
  19.2 2.2 %copy-start.4 = (f32[7,32,256]{2,1,0:T(8,128)S(1)}, f32[7,32,256]{2,1,0:T(8,128)}, u32[]{:S(2)}) copy-start(f32[7,32,256]{2,1,0:T(8,128)} %get-tuple-element.16.near) | copy-start | bytes 688132
  19.2 2.2 %copy-start.5 = (f32[7,8,256]{2,1,0:T(8,128)S(1)}, f32[7,8,256]{2,1,0:T(8,128)}, u32[]{:S(2)}) copy-start(f32[7,8,256]{2,1,0:T(8,128)} %get-tuple-element.17.other) | copy-start | bytes 172036
  19.2 2.2 %copy-start.6 = (f32[7,8,256]{2,1,0:T(8,128)S(1)}, f32[7,8,256]{2,1,0:T(8,128)}, u32[]{:S(2)}) copy-start(f32[7,8,256]{2,1,0:T(8,128)} %get-tuple-element.18.swap) | copy-start | bytes 172036
  22.9 13.0 %all-to-all-start.1 = ((f32[32,4,128]{2,1,0:T(4,128)}), f32[32,4,128]{2,1,0:T(4,128)S(1)}, u32[]{:S(2)}, u32[]{:S(2)}) async-start(f32[32,4,128]{2,1,0:T(4,128)} %get-tuple-element.21), calls=%async_computation.1 | async-start | bytes 131072 | tf_op jit(solution)/shard_map/all_to_all | solution.py:465

commit v9 on v8

--- a/solution.py
+++ b/solution.py
@@ -87,6 +87,34 @@
             self.made[k].wait()
 
 
+def slab_kernel(vort, velo, visc, near_out, far_out, near, far, sems):
+    cx = visc.shape[0]
+    copies = Copies(sems)
+    even = lax.axis_index("slab") % 2 == 0
+    for face, at in ((near, jnp.where(even, cx - 1, 0)), (far, jnp.where(even, 0, cx - 1))):
+        copies.start(vort.at[:, at], face.at[0:3])
+        copies.start(velo.at[:, at], face.at[3:6])
+        copies.start(visc.at[at], face.at[6])
+    copies.wait(0, 3)
+    copies.start(near, near_out)
+    copies.wait(3, 6)
+    copies.start(far, far_out)
+    copies.wait(6, 8)
+
+
+def slab_faces(vort, velo, visc):
+    _, _, cy, nz = vort.shape
+    made = (shaped(7, cy, nz), shaped(7, cy, nz))
+    return pl.pallas_call(
+        slab_kernel,
+        out_shape=made,
+        in_specs=[ANY] * 3,
+        out_specs=(ANY,) * 2,
+        scratch_shapes=[pltpu.VMEM(one.shape, jnp.float32) for one in made] + [pltpu.SemaphoreType.DMA((8,))],
+        compiler_params=FIRST_PARAMS,
+    )(vort, velo, visc)
+
+
 def send_kernel(
     cap,
     vort,
@@ -96,16 +124,13 @@
     cells_in,
     dest_in,
     count_in,
-    far_out,
-    near_out,
+    earlier,
+    swap_out,
     other_out,
-    swap_out,
     packets_out,
     moments_out,
-    far,
-    near,
+    swap,
     other,
-    swap,
     packets,
     moments,
     weights,
@@ -116,40 +141,29 @@
 ):
     cx, cy, nz = visc.shape
     copies = Copies(sems)
-    even = lax.axis_index("slab") % 2 == 0
-    for face, at in ((far, jnp.where(even, 0, cx - 1)), (near, jnp.where(even, cx - 1, 0))):
-        copies.start(vort.at[:, at], face.at[0:3])
-        copies.start(velo.at[:, at], face.at[3:6])
-        copies.start(visc.at[at], face.at[6])
     copies.start(weights_in, weights)
     copies.start(cells_in, cells)
     copies.start(dest_in, dest)
     copies.start(count_in, count)
     even = lax.axis_index("pencil") % 2 == 0
-    for face, at in ((other, jnp.where(even, 0, cy - 1)), (swap, jnp.where(even, cy - 1, 0))):
+    for face, at in ((swap, jnp.where(even, cy - 1, 0)), (other, jnp.where(even, 0, cy - 1))):
         copies.start(vort.at[:, :, at], face.at[0:3])
         copies.start(velo.at[:, :, at], face.at[3:6])
         copies.start(visc.at[:, at], face.at[6])
-    copies.wait(0, 3)
-    copies.start(far, far_out)
-    copies.wait(3, 6)
-    copies.start(near, near_out)
-    copies.wait(6, 10)
+    copies.wait(0, 4)
     pack_tiles(cap, cx * cy * nz, weights, cells, dest, count, packets)
     copies.start(packets, packets_out)
-    copies.wait(10, 16)
-    copies.start(other, other_out)
-    copies.start(swap, swap_out)
     tile_moments(cap, nz, packets, moments)
     copies.start(moments, moments_out)
-    copies.wait(16, 22)
-
-
-def to_send(vort, velo, visc, weights, cells, dest, count, n_slab, cap):
+    copies.wait(4, 10)
+    copies.start(swap, swap_out)
+    copies.start(other, other_out)
+    copies.wait(10, 14)
+
+
+def to_send(vort, velo, visc, weights, cells, dest, count, earlier, n_slab, cap):
     _, cx, cy, nz = vort.shape
     made = (
-        shaped(7, cy, nz),
-        shaped(7, cy, nz),
         shaped(7, cx, nz),
         shaped(7, cx, nz),
         shaped(n_slab * cap, 4, weights.shape[2]),
@@ -158,18 +172,18 @@
     return pl.pallas_call(
         functools.partial(send_kernel, cap),
         out_shape=made,
-        in_specs=[ANY] * 7,
-        out_specs=(ANY,) * 6,
+        in_specs=[ANY] * 8,
+        out_specs=(ANY,) * 4,
         scratch_shapes=[pltpu.VMEM(one.shape, jnp.float32) for one in made]
         + [
             pltpu.VMEM(weights.shape, jnp.float32),
             pltpu.VMEM(cells.shape, jnp.int32),
             pltpu.VMEM(dest.shape, jnp.int32),
             pltpu.SMEM(count.shape, jnp.int32),
-            pltpu.SemaphoreType.DMA((22,)),
+            pltpu.SemaphoreType.DMA((14,)),
         ],
         compiler_params=FIRST_PARAMS,
-    )(vort, velo, visc, weights, cells, dest, count)
+    )(vort, velo, visc, weights, cells, dest, count, earlier)
 
 
 def ahead(a, axis):
@@ -258,7 +272,7 @@
 
 
 def edge_kernel(
-    inside, moments, far, near, other, swap, far_in, near_in, other_in, swap_in, out, load_out, load, side_change, sem
+    inside, moments, near, far, swap, other, near_in, far_in, swap_in, other_in, out, load_out, load, side_change, sem
 ):
     _, cx, cy, nz = out.shape
     even = lax.axis_index("pencil") % 2 == 0
@@ -454,11 +468,12 @@
     n_pencil = lax.axis_size("pencil")
     cap = 2 * tile_weights.shape[0] // n_slab
     weights = jnp.transpose(tile_weights, (1, 0, 2))
-    count = tile_count
-    *faces, packets, tiles = to_send(
-        vorticity, velocity, viscosity, weights, tile_cells, tile_dest.T, count, n_slab, cap
-    )
-    halos = [swapped(face, axis, 1 - k % 2) for k, (face, axis) in enumerate(zip(faces, SIDES))]
+    near, far_face = slab_faces(vorticity, velocity, viscosity)
+    swap, other, packets, tiles = to_send(
+        vorticity, velocity, viscosity, weights, tile_cells, tile_dest.T, tile_count, far_face, n_slab, cap
+    )
+    faces = (near, far_face, swap, other)
+    halos = [swapped(face, axis, k % 2) for k, (face, axis) in enumerate(zip(faces, SIDES))]
     arrived = lax.all_to_all(packets, "slab", 0, 0, tiled=True)
     inside, moments = inner(vorticity, velocity, viscosity, tiles)
     advanced, load = edges(inside, moments, faces, halos, n_slab * n_pencil)

time: 37 us -> 38.5 us (1.041)
  waiting for transfers between devices: 3.9 us -> 7.74 us
  starting transfers between devices: 20.5 us -> 17.6 us
  Pallas kernels: 10.8 us -> 11.3 us
    ppermute x4, starting transfers between devices: 10.2 us -> 4.4 us  [swapped(): return lax.ppermute(array, axis, up + [(j, i) for i, j in up])]
    all_to_all x1, starting transfers between devices: 4.68 us -> 7.71 us  [per_device(): arrived = lax.all_to_all(packets, 'slab', 0, 0, tiled=True)]
    all_to_all x1, waiting for transfers between devices: 0.51 us -> 3.36 us  [per_device(): arrived = lax.all_to_all(packets, 'slab', 0, 0, tiled=True)]
    pallas_call x0 -> x1, Pallas kernels: none -> 1.81 us  [slab_faces(): pl.pallas_call(slab_kernel, out_shape=made, in_specs=[ANY] * 3, out_specs...]
    pallas_call x1, Pallas kernels: 4.06 us -> 3.03 us  [deposit(): pl.pallas_call(functools.partial(deposit_kernel, cap), out_shape=shaped(*...]
    all_to_all x1, waiting for transfers between devices: 3.35 us -> 4.38 us  [per_device(): load = lax.all_to_all(load, ('slab', 'pencil'), 0, 0, tiled=True)]
  transfers between devices with their start and end apart: 6 -> 6, of which waited for: 2 -> 2; matrix products, arithmetic and copies ran while one was open for 0% -> 0% of each run, Pallas kernels for 19% -> 23%
where the time goes in v9:
time: 38.5 us; the launch traced here: 38.2 us
  starting transfers between devices  17.6 us (46%)
  Pallas kernels  11.3 us (29%)
  waiting for transfers between devices  7.74 us (20%)
  between operations  1.49 us (4%)
    all_to_all x1, starting transfers between devices, per_device(): arrived = lax.all_to_all(packets, 'slab', 0, 0, tiled=True)  7.71 us
    all_to_all x1, starting transfers between devices, per_device(): load = lax.all_to_all(load, ('slab', 'pencil'), 0, 0, tiled=True)  5.46 us
    ppermute x4, starting transfers between devices, swapped(): return lax.ppermute(array, axis, up + [(j, i) for i, j in up])  4.4 us
    all_to_all x1, waiting for transfers between devices, per_device(): load = lax.all_to_all(load, ('slab', 'pencil'), 0, 0, tiled=True)  4.38 us
    all_to_all x1, waiting for transfers between devices, per_device(): arrived = lax.all_to_all(packets, 'slab', 0, 0, tiled=True)  3.36 us
    pallas_call x1, Pallas kernels, deposit(): pl.pallas_call(functools.partial(deposit_kernel, cap), out_shape=shaped(*...  3.03 us
    pallas_call x1, Pallas kernels, to_send(): pl.pallas_call(functools.partial(send_kernel, cap), out_shape=made, in_sp...  2.68 us
    pallas_call x1, Pallas kernels, inner(): pl.pallas_call(inner_kernel, out_shape=(shaped(*vort.shape), shaped(*tile...  2.07 us
  transfers between devices with their start and end apart: 6, of which 2 were waited for; matrix products, arithmetic and copies ran while one was open for 0% of the time, Pallas kernels for 23%

profile of v9, /device:TPU:0, one launch (start us, length us, event | category | flops | bytes accessed | tf_op | source)
XLA Modules:
  0.0 38.2 jit_solution(11202631555824670925)
XLA Ops:
  0.6 1.8 %shard_map.86 = (f32[7,32,256]{2,1,0:T(8,128)}, f32[7,32,256]{2,1,0:T(8,128)}) custom-call(f32[3,8,32,256]{3,2,1,0:T(8,128)} %vort.5, f32[3,8,32,256]{3,2,1,0:T(8,128)} %velo.5, f32[8,32,256]{2,1,0:T(8,128)} %visc.5), custom_call_target="tpu_custom_call" | custom-call | tf_op jit(solution)/shard_map/pallas_call | solution.py:108
  2.5 3.0 %collective-permute-start = (f32[7,32,256]{2,1,0:T(8,128)}, f32[7,32,256]{2,1,0:T(8,128)S(1)}, u32[]{:S(2)}, u32[]{:S(2)}) collective-permute-start(f32[7,32,256]{2,1,0:T(8,128)} %get-tuple-element.16.near), channel_id=1, source_target_pairs={{0,4},{8,12},{16,20},{24,28},{4,0},{12,8},{20,16},{28,24},{1,5},{9... | collective-permute-start | bytes 688136 | tf_op jit(solution)/shard_map/ppermute | solution.py:461
  5.5 0.7 %collective-permute-start.1 = (f32[7,32,256]{2,1,0:T(8,128)}, f32[7,32,256]{2,1,0:T(8,128)S(1)}, u32[]{:S(2)}, u32[]{:S(2)}) collective-permute-start(f32[7,32,256]{2,1,0:T(8,128)} %get-tuple-element.12.earlier.far), channel_id=1, source_target_pairs={{4,8},{12,16},{20,24},{8,4},{16,12},{24,20},{5,9},{13,17},{21,25},... | collective-permute-start | bytes 688136 | tf_op jit(solution)/shard_map/ppermute | solution.py:461
  6.8 0.0 copy-start
  6.8 0.0 copy-start.1
  6.8 2.7 %shard_map.87 = (f32[7,8,256]{2,1,0:T(8,128)}, f32[7,8,256]{2,1,0:T(8,128)}, f32[64,4,128]{2,1,0:T(4,128)}, f32[4,128]{1,0:T(4,128)}) custom-call(f32[3,8,32,256]{3,2,1,0:T(8,128)} %vort.5, f32[3,8,32,256]{3,2,1,0:T(8,128)} %velo.5, f32[8,32,256]{2,1,0:T(8,128)} %visc.5, f32[3,32,128]{2,1,0:T(8,128)} %bitcast.2, s32[32,128]{1,0:T(8,128)} %cells_in.1, ...), custom_call_target="tpu_custom_call" | custom-call | tf_op jit(solution)/shard_map/pallas_call | solution.py:172
  9.5 0.0 copy-start.2
  9.5 7.7 %all-to-all-start = ((f32[64,4,128]{2,1,0:T(4,128)}), f32[64,4,128]{2,1,0:T(4,128)S(1)}, u32[]{:S(2)}, u32[]{:S(2)}) async-start(f32[64,4,128]{2,1,0:T(4,128)} %get-tuple-element.20), calls=%async_computation | async-start | bytes 262144 | tf_op jit(solution)/shard_map/all_to_all | solution.py:477
  17.2 0.1 collective-permute-start.2
  17.3 0.7 %collective-permute-start.3 = (f32[7,8,256]{2,1,0:T(8,128)}, f32[7,8,256]{2,1,0:T(8,128)S(1)}, u32[]{:S(2)}, u32[]{:S(2)}) collective-permute-start(f32[7,8,256]{2,1,0:T(8,128)} %get-tuple-element.18.other), channel_id=1, source_target_pairs={{1,2},{2,1},{5,6},{6,5},{9,10},{10,9},{13,14},{14,13},{17,18},{18,... | collective-permute-start | bytes 172040 | tf_op jit(solution)/shard_map/ppermute | solution.py:461
  18.0 0.0 copy-start.4
  18.0 0.0 copy-start.5
  18.0 0.0 copy-start.6
  18.0 2.1 %shard_map.88 = (f32[3,8,32,256]{3,2,1,0:T(8,128)S(1)}, f32[4,128]{1,0:T(4,128)S(1)}) custom-call(f32[3,8,32,256]{3,2,1,0:T(8,128)S(1)} %copy-done, f32[3,8,32,256]{3,2,1,0:T(8,128)S(1)} %copy-done.1, f32[8,32,256]{2,1,0:T(8,128)S(1)} %copy-done.2, f32[4,128]{1,0:T(4,128)S(1)} %copy-done.7), custom_call_target="tpu_custom_call" | custom-call | tf_op jit(solution)/shard_map/pallas_call | solution.py:258
  20.1 0.0 collective-permute-done.2.swap_in
  20.1 0.0 collective-permute-done.3.other_in
  20.1 0.0 collective-permute-done.near_in
  20.2 0.0 collective-permute-done.1.far_in
  20.2 1.0 %shard_map.89 = (f32[3,8,32,256]{3,2,1,0:T(8,128)S(1)}, f32[32,4,128]{2,1,0:T(4,128)}) custom-call(f32[3,8,32,256]{3,2,1,0:T(8,128)S(1)} %get-tuple-element.14.inside, f32[4,128]{1,0:T(4,128)S(1)} %get-tuple-element.15.moments, f32[7,32,256]{2,1,0:T(8,128)S(1)} %copy-done.4, f32[7,32,256]{2,1,0:T(8,128)S(1)} %copy-done.3, f32[7,8,256]{2,1,0:T(8,128)S(1)} %copy-done.5, ...), custom_call_target="tpu_custom_call" | custom-call | tf_op jit(solution)/shard_map/pallas_call | solution.py:313
  21.2 3.4 %all-to-all-done.load = f32[64,4,128]{2,1,0:T(4,128)S(1)} async-done(((f32[64,4,128]{2,1,0:T(4,128)}), f32[64,4,128]{2,1,0:T(4,128)S(1)}, u32[]{:S(2)}, u32[]{:S(2)}) %all-to-all-start) | async-done | bytes 131104 | tf_op jit(solution)/shard_map/all_to_all | solution.py:477
  24.6 5.5 %all-to-all-start.1 = ((f32[32,4,128]{2,1,0:T(4,128)}), f32[32,4,128]{2,1,0:T(4,128)S(1)}, u32[]{:S(2)}, u32[]{:S(2)}) async-start(f32[32,4,128]{2,1,0:T(4,128)} %get-tuple-element.21), calls=%async_computation.1 | async-start | bytes 131072 | tf_op jit(solution)/shard_map/all_to_all | solution.py:480
  30.0 3.0 %shard_map.90 = f32[3,8,32,256]{3,2,1,0:T(8,128)} custom-call(f32[3,8,32,256]{3,2,1,0:T(8,128)S(1)} %get-tuple-element.19.inside, f32[64,4,128]{2,1,0:T(4,128)S(1)} %all-to-all-done.load), custom_call_target="tpu_custom_call" | custom-call | tf_op jit(solution)/shard_map/pallas_call | solution.py:446
  33.0 4.4 %all-to-all-done.1.load = f32[32,4,128]{2,1,0:T(4,128)S(1)} async-done(((f32[32,4,128]{2,1,0:T(4,128)}), f32[32,4,128]{2,1,0:T(4,128)S(1)}, u32[]{:S(2)}, u32[]{:S(2)}) %all-to-all-start.1) | async-done | bytes 65568 | tf_op jit(solution)/shard_map/all_to_all | solution.py:480
  37.4 0.7 %shard_map.91 = f32[3,1,1,16]{3,2,1,0:T(1,128)} custom-call(f32[32,4,128]{2,1,0:T(4,128)S(1)} %all-to-all-done.1.load), custom_call_target="tpu_custom_call" | custom-call | tf_op jit(solution)/shard_map/pallas_call | solution.py:365
  (10 shorter events, 0.0 us)
Async XLA Ops:
  2.5 17.7 %collective-permute-start = (f32[7,32,256]{2,1,0:T(8,128)}, f32[7,32,256]{2,1,0:T(8,128)S(1)}, u32[]{:S(2)}, u32[]{:S(2)}) collective-permute-start(f32[7,32,256]{2,1,0:T(8,128)} %get-tuple-element.16.near), channel_id=1, source_target_pairs={{0,4},{8,12},{16,20},{24,28},{4,0},{12,8},{20,16},{28,24},{1,5},{9... | collective-permute-start | bytes 688136 | tf_op jit(solution)/shard_map/ppermute | solution.py:461
  5.5 14.7 %collective-permute-start.1 = (f32[7,32,256]{2,1,0:T(8,128)}, f32[7,32,256]{2,1,0:T(8,128)S(1)}, u32[]{:S(2)}, u32[]{:S(2)}) collective-permute-start(f32[7,32,256]{2,1,0:T(8,128)} %get-tuple-element.12.earlier.far), channel_id=1, source_target_pairs={{4,8},{12,16},{20,24},{8,4},{16,12},{24,20},{5,9},{13,17},{21,25},... | collective-permute-start | bytes 688136 | tf_op jit(solution)/shard_map/ppermute | solution.py:461
  6.8 11.2 %copy-start = (f32[3,8,32,256]{3,2,1,0:T(8,128)S(1)}, f32[3,8,32,256]{3,2,1,0:T(8,128)}, u32[]{:S(2)}) copy-start(f32[3,8,32,256]{3,2,1,0:T(8,128)} %vort.5) | copy-start | bytes 2359300
  6.8 11.2 %copy-start.1 = (f32[3,8,32,256]{3,2,1,0:T(8,128)S(1)}, f32[3,8,32,256]{3,2,1,0:T(8,128)}, u32[]{:S(2)}) copy-start(f32[3,8,32,256]{3,2,1,0:T(8,128)} %velo.5) | copy-start | bytes 2359300
  9.5 8.5 %copy-start.2 = (f32[8,32,256]{2,1,0:T(8,128)S(1)}, f32[8,32,256]{2,1,0:T(8,128)}, u32[]{:S(2)}) copy-start(f32[8,32,256]{2,1,0:T(8,128)} %visc.5) | copy-start | bytes 786436
  9.5 15.1 %all-to-all-start = ((f32[64,4,128]{2,1,0:T(4,128)}), f32[64,4,128]{2,1,0:T(4,128)S(1)}, u32[]{:S(2)}, u32[]{:S(2)}) async-start(f32[64,4,128]{2,1,0:T(4,128)} %get-tuple-element.20), calls=%async_computation | async-start | bytes 262144 | tf_op jit(solution)/shard_map/all_to_all | solution.py:477
  17.2 0.8 %copy-start.7 = (f32[4,128]{1,0:T(4,128)S(1)}, f32[4,128]{1,0:T(4,128)}, u32[]{:S(2)}) copy-start(f32[4,128]{1,0:T(4,128)} %get-tuple-element.13.tiles_in) | copy-start | bytes 6148
  17.2 2.9 %collective-permute-start.2 = (f32[7,8,256]{2,1,0:T(8,128)}, f32[7,8,256]{2,1,0:T(8,128)S(1)}, u32[]{:S(2)}, u32[]{:S(2)}) collective-permute-start(f32[7,8,256]{2,1,0:T(8,128)} %get-tuple-element.17.swap), channel_id=1, source_target_pairs={{0,1},{2,3},{1,0},{3,2},{4,5},{6,7},{5,4},{7,6},{8,9},{10,11},{9,8... | collective-permute-start | bytes 172040 | tf_op jit(solution)/shard_map/ppermute | solution.py:461
  17.3 2.8 %collective-permute-start.3 = (f32[7,8,256]{2,1,0:T(8,128)}, f32[7,8,256]{2,1,0:T(8,128)S(1)}, u32[]{:S(2)}, u32[]{:S(2)}) collective-permute-start(f32[7,8,256]{2,1,0:T(8,128)} %get-tuple-element.18.other), channel_id=1, source_target_pairs={{1,2},{2,1},{5,6},{6,5},{9,10},{10,9},{13,14},{14,13},{17,18},{18,... | collective-permute-start | bytes 172040 | tf_op jit(solution)/shard_map/ppermute | solution.py:461
  18.0 2.2 %copy-start.3 = (f32[7,32,256]{2,1,0:T(8,128)S(1)}, f32[7,32,256]{2,1,0:T(8,128)}, u32[]{:S(2)}) copy-start(f32[7,32,256]{2,1,0:T(8,128)} %get-tuple-element.12.earlier.far) | copy-start | bytes 688132
  18.0 2.2 %copy-start.4 = (f32[7,32,256]{2,1,0:T(8,128)S(1)}, f32[7,32,256]{2,1,0:T(8,128)}, u32[]{:S(2)}) copy-start(f32[7,32,256]{2,1,0:T(8,128)} %get-tuple-element.16.near) | copy-start | bytes 688132
  18.0 2.2 %copy-start.5 = (f32[7,8,256]{2,1,0:T(8,128)S(1)}, f32[7,8,256]{2,1,0:T(8,128)}, u32[]{:S(2)}) copy-start(f32[7,8,256]{2,1,0:T(8,128)} %get-tuple-element.17.swap) | copy-start | bytes 172036
  18.0 2.2 %copy-start.6 = (f32[7,8,256]{2,1,0:T(8,128)S(1)}, f32[7,8,256]{2,1,0:T(8,128)}, u32[]{:S(2)}) copy-start(f32[7,8,256]{2,1,0:T(8,128)} %get-tuple-element.18.other) | copy-start | bytes 172036
  24.6 12.9 %all-to-all-start.1 = ((f32[32,4,128]{2,1,0:T(4,128)}), f32[32,4,128]{2,1,0:T(4,128)S(1)}, u32[]{:S(2)}, u32[]{:S(2)}) async-start(f32[32,4,128]{2,1,0:T(4,128)} %get-tuple-element.21), calls=%async_computation.1 | async-start | bytes 131072 | tf_op jit(solution)/shard_map/all_to_all | solution.py:480

commit v10 on v9

--- a/solution.py
+++ b/solution.py
@@ -115,75 +115,33 @@
     )(vort, velo, visc)
 
 
-def send_kernel(
-    cap,
-    vort,
-    velo,
-    visc,
-    weights_in,
-    cells_in,
-    dest_in,
-    count_in,
-    earlier,
-    swap_out,
-    other_out,
-    packets_out,
-    moments_out,
-    swap,
-    other,
-    packets,
-    moments,
-    weights,
-    cells,
-    dest,
-    count,
-    sems,
-):
+def send_kernel(cap, vort, velo, visc, weights, cells, dest, count, swap, other, packets, moments):
     cx, cy, nz = visc.shape
-    copies = Copies(sems)
-    copies.start(weights_in, weights)
-    copies.start(cells_in, cells)
-    copies.start(dest_in, dest)
-    copies.start(count_in, count)
     even = lax.axis_index("pencil") % 2 == 0
     for face, at in ((swap, jnp.where(even, cy - 1, 0)), (other, jnp.where(even, 0, cy - 1))):
-        copies.start(vort.at[:, :, at], face.at[0:3])
-        copies.start(velo.at[:, :, at], face.at[3:6])
-        copies.start(visc.at[:, at], face.at[6])
-    copies.wait(0, 4)
+        for x in range(cx):
+            for c in range(3):
+                face[c, x : x + 1, :] = vort[c, x, pl.ds(at, 1), :]
+                face[3 + c, x : x + 1, :] = velo[c, x, pl.ds(at, 1), :]
+            face[6, x : x + 1, :] = visc[x, pl.ds(at, 1), :]
     pack_tiles(cap, cx * cy * nz, weights, cells, dest, count, packets)
-    copies.start(packets, packets_out)
     tile_moments(cap, nz, packets, moments)
-    copies.start(moments, moments_out)
-    copies.wait(4, 10)
-    copies.start(swap, swap_out)
-    copies.start(other, other_out)
-    copies.wait(10, 14)
-
-
-def to_send(vort, velo, visc, weights, cells, dest, count, earlier, n_slab, cap):
+
+
+def to_send(vort, velo, visc, weights, cells, dest, count, n_slab, cap):
     _, cx, cy, nz = vort.shape
-    made = (
-        shaped(7, cx, nz),
-        shaped(7, cx, nz),
-        shaped(n_slab * cap, 4, weights.shape[2]),
-        shaped(4, n_slab * nz // CB),
-    )
     return pl.pallas_call(
         functools.partial(send_kernel, cap),
-        out_shape=made,
-        in_specs=[ANY] * 8,
-        out_specs=(ANY,) * 4,
-        scratch_shapes=[pltpu.VMEM(one.shape, jnp.float32) for one in made]
-        + [
-            pltpu.VMEM(weights.shape, jnp.float32),
-            pltpu.VMEM(cells.shape, jnp.int32),
-            pltpu.VMEM(dest.shape, jnp.int32),
-            pltpu.SMEM(count.shape, jnp.int32),
-            pltpu.SemaphoreType.DMA((14,)),
-        ],
-        compiler_params=FIRST_PARAMS,
-    )(vort, velo, visc, weights, cells, dest, count, earlier)
+        out_shape=(
+            shaped(7, cx, nz),
+            shaped(7, cx, nz),
+            shaped(n_slab * cap, 4, weights.shape[2]),
+            shaped(4, n_slab * nz // CB),
+        ),
+        in_specs=[VMEM] * 6 + [SMEM],
+        out_specs=(VMEM,) * 4,
+        compiler_params=PARAMS,
+    )(vort, velo, visc, weights, cells, dest, count)
 
 
 def ahead(a, axis):
@@ -410,7 +368,7 @@
     acc[...] += added[: 3 * rows] + added[3 * rows :]
 
 
-def deposit_kernel(cap, inside, load, out, acc, order):
+def deposit_kernel(cap, inside, load, out, acc, order, made, sems):
     _, cx, cy, nz = out.shape
     shape = (cx, cy, nz)
     acc[...] = jnp.zeros_like(acc)
@@ -436,10 +394,15 @@
     def _():
         deposit_step(GROUP // 2, whole * GROUP, listed, load, order, acc, shape)
 
-    for h in range(2):
-        span = slice(h * (cx // 2), (h + 1) * (cx // 2))
-        change = acc[:, h * nz : (h + 1) * nz].reshape(3, cx // 2, cy, nz)
-        out[:, span] = inside[:, span] + change
+    copies = Copies(sems)
+    rows = cx * cy // 2
+    for c in range(3):
+        for h in range(2):
+            span = slice(h * (cx // 2), (h + 1) * (cx // 2))
+            change = acc[c * rows : (c + 1) * rows, h * nz : (h + 1) * nz].reshape(cx // 2, cy, nz)
+            made[c, span] = inside[c, span] + change
+            copies.start(made.at[c, span], out.at[c, span])
+    copies.wait(0, 6)
 
 
 def deposit(inside, load, cap):
@@ -447,10 +410,12 @@
         functools.partial(deposit_kernel, cap),
         out_shape=shaped(*inside.shape),
         in_specs=[VMEM] * 2,
-        out_specs=VMEM,
+        out_specs=ANY,
         scratch_shapes=[
             pltpu.VMEM((3 * inside.shape[1] * inside.shape[2] // 2, 2 * inside.shape[3]), jnp.float32),
             pltpu.SMEM((load.shape[0] + max(cap, GROUP),), jnp.int32),
+            pltpu.VMEM(inside.shape, jnp.float32),
+            pltpu.SemaphoreType.DMA((6,)),
         ],
         compiler_params=PARAMS,
     )(inside, load)
@@ -470,7 +435,7 @@
     weights = jnp.transpose(tile_weights, (1, 0, 2))
     near, far_face = slab_faces(vorticity, velocity, viscosity)
     swap, other, packets, tiles = to_send(
-        vorticity, velocity, viscosity, weights, tile_cells, tile_dest.T, tile_count, far_face, n_slab, cap
+        vorticity, velocity, viscosity, weights, tile_cells, tile_dest.T, tile_count, n_slab, cap
     )
     faces = (near, far_face, swap, other)
     halos = [swapped(face, axis, k % 2) for k, (face, axis) in enumerate(zip(faces, SIDES))]

time: 38.5 us -> 38.9 us (1.010)
  local copies, waits for them, and re-layouts: 0.04 us -> 2.16 us
  waiting for transfers between devices: 7.74 us -> 6.05 us
  starting transfers between devices: 17.6 us -> 17.1 us
  Pallas kernels: 11.3 us -> 11.7 us
    unnamed x16, local copies, waits for them, and re-layouts: 0.04 us -> 2.16 us
    all_to_all x1, waiting for transfers between devices: 4.38 us -> 2.54 us  [per_device(): load = lax.all_to_all(load, ('slab', 'pencil'), 0, 0, tiled=True)]
    pallas_call x1, Pallas kernels: 3.03 us -> 4.86 us  [deposit(): pl.pallas_call(functools.partial(deposit_kernel, cap), out_shape=shaped(*...]
    pallas_call x1, Pallas kernels: 2.68 us -> 1.08 us  [to_send(): pl.pallas_call(functools.partial(send_kernel, cap), out_shape=(shaped(7,...]
where the time goes in v10:
time: 38.9 us; the launch traced here: 38.5 us
  starting transfers between devices  17.1 us (44%)
  Pallas kernels  11.7 us (30%)
  waiting for transfers between devices  6.05 us (16%)
  local copies, waits for them, and re-layouts  2.16 us (6%)
  between operations  1.46 us (4%)
    all_to_all x1, starting transfers between devices, per_device(): arrived = lax.all_to_all(packets, 'slab', 0, 0, tiled=True)  7.57 us
    all_to_all x1, starting transfers between devices, per_device(): load = lax.all_to_all(load, ('slab', 'pencil'), 0, 0, tiled=True)  5.22 us
    pallas_call x1, Pallas kernels, deposit(): pl.pallas_call(functools.partial(deposit_kernel, cap), out_shape=shaped(*...  4.86 us
    ppermute x4, starting transfers between devices, swapped(): return lax.ppermute(array, axis, up + [(j, i) for i, j in up])  4.33 us
    all_to_all x1, waiting for transfers between devices, per_device(): arrived = lax.all_to_all(packets, 'slab', 0, 0, tiled=True)  3.5 us
    all_to_all x1, waiting for transfers between devices, per_device(): load = lax.all_to_all(load, ('slab', 'pencil'), 0, 0, tiled=True)  2.54 us
    unnamed x16, local copies, waits for them, and re-layouts  2.16 us
    pallas_call x1, Pallas kernels, inner(): pl.pallas_call(inner_kernel, out_shape=(shaped(*vort.shape), shaped(*tile...  2.07 us
  transfers between devices with their start and end apart: 6, of which 2 were waited for; matrix products, arithmetic and copies ran while one was open for 0% of the time, Pallas kernels for 23%

profile of v10, /device:TPU:0, one launch (start us, length us, event | category | flops | bytes accessed | tf_op | source)
XLA Modules:
  0.0 38.5 jit_solution(1230030787407421031)
XLA Ops:
  0.7 1.9 %shard_map.88 = (f32[7,32,256]{2,1,0:T(8,128)}, f32[7,32,256]{2,1,0:T(8,128)}) custom-call(f32[3,8,32,256]{3,2,1,0:T(8,128)} %vort.5, f32[3,8,32,256]{3,2,1,0:T(8,128)} %velo.5, f32[8,32,256]{2,1,0:T(8,128)} %visc.5), custom_call_target="tpu_custom_call" | custom-call | tf_op jit(solution)/shard_map/pallas_call | solution.py:108
  2.6 3.0 %collective-permute-start = (f32[7,32,256]{2,1,0:T(8,128)}, f32[7,32,256]{2,1,0:T(8,128)S(1)}, u32[]{:S(2)}, u32[]{:S(2)}) collective-permute-start(f32[7,32,256]{2,1,0:T(8,128)} %get-tuple-element.15.near), channel_id=1, source_target_pairs={{0,4},{8,12},{16,20},{24,28},{4,0},{12,8},{20,16},{28,24},{1,5},{9... | collective-permute-start | bytes 688136 | tf_op jit(solution)/shard_map/ppermute | solution.py:426
  5.6 0.7 %collective-permute-start.1 = (f32[7,32,256]{2,1,0:T(8,128)}, f32[7,32,256]{2,1,0:T(8,128)S(1)}, u32[]{:S(2)}, u32[]{:S(2)}) collective-permute-start(f32[7,32,256]{2,1,0:T(8,128)} %get-tuple-element.16.far), channel_id=1, source_target_pairs={{4,8},{12,16},{20,24},{8,4},{16,12},{24,20},{5,9},{13,17},{21,25},... | collective-permute-start | bytes 688136 | tf_op jit(solution)/shard_map/ppermute | solution.py:426
  6.9 0.0 copy-start.7
  6.9 0.0 copy-done.2
  7.0 0.6 %copy-done.7 = s32[32,1]{0,1:T(1,128)S(1)} copy-done((s32[32,1]{0,1:T(1,128)S(1)}, s32[32,1]{0,1:T(1,128)}, u32[]{:S(2)}) %copy-start.7) | copy-done | bytes 152
  7.6 0.8 %copy-done.5 = f32[32,3,128]{2,0,1:T(8,128)S(1)} copy-done((f32[32,3,128]{2,0,1:T(8,128)S(1)}, f32[32,3,128]{2,0,1:T(8,128)}, u32[]{:S(2)}) %copy-start.5) | copy-done | bytes 49176
  8.4 0.7 %copy-done.6 = s32[32,128]{1,0:T(8,128)S(1)} copy-done((s32[32,128]{1,0:T(8,128)S(1)}, s32[32,128]{1,0:T(8,128)}, u32[]{:S(2)}) %copy-start.6) | copy-done | bytes 16408
  9.1 1.1 %shard_map.86 = (f32[7,8,256]{2,1,0:T(8,128)S(1)}, f32[7,8,256]{2,1,0:T(8,128)S(1)}, f32[64,4,128]{2,1,0:T(4,128)}, f32[4,128]{1,0:T(4,128)S(1)}) custom-call(f32[3,8,32,256]{3,2,1,0:T(8,128)S(1)} %copy-done, f32[3,8,32,256]{3,2,1,0:T(8,128)S(1)} %copy-done.1, f32[8,32,256]{2,1,0:T(8,128)S(1)} %copy-done.2, f32[3,32,128]{2,1,0:T(8,128)S(1)} %bitcast.2, ...), custom_call_target="tpu_custom_call" | custom-call | tf_op jit(solution)/shard_map/pallas_call | solution.py:133
  10.2 7.6 %all-to-all-start = ((f32[64,4,128]{2,1,0:T(4,128)}), f32[64,4,128]{2,1,0:T(4,128)S(1)}, u32[]{:S(2)}, u32[]{:S(2)}) async-start(f32[64,4,128]{2,1,0:T(4,128)} %get-tuple-element.20), calls=%async_computation | async-start | bytes 262144 | tf_op jit(solution)/shard_map/all_to_all | solution.py:442
  17.8 0.0 collective-permute-start.2
  17.8 0.7 %collective-permute-start.3 = (f32[7,8,256]{2,1,0:T(8,128)S(1)}, f32[7,8,256]{2,1,0:T(8,128)S(1)}, u32[]{:S(2)}, u32[]{:S(2)}) collective-permute-start(f32[7,8,256]{2,1,0:T(8,128)S(1)} %get-tuple-element.18.other), channel_id=1, source_target_pairs={{1,2},{2,1},{5,6},{6,5},{9,10},{10,9},{13,14},{14,13},{17,18},{18,... | collective-permute-start | bytes 172040 | tf_op jit(solution)/shard_map/ppermute | solution.py:426
  18.4 0.0 copy-start.3
  18.5 2.1 %shard_map.87 = (f32[3,8,32,256]{3,2,1,0:T(8,128)S(1)}, f32[4,128]{1,0:T(4,128)S(1)}) custom-call(f32[3,8,32,256]{3,2,1,0:T(8,128)S(1)} %copy-done, f32[3,8,32,256]{3,2,1,0:T(8,128)S(1)} %copy-done.1, f32[8,32,256]{2,1,0:T(8,128)S(1)} %copy-done.2, f32[4,128]{1,0:T(4,128)S(1)} %get-tuple-element.12.tiles_in), custom_call_target="tpu_custom_call" | custom-call | tf_op jit(solution)/shard_map/pallas_call | solution.py:216
  20.5 0.0 collective-permute-done.2.swap_in
  20.5 0.0 collective-permute-done.3.other_in
  20.6 0.0 collective-permute-done.near_in
  20.6 0.0 collective-permute-done.1.far_in
  20.6 1.0 %shard_map.89 = (f32[3,8,32,256]{3,2,1,0:T(8,128)S(1)}, f32[32,4,128]{2,1,0:T(4,128)}) custom-call(f32[3,8,32,256]{3,2,1,0:T(8,128)S(1)} %get-tuple-element.13.inside, f32[4,128]{1,0:T(4,128)S(1)} %get-tuple-element.14.moments, f32[7,32,256]{2,1,0:T(8,128)S(1)} %copy-done.3, f32[7,32,256]{2,1,0:T(8,128)S(1)} %copy-done.4, ...), custom_call_target="tpu_custom_call" | custom-call | tf_op jit(solution)/shard_map/pallas_call | solution.py:271
  21.6 3.5 %all-to-all-done.load = f32[64,4,128]{2,1,0:T(4,128)S(1)} async-done(((f32[64,4,128]{2,1,0:T(4,128)}), f32[64,4,128]{2,1,0:T(4,128)S(1)}, u32[]{:S(2)}, u32[]{:S(2)}) %all-to-all-start) | async-done | bytes 131104 | tf_op jit(solution)/shard_map/all_to_all | solution.py:442
  25.1 5.2 %all-to-all-start.1 = ((f32[32,4,128]{2,1,0:T(4,128)}), f32[32,4,128]{2,1,0:T(4,128)S(1)}, u32[]{:S(2)}, u32[]{:S(2)}) async-start(f32[32,4,128]{2,1,0:T(4,128)} %get-tuple-element.21), calls=%async_computation.1 | async-start | bytes 131072 | tf_op jit(solution)/shard_map/all_to_all | solution.py:445
  30.3 4.9 %shard_map.90 = f32[3,8,32,256]{3,2,1,0:T(8,128)} custom-call(f32[3,8,32,256]{3,2,1,0:T(8,128)S(1)} %get-tuple-element.19.inside, f32[64,4,128]{2,1,0:T(4,128)S(1)} %all-to-all-done.load), custom_call_target="tpu_custom_call" | custom-call | tf_op jit(solution)/shard_map/pallas_call | solution.py:409
  35.2 2.5 %all-to-all-done.1.load = f32[32,4,128]{2,1,0:T(4,128)S(1)} async-done(((f32[32,4,128]{2,1,0:T(4,128)}), f32[32,4,128]{2,1,0:T(4,128)S(1)}, u32[]{:S(2)}, u32[]{:S(2)}) %all-to-all-start.1) | async-done | bytes 65568 | tf_op jit(solution)/shard_map/all_to_all | solution.py:445
  37.7 0.7 %shard_map.91 = f32[3,1,1,16]{3,2,1,0:T(1,128)} custom-call(f32[32,4,128]{2,1,0:T(4,128)S(1)} %all-to-all-done.1.load), custom_call_target="tpu_custom_call" | custom-call | tf_op jit(solution)/shard_map/pallas_call | solution.py:323
  (10 shorter events, 0.0 us)
Async XLA Ops:
  0.6 6.3 %copy-start.2 = (f32[8,32,256]{2,1,0:T(8,128)S(1)}, f32[8,32,256]{2,1,0:T(8,128)}, u32[]{:S(2)}) copy-start(f32[8,32,256]{2,1,0:T(8,128)} %visc.5) | copy-start | bytes 786436
  0.6 6.3 %copy-start.1 = (f32[3,8,32,256]{3,2,1,0:T(8,128)S(1)}, f32[3,8,32,256]{3,2,1,0:T(8,128)}, u32[]{:S(2)}) copy-start(f32[3,8,32,256]{3,2,1,0:T(8,128)} %velo.5) | copy-start | bytes 2359300
  0.6 6.3 %copy-start = (f32[3,8,32,256]{3,2,1,0:T(8,128)S(1)}, f32[3,8,32,256]{3,2,1,0:T(8,128)}, u32[]{:S(2)}) copy-start(f32[3,8,32,256]{3,2,1,0:T(8,128)} %vort.5) | copy-start | bytes 2359300
  2.6 18.0 %collective-permute-start = (f32[7,32,256]{2,1,0:T(8,128)}, f32[7,32,256]{2,1,0:T(8,128)S(1)}, u32[]{:S(2)}, u32[]{:S(2)}) collective-permute-start(f32[7,32,256]{2,1,0:T(8,128)} %get-tuple-element.15.near), channel_id=1, source_target_pairs={{0,4},{8,12},{16,20},{24,28},{4,0},{12,8},{20,16},{28,24},{1,5},{9... | collective-permute-start | bytes 688136 | tf_op jit(solution)/shard_map/ppermute | solution.py:426
  5.6 15.0 %collective-permute-start.1 = (f32[7,32,256]{2,1,0:T(8,128)}, f32[7,32,256]{2,1,0:T(8,128)S(1)}, u32[]{:S(2)}, u32[]{:S(2)}) collective-permute-start(f32[7,32,256]{2,1,0:T(8,128)} %get-tuple-element.16.far), channel_id=1, source_target_pairs={{4,8},{12,16},{20,24},{8,4},{16,12},{24,20},{5,9},{13,17},{21,25},... | collective-permute-start | bytes 688136 | tf_op jit(solution)/shard_map/ppermute | solution.py:426
  6.9 0.7 %copy-start.7 = (s32[32,1]{0,1:T(1,128)S(1)}, s32[32,1]{0,1:T(1,128)}, u32[]{:S(2)}) copy-start(s32[32,1]{0,1:T(1,128)} %param.12) | copy-start | bytes 388
  7.6 0.8 %copy-start.5 = (f32[32,3,128]{2,0,1:T(8,128)S(1)}, f32[32,3,128]{2,0,1:T(8,128)}, u32[]{:S(2)}) copy-start(f32[32,3,128]{2,0,1:T(8,128)} %param.10) | copy-start | bytes 147460
  8.4 0.7 %copy-start.6 = (s32[32,128]{1,0:T(8,128)S(1)}, s32[32,128]{1,0:T(8,128)}, u32[]{:S(2)}) copy-start(s32[32,128]{1,0:T(8,128)} %cells.1) | copy-start | bytes 49156
  10.2 14.9 %all-to-all-start = ((f32[64,4,128]{2,1,0:T(4,128)}), f32[64,4,128]{2,1,0:T(4,128)S(1)}, u32[]{:S(2)}, u32[]{:S(2)}) async-start(f32[64,4,128]{2,1,0:T(4,128)} %get-tuple-element.20), calls=%async_computation | async-start | bytes 262144 | tf_op jit(solution)/shard_map/all_to_all | solution.py:442
  17.8 2.8 %collective-permute-start.2 = (f32[7,8,256]{2,1,0:T(8,128)S(1)}, f32[7,8,256]{2,1,0:T(8,128)S(1)}, u32[]{:S(2)}, u32[]{:S(2)}) collective-permute-start(f32[7,8,256]{2,1,0:T(8,128)S(1)} %get-tuple-element.17.swap), channel_id=1, source_target_pairs={{0,1},{2,3},{1,0},{3,2},{4,5},{6,7},{5,4},{7,6},{8,9},{10,11},{9,8... | collective-permute-start | bytes 172040 | tf_op jit(solution)/shard_map/ppermute | solution.py:426
  17.8 2.8 %collective-permute-start.3 = (f32[7,8,256]{2,1,0:T(8,128)S(1)}, f32[7,8,256]{2,1,0:T(8,128)S(1)}, u32[]{:S(2)}, u32[]{:S(2)}) collective-permute-start(f32[7,8,256]{2,1,0:T(8,128)S(1)} %get-tuple-element.18.other), channel_id=1, source_target_pairs={{1,2},{2,1},{5,6},{6,5},{9,10},{10,9},{13,14},{14,13},{17,18},{18,... | collective-permute-start | bytes 172040 | tf_op jit(solution)/shard_map/ppermute | solution.py:426
  18.4 2.1 %copy-start.3 = (f32[7,32,256]{2,1,0:T(8,128)S(1)}, f32[7,32,256]{2,1,0:T(8,128)}, u32[]{:S(2)}) copy-start(f32[7,32,256]{2,1,0:T(8,128)} %get-tuple-element.15.near) | copy-start | bytes 688132
  18.4 2.1 %copy-start.4 = (f32[7,32,256]{2,1,0:T(8,128)S(1)}, f32[7,32,256]{2,1,0:T(8,128)}, u32[]{:S(2)}) copy-start(f32[7,32,256]{2,1,0:T(8,128)} %get-tuple-element.16.far) | copy-start | bytes 688132
  25.1 12.6 %all-to-all-start.1 = ((f32[32,4,128]{2,1,0:T(4,128)}), f32[32,4,128]{2,1,0:T(4,128)S(1)}, u32[]{:S(2)}, u32[]{:S(2)}) async-start(f32[32,4,128]{2,1,0:T(4,128)} %get-tuple-element.21), calls=%async_computation.1 | async-start | bytes 131072 | tf_op jit(solution)/shard_map/all_to_all | solution.py:445

commit v11 on v8

--- a/solution.py
+++ b/solution.py
@@ -28,6 +28,12 @@
 def split(w):
     high = w.astype(jnp.bfloat16).astype(jnp.float32)
     return high, w - high
+
+
+def thirds(w):
+    high, rest = split(w)
+    middle, low = split(rest)
+    return [piece.astype(jnp.bfloat16) for piece in (high, middle, low)]
 
 
 def pack_tiles(cap, cells_dev, weights, cells, dest, count, packets):
@@ -45,9 +51,8 @@
     held = jnp.sum((slot == names * cap).astype(jnp.float32) * live, axis=1, keepdims=True)
     rows = [weights[0], weights[1], weights[2], cells[...].astype(jnp.float32)]
     found = jnp.dot(
-        placed,
-        jnp.concatenate(rows, axis=1),
-        precision=lax.Precision.HIGHEST,
+        jnp.concatenate([placed] * 3, axis=1).astype(jnp.bfloat16),
+        jnp.concatenate(thirds(jnp.concatenate(rows, axis=1)), axis=0),
         preferred_element_type=jnp.float32,
     )
     length = cells.shape[1]
@@ -96,16 +101,16 @@
     cells_in,
     dest_in,
     count_in,
+    near_out,
     far_out,
-    near_out,
+    swap_out,
     other_out,
-    swap_out,
     packets_out,
     moments_out,
+    near,
     far,
-    near,
+    swap,
     other,
-    swap,
     packets,
     moments,
     weights,
@@ -116,32 +121,31 @@
 ):
     cx, cy, nz = visc.shape
     copies = Copies(sems)
-    even = lax.axis_index("slab") % 2 == 0
-    for face, at in ((far, jnp.where(even, 0, cx - 1)), (near, jnp.where(even, cx - 1, 0))):
-        copies.start(vort.at[:, at], face.at[0:3])
-        copies.start(velo.at[:, at], face.at[3:6])
-        copies.start(visc.at[at], face.at[6])
     copies.start(weights_in, weights)
     copies.start(cells_in, cells)
     copies.start(dest_in, dest)
     copies.start(count_in, count)
+    even = lax.axis_index("slab") % 2 == 0
+    for face, at in ((near, jnp.where(even, cx - 1, 0)), (far, jnp.where(even, 0, cx - 1))):
+        copies.start(vort.at[:, at], face.at[0:3])
+        copies.start(velo.at[:, at], face.at[3:6])
+        copies.start(visc.at[at], face.at[6])
     even = lax.axis_index("pencil") % 2 == 0
-    for face, at in ((other, jnp.where(even, 0, cy - 1)), (swap, jnp.where(even, cy - 1, 0))):
+    for face, at in ((swap, jnp.where(even, cy - 1, 0)), (other, jnp.where(even, 0, cy - 1))):
         copies.start(vort.at[:, :, at], face.at[0:3])
         copies.start(velo.at[:, :, at], face.at[3:6])
         copies.start(visc.at[:, at], face.at[6])
-    copies.wait(0, 3)
-    copies.start(far, far_out)
-    copies.wait(3, 6)
-    copies.start(near, near_out)
-    copies.wait(6, 10)
+    copies.wait(0, 4)
     pack_tiles(cap, cx * cy * nz, weights, cells, dest, count, packets)
     copies.start(packets, packets_out)
-    copies.wait(10, 16)
-    copies.start(other, other_out)
-    copies.start(swap, swap_out)
+    copies.wait(4, 10)
+    copies.start(near, near_out)
+    copies.start(far, far_out)
     tile_moments(cap, nz, packets, moments)
     copies.start(moments, moments_out)
+    copies.wait(10, 16)
+    copies.start(swap, swap_out)
+    copies.start(other, other_out)
     copies.wait(16, 22)
 
 
@@ -227,9 +231,10 @@
     shape = (nz, width)
     level = lax.broadcasted_iota(jnp.int32, shape, 0) // CB
     lane = lax.broadcasted_iota(jnp.int32, shape, 1)
-    pick = (lane == lax.axis_index("slab") * (nz // CB) + level).astype(jnp.float32)
+    pick = (lane == lax.axis_index("slab") * (nz // CB) + level).astype(jnp.float32).astype(jnp.bfloat16)
     rows = jnp.concatenate(totals + [jnp.zeros_like(totals[0])], axis=0)
-    return jnp.dot(rows, pick, precision=lax.Precision.HIGHEST, preferred_element_type=jnp.float32)
+    found = jnp.dot(jnp.concatenate(thirds(rows), axis=0), pick, preferred_element_type=jnp.float32)
+    return found[0:4] + (found[4:8] + found[8:12])
 
 
 def inner_kernel(vort, velo, visc, tiles_in, out, moments, tiles, sem):
@@ -258,7 +263,7 @@
 
 
 def edge_kernel(
-    inside, moments, far, near, other, swap, far_in, near_in, other_in, swap_in, out, load_out, load, side_change, sem
+    inside, moments, near, far, swap, other, near_in, far_in, swap_in, other_in, out, load_out, load, side_change, sem
 ):
     _, cx, cy, nz = out.shape
     even = lax.axis_index("pencil") % 2 == 0
@@ -335,16 +340,11 @@
         turned[0] = turned[0] + weight * (rel_z * second - rel_y * third)
         turned[1] = turned[1] + weight * (rel_x * third - rel_z * first)
         turned[2] = turned[2] + weight * (rel_y * first - rel_x * second)
-    ones = jnp.ones((8, shape[1]), jnp.float32)
+    pieces = jnp.concatenate(thirds(jnp.concatenate(turned, axis=0)), axis=1)
+    ones = jnp.ones((16, pieces.shape[1]), jnp.bfloat16)
+    rows = lax.dot_general(ones, pieces, (((1,), (1,)), ((), ())), preferred_element_type=jnp.float32)
     for c in range(3):
-        row = lax.dot_general(
-            ones,
-            turned[c],
-            (((1,), (1,)), ((), ())),
-            precision=lax.Precision.HIGHEST,
-            preferred_element_type=jnp.float32,
-        )
-        out[c, 0] = row[0:1]
+        out[c, 0] = rows[0:1, c * ncl : (c + 1) * ncl]
 
 
 def far(load, cx, cy, ncl, n_pencil):
@@ -396,7 +396,7 @@
     acc[...] += added[: 3 * rows] + added[3 * rows :]
 
 
-def deposit_kernel(cap, inside, load, out, acc, order):
+def deposit_kernel(cap, inside, load, out, acc, order, made, sems):
     _, cx, cy, nz = out.shape
     shape = (cx, cy, nz)
     acc[...] = jnp.zeros_like(acc)
@@ -422,10 +422,15 @@
     def _():
         deposit_step(GROUP // 2, whole * GROUP, listed, load, order, acc, shape)
 
-    for h in range(2):
-        span = slice(h * (cx // 2), (h + 1) * (cx // 2))
-        change = acc[:, h * nz : (h + 1) * nz].reshape(3, cx // 2, cy, nz)
-        out[:, span] = inside[:, span] + change
+    copies = Copies(sems)
+    rows = cx * cy // 2
+    for c in range(3):
+        for h in range(2):
+            span = slice(h * (cx // 2), (h + 1) * (cx // 2))
+            change = acc[c * rows : (c + 1) * rows, h * nz : (h + 1) * nz].reshape(cx // 2, cy, nz)
+            made[c, span] = inside[c, span] + change
+            copies.start(made.at[c, span], out.at[c, span])
+    copies.wait(0, 6)
 
 
 def deposit(inside, load, cap):
@@ -433,10 +438,12 @@
         functools.partial(deposit_kernel, cap),
         out_shape=shaped(*inside.shape),
         in_specs=[VMEM] * 2,
-        out_specs=VMEM,
+        out_specs=ANY,
         scratch_shapes=[
             pltpu.VMEM((3 * inside.shape[1] * inside.shape[2] // 2, 2 * inside.shape[3]), jnp.float32),
             pltpu.SMEM((load.shape[0] + max(cap, GROUP),), jnp.int32),
+            pltpu.VMEM(inside.shape, jnp.float32),
+            pltpu.SemaphoreType.DMA((6,)),
         ],
         compiler_params=PARAMS,
     )(inside, load)
@@ -458,7 +465,7 @@
     *faces, packets, tiles = to_send(
         vorticity, velocity, viscosity, weights, tile_cells, tile_dest.T, count, n_slab, cap
     )
-    halos = [swapped(face, axis, 1 - k % 2) for k, (face, axis) in enumerate(zip(faces, SIDES))]
+    halos = [swapped(face, axis, k % 2) for k, (face, axis) in enumerate(zip(faces, SIDES))]
     arrived = lax.all_to_all(packets, "slab", 0, 0, tiled=True)
     inside, moments = inner(vorticity, velocity, viscosity, tiles)
     advanced, load = edges(inside, moments, faces, halos, n_slab * n_pencil)

time: 37 us -> 36.6 us (0.989)
  starting transfers between devices: 20.5 us -> 17.4 us
  waiting for transfers between devices: 3.9 us -> 6.81 us
    ppermute x4, starting transfers between devices: 10.2 us -> 4.4 us  [swapped(): return lax.ppermute(array, axis, up + [(j, i) for i, j in up])]
    all_to_all x1, waiting for transfers between devices: 0.51 us -> 3.45 us  [per_device(): arrived = lax.all_to_all(packets, 'slab', 0, 0, tiled=True)]
    all_to_all x1, starting transfers between devices: 4.68 us -> 7.59 us  [per_device(): arrived = lax.all_to_all(packets, 'slab', 0, 0, tiled=True)]
where the time goes in v11:
time: 36.6 us; the launch traced here: 36.2 us
  starting transfers between devices  17.4 us (48%)
  Pallas kernels  10.5 us (29%)
  waiting for transfers between devices  6.81 us (19%)
  between operations  1.5 us (4%)
    all_to_all x1, starting transfers between devices, per_device(): arrived = lax.all_to_all(packets, 'slab', 0, 0, tiled=True)  7.59 us
    all_to_all x1, starting transfers between devices, per_device(): load = lax.all_to_all(load, ('slab', 'pencil'), 0, 0, tiled=True)  5.39 us
    ppermute x4, starting transfers between devices, swapped(): return lax.ppermute(array, axis, up + [(j, i) for i, j in up])  4.4 us
    pallas_call x1, Pallas kernels, deposit(): pl.pallas_call(functools.partial(deposit_kernel, cap), out_shape=shaped(*...  4.06 us
    all_to_all x1, waiting for transfers between devices, per_device(): arrived = lax.all_to_all(packets, 'slab', 0, 0, tiled=True)  3.45 us
    all_to_all x1, waiting for transfers between devices, per_device(): load = lax.all_to_all(load, ('slab', 'pencil'), 0, 0, tiled=True)  3.34 us
    pallas_call x1, Pallas kernels, to_send(): pl.pallas_call(functools.partial(send_kernel, cap), out_shape=made, in_sp...  2.71 us
    pallas_call x1, Pallas kernels, inner(): pl.pallas_call(inner_kernel, out_shape=(shaped(*vort.shape), shaped(*tile...  2.05 us
  transfers between devices with their start and end apart: 6, of which 2 were waited for; matrix products, arithmetic and copies ran while one was open for 0% of the time, Pallas kernels for 19%

profile of v11, /device:TPU:0, one launch (start us, length us, event | category | flops | bytes accessed | tf_op | source)
XLA Modules:
  0.0 36.2 jit_solution(18031712313880101655)
XLA Ops:
  1.3 0.0 copy-start
  1.3 0.0 copy-start.1
  1.3 2.7 %shard_map.86 = (f32[7,32,256]{2,1,0:T(8,128)}, f32[7,32,256]{2,1,0:T(8,128)}, f32[7,8,256]{2,1,0:T(8,128)}, f32[7,8,256]{2,1,0:T(8,128)}, f32[64,4,128]{2,1,0:T(4,128)}, /*index=5*/f32[4,128]{1,0:T(4,128)}) custom-call(f32[3,8,32,256]{3,2,1,0:T(8,128)} %vort.3, f32[3,8,32,256]{3,2,1,0:T(8,128)} %velo.3, f32[8,32,256]{2,1,0:T(8,128)} %visc.3, ...), custom_call_target="tpu_custom_call" | custom-call | tf_op jit(solution)/shard_map/pallas_call | solution.py:162
  4.0 0.0 copy-start.2
  4.0 3.0 %collective-permute-start = (f32[7,32,256]{2,1,0:T(8,128)}, f32[7,32,256]{2,1,0:T(8,128)S(1)}, u32[]{:S(2)}, u32[]{:S(2)}) collective-permute-start(f32[7,32,256]{2,1,0:T(8,128)} %get-tuple-element.15.near), channel_id=1, source_target_pairs={{0,4},{8,12},{16,20},{24,28},{4,0},{12,8},{20,16},{28,24},{1,5},{9... | collective-permute-start | bytes 688136 | tf_op jit(solution)/shard_map/ppermute | solution.py:454
  7.0 0.7 %collective-permute-start.1 = (f32[7,32,256]{2,1,0:T(8,128)}, f32[7,32,256]{2,1,0:T(8,128)S(1)}, u32[]{:S(2)}, u32[]{:S(2)}) collective-permute-start(f32[7,32,256]{2,1,0:T(8,128)} %get-tuple-element.16.far), channel_id=1, source_target_pairs={{4,8},{12,16},{20,24},{8,4},{16,12},{24,20},{5,9},{13,17},{21,25},... | collective-permute-start | bytes 688136 | tf_op jit(solution)/shard_map/ppermute | solution.py:454
  7.7 7.6 %all-to-all-start = ((f32[64,4,128]{2,1,0:T(4,128)}), f32[64,4,128]{2,1,0:T(4,128)S(1)}, u32[]{:S(2)}, u32[]{:S(2)}) async-start(f32[64,4,128]{2,1,0:T(4,128)} %get-tuple-element.20), calls=%async_computation | async-start | bytes 262144 | tf_op jit(solution)/shard_map/all_to_all | solution.py:469
  15.3 0.1 collective-permute-start.2
  15.4 0.7 %collective-permute-start.3 = (f32[7,8,256]{2,1,0:T(8,128)}, f32[7,8,256]{2,1,0:T(8,128)S(1)}, u32[]{:S(2)}, u32[]{:S(2)}) collective-permute-start(f32[7,8,256]{2,1,0:T(8,128)} %get-tuple-element.18.other), channel_id=1, source_target_pairs={{1,2},{2,1},{5,6},{6,5},{9,10},{10,9},{13,14},{14,13},{17,18},{18,... | collective-permute-start | bytes 172040 | tf_op jit(solution)/shard_map/ppermute | solution.py:454
  16.0 0.0 copy-done
  16.1 0.0 copy-done.1
  16.1 0.0 copy-done.2
  16.1 0.0 copy-start.3
  16.1 2.0 %shard_map.87 = (f32[3,8,32,256]{3,2,1,0:T(8,128)S(1)}, f32[4,128]{1,0:T(4,128)S(1)}) custom-call(f32[3,8,32,256]{3,2,1,0:T(8,128)S(1)} %copy-done, f32[3,8,32,256]{3,2,1,0:T(8,128)S(1)} %copy-done.1, f32[8,32,256]{2,1,0:T(8,128)S(1)} %copy-done.2, f32[4,128]{1,0:T(4,128)S(1)} %copy-done.7), custom_call_target="tpu_custom_call" | custom-call | tf_op jit(solution)/shard_map/pallas_call | solution.py:249
  18.2 0.0 collective-permute-done.2.swap_in
  18.2 0.0 collective-permute-done.3.other_in
  18.2 0.0 collective-permute-done.near_in
  18.2 0.0 collective-permute-done.1.far_in
  18.3 0.9 %shard_map.88 = (f32[3,8,32,256]{3,2,1,0:T(8,128)S(1)}, f32[32,4,128]{2,1,0:T(4,128)}) custom-call(f32[3,8,32,256]{3,2,1,0:T(8,128)S(1)} %get-tuple-element.13.inside, f32[4,128]{1,0:T(4,128)S(1)} %get-tuple-element.14.moments, f32[7,32,256]{2,1,0:T(8,128)S(1)} %copy-done.3, f32[7,32,256]{2,1,0:T(8,128)S(1)} %copy-done.4, f32[7,8,256]{2,1,0:T(8,128)S(1)} %copy-done.5, ...), custom_call_target="tpu_custom_call" | custom-call | tf_op jit(solution)/shard_map/pallas_call | solution.py:304
  19.2 3.5 %all-to-all-done.load = f32[64,4,128]{2,1,0:T(4,128)S(1)} async-done(((f32[64,4,128]{2,1,0:T(4,128)}), f32[64,4,128]{2,1,0:T(4,128)S(1)}, u32[]{:S(2)}, u32[]{:S(2)}) %all-to-all-start) | async-done | bytes 131104 | tf_op jit(solution)/shard_map/all_to_all | solution.py:469
  22.6 5.4 %all-to-all-start.1 = ((f32[32,4,128]{2,1,0:T(4,128)}), f32[32,4,128]{2,1,0:T(4,128)S(1)}, u32[]{:S(2)}, u32[]{:S(2)}) async-start(f32[32,4,128]{2,1,0:T(4,128)} %get-tuple-element.21), calls=%async_computation.1 | async-start | bytes 131072 | tf_op jit(solution)/shard_map/all_to_all | solution.py:472
  28.0 4.1 %shard_map.89 = f32[3,8,32,256]{3,2,1,0:T(8,128)} custom-call(f32[3,8,32,256]{3,2,1,0:T(8,128)S(1)} %get-tuple-element.19.inside, f32[64,4,128]{2,1,0:T(4,128)S(1)} %all-to-all-done.load), custom_call_target="tpu_custom_call" | custom-call | tf_op jit(solution)/shard_map/pallas_call | solution.py:437
  32.1 3.3 %all-to-all-done.1.load = f32[32,4,128]{2,1,0:T(4,128)S(1)} async-done(((f32[32,4,128]{2,1,0:T(4,128)}), f32[32,4,128]{2,1,0:T(4,128)S(1)}, u32[]{:S(2)}, u32[]{:S(2)}) %all-to-all-start.1) | async-done | bytes 65568 | tf_op jit(solution)/shard_map/all_to_all | solution.py:472
  35.4 0.8 %shard_map.90 = f32[3,1,1,16]{3,2,1,0:T(1,128)} custom-call(f32[32,4,128]{2,1,0:T(4,128)S(1)} %all-to-all-done.1.load), custom_call_target="tpu_custom_call" | custom-call | tf_op jit(solution)/shard_map/pallas_call | solution.py:351
  (9 shorter events, 0.0 us)
Async XLA Ops:
  1.3 14.8 %copy-start = (f32[3,8,32,256]{3,2,1,0:T(8,128)S(1)}, f32[3,8,32,256]{3,2,1,0:T(8,128)}, u32[]{:S(2)}) copy-start(f32[3,8,32,256]{3,2,1,0:T(8,128)} %vort.3) | copy-start | bytes 2359300
  1.3 14.8 %copy-start.1 = (f32[3,8,32,256]{3,2,1,0:T(8,128)S(1)}, f32[3,8,32,256]{3,2,1,0:T(8,128)}, u32[]{:S(2)}) copy-start(f32[3,8,32,256]{3,2,1,0:T(8,128)} %velo.3) | copy-start | bytes 2359300
  4.0 12.0 %copy-start.2 = (f32[8,32,256]{2,1,0:T(8,128)S(1)}, f32[8,32,256]{2,1,0:T(8,128)}, u32[]{:S(2)}) copy-start(f32[8,32,256]{2,1,0:T(8,128)} %visc.3) | copy-start | bytes 786436
  4.0 14.2 %collective-permute-start = (f32[7,32,256]{2,1,0:T(8,128)}, f32[7,32,256]{2,1,0:T(8,128)S(1)}, u32[]{:S(2)}, u32[]{:S(2)}) collective-permute-start(f32[7,32,256]{2,1,0:T(8,128)} %get-tuple-element.15.near), channel_id=1, source_target_pairs={{0,4},{8,12},{16,20},{24,28},{4,0},{12,8},{20,16},{28,24},{1,5},{9... | collective-permute-start | bytes 688136 | tf_op jit(solution)/shard_map/ppermute | solution.py:454
  7.0 11.2 %collective-permute-start.1 = (f32[7,32,256]{2,1,0:T(8,128)}, f32[7,32,256]{2,1,0:T(8,128)S(1)}, u32[]{:S(2)}, u32[]{:S(2)}) collective-permute-start(f32[7,32,256]{2,1,0:T(8,128)} %get-tuple-element.16.far), channel_id=1, source_target_pairs={{4,8},{12,16},{20,24},{8,4},{16,12},{24,20},{5,9},{13,17},{21,25},... | collective-permute-start | bytes 688136 | tf_op jit(solution)/shard_map/ppermute | solution.py:454
  7.7 14.9 %all-to-all-start = ((f32[64,4,128]{2,1,0:T(4,128)}), f32[64,4,128]{2,1,0:T(4,128)S(1)}, u32[]{:S(2)}, u32[]{:S(2)}) async-start(f32[64,4,128]{2,1,0:T(4,128)} %get-tuple-element.20), calls=%async_computation | async-start | bytes 262144 | tf_op jit(solution)/shard_map/all_to_all | solution.py:469
  15.3 0.8 %copy-start.7 = (f32[4,128]{1,0:T(4,128)S(1)}, f32[4,128]{1,0:T(4,128)}, u32[]{:S(2)}) copy-start(f32[4,128]{1,0:T(4,128)} %get-tuple-element.12.tiles_in) | copy-start | bytes 6148
  15.3 2.9 %collective-permute-start.2 = (f32[7,8,256]{2,1,0:T(8,128)}, f32[7,8,256]{2,1,0:T(8,128)S(1)}, u32[]{:S(2)}, u32[]{:S(2)}) collective-permute-start(f32[7,8,256]{2,1,0:T(8,128)} %get-tuple-element.17.swap), channel_id=1, source_target_pairs={{0,1},{2,3},{1,0},{3,2},{4,5},{6,7},{5,4},{7,6},{8,9},{10,11},{9,8... | collective-permute-start | bytes 172040 | tf_op jit(solution)/shard_map/ppermute | solution.py:454
  15.4 2.8 %collective-permute-start.3 = (f32[7,8,256]{2,1,0:T(8,128)}, f32[7,8,256]{2,1,0:T(8,128)S(1)}, u32[]{:S(2)}, u32[]{:S(2)}) collective-permute-start(f32[7,8,256]{2,1,0:T(8,128)} %get-tuple-element.18.other), channel_id=1, source_target_pairs={{1,2},{2,1},{5,6},{6,5},{9,10},{10,9},{13,14},{14,13},{17,18},{18,... | collective-permute-start | bytes 172040 | tf_op jit(solution)/shard_map/ppermute | solution.py:454
  16.1 2.1 %copy-start.3 = (f32[7,32,256]{2,1,0:T(8,128)S(1)}, f32[7,32,256]{2,1,0:T(8,128)}, u32[]{:S(2)}) copy-start(f32[7,32,256]{2,1,0:T(8,128)} %get-tuple-element.15.near) | copy-start | bytes 688132
  16.1 2.1 %copy-start.4 = (f32[7,32,256]{2,1,0:T(8,128)S(1)}, f32[7,32,256]{2,1,0:T(8,128)}, u32[]{:S(2)}) copy-start(f32[7,32,256]{2,1,0:T(8,128)} %get-tuple-element.16.far) | copy-start | bytes 688132
  16.1 2.1 %copy-start.5 = (f32[7,8,256]{2,1,0:T(8,128)S(1)}, f32[7,8,256]{2,1,0:T(8,128)}, u32[]{:S(2)}) copy-start(f32[7,8,256]{2,1,0:T(8,128)} %get-tuple-element.17.swap) | copy-start | bytes 172036
  16.1 2.1 %copy-start.6 = (f32[7,8,256]{2,1,0:T(8,128)S(1)}, f32[7,8,256]{2,1,0:T(8,128)}, u32[]{:S(2)}) copy-start(f32[7,8,256]{2,1,0:T(8,128)} %get-tuple-element.18.other) | copy-start | bytes 172036
  22.6 12.8 %all-to-all-start.1 = ((f32[32,4,128]{2,1,0:T(4,128)}), f32[32,4,128]{2,1,0:T(4,128)S(1)}, u32[]{:S(2)}, u32[]{:S(2)}) async-start(f32[32,4,128]{2,1,0:T(4,128)} %get-tuple-element.21), calls=%async_computation.1 | async-start | bytes 131072 | tf_op jit(solution)/shard_map/all_to_all | solution.py:472

commit v12 on v11

--- a/solution.py
+++ b/solution.py
@@ -36,10 +36,17 @@
     return [piece.astype(jnp.bfloat16) for piece in (high, middle, low)]
 
 
+def outward(count):
+    half = count // 2
+    return [half + k // 2 if k % 2 else half - 1 - k // 2 for k in range(count)]
+
+
 def pack_tiles(cap, cells_dev, weights, cells, dest, count, packets):
     slots = packets.shape[0]
     tiles = cells.shape[0]
+    half = slots // cap // 2
     names = dest[...]
+    names = jnp.where(names < half, 2 * (half - 1 - names), 2 * (names - half) + 1)
     live = (lax.broadcasted_iota(jnp.int32, (1, tiles), 1) < count[0]).astype(jnp.float32)
     same = (lax.broadcasted_iota(jnp.int32, (slots // cap, tiles), 0) == names).astype(jnp.float32)
     shape = (tiles, tiles)
@@ -67,8 +74,9 @@
     wide = cap * packets.shape[2]
     level = lax.broadcasted_iota(jnp.int32, (ncl, wide), 0)
     found = []
+    order = outward(n_slab)
     for d in range(n_slab):
-        block = jnp.concatenate([packets[d * cap + k] for k in range(cap)], axis=1)
+        block = jnp.concatenate([packets[order.index(d) * cap + k] for k in range(cap)], axis=1)
         cell = block[3:4, :].astype(jnp.int32)
         spots = (level == cell % nz // CB).astype(jnp.float32).astype(jnp.bfloat16)
         high, low = split(block)
@@ -466,10 +474,12 @@
         vorticity, velocity, viscosity, weights, tile_cells, tile_dest.T, count, n_slab, cap
     )
     halos = [swapped(face, axis, k % 2) for k, (face, axis) in enumerate(zip(faces, SIDES))]
-    arrived = lax.all_to_all(packets, "slab", 0, 0, tiled=True)
+    order = outward(n_slab)
+    arrived = lax.all_to_all(packets, "slab", 0, 0, axis_index_groups=[order], tiled=True)
     inside, moments = inner(vorticity, velocity, viscosity, tiles)
     advanced, load = edges(inside, moments, faces, halos, n_slab * n_pencil)
-    load = lax.all_to_all(load, ("slab", "pencil"), 0, 0, tiled=True)
+    everyone = [s * n_pencil + p for s in order for p in range(n_pencil)]
+    load = lax.all_to_all(load, ("slab", "pencil"), 0, 0, axis_index_groups=[everyone], tiled=True)
     vorticity_out = deposit(advanced, arrived, cap)
     return (vorticity_out, far(load, cx, cy, ncl, n_pencil))
 

time: 36.6 us -> 35.4 us (0.967)
  waiting for transfers between devices: 6.81 us -> 2.8 us
  Pallas kernels: 10.5 us -> 12.4 us
  starting transfers between devices: 17.4 us -> 18.3 us
    all_to_all x2, waiting for transfers between devices: 6.79 us -> 2.79 us  [the longest x1 1.63 us: per_device(): lax.all_to_all(load, ('slab', 'pencil'), 0, 0, axis_index_groups=[everyon...]
    pallas_call x1, Pallas kernels: 4.06 us -> 5.9 us  [deposit(): pl.pallas_call(functools.partial(deposit_kernel, cap), out_shape=shaped(*...]
    all_to_all x2, starting transfers between devices: 13 us -> 14 us  [the longest x1 8.6 us: per_device(): lax.all_to_all(packets, 'slab', 0, 0, axis_index_groups=[order], tiled=True)]
  transfers between devices with their start and end apart: 6 -> 6, of which waited for: 2 -> 2; matrix products, arithmetic and copies ran while one was open for 0% -> 0% of each run, Pallas kernels for 19% -> 25%
where the time goes in v12:
time: 35.4 us; the launch traced here: 35 us
  starting transfers between devices  18.3 us (52%)
  Pallas kernels  12.4 us (35%)
  waiting for transfers between devices  2.8 us (8%)
  between operations  1.49 us (4%)
    all_to_all x1, starting transfers between devices, per_device(): lax.all_to_all(packets, 'slab', 0, 0, axis_index_groups=[order], tiled=True)  8.6 us
    pallas_call x1, Pallas kernels, deposit(): pl.pallas_call(functools.partial(deposit_kernel, cap), out_shape=shaped(*...  5.9 us
    all_to_all x1, starting transfers between devices, per_device(): lax.all_to_all(load, ('slab', 'pencil'), 0, 0, axis_index_groups=[everyon...  5.4 us
    ppermute x4, starting transfers between devices, swapped(): return lax.ppermute(array, axis, up + [(j, i) for i, j in up])  4.33 us
    pallas_call x1, Pallas kernels, to_send(): pl.pallas_call(functools.partial(send_kernel, cap), out_shape=made, in_sp...  2.71 us
    pallas_call x1, Pallas kernels, inner(): pl.pallas_call(inner_kernel, out_shape=(shaped(*vort.shape), shaped(*tile...  2.05 us
    all_to_all x1, waiting for transfers between devices, per_device(): lax.all_to_all(load, ('slab', 'pencil'), 0, 0, axis_index_groups=[everyon...  1.63 us
    all_to_all x1, waiting for transfers between devices, per_device(): lax.all_to_all(packets, 'slab', 0, 0, axis_index_groups=[order], tiled=True)  1.16 us
  transfers between devices with their start and end apart: 6, of which 2 were waited for; matrix products, arithmetic and copies ran while one was open for 0% of the time, Pallas kernels for 25%

profile of v12, /device:TPU:0, one launch (start us, length us, event | category | flops | bytes accessed | tf_op | source)
XLA Modules:
  0.0 35.0 jit_solution(8160835294972963301)
XLA Ops:
  1.3 2.7 %shard_map.86 = (f32[7,32,256]{2,1,0:T(8,128)}, f32[7,32,256]{2,1,0:T(8,128)}, f32[7,8,256]{2,1,0:T(8,128)}, f32[7,8,256]{2,1,0:T(8,128)}, f32[64,4,128]{2,1,0:T(4,128)}, /*index=5*/f32[4,128]{1,0:T(4,128)}) custom-call(f32[3,8,32,256]{3,2,1,0:T(8,128)} %vort.3, f32[3,8,32,256]{3,2,1,0:T(8,128)} %velo.3, f32[8,32,256]{2,1,0:T(8,128)} %visc.3, ...), custom_call_target="tpu_custom_call" | custom-call | tf_op jit(solution)/shard_map/pallas_call | solution.py:170
  4.0 0.0 copy-start.2
  4.0 3.0 %collective-permute-start = (f32[7,32,256]{2,1,0:T(8,128)}, f32[7,32,256]{2,1,0:T(8,128)S(1)}, u32[]{:S(2)}, u32[]{:S(2)}) collective-permute-start(f32[7,32,256]{2,1,0:T(8,128)} %get-tuple-element.15.near), channel_id=1, source_target_pairs={{0,4},{8,12},{16,20},{24,28},{4,0},{12,8},{20,16},{28,24},{1,5},{9... | collective-permute-start | bytes 688136 | tf_op jit(solution)/shard_map/ppermute | solution.py:462
  7.0 0.7 %collective-permute-start.1 = (f32[7,32,256]{2,1,0:T(8,128)}, f32[7,32,256]{2,1,0:T(8,128)S(1)}, u32[]{:S(2)}, u32[]{:S(2)}) collective-permute-start(f32[7,32,256]{2,1,0:T(8,128)} %get-tuple-element.16.far), channel_id=1, source_target_pairs={{4,8},{12,16},{20,24},{8,4},{16,12},{24,20},{5,9},{13,17},{21,25},... | collective-permute-start | bytes 688136 | tf_op jit(solution)/shard_map/ppermute | solution.py:462
  7.7 8.6 %all-to-all-start = ((f32[64,4,128]{2,1,0:T(4,128)}), f32[64,4,128]{2,1,0:T(4,128)S(1)}, u32[]{:S(2)}, u32[]{:S(2)}) async-start(f32[64,4,128]{2,1,0:T(4,128)} %get-tuple-element.20), calls=%async_computation | async-start | bytes 262144 | tf_op jit(solution)/shard_map/all_to_all | solution.py:478
  16.3 0.0 collective-permute-start.2
  16.3 0.7 %collective-permute-start.3 = (f32[7,8,256]{2,1,0:T(8,128)}, f32[7,8,256]{2,1,0:T(8,128)S(1)}, u32[]{:S(2)}, u32[]{:S(2)}) collective-permute-start(f32[7,8,256]{2,1,0:T(8,128)} %get-tuple-element.18.other), channel_id=1, source_target_pairs={{1,2},{2,1},{5,6},{6,5},{9,10},{10,9},{13,14},{14,13},{17,18},{18,... | collective-permute-start | bytes 172040 | tf_op jit(solution)/shard_map/ppermute | solution.py:462
  17.0 0.0 copy-done
  17.0 0.0 copy-done.1
  17.0 0.0 copy-done.2
  17.0 0.0 copy-done.7
  17.0 0.0 copy-start.3
  17.1 2.0 %shard_map.87 = (f32[3,8,32,256]{3,2,1,0:T(8,128)S(1)}, f32[4,128]{1,0:T(4,128)S(1)}) custom-call(f32[3,8,32,256]{3,2,1,0:T(8,128)S(1)} %copy-done, f32[3,8,32,256]{3,2,1,0:T(8,128)S(1)} %copy-done.1, f32[8,32,256]{2,1,0:T(8,128)S(1)} %copy-done.2, f32[4,128]{1,0:T(4,128)S(1)} %copy-done.7), custom_call_target="tpu_custom_call" | custom-call | tf_op jit(solution)/shard_map/pallas_call | solution.py:257
  19.1 0.0 collective-permute-done.2.swap_in
  19.1 0.0 collective-permute-done.3.other_in
  19.1 0.0 collective-permute-done.near_in
  19.2 0.0 collective-permute-done.1.far_in
  19.2 0.0 copy-done.3
  19.2 0.9 %shard_map.88 = (f32[3,8,32,256]{3,2,1,0:T(8,128)S(1)}, f32[32,4,128]{2,1,0:T(4,128)}) custom-call(f32[3,8,32,256]{3,2,1,0:T(8,128)S(1)} %get-tuple-element.13.inside, f32[4,128]{1,0:T(4,128)S(1)} %get-tuple-element.14.moments, f32[7,32,256]{2,1,0:T(8,128)S(1)} %copy-done.3, f32[7,32,256]{2,1,0:T(8,128)S(1)} %copy-done.4, f32[7,8,256]{2,1,0:T(8,128)S(1)} %copy-done.5, ...), custom_call_target="tpu_custom_call" | custom-call | tf_op jit(solution)/shard_map/pallas_call | solution.py:312
  20.1 1.2 %all-to-all-done.load = f32[64,4,128]{2,1,0:T(4,128)S(1)} async-done(((f32[64,4,128]{2,1,0:T(4,128)}), f32[64,4,128]{2,1,0:T(4,128)S(1)}, u32[]{:S(2)}, u32[]{:S(2)}) %all-to-all-start) | async-done | bytes 131104 | tf_op jit(solution)/shard_map/all_to_all | solution.py:478
  21.3 5.4 %all-to-all-start.1 = ((f32[32,4,128]{2,1,0:T(4,128)}), f32[32,4,128]{2,1,0:T(4,128)S(1)}, u32[]{:S(2)}, u32[]{:S(2)}) async-start(f32[32,4,128]{2,1,0:T(4,128)} %get-tuple-element.21), calls=%async_computation.1 | async-start | bytes 131072 | tf_op jit(solution)/shard_map/all_to_all | solution.py:482
  26.7 5.9 %shard_map.89 = f32[3,8,32,256]{3,2,1,0:T(8,128)} custom-call(f32[3,8,32,256]{3,2,1,0:T(8,128)S(1)} %get-tuple-element.19.inside, f32[64,4,128]{2,1,0:T(4,128)S(1)} %all-to-all-done.load), custom_call_target="tpu_custom_call" | custom-call | tf_op jit(solution)/shard_map/pallas_call | solution.py:445
  32.6 1.6 %all-to-all-done.1.load = f32[32,4,128]{2,1,0:T(4,128)S(1)} async-done(((f32[32,4,128]{2,1,0:T(4,128)}), f32[32,4,128]{2,1,0:T(4,128)S(1)}, u32[]{:S(2)}, u32[]{:S(2)}) %all-to-all-start.1) | async-done | bytes 65568 | tf_op jit(solution)/shard_map/all_to_all | solution.py:482
  34.2 0.8 %shard_map.90 = f32[3,1,1,16]{3,2,1,0:T(1,128)} custom-call(f32[32,4,128]{2,1,0:T(4,128)S(1)} %all-to-all-done.1.load), custom_call_target="tpu_custom_call" | custom-call | tf_op jit(solution)/shard_map/pallas_call | solution.py:359
  (9 shorter events, 0.0 us)
Async XLA Ops:
  1.3 15.7 %copy-start = (f32[3,8,32,256]{3,2,1,0:T(8,128)S(1)}, f32[3,8,32,256]{3,2,1,0:T(8,128)}, u32[]{:S(2)}) copy-start(f32[3,8,32,256]{3,2,1,0:T(8,128)} %vort.3) | copy-start | bytes 2359300
  1.3 15.7 %copy-start.1 = (f32[3,8,32,256]{3,2,1,0:T(8,128)S(1)}, f32[3,8,32,256]{3,2,1,0:T(8,128)}, u32[]{:S(2)}) copy-start(f32[3,8,32,256]{3,2,1,0:T(8,128)} %velo.3) | copy-start | bytes 2359300
  4.0 13.0 %copy-start.2 = (f32[8,32,256]{2,1,0:T(8,128)S(1)}, f32[8,32,256]{2,1,0:T(8,128)}, u32[]{:S(2)}) copy-start(f32[8,32,256]{2,1,0:T(8,128)} %visc.3) | copy-start | bytes 786436
  4.0 15.1 %collective-permute-start = (f32[7,32,256]{2,1,0:T(8,128)}, f32[7,32,256]{2,1,0:T(8,128)S(1)}, u32[]{:S(2)}, u32[]{:S(2)}) collective-permute-start(f32[7,32,256]{2,1,0:T(8,128)} %get-tuple-element.15.near), channel_id=1, source_target_pairs={{0,4},{8,12},{16,20},{24,28},{4,0},{12,8},{20,16},{28,24},{1,5},{9... | collective-permute-start | bytes 688136 | tf_op jit(solution)/shard_map/ppermute | solution.py:462
  7.0 12.1 %collective-permute-start.1 = (f32[7,32,256]{2,1,0:T(8,128)}, f32[7,32,256]{2,1,0:T(8,128)S(1)}, u32[]{:S(2)}, u32[]{:S(2)}) collective-permute-start(f32[7,32,256]{2,1,0:T(8,128)} %get-tuple-element.16.far), channel_id=1, source_target_pairs={{4,8},{12,16},{20,24},{8,4},{16,12},{24,20},{5,9},{13,17},{21,25},... | collective-permute-start | bytes 688136 | tf_op jit(solution)/shard_map/ppermute | solution.py:462
  7.7 13.6 %all-to-all-start = ((f32[64,4,128]{2,1,0:T(4,128)}), f32[64,4,128]{2,1,0:T(4,128)S(1)}, u32[]{:S(2)}, u32[]{:S(2)}) async-start(f32[64,4,128]{2,1,0:T(4,128)} %get-tuple-element.20), calls=%async_computation | async-start | bytes 262144 | tf_op jit(solution)/shard_map/all_to_all | solution.py:478
  16.3 0.7 %copy-start.7 = (f32[4,128]{1,0:T(4,128)S(1)}, f32[4,128]{1,0:T(4,128)}, u32[]{:S(2)}) copy-start(f32[4,128]{1,0:T(4,128)} %get-tuple-element.12.tiles_in) | copy-start | bytes 6148
  16.3 2.8 %collective-permute-start.2 = (f32[7,8,256]{2,1,0:T(8,128)}, f32[7,8,256]{2,1,0:T(8,128)S(1)}, u32[]{:S(2)}, u32[]{:S(2)}) collective-permute-start(f32[7,8,256]{2,1,0:T(8,128)} %get-tuple-element.17.swap), channel_id=1, source_target_pairs={{0,1},{2,3},{1,0},{3,2},{4,5},{6,7},{5,4},{7,6},{8,9},{10,11},{9,8... | collective-permute-start | bytes 172040 | tf_op jit(solution)/shard_map/ppermute | solution.py:462
  16.3 2.8 %collective-permute-start.3 = (f32[7,8,256]{2,1,0:T(8,128)}, f32[7,8,256]{2,1,0:T(8,128)S(1)}, u32[]{:S(2)}, u32[]{:S(2)}) collective-permute-start(f32[7,8,256]{2,1,0:T(8,128)} %get-tuple-element.18.other), channel_id=1, source_target_pairs={{1,2},{2,1},{5,6},{6,5},{9,10},{10,9},{13,14},{14,13},{17,18},{18,... | collective-permute-start | bytes 172040 | tf_op jit(solution)/shard_map/ppermute | solution.py:462
  17.0 2.1 %copy-start.3 = (f32[7,32,256]{2,1,0:T(8,128)S(1)}, f32[7,32,256]{2,1,0:T(8,128)}, u32[]{:S(2)}) copy-start(f32[7,32,256]{2,1,0:T(8,128)} %get-tuple-element.15.near) | copy-start | bytes 688132
  17.0 2.1 %copy-start.4 = (f32[7,32,256]{2,1,0:T(8,128)S(1)}, f32[7,32,256]{2,1,0:T(8,128)}, u32[]{:S(2)}) copy-start(f32[7,32,256]{2,1,0:T(8,128)} %get-tuple-element.16.far) | copy-start | bytes 688132
  17.1 2.1 %copy-start.5 = (f32[7,8,256]{2,1,0:T(8,128)S(1)}, f32[7,8,256]{2,1,0:T(8,128)}, u32[]{:S(2)}) copy-start(f32[7,8,256]{2,1,0:T(8,128)} %get-tuple-element.17.swap) | copy-start | bytes 172036
  17.1 2.1 %copy-start.6 = (f32[7,8,256]{2,1,0:T(8,128)S(1)}, f32[7,8,256]{2,1,0:T(8,128)}, u32[]{:S(2)}) copy-start(f32[7,8,256]{2,1,0:T(8,128)} %get-tuple-element.18.other) | copy-start | bytes 172036
  21.3 12.9 %all-to-all-start.1 = ((f32[32,4,128]{2,1,0:T(4,128)}), f32[32,4,128]{2,1,0:T(4,128)S(1)}, u32[]{:S(2)}, u32[]{:S(2)}) async-start(f32[32,4,128]{2,1,0:T(4,128)} %get-tuple-element.21), calls=%async_computation.1 | async-start | bytes 131072 | tf_op jit(solution)/shard_map/all_to_all | solution.py:482

commit v13 on v12

--- a/solution.py
+++ b/solution.py
@@ -38,7 +38,7 @@
 
 def outward(count):
     half = count // 2
-    return [half + k // 2 if k % 2 else half - 1 - k // 2 for k in range(count)]
+    return [half - 1 - k // 2 if k % 2 else half + k // 2 for k in range(count)]
 
 
 def pack_tiles(cap, cells_dev, weights, cells, dest, count, packets):
@@ -46,7 +46,7 @@
     tiles = cells.shape[0]
     half = slots // cap // 2
     names = dest[...]
-    names = jnp.where(names < half, 2 * (half - 1 - names), 2 * (names - half) + 1)
+    names = jnp.where(names < half, 2 * (half - 1 - names) + 1, 2 * (names - half))
     live = (lax.broadcasted_iota(jnp.int32, (1, tiles), 1) < count[0]).astype(jnp.float32)
     same = (lax.broadcasted_iota(jnp.int32, (slots // cap, tiles), 0) == names).astype(jnp.float32)
     shape = (tiles, tiles)

time: 35.4 us -> 34.8 us (0.983)
  Pallas kernels: 12.4 us -> 8.68 us
  waiting for transfers between devices: 2.8 us -> 6.35 us
  starting transfers between devices: 18.3 us -> 17.9 us
    pallas_call x1, Pallas kernels: 5.9 us -> 2.21 us  [deposit(): pl.pallas_call(functools.partial(deposit_kernel, cap), out_shape=shaped(*...]
    all_to_all x1, waiting for transfers between devices: 1.63 us -> 5.17 us  [per_device(): lax.all_to_all(load, ('slab', 'pencil'), 0, 0, axis_index_groups=[everyon...]
    all_to_all x1, starting transfers between devices: 8.6 us -> 8.15 us  [per_device(): lax.all_to_all(packets, 'slab', 0, 0, axis_index_groups=[order], tiled=True)]
  transfers between devices with their start and end apart: 6 -> 6, of which waited for: 2 -> 2; matrix products, arithmetic and copies ran while one was open for 0% -> 0% of each run, Pallas kernels for 25% -> 15%
where the time goes in v13:
time: 34.8 us; the launch traced here: 34.4 us
  starting transfers between devices  17.9 us (51%)
  Pallas kernels  8.68 us (25%)
  waiting for transfers between devices  6.35 us (18%)
  between operations  1.49 us (4%)
    all_to_all x1, starting transfers between devices, per_device(): lax.all_to_all(packets, 'slab', 0, 0, axis_index_groups=[order], tiled=True)  8.15 us
    all_to_all x1, starting transfers between devices, per_device(): lax.all_to_all(load, ('slab', 'pencil'), 0, 0, axis_index_groups=[everyon...  5.39 us
    all_to_all x1, waiting for transfers between devices, per_device(): lax.all_to_all(load, ('slab', 'pencil'), 0, 0, axis_index_groups=[everyon...  5.17 us
    ppermute x4, starting transfers between devices, swapped(): return lax.ppermute(array, axis, up + [(j, i) for i, j in up])  4.33 us
    pallas_call x1, Pallas kernels, to_send(): pl.pallas_call(functools.partial(send_kernel, cap), out_shape=made, in_sp...  2.71 us
    pallas_call x1, Pallas kernels, deposit(): pl.pallas_call(functools.partial(deposit_kernel, cap), out_shape=shaped(*...  2.21 us
    pallas_call x1, Pallas kernels, inner(): pl.pallas_call(inner_kernel, out_shape=(shaped(*vort.shape), shaped(*tile...  2.05 us
    all_to_all x1, waiting for transfers between devices, per_device(): lax.all_to_all(packets, 'slab', 0, 0, axis_index_groups=[order], tiled=True)  1.17 us
  transfers between devices with their start and end apart: 6, of which 2 were waited for; matrix products, arithmetic and copies ran while one was open for 0% of the time, Pallas kernels for 15%

profile of v13, /device:TPU:0, one launch (start us, length us, event | category | flops | bytes accessed | tf_op | source)
XLA Modules:
  0.0 34.4 jit_solution(12764434785723443732)
XLA Ops:
  1.3 0.0 copy-start
  1.3 0.0 copy-start.1
  1.3 2.7 %shard_map.86 = (f32[7,32,256]{2,1,0:T(8,128)}, f32[7,32,256]{2,1,0:T(8,128)}, f32[7,8,256]{2,1,0:T(8,128)}, f32[7,8,256]{2,1,0:T(8,128)}, f32[64,4,128]{2,1,0:T(4,128)}, /*index=5*/f32[4,128]{1,0:T(4,128)}) custom-call(f32[3,8,32,256]{3,2,1,0:T(8,128)} %vort.3, f32[3,8,32,256]{3,2,1,0:T(8,128)} %velo.3, f32[8,32,256]{2,1,0:T(8,128)} %visc.3, ...), custom_call_target="tpu_custom_call" | custom-call | tf_op jit(solution)/shard_map/pallas_call | solution.py:170
  4.0 0.0 copy-start.2
  4.0 3.0 %collective-permute-start = (f32[7,32,256]{2,1,0:T(8,128)}, f32[7,32,256]{2,1,0:T(8,128)S(1)}, u32[]{:S(2)}, u32[]{:S(2)}) collective-permute-start(f32[7,32,256]{2,1,0:T(8,128)} %get-tuple-element.15.near), channel_id=1, source_target_pairs={{0,4},{8,12},{16,20},{24,28},{4,0},{12,8},{20,16},{28,24},{1,5},{9... | collective-permute-start | bytes 688136 | tf_op jit(solution)/shard_map/ppermute | solution.py:462
  7.0 0.7 %collective-permute-start.1 = (f32[7,32,256]{2,1,0:T(8,128)}, f32[7,32,256]{2,1,0:T(8,128)S(1)}, u32[]{:S(2)}, u32[]{:S(2)}) collective-permute-start(f32[7,32,256]{2,1,0:T(8,128)} %get-tuple-element.16.far), channel_id=1, source_target_pairs={{4,8},{12,16},{20,24},{8,4},{16,12},{24,20},{5,9},{13,17},{21,25},... | collective-permute-start | bytes 688136 | tf_op jit(solution)/shard_map/ppermute | solution.py:462
  7.7 8.1 %all-to-all-start = ((f32[64,4,128]{2,1,0:T(4,128)}), f32[64,4,128]{2,1,0:T(4,128)S(1)}, u32[]{:S(2)}, u32[]{:S(2)}) async-start(f32[64,4,128]{2,1,0:T(4,128)} %get-tuple-element.20), calls=%async_computation | async-start | bytes 262144 | tf_op jit(solution)/shard_map/all_to_all | solution.py:478
  15.9 0.0 collective-permute-start.2
  15.9 0.7 %collective-permute-start.3 = (f32[7,8,256]{2,1,0:T(8,128)}, f32[7,8,256]{2,1,0:T(8,128)S(1)}, u32[]{:S(2)}, u32[]{:S(2)}) collective-permute-start(f32[7,8,256]{2,1,0:T(8,128)} %get-tuple-element.18.other), channel_id=1, source_target_pairs={{1,2},{2,1},{5,6},{6,5},{9,10},{10,9},{13,14},{14,13},{17,18},{18,... | collective-permute-start | bytes 172040 | tf_op jit(solution)/shard_map/ppermute | solution.py:462
  16.5 0.0 copy-done
  16.5 0.0 copy-done.1
  16.6 0.0 copy-done.2
  16.6 0.0 copy-start.3
  16.6 2.0 %shard_map.87 = (f32[3,8,32,256]{3,2,1,0:T(8,128)S(1)}, f32[4,128]{1,0:T(4,128)S(1)}) custom-call(f32[3,8,32,256]{3,2,1,0:T(8,128)S(1)} %copy-done, f32[3,8,32,256]{3,2,1,0:T(8,128)S(1)} %copy-done.1, f32[8,32,256]{2,1,0:T(8,128)S(1)} %copy-done.2, f32[4,128]{1,0:T(4,128)S(1)} %copy-done.7), custom_call_target="tpu_custom_call" | custom-call | tf_op jit(solution)/shard_map/pallas_call | solution.py:257
  18.7 0.0 collective-permute-done.2.swap_in
  18.7 0.0 collective-permute-done.3.other_in
  18.7 0.0 collective-permute-done.near_in
  18.7 0.0 collective-permute-done.1.far_in
  18.8 0.9 %shard_map.88 = (f32[3,8,32,256]{3,2,1,0:T(8,128)S(1)}, f32[32,4,128]{2,1,0:T(4,128)}) custom-call(f32[3,8,32,256]{3,2,1,0:T(8,128)S(1)} %get-tuple-element.13.inside, f32[4,128]{1,0:T(4,128)S(1)} %get-tuple-element.14.moments, f32[7,32,256]{2,1,0:T(8,128)S(1)} %copy-done.3, f32[7,32,256]{2,1,0:T(8,128)S(1)} %copy-done.4, f32[7,8,256]{2,1,0:T(8,128)S(1)} %copy-done.5, ...), custom_call_target="tpu_custom_call" | custom-call | tf_op jit(solution)/shard_map/pallas_call | solution.py:312
  19.7 1.2 %all-to-all-done.load = f32[64,4,128]{2,1,0:T(4,128)S(1)} async-done(((f32[64,4,128]{2,1,0:T(4,128)}), f32[64,4,128]{2,1,0:T(4,128)S(1)}, u32[]{:S(2)}, u32[]{:S(2)}) %all-to-all-start) | async-done | bytes 131104 | tf_op jit(solution)/shard_map/all_to_all | solution.py:478
  20.8 5.4 %all-to-all-start.1 = ((f32[32,4,128]{2,1,0:T(4,128)}), f32[32,4,128]{2,1,0:T(4,128)S(1)}, u32[]{:S(2)}, u32[]{:S(2)}) async-start(f32[32,4,128]{2,1,0:T(4,128)} %get-tuple-element.21), calls=%async_computation.1 | async-start | bytes 131072 | tf_op jit(solution)/shard_map/all_to_all | solution.py:482
  26.2 2.2 %shard_map.89 = f32[3,8,32,256]{3,2,1,0:T(8,128)} custom-call(f32[3,8,32,256]{3,2,1,0:T(8,128)S(1)} %get-tuple-element.19.inside, f32[64,4,128]{2,1,0:T(4,128)S(1)} %all-to-all-done.load), custom_call_target="tpu_custom_call" | custom-call | tf_op jit(solution)/shard_map/pallas_call | solution.py:445
  28.5 5.2 %all-to-all-done.1.load = f32[32,4,128]{2,1,0:T(4,128)S(1)} async-done(((f32[32,4,128]{2,1,0:T(4,128)}), f32[32,4,128]{2,1,0:T(4,128)S(1)}, u32[]{:S(2)}, u32[]{:S(2)}) %all-to-all-start.1) | async-done | bytes 65568 | tf_op jit(solution)/shard_map/all_to_all | solution.py:482
  33.6 0.8 %shard_map.90 = f32[3,1,1,16]{3,2,1,0:T(1,128)} custom-call(f32[32,4,128]{2,1,0:T(4,128)S(1)} %all-to-all-done.1.load), custom_call_target="tpu_custom_call" | custom-call | tf_op jit(solution)/shard_map/pallas_call | solution.py:359
  (9 shorter events, 0.0 us)
Async XLA Ops:
  1.3 15.3 %copy-start = (f32[3,8,32,256]{3,2,1,0:T(8,128)S(1)}, f32[3,8,32,256]{3,2,1,0:T(8,128)}, u32[]{:S(2)}) copy-start(f32[3,8,32,256]{3,2,1,0:T(8,128)} %vort.3) | copy-start | bytes 2359300
  1.3 15.3 %copy-start.1 = (f32[3,8,32,256]{3,2,1,0:T(8,128)S(1)}, f32[3,8,32,256]{3,2,1,0:T(8,128)}, u32[]{:S(2)}) copy-start(f32[3,8,32,256]{3,2,1,0:T(8,128)} %velo.3) | copy-start | bytes 2359300
  4.0 12.5 %copy-start.2 = (f32[8,32,256]{2,1,0:T(8,128)S(1)}, f32[8,32,256]{2,1,0:T(8,128)}, u32[]{:S(2)}) copy-start(f32[8,32,256]{2,1,0:T(8,128)} %visc.3) | copy-start | bytes 786436
  4.0 14.7 %collective-permute-start = (f32[7,32,256]{2,1,0:T(8,128)}, f32[7,32,256]{2,1,0:T(8,128)S(1)}, u32[]{:S(2)}, u32[]{:S(2)}) collective-permute-start(f32[7,32,256]{2,1,0:T(8,128)} %get-tuple-element.15.near), channel_id=1, source_target_pairs={{0,4},{8,12},{16,20},{24,28},{4,0},{12,8},{20,16},{28,24},{1,5},{9... | collective-permute-start | bytes 688136 | tf_op jit(solution)/shard_map/ppermute | solution.py:462
  7.0 11.7 %collective-permute-start.1 = (f32[7,32,256]{2,1,0:T(8,128)}, f32[7,32,256]{2,1,0:T(8,128)S(1)}, u32[]{:S(2)}, u32[]{:S(2)}) collective-permute-start(f32[7,32,256]{2,1,0:T(8,128)} %get-tuple-element.16.far), channel_id=1, source_target_pairs={{4,8},{12,16},{20,24},{8,4},{16,12},{24,20},{5,9},{13,17},{21,25},... | collective-permute-start | bytes 688136 | tf_op jit(solution)/shard_map/ppermute | solution.py:462
  7.7 13.1 %all-to-all-start = ((f32[64,4,128]{2,1,0:T(4,128)}), f32[64,4,128]{2,1,0:T(4,128)S(1)}, u32[]{:S(2)}, u32[]{:S(2)}) async-start(f32[64,4,128]{2,1,0:T(4,128)} %get-tuple-element.20), calls=%async_computation | async-start | bytes 262144 | tf_op jit(solution)/shard_map/all_to_all | solution.py:478
  15.9 0.7 %copy-start.7 = (f32[4,128]{1,0:T(4,128)S(1)}, f32[4,128]{1,0:T(4,128)}, u32[]{:S(2)}) copy-start(f32[4,128]{1,0:T(4,128)} %get-tuple-element.12.tiles_in) | copy-start | bytes 6148
  15.9 2.8 %collective-permute-start.2 = (f32[7,8,256]{2,1,0:T(8,128)}, f32[7,8,256]{2,1,0:T(8,128)S(1)}, u32[]{:S(2)}, u32[]{:S(2)}) collective-permute-start(f32[7,8,256]{2,1,0:T(8,128)} %get-tuple-element.17.swap), channel_id=1, source_target_pairs={{0,1},{2,3},{1,0},{3,2},{4,5},{6,7},{5,4},{7,6},{8,9},{10,11},{9,8... | collective-permute-start | bytes 172040 | tf_op jit(solution)/shard_map/ppermute | solution.py:462
  15.9 2.8 %collective-permute-start.3 = (f32[7,8,256]{2,1,0:T(8,128)}, f32[7,8,256]{2,1,0:T(8,128)S(1)}, u32[]{:S(2)}, u32[]{:S(2)}) collective-permute-start(f32[7,8,256]{2,1,0:T(8,128)} %get-tuple-element.18.other), channel_id=1, source_target_pairs={{1,2},{2,1},{5,6},{6,5},{9,10},{10,9},{13,14},{14,13},{17,18},{18,... | collective-permute-start | bytes 172040 | tf_op jit(solution)/shard_map/ppermute | solution.py:462
  16.6 2.1 %copy-start.3 = (f32[7,32,256]{2,1,0:T(8,128)S(1)}, f32[7,32,256]{2,1,0:T(8,128)}, u32[]{:S(2)}) copy-start(f32[7,32,256]{2,1,0:T(8,128)} %get-tuple-element.15.near) | copy-start | bytes 688132
  16.6 2.1 %copy-start.4 = (f32[7,32,256]{2,1,0:T(8,128)S(1)}, f32[7,32,256]{2,1,0:T(8,128)}, u32[]{:S(2)}) copy-start(f32[7,32,256]{2,1,0:T(8,128)} %get-tuple-element.16.far) | copy-start | bytes 688132
  16.6 2.1 %copy-start.5 = (f32[7,8,256]{2,1,0:T(8,128)S(1)}, f32[7,8,256]{2,1,0:T(8,128)}, u32[]{:S(2)}) copy-start(f32[7,8,256]{2,1,0:T(8,128)} %get-tuple-element.17.swap) | copy-start | bytes 172036
  16.6 2.1 %copy-start.6 = (f32[7,8,256]{2,1,0:T(8,128)S(1)}, f32[7,8,256]{2,1,0:T(8,128)}, u32[]{:S(2)}) copy-start(f32[7,8,256]{2,1,0:T(8,128)} %get-tuple-element.18.other) | copy-start | bytes 172036
  20.8 12.8 %all-to-all-start.1 = ((f32[32,4,128]{2,1,0:T(4,128)}), f32[32,4,128]{2,1,0:T(4,128)S(1)}, u32[]{:S(2)}, u32[]{:S(2)}) async-start(f32[32,4,128]{2,1,0:T(4,128)} %get-tuple-element.21), calls=%async_computation.1 | async-start | bytes 131072 | tf_op jit(solution)/shard_map/all_to_all | solution.py:482

commit v14 on v13

--- a/solution.py
+++ b/solution.py
@@ -196,38 +196,33 @@
     cx, cy, nz = visc.shape
     has_ahead = lax.broadcasted_iota(jnp.int32, (cy, nz), 0) < cy - 1
     totals = [jnp.zeros((8, nz), jnp.float32) for _ in range(3)]
-    flux_x = [None] * 3
     for x in range(cx):
         nu = visc[x]
-        spin = [vort[c, x] for c in range(3)]
-        mean_y = jnp.where(has_ahead, 0.5 * (nu + ahead(nu, 0)), 0.0)
-        mean_z = 0.5 * (nu + ahead(nu, 1))
-        half_y = 0.5 * spin[1]
-        half_z = 0.5 * spin[2]
-        next_y = jnp.where(has_ahead, ahead(half_y, 0), 0.0)
-        next_z = ahead(half_z, 1)
-        half_y = jnp.where(has_ahead, half_y, 0.0)
-        half_x = 0.5 * spin[0]
-        if x < cx - 1:
-            mean_x = 0.5 * (nu + visc[x + 1])
+        half = 0.5 * vort[1, x]
+        mean = jnp.where(has_ahead, 0.5 * (nu + ahead(nu, 0)), 0.0)
+        shifted = jnp.where(has_ahead, ahead(half, 0), 0.0)
+        half = jnp.where(has_ahead, half, 0.0)
         for c in range(3):
-            w = spin[c]
-            u = velo[c, x]
-            flux_y = mean_y * (ahead(w, 0) - w)
-            flux_z = mean_z * (ahead(w, 1) - w)
-            change = flux_y + half_y * ahead(u, 0) - behind(flux_y + next_y * u, 0)
-            change = change + (flux_z + half_z * ahead(u, 1) - behind(flux_z + next_z * u, 1))
-            if x == 0:
-                change = change + half_x * velo[c, x + 1]
-            elif x == cx - 1:
-                change = change - half_x * velo[c, x - 1]
-            else:
-                change = change + half_x * (velo[c, x + 1] - velo[c, x - 1])
+            w, u = vort[c, x], velo[c, x]
+            flux = mean * (ahead(w, 0) - w)
+            out[c, x] = flux + half * ahead(u, 0) - behind(flux + shifted * u, 0)
+        half = 0.5 * vort[2, x]
+        mean = 0.5 * (nu + ahead(nu, 1))
+        shifted = ahead(half, 1)
+        for c in range(3):
+            w, u = vort[c, x], velo[c, x]
+            flux = mean * (ahead(w, 1) - w)
+            out[c, x] = out[c, x] + (flux + half * ahead(u, 1) - behind(flux + shifted * u, 1))
+        half = 0.5 * vort[0, x]
+        for c in range(3):
+            w = vort[c, x]
+            change = out[c, x]
+            if x < cx - 1:
+                mean = 0.5 * (nu + visc[x + 1])
+                change = change + half * velo[c, x + 1] + mean * (vort[c, x + 1] - w)
             if x > 0:
-                change = change - flux_x[c]
-            if x < cx - 1:
-                flux_x[c] = mean_x * (vort[c, x + 1] - w)
-                change = change + flux_x[c]
+                mean = 0.5 * (nu + visc[x - 1])
+                change = change - half * velo[c, x - 1] + mean * (vort[c, x - 1] - w)
             new = w + TIME_STEP * change
             out[c, x] = new
             totals[c] = totals[c] + jnp.sum(new.reshape(cy // 8, 8, nz), axis=0)

time: 34.8 us -> 34.8 us (level)
  waiting for transfers between devices: 6.35 us -> 5.48 us
  Pallas kernels: 8.68 us -> 9.54 us
    pallas_call x1, Pallas kernels: 2.21 us -> 3.01 us  [deposit(): pl.pallas_call(functools.partial(deposit_kernel, cap), out_shape=shaped(*...]
    all_to_all x1, waiting for transfers between devices: 5.17 us -> 4.37 us  [per_device(): lax.all_to_all(load, ('slab', 'pencil'), 0, 0, axis_index_groups=[everyon...]
  transfers between devices with their start and end apart: 6 -> 6, of which waited for: 2 -> 2; matrix products, arithmetic and copies ran while one was open for 0% -> 0% of each run, Pallas kernels for 15% -> 18%
where the time goes in v14:
time: 34.8 us; the launch traced here: 34.4 us
  starting transfers between devices  17.9 us (51%)
  Pallas kernels  9.54 us (27%)
  waiting for transfers between devices  5.48 us (16%)
  between operations  1.49 us (4%)
    all_to_all x1, starting transfers between devices, per_device(): lax.all_to_all(packets, 'slab', 0, 0, axis_index_groups=[order], tiled=True)  8.15 us
    all_to_all x1, starting transfers between devices, per_device(): lax.all_to_all(load, ('slab', 'pencil'), 0, 0, axis_index_groups=[everyon...  5.39 us
    all_to_all x1, waiting for transfers between devices, per_device(): lax.all_to_all(load, ('slab', 'pencil'), 0, 0, axis_index_groups=[everyon...  4.37 us
    ppermute x4, starting transfers between devices, swapped(): return lax.ppermute(array, axis, up + [(j, i) for i, j in up])  4.33 us
    pallas_call x1, Pallas kernels, deposit(): pl.pallas_call(functools.partial(deposit_kernel, cap), out_shape=shaped(*...  3.01 us
    pallas_call x1, Pallas kernels, to_send(): pl.pallas_call(functools.partial(send_kernel, cap), out_shape=made, in_sp...  2.71 us
    pallas_call x1, Pallas kernels, inner(): pl.pallas_call(inner_kernel, out_shape=(shaped(*vort.shape), shaped(*tile...  2.11 us
    all_to_all x1, waiting for transfers between devices, per_device(): lax.all_to_all(packets, 'slab', 0, 0, axis_index_groups=[order], tiled=True)  1.1 us
  transfers between devices with their start and end apart: 6, of which 2 were waited for; matrix products, arithmetic and copies ran while one was open for 0% of the time, Pallas kernels for 18%

profile of v14, /device:TPU:0, one launch (start us, length us, event | category | flops | bytes accessed | tf_op | source)
XLA Modules:
  0.0 34.4 jit_solution(9106988517037503426)
XLA Ops:
  1.3 2.7 %shard_map.86 = (f32[7,32,256]{2,1,0:T(8,128)}, f32[7,32,256]{2,1,0:T(8,128)}, f32[7,8,256]{2,1,0:T(8,128)}, f32[7,8,256]{2,1,0:T(8,128)}, f32[64,4,128]{2,1,0:T(4,128)}, /*index=5*/f32[4,128]{1,0:T(4,128)}) custom-call(f32[3,8,32,256]{3,2,1,0:T(8,128)} %vort.3, f32[3,8,32,256]{3,2,1,0:T(8,128)} %velo.3, f32[8,32,256]{2,1,0:T(8,128)} %visc.3, ...), custom_call_target="tpu_custom_call" | custom-call | tf_op jit(solution)/shard_map/pallas_call | solution.py:170
  4.0 0.0 copy-start.2
  4.0 3.0 %collective-permute-start = (f32[7,32,256]{2,1,0:T(8,128)}, f32[7,32,256]{2,1,0:T(8,128)S(1)}, u32[]{:S(2)}, u32[]{:S(2)}) collective-permute-start(f32[7,32,256]{2,1,0:T(8,128)} %get-tuple-element.15.near), channel_id=1, source_target_pairs={{0,4},{8,12},{16,20},{24,28},{4,0},{12,8},{20,16},{28,24},{1,5},{9... | collective-permute-start | bytes 688136 | tf_op jit(solution)/shard_map/ppermute | solution.py:457
  7.0 0.7 %collective-permute-start.1 = (f32[7,32,256]{2,1,0:T(8,128)}, f32[7,32,256]{2,1,0:T(8,128)S(1)}, u32[]{:S(2)}, u32[]{:S(2)}) collective-permute-start(f32[7,32,256]{2,1,0:T(8,128)} %get-tuple-element.16.far), channel_id=1, source_target_pairs={{4,8},{12,16},{20,24},{8,4},{16,12},{24,20},{5,9},{13,17},{21,25},... | collective-permute-start | bytes 688136 | tf_op jit(solution)/shard_map/ppermute | solution.py:457
  7.7 8.1 %all-to-all-start = ((f32[64,4,128]{2,1,0:T(4,128)}), f32[64,4,128]{2,1,0:T(4,128)S(1)}, u32[]{:S(2)}, u32[]{:S(2)}) async-start(f32[64,4,128]{2,1,0:T(4,128)} %get-tuple-element.20), calls=%async_computation | async-start | bytes 262144 | tf_op jit(solution)/shard_map/all_to_all | solution.py:473
  15.9 0.0 collective-permute-start.2
  15.9 0.7 %collective-permute-start.3 = (f32[7,8,256]{2,1,0:T(8,128)}, f32[7,8,256]{2,1,0:T(8,128)S(1)}, u32[]{:S(2)}, u32[]{:S(2)}) collective-permute-start(f32[7,8,256]{2,1,0:T(8,128)} %get-tuple-element.18.other), channel_id=1, source_target_pairs={{1,2},{2,1},{5,6},{6,5},{9,10},{10,9},{13,14},{14,13},{17,18},{18,... | collective-permute-start | bytes 172040 | tf_op jit(solution)/shard_map/ppermute | solution.py:457
  16.5 0.0 copy-done
  16.5 0.0 copy-done.1
  16.6 0.0 copy-done.2
  16.6 0.0 copy-done.7
  16.6 0.0 copy-start.3
  16.6 2.1 %shard_map.87 = (f32[3,8,32,256]{3,2,1,0:T(8,128)S(1)}, f32[4,128]{1,0:T(4,128)S(1)}) custom-call(f32[3,8,32,256]{3,2,1,0:T(8,128)S(1)} %copy-done, f32[3,8,32,256]{3,2,1,0:T(8,128)S(1)} %copy-done.1, f32[8,32,256]{2,1,0:T(8,128)S(1)} %copy-done.2, f32[4,128]{1,0:T(4,128)S(1)} %copy-done.7), custom_call_target="tpu_custom_call" | custom-call | tf_op jit(solution)/shard_map/pallas_call | solution.py:252
  18.7 0.0 collective-permute-done.2.swap_in
  18.7 0.0 collective-permute-done.3.other_in
  18.8 0.0 collective-permute-done.near_in
  18.8 0.0 collective-permute-done.1.far_in
  18.8 0.0 copy-done.3
  18.8 0.9 %shard_map.88 = (f32[3,8,32,256]{3,2,1,0:T(8,128)S(1)}, f32[32,4,128]{2,1,0:T(4,128)}) custom-call(f32[3,8,32,256]{3,2,1,0:T(8,128)S(1)} %get-tuple-element.13.inside, f32[4,128]{1,0:T(4,128)S(1)} %get-tuple-element.14.moments, f32[7,32,256]{2,1,0:T(8,128)S(1)} %copy-done.3, f32[7,32,256]{2,1,0:T(8,128)S(1)} %copy-done.4, f32[7,8,256]{2,1,0:T(8,128)S(1)} %copy-done.5, ...), custom_call_target="tpu_custom_call" | custom-call | tf_op jit(solution)/shard_map/pallas_call | solution.py:307
  19.7 1.1 %all-to-all-done.load = f32[64,4,128]{2,1,0:T(4,128)S(1)} async-done(((f32[64,4,128]{2,1,0:T(4,128)}), f32[64,4,128]{2,1,0:T(4,128)S(1)}, u32[]{:S(2)}, u32[]{:S(2)}) %all-to-all-start) | async-done | bytes 131104 | tf_op jit(solution)/shard_map/all_to_all | solution.py:473
  20.8 5.4 %all-to-all-start.1 = ((f32[32,4,128]{2,1,0:T(4,128)}), f32[32,4,128]{2,1,0:T(4,128)S(1)}, u32[]{:S(2)}, u32[]{:S(2)}) async-start(f32[32,4,128]{2,1,0:T(4,128)} %get-tuple-element.21), calls=%async_computation.1 | async-start | bytes 131072 | tf_op jit(solution)/shard_map/all_to_all | solution.py:477
  26.2 3.0 %shard_map.89 = f32[3,8,32,256]{3,2,1,0:T(8,128)} custom-call(f32[3,8,32,256]{3,2,1,0:T(8,128)S(1)} %get-tuple-element.19.inside, f32[64,4,128]{2,1,0:T(4,128)S(1)} %all-to-all-done.load), custom_call_target="tpu_custom_call" | custom-call | tf_op jit(solution)/shard_map/pallas_call | solution.py:440
  29.2 4.4 %all-to-all-done.1.load = f32[32,4,128]{2,1,0:T(4,128)S(1)} async-done(((f32[32,4,128]{2,1,0:T(4,128)}), f32[32,4,128]{2,1,0:T(4,128)S(1)}, u32[]{:S(2)}, u32[]{:S(2)}) %all-to-all-start.1) | async-done | bytes 65568 | tf_op jit(solution)/shard_map/all_to_all | solution.py:477
  33.6 0.8 %shard_map.90 = f32[3,1,1,16]{3,2,1,0:T(1,128)} custom-call(f32[32,4,128]{2,1,0:T(4,128)S(1)} %all-to-all-done.1.load), custom_call_target="tpu_custom_call" | custom-call | tf_op jit(solution)/shard_map/pallas_call | solution.py:354
  (9 shorter events, 0.0 us)
Async XLA Ops:
  1.3 15.3 %copy-start = (f32[3,8,32,256]{3,2,1,0:T(8,128)S(1)}, f32[3,8,32,256]{3,2,1,0:T(8,128)}, u32[]{:S(2)}) copy-start(f32[3,8,32,256]{3,2,1,0:T(8,128)} %vort.3) | copy-start | bytes 2359300
  1.3 15.3 %copy-start.1 = (f32[3,8,32,256]{3,2,1,0:T(8,128)S(1)}, f32[3,8,32,256]{3,2,1,0:T(8,128)}, u32[]{:S(2)}) copy-start(f32[3,8,32,256]{3,2,1,0:T(8,128)} %velo.3) | copy-start | bytes 2359300
  4.0 12.5 %copy-start.2 = (f32[8,32,256]{2,1,0:T(8,128)S(1)}, f32[8,32,256]{2,1,0:T(8,128)}, u32[]{:S(2)}) copy-start(f32[8,32,256]{2,1,0:T(8,128)} %visc.3) | copy-start | bytes 786436
  4.0 14.7 %collective-permute-start = (f32[7,32,256]{2,1,0:T(8,128)}, f32[7,32,256]{2,1,0:T(8,128)S(1)}, u32[]{:S(2)}, u32[]{:S(2)}) collective-permute-start(f32[7,32,256]{2,1,0:T(8,128)} %get-tuple-element.15.near), channel_id=1, source_target_pairs={{0,4},{8,12},{16,20},{24,28},{4,0},{12,8},{20,16},{28,24},{1,5},{9... | collective-permute-start | bytes 688136 | tf_op jit(solution)/shard_map/ppermute | solution.py:457
  7.0 11.7 %collective-permute-start.1 = (f32[7,32,256]{2,1,0:T(8,128)}, f32[7,32,256]{2,1,0:T(8,128)S(1)}, u32[]{:S(2)}, u32[]{:S(2)}) collective-permute-start(f32[7,32,256]{2,1,0:T(8,128)} %get-tuple-element.16.far), channel_id=1, source_target_pairs={{4,8},{12,16},{20,24},{8,4},{16,12},{24,20},{5,9},{13,17},{21,25},... | collective-permute-start | bytes 688136 | tf_op jit(solution)/shard_map/ppermute | solution.py:457
  7.7 13.1 %all-to-all-start = ((f32[64,4,128]{2,1,0:T(4,128)}), f32[64,4,128]{2,1,0:T(4,128)S(1)}, u32[]{:S(2)}, u32[]{:S(2)}) async-start(f32[64,4,128]{2,1,0:T(4,128)} %get-tuple-element.20), calls=%async_computation | async-start | bytes 262144 | tf_op jit(solution)/shard_map/all_to_all | solution.py:473
  15.9 0.7 %copy-start.7 = (f32[4,128]{1,0:T(4,128)S(1)}, f32[4,128]{1,0:T(4,128)}, u32[]{:S(2)}) copy-start(f32[4,128]{1,0:T(4,128)} %get-tuple-element.12.tiles_in) | copy-start | bytes 6148
  15.9 2.9 %collective-permute-start.2 = (f32[7,8,256]{2,1,0:T(8,128)}, f32[7,8,256]{2,1,0:T(8,128)S(1)}, u32[]{:S(2)}, u32[]{:S(2)}) collective-permute-start(f32[7,8,256]{2,1,0:T(8,128)} %get-tuple-element.17.swap), channel_id=1, source_target_pairs={{0,1},{2,3},{1,0},{3,2},{4,5},{6,7},{5,4},{7,6},{8,9},{10,11},{9,8... | collective-permute-start | bytes 172040 | tf_op jit(solution)/shard_map/ppermute | solution.py:457
  15.9 2.9 %collective-permute-start.3 = (f32[7,8,256]{2,1,0:T(8,128)}, f32[7,8,256]{2,1,0:T(8,128)S(1)}, u32[]{:S(2)}, u32[]{:S(2)}) collective-permute-start(f32[7,8,256]{2,1,0:T(8,128)} %get-tuple-element.18.other), channel_id=1, source_target_pairs={{1,2},{2,1},{5,6},{6,5},{9,10},{10,9},{13,14},{14,13},{17,18},{18,... | collective-permute-start | bytes 172040 | tf_op jit(solution)/shard_map/ppermute | solution.py:457
  16.6 2.2 %copy-start.3 = (f32[7,32,256]{2,1,0:T(8,128)S(1)}, f32[7,32,256]{2,1,0:T(8,128)}, u32[]{:S(2)}) copy-start(f32[7,32,256]{2,1,0:T(8,128)} %get-tuple-element.15.near) | copy-start | bytes 688132
  16.6 2.2 %copy-start.4 = (f32[7,32,256]{2,1,0:T(8,128)S(1)}, f32[7,32,256]{2,1,0:T(8,128)}, u32[]{:S(2)}) copy-start(f32[7,32,256]{2,1,0:T(8,128)} %get-tuple-element.16.far) | copy-start | bytes 688132
  16.6 2.2 %copy-start.5 = (f32[7,8,256]{2,1,0:T(8,128)S(1)}, f32[7,8,256]{2,1,0:T(8,128)}, u32[]{:S(2)}) copy-start(f32[7,8,256]{2,1,0:T(8,128)} %get-tuple-element.17.swap) | copy-start | bytes 172036
  16.6 2.2 %copy-start.6 = (f32[7,8,256]{2,1,0:T(8,128)S(1)}, f32[7,8,256]{2,1,0:T(8,128)}, u32[]{:S(2)}) copy-start(f32[7,8,256]{2,1,0:T(8,128)} %get-tuple-element.18.other) | copy-start | bytes 172036
  20.8 12.8 %all-to-all-start.1 = ((f32[32,4,128]{2,1,0:T(4,128)}), f32[32,4,128]{2,1,0:T(4,128)S(1)}, u32[]{:S(2)}, u32[]{:S(2)}) async-start(f32[32,4,128]{2,1,0:T(4,128)} %get-tuple-element.21), calls=%async_computation.1 | async-start | bytes 131072 | tf_op jit(solution)/shard_map/all_to_all | solution.py:477

commit v15 on v13

--- a/solution.py
+++ b/solution.py
@@ -348,11 +348,16 @@
         turned[0] = turned[0] + weight * (rel_z * second - rel_y * third)
         turned[1] = turned[1] + weight * (rel_x * third - rel_z * first)
         turned[2] = turned[2] + weight * (rel_y * first - rel_x * second)
-    pieces = jnp.concatenate(thirds(jnp.concatenate(turned, axis=0)), axis=1)
-    ones = jnp.ones((16, pieces.shape[1]), jnp.bfloat16)
-    rows = lax.dot_general(ones, pieces, (((1,), (1,)), ((), ())), preferred_element_type=jnp.float32)
+    ones = jnp.ones((8, shape[1]), jnp.float32)
     for c in range(3):
-        out[c, 0] = rows[0:1, c * ncl : (c + 1) * ncl]
+        row = lax.dot_general(
+            ones,
+            turned[c],
+            (((1,), (1,)), ((), ())),
+            precision=lax.Precision.HIGHEST,
+            preferred_element_type=jnp.float32,
+        )
+        out[c, 0] = row[0:1]
 
 
 def far(load, cx, cy, ncl, n_pencil):
@@ -401,13 +406,14 @@
         (((1,), (1,)), ((), ())),
         preferred_element_type=jnp.float32,
     )
-    acc[...] += added[: 3 * rows] + added[3 * rows :]
-
-
-def deposit_kernel(cap, inside, load, out, acc, order, made, sems):
+    acc[...] += (added[: 3 * rows] + added[3 * rows :]).reshape(acc.shape)
+
+
+def deposit_kernel(cap, inside, load, out, acc, order, sems):
     _, cx, cy, nz = out.shape
     shape = (cx, cy, nz)
-    acc[...] = jnp.zeros_like(acc)
+    for h in range(2):
+        acc[:, :, :, h * nz : (h + 1) * nz] = inside[:, h * (cx // 2) : (h + 1) * (cx // 2)]
     listed = jnp.int32(0)
     for d in range(load.shape[0] // cap):
         first = d * cap
@@ -431,13 +437,10 @@
         deposit_step(GROUP // 2, whole * GROUP, listed, load, order, acc, shape)
 
     copies = Copies(sems)
-    rows = cx * cy // 2
     for c in range(3):
         for h in range(2):
-            span = slice(h * (cx // 2), (h + 1) * (cx // 2))
-            change = acc[c * rows : (c + 1) * rows, h * nz : (h + 1) * nz].reshape(cx // 2, cy, nz)
-            made[c, span] = inside[c, span] + change
-            copies.start(made.at[c, span], out.at[c, span])
+            part = acc.at[c, :, :, h * nz : (h + 1) * nz]
+            copies.start(part, out.at[c, h * (cx // 2) : (h + 1) * (cx // 2)])
     copies.wait(0, 6)
 
 
@@ -448,9 +451,8 @@
         in_specs=[VMEM] * 2,
         out_specs=ANY,
         scratch_shapes=[
-            pltpu.VMEM((3 * inside.shape[1] * inside.shape[2] // 2, 2 * inside.shape[3]), jnp.float32),
+            pltpu.VMEM((3, inside.shape[1] // 2, inside.shape[2], 2 * inside.shape[3]), jnp.float32),
             pltpu.SMEM((load.shape[0] + max(cap, GROUP),), jnp.int32),
-            pltpu.VMEM(inside.shape, jnp.float32),
             pltpu.SemaphoreType.DMA((6,)),
         ],
         compiler_params=PARAMS,

time: 34.8 us -> 34.7 us (level)
  waiting for transfers between devices: 6.35 us -> 5.55 us
  Pallas kernels: 8.68 us -> 9.42 us
    all_to_all x1, waiting for transfers between devices: 5.17 us -> 4.38 us  [per_device(): lax.all_to_all(load, ('slab', 'pencil'), 0, 0, axis_index_groups=[everyon...]
    pallas_call x1, Pallas kernels: 2.21 us -> 3 us  [deposit(): pl.pallas_call(functools.partial(deposit_kernel, cap), out_shape=shaped(*...]
  transfers between devices with their start and end apart: 6 -> 6, of which waited for: 2 -> 2; matrix products, arithmetic and copies ran while one was open for 0% -> 0% of each run, Pallas kernels for 15% -> 17%
where the time goes in v15:
time: 34.7 us; the launch traced here: 34.4 us
  starting transfers between devices  17.9 us (52%)
  Pallas kernels  9.42 us (27%)
  waiting for transfers between devices  5.55 us (16%)
  between operations  1.49 us (4%)
    all_to_all x1, starting transfers between devices, per_device(): lax.all_to_all(packets, 'slab', 0, 0, axis_index_groups=[order], tiled=True)  8.15 us
    all_to_all x1, starting transfers between devices, per_device(): lax.all_to_all(load, ('slab', 'pencil'), 0, 0, axis_index_groups=[everyon...  5.39 us
    all_to_all x1, waiting for transfers between devices, per_device(): lax.all_to_all(load, ('slab', 'pencil'), 0, 0, axis_index_groups=[everyon...  4.38 us
    ppermute x4, starting transfers between devices, swapped(): return lax.ppermute(array, axis, up + [(j, i) for i, j in up])  4.33 us
    pallas_call x1, Pallas kernels, deposit(): pl.pallas_call(functools.partial(deposit_kernel, cap), out_shape=shaped(*...  3 us
    pallas_call x1, Pallas kernels, to_send(): pl.pallas_call(functools.partial(send_kernel, cap), out_shape=made, in_sp...  2.71 us
    pallas_call x1, Pallas kernels, inner(): pl.pallas_call(inner_kernel, out_shape=(shaped(*vort.shape), shaped(*tile...  2.05 us
    all_to_all x1, waiting for transfers between devices, per_device(): lax.all_to_all(packets, 'slab', 0, 0, axis_index_groups=[order], tiled=True)  1.17 us
  transfers between devices with their start and end apart: 6, of which 2 were waited for; matrix products, arithmetic and copies ran while one was open for 0% of the time, Pallas kernels for 17%

profile of v15, /device:TPU:0, one launch (start us, length us, event | category | flops | bytes accessed | tf_op | source)
XLA Modules:
  0.0 34.4 jit_solution(4605460110518479774)
XLA Ops:
  1.3 0.0 copy-start
  1.3 0.0 copy-start.1
  1.3 2.7 %shard_map.86 = (f32[7,32,256]{2,1,0:T(8,128)}, f32[7,32,256]{2,1,0:T(8,128)}, f32[7,8,256]{2,1,0:T(8,128)}, f32[7,8,256]{2,1,0:T(8,128)}, f32[64,4,128]{2,1,0:T(4,128)}, /*index=5*/f32[4,128]{1,0:T(4,128)}) custom-call(f32[3,8,32,256]{3,2,1,0:T(8,128)} %vort.3, f32[3,8,32,256]{3,2,1,0:T(8,128)} %velo.3, f32[8,32,256]{2,1,0:T(8,128)} %visc.3, ...), custom_call_target="tpu_custom_call" | custom-call | tf_op jit(solution)/shard_map/pallas_call | solution.py:170
  4.0 0.0 copy-start.2
  4.0 3.0 %collective-permute-start = (f32[7,32,256]{2,1,0:T(8,128)}, f32[7,32,256]{2,1,0:T(8,128)S(1)}, u32[]{:S(2)}, u32[]{:S(2)}) collective-permute-start(f32[7,32,256]{2,1,0:T(8,128)} %get-tuple-element.15.near), channel_id=1, source_target_pairs={{0,4},{8,12},{16,20},{24,28},{4,0},{12,8},{20,16},{28,24},{1,5},{9... | collective-permute-start | bytes 688136 | tf_op jit(solution)/shard_map/ppermute | solution.py:464
  7.0 0.7 %collective-permute-start.1 = (f32[7,32,256]{2,1,0:T(8,128)}, f32[7,32,256]{2,1,0:T(8,128)S(1)}, u32[]{:S(2)}, u32[]{:S(2)}) collective-permute-start(f32[7,32,256]{2,1,0:T(8,128)} %get-tuple-element.16.far), channel_id=1, source_target_pairs={{4,8},{12,16},{20,24},{8,4},{16,12},{24,20},{5,9},{13,17},{21,25},... | collective-permute-start | bytes 688136 | tf_op jit(solution)/shard_map/ppermute | solution.py:464
  7.7 8.1 %all-to-all-start = ((f32[64,4,128]{2,1,0:T(4,128)}), f32[64,4,128]{2,1,0:T(4,128)S(1)}, u32[]{:S(2)}, u32[]{:S(2)}) async-start(f32[64,4,128]{2,1,0:T(4,128)} %get-tuple-element.20), calls=%async_computation | async-start | bytes 262144 | tf_op jit(solution)/shard_map/all_to_all | solution.py:480
  15.9 0.0 collective-permute-start.2
  15.9 0.7 %collective-permute-start.3 = (f32[7,8,256]{2,1,0:T(8,128)}, f32[7,8,256]{2,1,0:T(8,128)S(1)}, u32[]{:S(2)}, u32[]{:S(2)}) collective-permute-start(f32[7,8,256]{2,1,0:T(8,128)} %get-tuple-element.18.other), channel_id=1, source_target_pairs={{1,2},{2,1},{5,6},{6,5},{9,10},{10,9},{13,14},{14,13},{17,18},{18,... | collective-permute-start | bytes 172040 | tf_op jit(solution)/shard_map/ppermute | solution.py:464
  16.5 0.0 copy-done
  16.5 0.0 copy-done.1
  16.6 0.0 copy-done.2
  16.6 0.0 copy-start.3
  16.6 2.0 %shard_map.87 = (f32[3,8,32,256]{3,2,1,0:T(8,128)S(1)}, f32[4,128]{1,0:T(4,128)S(1)}) custom-call(f32[3,8,32,256]{3,2,1,0:T(8,128)S(1)} %copy-done, f32[3,8,32,256]{3,2,1,0:T(8,128)S(1)} %copy-done.1, f32[8,32,256]{2,1,0:T(8,128)S(1)} %copy-done.2, f32[4,128]{1,0:T(4,128)S(1)} %copy-done.7), custom_call_target="tpu_custom_call" | custom-call | tf_op jit(solution)/shard_map/pallas_call | solution.py:257
  18.7 0.0 collective-permute-done.2.swap_in
  18.7 0.0 collective-permute-done.3.other_in
  18.7 0.0 collective-permute-done.near_in
  18.7 0.0 collective-permute-done.1.far_in
  18.8 0.9 %shard_map.88 = (f32[3,8,32,256]{3,2,1,0:T(8,128)S(1)}, f32[32,4,128]{2,1,0:T(4,128)}) custom-call(f32[3,8,32,256]{3,2,1,0:T(8,128)S(1)} %get-tuple-element.13.inside, f32[4,128]{1,0:T(4,128)S(1)} %get-tuple-element.14.moments, f32[7,32,256]{2,1,0:T(8,128)S(1)} %copy-done.3, f32[7,32,256]{2,1,0:T(8,128)S(1)} %copy-done.4, f32[7,8,256]{2,1,0:T(8,128)S(1)} %copy-done.5, ...), custom_call_target="tpu_custom_call" | custom-call | tf_op jit(solution)/shard_map/pallas_call | solution.py:312
  19.7 1.2 %all-to-all-done.load = f32[64,4,128]{2,1,0:T(4,128)S(1)} async-done(((f32[64,4,128]{2,1,0:T(4,128)}), f32[64,4,128]{2,1,0:T(4,128)S(1)}, u32[]{:S(2)}, u32[]{:S(2)}) %all-to-all-start) | async-done | bytes 131104 | tf_op jit(solution)/shard_map/all_to_all | solution.py:480
  20.8 5.4 %all-to-all-start.1 = ((f32[32,4,128]{2,1,0:T(4,128)}), f32[32,4,128]{2,1,0:T(4,128)S(1)}, u32[]{:S(2)}, u32[]{:S(2)}) async-start(f32[32,4,128]{2,1,0:T(4,128)} %get-tuple-element.21), calls=%async_computation.1 | async-start | bytes 131072 | tf_op jit(solution)/shard_map/all_to_all | solution.py:484
  26.2 3.0 %shard_map.89 = f32[3,8,32,256]{3,2,1,0:T(8,128)} custom-call(f32[3,8,32,256]{3,2,1,0:T(8,128)S(1)} %get-tuple-element.19.inside, f32[64,4,128]{2,1,0:T(4,128)S(1)} %all-to-all-done.load), custom_call_target="tpu_custom_call" | custom-call | tf_op jit(solution)/shard_map/pallas_call | solution.py:448
  29.2 4.4 %all-to-all-done.1.load = f32[32,4,128]{2,1,0:T(4,128)S(1)} async-done(((f32[32,4,128]{2,1,0:T(4,128)}), f32[32,4,128]{2,1,0:T(4,128)S(1)}, u32[]{:S(2)}, u32[]{:S(2)}) %all-to-all-start.1) | async-done | bytes 65568 | tf_op jit(solution)/shard_map/all_to_all | solution.py:484
  33.6 0.7 %shard_map.90 = f32[3,1,1,16]{3,2,1,0:T(1,128)} custom-call(f32[32,4,128]{2,1,0:T(4,128)S(1)} %all-to-all-done.1.load), custom_call_target="tpu_custom_call" | custom-call | tf_op jit(solution)/shard_map/pallas_call | solution.py:364
  (9 shorter events, 0.0 us)
Async XLA Ops:
  1.3 15.3 %copy-start = (f32[3,8,32,256]{3,2,1,0:T(8,128)S(1)}, f32[3,8,32,256]{3,2,1,0:T(8,128)}, u32[]{:S(2)}) copy-start(f32[3,8,32,256]{3,2,1,0:T(8,128)} %vort.3) | copy-start | bytes 2359300
  1.3 15.3 %copy-start.1 = (f32[3,8,32,256]{3,2,1,0:T(8,128)S(1)}, f32[3,8,32,256]{3,2,1,0:T(8,128)}, u32[]{:S(2)}) copy-start(f32[3,8,32,256]{3,2,1,0:T(8,128)} %velo.3) | copy-start | bytes 2359300
  4.0 12.5 %copy-start.2 = (f32[8,32,256]{2,1,0:T(8,128)S(1)}, f32[8,32,256]{2,1,0:T(8,128)}, u32[]{:S(2)}) copy-start(f32[8,32,256]{2,1,0:T(8,128)} %visc.3) | copy-start | bytes 786436
  4.0 14.7 %collective-permute-start = (f32[7,32,256]{2,1,0:T(8,128)}, f32[7,32,256]{2,1,0:T(8,128)S(1)}, u32[]{:S(2)}, u32[]{:S(2)}) collective-permute-start(f32[7,32,256]{2,1,0:T(8,128)} %get-tuple-element.15.near), channel_id=1, source_target_pairs={{0,4},{8,12},{16,20},{24,28},{4,0},{12,8},{20,16},{28,24},{1,5},{9... | collective-permute-start | bytes 688136 | tf_op jit(solution)/shard_map/ppermute | solution.py:464
  7.0 11.7 %collective-permute-start.1 = (f32[7,32,256]{2,1,0:T(8,128)}, f32[7,32,256]{2,1,0:T(8,128)S(1)}, u32[]{:S(2)}, u32[]{:S(2)}) collective-permute-start(f32[7,32,256]{2,1,0:T(8,128)} %get-tuple-element.16.far), channel_id=1, source_target_pairs={{4,8},{12,16},{20,24},{8,4},{16,12},{24,20},{5,9},{13,17},{21,25},... | collective-permute-start | bytes 688136 | tf_op jit(solution)/shard_map/ppermute | solution.py:464
  7.7 13.1 %all-to-all-start = ((f32[64,4,128]{2,1,0:T(4,128)}), f32[64,4,128]{2,1,0:T(4,128)S(1)}, u32[]{:S(2)}, u32[]{:S(2)}) async-start(f32[64,4,128]{2,1,0:T(4,128)} %get-tuple-element.20), calls=%async_computation | async-start | bytes 262144 | tf_op jit(solution)/shard_map/all_to_all | solution.py:480
  15.9 0.7 %copy-start.7 = (f32[4,128]{1,0:T(4,128)S(1)}, f32[4,128]{1,0:T(4,128)}, u32[]{:S(2)}) copy-start(f32[4,128]{1,0:T(4,128)} %get-tuple-element.12.tiles_in) | copy-start | bytes 6148
  15.9 2.8 %collective-permute-start.2 = (f32[7,8,256]{2,1,0:T(8,128)}, f32[7,8,256]{2,1,0:T(8,128)S(1)}, u32[]{:S(2)}, u32[]{:S(2)}) collective-permute-start(f32[7,8,256]{2,1,0:T(8,128)} %get-tuple-element.17.swap), channel_id=1, source_target_pairs={{0,1},{2,3},{1,0},{3,2},{4,5},{6,7},{5,4},{7,6},{8,9},{10,11},{9,8... | collective-permute-start | bytes 172040 | tf_op jit(solution)/shard_map/ppermute | solution.py:464
  15.9 2.8 %collective-permute-start.3 = (f32[7,8,256]{2,1,0:T(8,128)}, f32[7,8,256]{2,1,0:T(8,128)S(1)}, u32[]{:S(2)}, u32[]{:S(2)}) collective-permute-start(f32[7,8,256]{2,1,0:T(8,128)} %get-tuple-element.18.other), channel_id=1, source_target_pairs={{1,2},{2,1},{5,6},{6,5},{9,10},{10,9},{13,14},{14,13},{17,18},{18,... | collective-permute-start | bytes 172040 | tf_op jit(solution)/shard_map/ppermute | solution.py:464
  16.6 2.1 %copy-start.3 = (f32[7,32,256]{2,1,0:T(8,128)S(1)}, f32[7,32,256]{2,1,0:T(8,128)}, u32[]{:S(2)}) copy-start(f32[7,32,256]{2,1,0:T(8,128)} %get-tuple-element.15.near) | copy-start | bytes 688132
  16.6 2.1 %copy-start.4 = (f32[7,32,256]{2,1,0:T(8,128)S(1)}, f32[7,32,256]{2,1,0:T(8,128)}, u32[]{:S(2)}) copy-start(f32[7,32,256]{2,1,0:T(8,128)} %get-tuple-element.16.far) | copy-start | bytes 688132
  16.6 2.1 %copy-start.5 = (f32[7,8,256]{2,1,0:T(8,128)S(1)}, f32[7,8,256]{2,1,0:T(8,128)}, u32[]{:S(2)}) copy-start(f32[7,8,256]{2,1,0:T(8,128)} %get-tuple-element.17.swap) | copy-start | bytes 172036
  16.6 2.1 %copy-start.6 = (f32[7,8,256]{2,1,0:T(8,128)S(1)}, f32[7,8,256]{2,1,0:T(8,128)}, u32[]{:S(2)}) copy-start(f32[7,8,256]{2,1,0:T(8,128)} %get-tuple-element.18.other) | copy-start | bytes 172036
  20.8 12.8 %all-to-all-start.1 = ((f32[32,4,128]{2,1,0:T(4,128)}), f32[32,4,128]{2,1,0:T(4,128)S(1)}, u32[]{:S(2)}, u32[]{:S(2)}) async-start(f32[32,4,128]{2,1,0:T(4,128)} %get-tuple-element.21), calls=%async_computation.1 | async-start | bytes 131072 | tf_op jit(solution)/shard_map/all_to_all | solution.py:484

commit v16 on v15

--- a/solution.py
+++ b/solution.py
@@ -38,7 +38,7 @@
 
 def outward(count):
     half = count // 2
-    return [half - 1 - k // 2 if k % 2 else half + k // 2 for k in range(count)]
+    return [(half + (k + 1) // 2) % count if k % 2 else half - k // 2 for k in range(count)]
 
 
 def pack_tiles(cap, cells_dev, weights, cells, dest, count, packets):
@@ -46,7 +46,8 @@
     tiles = cells.shape[0]
     half = slots // cap // 2
     names = dest[...]
-    names = jnp.where(names < half, 2 * (half - 1 - names) + 1, 2 * (names - half))
+    names = jnp.where(names > half, 2 * (names - half) - 1, 2 * (half - names))
+    names = jnp.minimum(names, 2 * half - 1)
     live = (lax.broadcasted_iota(jnp.int32, (1, tiles), 1) < count[0]).astype(jnp.float32)
     same = (lax.broadcasted_iota(jnp.int32, (slots // cap, tiles), 0) == names).astype(jnp.float32)
     shape = (tiles, tiles)

time: 34.7 us -> 34.5 us (level)
  waiting for transfers between devices: 5.55 us -> 3.95 us
  Pallas kernels: 9.42 us -> 10.5 us
    all_to_all x1, waiting for transfers between devices: 4.38 us -> 3.12 us  [per_device(): lax.all_to_all(load, ('slab', 'pencil'), 0, 0, axis_index_groups=[everyon...]
    pallas_call x1, Pallas kernels: 3 us -> 4.04 us  [deposit(): pl.pallas_call(functools.partial(deposit_kernel, cap), out_shape=shaped(*...]
    all_to_all x1, waiting for transfers between devices: 1.17 us -> 0.81 us  [per_device(): lax.all_to_all(packets, 'slab', 0, 0, axis_index_groups=[order], tiled=True)]
    all_to_all x1, starting transfers between devices: 5.39 us -> 5.74 us  [per_device(): lax.all_to_all(load, ('slab', 'pencil'), 0, 0, axis_index_groups=[everyon...]
  transfers between devices with their start and end apart: 6 -> 6, of which waited for: 2 -> 2; matrix products, arithmetic and copies ran while one was open for 0% -> 0% of each run, Pallas kernels for 17% -> 21%
where the time goes in v16:
time: 34.5 us; the launch traced here: 34.1 us
  starting transfers between devices  18.2 us (53%)
  Pallas kernels  10.5 us (30%)
  waiting for transfers between devices  3.95 us (11%)
  between operations  1.49 us (4%)
    all_to_all x1, starting transfers between devices, per_device(): lax.all_to_all(packets, 'slab', 0, 0, axis_index_groups=[order], tiled=True)  8.15 us
    all_to_all x1, starting transfers between devices, per_device(): lax.all_to_all(load, ('slab', 'pencil'), 0, 0, axis_index_groups=[everyon...  5.74 us
    ppermute x4, starting transfers between devices, swapped(): return lax.ppermute(array, axis, up + [(j, i) for i, j in up])  4.33 us
    pallas_call x1, Pallas kernels, deposit(): pl.pallas_call(functools.partial(deposit_kernel, cap), out_shape=shaped(*...  4.04 us
    all_to_all x1, waiting for transfers between devices, per_device(): lax.all_to_all(load, ('slab', 'pencil'), 0, 0, axis_index_groups=[everyon...  3.12 us
    pallas_call x1, Pallas kernels, to_send(): pl.pallas_call(functools.partial(send_kernel, cap), out_shape=made, in_sp...  2.71 us
    pallas_call x1, Pallas kernels, inner(): pl.pallas_call(inner_kernel, out_shape=(shaped(*vort.shape), shaped(*tile...  2.05 us
    pallas_call x1, Pallas kernels, edges(): pl.pallas_call(edge_kernel, out_shape=(shaped(*inside.shape), load), in_s...  0.91 us
  transfers between devices with their start and end apart: 6, of which 2 were waited for; matrix products, arithmetic and copies ran while one was open for 0% of the time, Pallas kernels for 21%

profile of v16, /device:TPU:0, one launch (start us, length us, event | category | flops | bytes accessed | tf_op | source)
XLA Modules:
  0.0 34.1 jit_solution(11804150768545573037)
XLA Ops:
  1.3 2.7 %shard_map.86 = (f32[7,32,256]{2,1,0:T(8,128)}, f32[7,32,256]{2,1,0:T(8,128)}, f32[7,8,256]{2,1,0:T(8,128)}, f32[7,8,256]{2,1,0:T(8,128)}, f32[64,4,128]{2,1,0:T(4,128)}, /*index=5*/f32[4,128]{1,0:T(4,128)}) custom-call(f32[3,8,32,256]{3,2,1,0:T(8,128)} %vort.3, f32[3,8,32,256]{3,2,1,0:T(8,128)} %velo.3, f32[8,32,256]{2,1,0:T(8,128)} %visc.3, ...), custom_call_target="tpu_custom_call" | custom-call | tf_op jit(solution)/shard_map/pallas_call | solution.py:171
  4.0 0.0 copy-start.2
  4.0 3.0 %collective-permute-start = (f32[7,32,256]{2,1,0:T(8,128)}, f32[7,32,256]{2,1,0:T(8,128)S(1)}, u32[]{:S(2)}, u32[]{:S(2)}) collective-permute-start(f32[7,32,256]{2,1,0:T(8,128)} %get-tuple-element.15.near), channel_id=1, source_target_pairs={{0,4},{8,12},{16,20},{24,28},{4,0},{12,8},{20,16},{28,24},{1,5},{9... | collective-permute-start | bytes 688136 | tf_op jit(solution)/shard_map/ppermute | solution.py:465
  7.0 0.7 %collective-permute-start.1 = (f32[7,32,256]{2,1,0:T(8,128)}, f32[7,32,256]{2,1,0:T(8,128)S(1)}, u32[]{:S(2)}, u32[]{:S(2)}) collective-permute-start(f32[7,32,256]{2,1,0:T(8,128)} %get-tuple-element.16.far), channel_id=1, source_target_pairs={{4,8},{12,16},{20,24},{8,4},{16,12},{24,20},{5,9},{13,17},{21,25},... | collective-permute-start | bytes 688136 | tf_op jit(solution)/shard_map/ppermute | solution.py:465
  7.7 8.1 %all-to-all-start = ((f32[64,4,128]{2,1,0:T(4,128)}), f32[64,4,128]{2,1,0:T(4,128)S(1)}, u32[]{:S(2)}, u32[]{:S(2)}) async-start(f32[64,4,128]{2,1,0:T(4,128)} %get-tuple-element.20), calls=%async_computation | async-start | bytes 262144 | tf_op jit(solution)/shard_map/all_to_all | solution.py:481
  15.9 0.0 collective-permute-start.2
  15.9 0.7 %collective-permute-start.3 = (f32[7,8,256]{2,1,0:T(8,128)}, f32[7,8,256]{2,1,0:T(8,128)S(1)}, u32[]{:S(2)}, u32[]{:S(2)}) collective-permute-start(f32[7,8,256]{2,1,0:T(8,128)} %get-tuple-element.18.other), channel_id=1, source_target_pairs={{1,2},{2,1},{5,6},{6,5},{9,10},{10,9},{13,14},{14,13},{17,18},{18,... | collective-permute-start | bytes 172040 | tf_op jit(solution)/shard_map/ppermute | solution.py:465
  16.5 0.0 copy-done
  16.5 0.0 copy-done.1
  16.6 0.0 copy-done.2
  16.6 0.0 copy-done.7
  16.6 0.0 copy-start.3
  16.6 2.0 %shard_map.87 = (f32[3,8,32,256]{3,2,1,0:T(8,128)S(1)}, f32[4,128]{1,0:T(4,128)S(1)}) custom-call(f32[3,8,32,256]{3,2,1,0:T(8,128)S(1)} %copy-done, f32[3,8,32,256]{3,2,1,0:T(8,128)S(1)} %copy-done.1, f32[8,32,256]{2,1,0:T(8,128)S(1)} %copy-done.2, f32[4,128]{1,0:T(4,128)S(1)} %copy-done.7), custom_call_target="tpu_custom_call" | custom-call | tf_op jit(solution)/shard_map/pallas_call | solution.py:258
  18.7 0.0 collective-permute-done.2.swap_in
  18.7 0.0 collective-permute-done.3.other_in
  18.7 0.0 collective-permute-done.near_in
  18.7 0.0 collective-permute-done.1.far_in
  18.7 0.0 copy-done.3
  18.8 0.9 %shard_map.88 = (f32[3,8,32,256]{3,2,1,0:T(8,128)S(1)}, f32[32,4,128]{2,1,0:T(4,128)}) custom-call(f32[3,8,32,256]{3,2,1,0:T(8,128)S(1)} %get-tuple-element.13.inside, f32[4,128]{1,0:T(4,128)S(1)} %get-tuple-element.14.moments, f32[7,32,256]{2,1,0:T(8,128)S(1)} %copy-done.3, f32[7,32,256]{2,1,0:T(8,128)S(1)} %copy-done.4, f32[7,8,256]{2,1,0:T(8,128)S(1)} %copy-done.5, ...), custom_call_target="tpu_custom_call" | custom-call | tf_op jit(solution)/shard_map/pallas_call | solution.py:313
  19.7 0.8 %all-to-all-done.load = f32[64,4,128]{2,1,0:T(4,128)S(1)} async-done(((f32[64,4,128]{2,1,0:T(4,128)}), f32[64,4,128]{2,1,0:T(4,128)S(1)}, u32[]{:S(2)}, u32[]{:S(2)}) %all-to-all-start) | async-done | bytes 131104 | tf_op jit(solution)/shard_map/all_to_all | solution.py:481
  20.5 5.7 %all-to-all-start.1 = ((f32[32,4,128]{2,1,0:T(4,128)}), f32[32,4,128]{2,1,0:T(4,128)S(1)}, u32[]{:S(2)}, u32[]{:S(2)}) async-start(f32[32,4,128]{2,1,0:T(4,128)} %get-tuple-element.21), calls=%async_computation.1 | async-start | bytes 131072 | tf_op jit(solution)/shard_map/all_to_all | solution.py:485
  26.2 4.0 %shard_map.89 = f32[3,8,32,256]{3,2,1,0:T(8,128)} custom-call(f32[3,8,32,256]{3,2,1,0:T(8,128)S(1)} %get-tuple-element.19.inside, f32[64,4,128]{2,1,0:T(4,128)S(1)} %all-to-all-done.load), custom_call_target="tpu_custom_call" | custom-call | tf_op jit(solution)/shard_map/pallas_call | solution.py:449
  30.3 3.1 %all-to-all-done.1.load = f32[32,4,128]{2,1,0:T(4,128)S(1)} async-done(((f32[32,4,128]{2,1,0:T(4,128)}), f32[32,4,128]{2,1,0:T(4,128)S(1)}, u32[]{:S(2)}, u32[]{:S(2)}) %all-to-all-start.1) | async-done | bytes 65568 | tf_op jit(solution)/shard_map/all_to_all | solution.py:485
  33.4 0.7 %shard_map.90 = f32[3,1,1,16]{3,2,1,0:T(1,128)} custom-call(f32[32,4,128]{2,1,0:T(4,128)S(1)} %all-to-all-done.1.load), custom_call_target="tpu_custom_call" | custom-call | tf_op jit(solution)/shard_map/pallas_call | solution.py:365
  (9 shorter events, 0.0 us)
Async XLA Ops:
  1.3 15.3 %copy-start = (f32[3,8,32,256]{3,2,1,0:T(8,128)S(1)}, f32[3,8,32,256]{3,2,1,0:T(8,128)}, u32[]{:S(2)}) copy-start(f32[3,8,32,256]{3,2,1,0:T(8,128)} %vort.3) | copy-start | bytes 2359300
  1.3 15.3 %copy-start.1 = (f32[3,8,32,256]{3,2,1,0:T(8,128)S(1)}, f32[3,8,32,256]{3,2,1,0:T(8,128)}, u32[]{:S(2)}) copy-start(f32[3,8,32,256]{3,2,1,0:T(8,128)} %velo.3) | copy-start | bytes 2359300
  4.0 12.5 %copy-start.2 = (f32[8,32,256]{2,1,0:T(8,128)S(1)}, f32[8,32,256]{2,1,0:T(8,128)}, u32[]{:S(2)}) copy-start(f32[8,32,256]{2,1,0:T(8,128)} %visc.3) | copy-start | bytes 786436
  4.0 14.7 %collective-permute-start = (f32[7,32,256]{2,1,0:T(8,128)}, f32[7,32,256]{2,1,0:T(8,128)S(1)}, u32[]{:S(2)}, u32[]{:S(2)}) collective-permute-start(f32[7,32,256]{2,1,0:T(8,128)} %get-tuple-element.15.near), channel_id=1, source_target_pairs={{0,4},{8,12},{16,20},{24,28},{4,0},{12,8},{20,16},{28,24},{1,5},{9... | collective-permute-start | bytes 688136 | tf_op jit(solution)/shard_map/ppermute | solution.py:465
  7.0 11.7 %collective-permute-start.1 = (f32[7,32,256]{2,1,0:T(8,128)}, f32[7,32,256]{2,1,0:T(8,128)S(1)}, u32[]{:S(2)}, u32[]{:S(2)}) collective-permute-start(f32[7,32,256]{2,1,0:T(8,128)} %get-tuple-element.16.far), channel_id=1, source_target_pairs={{4,8},{12,16},{20,24},{8,4},{16,12},{24,20},{5,9},{13,17},{21,25},... | collective-permute-start | bytes 688136 | tf_op jit(solution)/shard_map/ppermute | solution.py:465
  7.7 12.8 %all-to-all-start = ((f32[64,4,128]{2,1,0:T(4,128)}), f32[64,4,128]{2,1,0:T(4,128)S(1)}, u32[]{:S(2)}, u32[]{:S(2)}) async-start(f32[64,4,128]{2,1,0:T(4,128)} %get-tuple-element.20), calls=%async_computation | async-start | bytes 262144 | tf_op jit(solution)/shard_map/all_to_all | solution.py:481
  15.9 0.7 %copy-start.7 = (f32[4,128]{1,0:T(4,128)S(1)}, f32[4,128]{1,0:T(4,128)}, u32[]{:S(2)}) copy-start(f32[4,128]{1,0:T(4,128)} %get-tuple-element.12.tiles_in) | copy-start | bytes 6148
  15.9 2.8 %collective-permute-start.2 = (f32[7,8,256]{2,1,0:T(8,128)}, f32[7,8,256]{2,1,0:T(8,128)S(1)}, u32[]{:S(2)}, u32[]{:S(2)}) collective-permute-start(f32[7,8,256]{2,1,0:T(8,128)} %get-tuple-element.17.swap), channel_id=1, source_target_pairs={{0,1},{2,3},{1,0},{3,2},{4,5},{6,7},{5,4},{7,6},{8,9},{10,11},{9,8... | collective-permute-start | bytes 172040 | tf_op jit(solution)/shard_map/ppermute | solution.py:465
  15.9 2.8 %collective-permute-start.3 = (f32[7,8,256]{2,1,0:T(8,128)}, f32[7,8,256]{2,1,0:T(8,128)S(1)}, u32[]{:S(2)}, u32[]{:S(2)}) collective-permute-start(f32[7,8,256]{2,1,0:T(8,128)} %get-tuple-element.18.other), channel_id=1, source_target_pairs={{1,2},{2,1},{5,6},{6,5},{9,10},{10,9},{13,14},{14,13},{17,18},{18,... | collective-permute-start | bytes 172040 | tf_op jit(solution)/shard_map/ppermute | solution.py:465
  16.6 2.1 %copy-start.3 = (f32[7,32,256]{2,1,0:T(8,128)S(1)}, f32[7,32,256]{2,1,0:T(8,128)}, u32[]{:S(2)}) copy-start(f32[7,32,256]{2,1,0:T(8,128)} %get-tuple-element.15.near) | copy-start | bytes 688132
  16.6 2.1 %copy-start.4 = (f32[7,32,256]{2,1,0:T(8,128)S(1)}, f32[7,32,256]{2,1,0:T(8,128)}, u32[]{:S(2)}) copy-start(f32[7,32,256]{2,1,0:T(8,128)} %get-tuple-element.16.far) | copy-start | bytes 688132
  16.6 2.1 %copy-start.5 = (f32[7,8,256]{2,1,0:T(8,128)S(1)}, f32[7,8,256]{2,1,0:T(8,128)}, u32[]{:S(2)}) copy-start(f32[7,8,256]{2,1,0:T(8,128)} %get-tuple-element.17.swap) | copy-start | bytes 172036
  16.6 2.1 %copy-start.6 = (f32[7,8,256]{2,1,0:T(8,128)S(1)}, f32[7,8,256]{2,1,0:T(8,128)}, u32[]{:S(2)}) copy-start(f32[7,8,256]{2,1,0:T(8,128)} %get-tuple-element.18.other) | copy-start | bytes 172036
  20.5 12.9 %all-to-all-start.1 = ((f32[32,4,128]{2,1,0:T(4,128)}), f32[32,4,128]{2,1,0:T(4,128)S(1)}, u32[]{:S(2)}, u32[]{:S(2)}) async-start(f32[32,4,128]{2,1,0:T(4,128)} %get-tuple-element.21), calls=%async_computation.1 | async-start | bytes 131072 | tf_op jit(solution)/shard_map/all_to_all | solution.py:485

commit v17 on v16

--- a/solution.py
+++ b/solution.py
@@ -130,24 +130,24 @@
 ):
     cx, cy, nz = visc.shape
     copies = Copies(sems)
-    copies.start(weights_in, weights)
-    copies.start(cells_in, cells)
-    copies.start(dest_in, dest)
-    copies.start(count_in, count)
     even = lax.axis_index("slab") % 2 == 0
     for face, at in ((near, jnp.where(even, cx - 1, 0)), (far, jnp.where(even, 0, cx - 1))):
         copies.start(vort.at[:, at], face.at[0:3])
         copies.start(velo.at[:, at], face.at[3:6])
         copies.start(visc.at[at], face.at[6])
+    copies.start(weights_in, weights)
+    copies.start(cells_in, cells)
+    copies.start(dest_in, dest)
+    copies.start(count_in, count)
     even = lax.axis_index("pencil") % 2 == 0
     for face, at in ((swap, jnp.where(even, cy - 1, 0)), (other, jnp.where(even, 0, cy - 1))):
         copies.start(vort.at[:, :, at], face.at[0:3])
         copies.start(velo.at[:, :, at], face.at[3:6])
         copies.start(visc.at[:, at], face.at[6])
-    copies.wait(0, 4)
+    copies.wait(6, 10)
     pack_tiles(cap, cx * cy * nz, weights, cells, dest, count, packets)
     copies.start(packets, packets_out)
-    copies.wait(4, 10)
+    copies.wait(0, 6)
     copies.start(near, near_out)
     copies.start(far, far_out)
     tile_moments(cap, nz, packets, moments)
@@ -416,12 +416,18 @@
     for h in range(2):
         acc[:, :, :, h * nz : (h + 1) * nz] = inside[:, h * (cx // 2) : (h + 1) * (cx // 2)]
     listed = jnp.int32(0)
-    for d in range(load.shape[0] // cap):
-        first = d * cap
-        held = jnp.max(load[first, 3:4, :]).astype(jnp.int32) // (cx * cy * nz)
-        for k in range(cap):
-            order[listed + k] = first + k
-        listed = listed + held
+    for d in range(0, load.shape[0] // cap, 4):
+        rows = jnp.concatenate([load[(d + k) * cap, 3:4, :] for k in range(4)], axis=0)
+        held = rows.astype(jnp.int32) // (cx * cy * nz)
+        place = lax.broadcasted_iota(jnp.int32, held.shape, 0)
+        scale = jnp.where(place < 2, jnp.where(place == 0, 1, 16), jnp.where(place == 2, 256, 4096))
+        packed = jnp.max(jnp.sum((held * scale).astype(jnp.float32), axis=0, keepdims=True)).astype(jnp.int32)
+        for k in range(4):
+            first = (d + k) * cap
+            for j in range(cap):
+                order[listed + j] = first + j
+            listed = listed + packed % 16
+            packed = packed // 16
     for k in range(GROUP):
         order[listed + k] = 0
     rest = listed % GROUP

time: 34.5 us -> 34.7 us (level)
  waiting for transfers between devices: 3.95 us -> 4.97 us
  Pallas kernels: 10.5 us -> 9.66 us
    pallas_call x1, Pallas kernels: 4.04 us -> 3.01 us  [deposit(): pl.pallas_call(functools.partial(deposit_kernel, cap), out_shape=shaped(*...]
    all_to_all x1, waiting for transfers between devices: 3.12 us -> 4.15 us  [per_device(): lax.all_to_all(load, ('slab', 'pencil'), 0, 0, axis_index_groups=[everyon...]
  transfers between devices with their start and end apart: 6 -> 6, of which waited for: 2 -> 2; matrix products, arithmetic and copies ran while one was open for 0% -> 0% of each run, Pallas kernels for 21% -> 17%
where the time goes in v17:
time: 34.7 us; the launch traced here: 34.4 us
  starting transfers between devices  18.2 us (52%)
  Pallas kernels  9.66 us (28%)
  waiting for transfers between devices  4.97 us (14%)
  between operations  1.49 us (4%)
    all_to_all x1, starting transfers between devices, per_device(): lax.all_to_all(packets, 'slab', 0, 0, axis_index_groups=[order], tiled=True)  8.15 us
    all_to_all x1, starting transfers between devices, per_device(): lax.all_to_all(load, ('slab', 'pencil'), 0, 0, axis_index_groups=[everyon...  5.74 us
    ppermute x4, starting transfers between devices, swapped(): return lax.ppermute(array, axis, up + [(j, i) for i, j in up])  4.33 us
    all_to_all x1, waiting for transfers between devices, per_device(): lax.all_to_all(load, ('slab', 'pencil'), 0, 0, axis_index_groups=[everyon...  4.15 us
    pallas_call x1, Pallas kernels, deposit(): pl.pallas_call(functools.partial(deposit_kernel, cap), out_shape=shaped(*...  3.01 us
    pallas_call x1, Pallas kernels, to_send(): pl.pallas_call(functools.partial(send_kernel, cap), out_shape=made, in_sp...  2.95 us
    pallas_call x1, Pallas kernels, inner(): pl.pallas_call(inner_kernel, out_shape=(shaped(*vort.shape), shaped(*tile...  2.05 us
    pallas_call x1, Pallas kernels, edges(): pl.pallas_call(edge_kernel, out_shape=(shaped(*inside.shape), load), in_s...  0.91 us
  transfers between devices with their start and end apart: 6, of which 2 were waited for; matrix products, arithmetic and copies ran while one was open for 0% of the time, Pallas kernels for 17%

profile of v17, /device:TPU:0, one launch (start us, length us, event | category | flops | bytes accessed | tf_op | source)
XLA Modules:
  0.0 34.4 jit_solution(2662910374716038203)
XLA Ops:
  1.3 0.0 copy-start
  1.3 0.0 copy-start.1
  1.3 2.9 %shard_map.86 = (f32[7,32,256]{2,1,0:T(8,128)}, f32[7,32,256]{2,1,0:T(8,128)}, f32[7,8,256]{2,1,0:T(8,128)}, f32[7,8,256]{2,1,0:T(8,128)}, f32[64,4,128]{2,1,0:T(4,128)}, /*index=5*/f32[4,128]{1,0:T(4,128)}) custom-call(f32[3,8,32,256]{3,2,1,0:T(8,128)} %vort.3, f32[3,8,32,256]{3,2,1,0:T(8,128)} %velo.3, f32[8,32,256]{2,1,0:T(8,128)} %visc.3, ...), custom_call_target="tpu_custom_call" | custom-call | tf_op jit(solution)/shard_map/pallas_call | solution.py:171
  4.3 0.0 copy-start.2
  4.3 3.0 %collective-permute-start = (f32[7,32,256]{2,1,0:T(8,128)}, f32[7,32,256]{2,1,0:T(8,128)S(1)}, u32[]{:S(2)}, u32[]{:S(2)}) collective-permute-start(f32[7,32,256]{2,1,0:T(8,128)} %get-tuple-element.15.near), channel_id=1, source_target_pairs={{0,4},{8,12},{16,20},{24,28},{4,0},{12,8},{20,16},{28,24},{1,5},{9... | collective-permute-start | bytes 688136 | tf_op jit(solution)/shard_map/ppermute | solution.py:471
  7.3 0.7 %collective-permute-start.1 = (f32[7,32,256]{2,1,0:T(8,128)}, f32[7,32,256]{2,1,0:T(8,128)S(1)}, u32[]{:S(2)}, u32[]{:S(2)}) collective-permute-start(f32[7,32,256]{2,1,0:T(8,128)} %get-tuple-element.16.far), channel_id=1, source_target_pairs={{4,8},{12,16},{20,24},{8,4},{16,12},{24,20},{5,9},{13,17},{21,25},... | collective-permute-start | bytes 688136 | tf_op jit(solution)/shard_map/ppermute | solution.py:471
  7.9 8.1 %all-to-all-start = ((f32[64,4,128]{2,1,0:T(4,128)}), f32[64,4,128]{2,1,0:T(4,128)S(1)}, u32[]{:S(2)}, u32[]{:S(2)}) async-start(f32[64,4,128]{2,1,0:T(4,128)} %get-tuple-element.20), calls=%async_computation | async-start | bytes 262144 | tf_op jit(solution)/shard_map/all_to_all | solution.py:487
  16.1 0.0 collective-permute-start.2
  16.1 0.7 %collective-permute-start.3 = (f32[7,8,256]{2,1,0:T(8,128)}, f32[7,8,256]{2,1,0:T(8,128)S(1)}, u32[]{:S(2)}, u32[]{:S(2)}) collective-permute-start(f32[7,8,256]{2,1,0:T(8,128)} %get-tuple-element.18.other), channel_id=1, source_target_pairs={{1,2},{2,1},{5,6},{6,5},{9,10},{10,9},{13,14},{14,13},{17,18},{18,... | collective-permute-start | bytes 172040 | tf_op jit(solution)/shard_map/ppermute | solution.py:471
  16.8 0.0 copy-done
  16.8 0.0 copy-done.1
  16.8 0.0 copy-done.2
  16.8 0.0 copy-start.3
  16.9 2.0 %shard_map.87 = (f32[3,8,32,256]{3,2,1,0:T(8,128)S(1)}, f32[4,128]{1,0:T(4,128)S(1)}) custom-call(f32[3,8,32,256]{3,2,1,0:T(8,128)S(1)} %copy-done, f32[3,8,32,256]{3,2,1,0:T(8,128)S(1)} %copy-done.1, f32[8,32,256]{2,1,0:T(8,128)S(1)} %copy-done.2, f32[4,128]{1,0:T(4,128)S(1)} %copy-done.7), custom_call_target="tpu_custom_call" | custom-call | tf_op jit(solution)/shard_map/pallas_call | solution.py:258
  18.9 0.0 collective-permute-done.2.swap_in
  18.9 0.0 collective-permute-done.3.other_in
  18.9 0.0 collective-permute-done.near_in
  18.9 0.0 collective-permute-done.1.far_in
  19.0 0.9 %shard_map.88 = (f32[3,8,32,256]{3,2,1,0:T(8,128)S(1)}, f32[32,4,128]{2,1,0:T(4,128)}) custom-call(f32[3,8,32,256]{3,2,1,0:T(8,128)S(1)} %get-tuple-element.13.inside, f32[4,128]{1,0:T(4,128)S(1)} %get-tuple-element.14.moments, f32[7,32,256]{2,1,0:T(8,128)S(1)} %copy-done.3, f32[7,32,256]{2,1,0:T(8,128)S(1)} %copy-done.4, f32[7,8,256]{2,1,0:T(8,128)S(1)} %copy-done.5, ...), custom_call_target="tpu_custom_call" | custom-call | tf_op jit(solution)/shard_map/pallas_call | solution.py:313
  19.9 0.8 %all-to-all-done.load = f32[64,4,128]{2,1,0:T(4,128)S(1)} async-done(((f32[64,4,128]{2,1,0:T(4,128)}), f32[64,4,128]{2,1,0:T(4,128)S(1)}, u32[]{:S(2)}, u32[]{:S(2)}) %all-to-all-start) | async-done | bytes 131104 | tf_op jit(solution)/shard_map/all_to_all | solution.py:487
  20.7 5.7 %all-to-all-start.1 = ((f32[32,4,128]{2,1,0:T(4,128)}), f32[32,4,128]{2,1,0:T(4,128)S(1)}, u32[]{:S(2)}, u32[]{:S(2)}) async-start(f32[32,4,128]{2,1,0:T(4,128)} %get-tuple-element.21), calls=%async_computation.1 | async-start | bytes 131072 | tf_op jit(solution)/shard_map/all_to_all | solution.py:491
  26.5 3.0 %shard_map.89 = f32[3,8,32,256]{3,2,1,0:T(8,128)} custom-call(f32[3,8,32,256]{3,2,1,0:T(8,128)S(1)} %get-tuple-element.19.inside, f32[64,4,128]{2,1,0:T(4,128)S(1)} %all-to-all-done.load), custom_call_target="tpu_custom_call" | custom-call | tf_op jit(solution)/shard_map/pallas_call | solution.py:455
  29.5 4.1 %all-to-all-done.1.load = f32[32,4,128]{2,1,0:T(4,128)S(1)} async-done(((f32[32,4,128]{2,1,0:T(4,128)}), f32[32,4,128]{2,1,0:T(4,128)S(1)}, u32[]{:S(2)}, u32[]{:S(2)}) %all-to-all-start.1) | async-done | bytes 65568 | tf_op jit(solution)/shard_map/all_to_all | solution.py:491
  33.6 0.7 %shard_map.90 = f32[3,1,1,16]{3,2,1,0:T(1,128)} custom-call(f32[32,4,128]{2,1,0:T(4,128)S(1)} %all-to-all-done.1.load), custom_call_target="tpu_custom_call" | custom-call | tf_op jit(solution)/shard_map/pallas_call | solution.py:365
  (9 shorter events, 0.0 us)
Async XLA Ops:
  1.3 15.5 %copy-start = (f32[3,8,32,256]{3,2,1,0:T(8,128)S(1)}, f32[3,8,32,256]{3,2,1,0:T(8,128)}, u32[]{:S(2)}) copy-start(f32[3,8,32,256]{3,2,1,0:T(8,128)} %vort.3) | copy-start | bytes 2359300
  1.3 15.5 %copy-start.1 = (f32[3,8,32,256]{3,2,1,0:T(8,128)S(1)}, f32[3,8,32,256]{3,2,1,0:T(8,128)}, u32[]{:S(2)}) copy-start(f32[3,8,32,256]{3,2,1,0:T(8,128)} %velo.3) | copy-start | bytes 2359300
  4.3 12.5 %copy-start.2 = (f32[8,32,256]{2,1,0:T(8,128)S(1)}, f32[8,32,256]{2,1,0:T(8,128)}, u32[]{:S(2)}) copy-start(f32[8,32,256]{2,1,0:T(8,128)} %visc.3) | copy-start | bytes 786436
  4.3 14.7 %collective-permute-start = (f32[7,32,256]{2,1,0:T(8,128)}, f32[7,32,256]{2,1,0:T(8,128)S(1)}, u32[]{:S(2)}, u32[]{:S(2)}) collective-permute-start(f32[7,32,256]{2,1,0:T(8,128)} %get-tuple-element.15.near), channel_id=1, source_target_pairs={{0,4},{8,12},{16,20},{24,28},{4,0},{12,8},{20,16},{28,24},{1,5},{9... | collective-permute-start | bytes 688136 | tf_op jit(solution)/shard_map/ppermute | solution.py:471
  7.3 11.7 %collective-permute-start.1 = (f32[7,32,256]{2,1,0:T(8,128)}, f32[7,32,256]{2,1,0:T(8,128)S(1)}, u32[]{:S(2)}, u32[]{:S(2)}) collective-permute-start(f32[7,32,256]{2,1,0:T(8,128)} %get-tuple-element.16.far), channel_id=1, source_target_pairs={{4,8},{12,16},{20,24},{8,4},{16,12},{24,20},{5,9},{13,17},{21,25},... | collective-permute-start | bytes 688136 | tf_op jit(solution)/shard_map/ppermute | solution.py:471
  7.9 12.8 %all-to-all-start = ((f32[64,4,128]{2,1,0:T(4,128)}), f32[64,4,128]{2,1,0:T(4,128)S(1)}, u32[]{:S(2)}, u32[]{:S(2)}) async-start(f32[64,4,128]{2,1,0:T(4,128)} %get-tuple-element.20), calls=%async_computation | async-start | bytes 262144 | tf_op jit(solution)/shard_map/all_to_all | solution.py:487
  16.1 0.7 %copy-start.7 = (f32[4,128]{1,0:T(4,128)S(1)}, f32[4,128]{1,0:T(4,128)}, u32[]{:S(2)}) copy-start(f32[4,128]{1,0:T(4,128)} %get-tuple-element.12.tiles_in) | copy-start | bytes 6148
  16.1 2.8 %collective-permute-start.2 = (f32[7,8,256]{2,1,0:T(8,128)}, f32[7,8,256]{2,1,0:T(8,128)S(1)}, u32[]{:S(2)}, u32[]{:S(2)}) collective-permute-start(f32[7,8,256]{2,1,0:T(8,128)} %get-tuple-element.17.swap), channel_id=1, source_target_pairs={{0,1},{2,3},{1,0},{3,2},{4,5},{6,7},{5,4},{7,6},{8,9},{10,11},{9,8... | collective-permute-start | bytes 172040 | tf_op jit(solution)/shard_map/ppermute | solution.py:471
  16.1 2.8 %collective-permute-start.3 = (f32[7,8,256]{2,1,0:T(8,128)}, f32[7,8,256]{2,1,0:T(8,128)S(1)}, u32[]{:S(2)}, u32[]{:S(2)}) collective-permute-start(f32[7,8,256]{2,1,0:T(8,128)} %get-tuple-element.18.other), channel_id=1, source_target_pairs={{1,2},{2,1},{5,6},{6,5},{9,10},{10,9},{13,14},{14,13},{17,18},{18,... | collective-permute-start | bytes 172040 | tf_op jit(solution)/shard_map/ppermute | solution.py:471
  16.8 2.1 %copy-start.3 = (f32[7,32,256]{2,1,0:T(8,128)S(1)}, f32[7,32,256]{2,1,0:T(8,128)}, u32[]{:S(2)}) copy-start(f32[7,32,256]{2,1,0:T(8,128)} %get-tuple-element.15.near) | copy-start | bytes 688132
  16.8 2.1 %copy-start.4 = (f32[7,32,256]{2,1,0:T(8,128)S(1)}, f32[7,32,256]{2,1,0:T(8,128)}, u32[]{:S(2)}) copy-start(f32[7,32,256]{2,1,0:T(8,128)} %get-tuple-element.16.far) | copy-start | bytes 688132
  16.8 2.1 %copy-start.5 = (f32[7,8,256]{2,1,0:T(8,128)S(1)}, f32[7,8,256]{2,1,0:T(8,128)}, u32[]{:S(2)}) copy-start(f32[7,8,256]{2,1,0:T(8,128)} %get-tuple-element.17.swap) | copy-start | bytes 172036
  16.8 2.1 %copy-start.6 = (f32[7,8,256]{2,1,0:T(8,128)S(1)}, f32[7,8,256]{2,1,0:T(8,128)}, u32[]{:S(2)}) copy-start(f32[7,8,256]{2,1,0:T(8,128)} %get-tuple-element.18.other) | copy-start | bytes 172036
  20.7 12.9 %all-to-all-start.1 = ((f32[32,4,128]{2,1,0:T(4,128)}), f32[32,4,128]{2,1,0:T(4,128)S(1)}, u32[]{:S(2)}, u32[]{:S(2)}) async-start(f32[32,4,128]{2,1,0:T(4,128)} %get-tuple-element.21), calls=%async_computation.1 | async-start | bytes 131072 | tf_op jit(solution)/shard_map/all_to_all | solution.py:491

commit v18 on v16

--- a/solution.py
+++ b/solution.py
@@ -147,11 +147,11 @@
     copies.wait(0, 4)
     pack_tiles(cap, cx * cy * nz, weights, cells, dest, count, packets)
     copies.start(packets, packets_out)
+    tile_moments(cap, nz, packets, moments)
+    copies.start(moments, moments_out)
     copies.wait(4, 10)
     copies.start(near, near_out)
     copies.start(far, far_out)
-    tile_moments(cap, nz, packets, moments)
-    copies.start(moments, moments_out)
     copies.wait(10, 16)
     copies.start(swap, swap_out)
     copies.start(other, other_out)

time: 34.5 us -> 34.6 us (level)
  Pallas kernels: 10.5 us -> 11.4 us
  waiting for transfers between devices: 3.95 us -> 3.14 us
    all_to_all x1, waiting for transfers between devices: 3.12 us -> 2.31 us  [per_device(): lax.all_to_all(load, ('slab', 'pencil'), 0, 0, axis_index_groups=[everyon...]
    pallas_call x1, Pallas kernels: 4.04 us -> 4.85 us  [deposit(): pl.pallas_call(functools.partial(deposit_kernel, cap), out_shape=shaped(*...]
  transfers between devices with their start and end apart: 6 -> 6, of which waited for: 2 -> 2; matrix products, arithmetic and copies ran while one was open for 0% -> 0% of each run, Pallas kernels for 21% -> 23%
where the time goes in v18:
time: 34.6 us; the launch traced here: 34.3 us
  starting transfers between devices  18.2 us (53%)
  Pallas kernels  11.4 us (33%)
  waiting for transfers between devices  3.14 us (9%)
  between operations  1.49 us (4%)
    all_to_all x1, starting transfers between devices, per_device(): lax.all_to_all(packets, 'slab', 0, 0, axis_index_groups=[order], tiled=True)  8.15 us
    all_to_all x1, starting transfers between devices, per_device(): lax.all_to_all(load, ('slab', 'pencil'), 0, 0, axis_index_groups=[everyon...  5.74 us
    pallas_call x1, Pallas kernels, deposit(): pl.pallas_call(functools.partial(deposit_kernel, cap), out_shape=shaped(*...  4.85 us
    ppermute x4, starting transfers between devices, swapped(): return lax.ppermute(array, axis, up + [(j, i) for i, j in up])  4.33 us
    pallas_call x1, Pallas kernels, to_send(): pl.pallas_call(functools.partial(send_kernel, cap), out_shape=made, in_sp...  2.85 us
    all_to_all x1, waiting for transfers between devices, per_device(): lax.all_to_all(load, ('slab', 'pencil'), 0, 0, axis_index_groups=[everyon...  2.31 us
    pallas_call x1, Pallas kernels, inner(): pl.pallas_call(inner_kernel, out_shape=(shaped(*vort.shape), shaped(*tile...  2.05 us
    pallas_call x1, Pallas kernels, edges(): pl.pallas_call(edge_kernel, out_shape=(shaped(*inside.shape), load), in_s...  0.91 us
  transfers between devices with their start and end apart: 6, of which 2 were waited for; matrix products, arithmetic and copies ran while one was open for 0% of the time, Pallas kernels for 23%

profile of v18, /device:TPU:0, one launch (start us, length us, event | category | flops | bytes accessed | tf_op | source)
XLA Modules:
  0.0 34.3 jit_solution(7656524007317042885)
XLA Ops:
  1.3 2.9 %shard_map.86 = (f32[7,32,256]{2,1,0:T(8,128)}, f32[7,32,256]{2,1,0:T(8,128)}, f32[7,8,256]{2,1,0:T(8,128)}, f32[7,8,256]{2,1,0:T(8,128)}, f32[64,4,128]{2,1,0:T(4,128)}, /*index=5*/f32[4,128]{1,0:T(4,128)}) custom-call(f32[3,8,32,256]{3,2,1,0:T(8,128)} %vort.3, f32[3,8,32,256]{3,2,1,0:T(8,128)} %velo.3, f32[8,32,256]{2,1,0:T(8,128)} %visc.3, ...), custom_call_target="tpu_custom_call" | custom-call | tf_op jit(solution)/shard_map/pallas_call | solution.py:171
  4.2 0.0 copy-start.2
  4.2 3.0 %collective-permute-start = (f32[7,32,256]{2,1,0:T(8,128)}, f32[7,32,256]{2,1,0:T(8,128)S(1)}, u32[]{:S(2)}, u32[]{:S(2)}) collective-permute-start(f32[7,32,256]{2,1,0:T(8,128)} %get-tuple-element.15.near), channel_id=1, source_target_pairs={{0,4},{8,12},{16,20},{24,28},{4,0},{12,8},{20,16},{28,24},{1,5},{9... | collective-permute-start | bytes 688136 | tf_op jit(solution)/shard_map/ppermute | solution.py:465
  7.2 0.7 %collective-permute-start.1 = (f32[7,32,256]{2,1,0:T(8,128)}, f32[7,32,256]{2,1,0:T(8,128)S(1)}, u32[]{:S(2)}, u32[]{:S(2)}) collective-permute-start(f32[7,32,256]{2,1,0:T(8,128)} %get-tuple-element.16.far), channel_id=1, source_target_pairs={{4,8},{12,16},{20,24},{8,4},{16,12},{24,20},{5,9},{13,17},{21,25},... | collective-permute-start | bytes 688136 | tf_op jit(solution)/shard_map/ppermute | solution.py:465
  7.8 8.1 %all-to-all-start = ((f32[64,4,128]{2,1,0:T(4,128)}), f32[64,4,128]{2,1,0:T(4,128)S(1)}, u32[]{:S(2)}, u32[]{:S(2)}) async-start(f32[64,4,128]{2,1,0:T(4,128)} %get-tuple-element.20), calls=%async_computation | async-start | bytes 262144 | tf_op jit(solution)/shard_map/all_to_all | solution.py:481
  16.0 0.0 collective-permute-start.2
  16.0 0.7 %collective-permute-start.3 = (f32[7,8,256]{2,1,0:T(8,128)}, f32[7,8,256]{2,1,0:T(8,128)S(1)}, u32[]{:S(2)}, u32[]{:S(2)}) collective-permute-start(f32[7,8,256]{2,1,0:T(8,128)} %get-tuple-element.18.other), channel_id=1, source_target_pairs={{1,2},{2,1},{5,6},{6,5},{9,10},{10,9},{13,14},{14,13},{17,18},{18,... | collective-permute-start | bytes 172040 | tf_op jit(solution)/shard_map/ppermute | solution.py:465
  16.7 0.0 copy-done
  16.7 0.0 copy-done.1
  16.7 0.0 copy-done.2
  16.7 0.0 copy-done.7
  16.7 0.0 copy-start.3
  16.8 2.0 %shard_map.87 = (f32[3,8,32,256]{3,2,1,0:T(8,128)S(1)}, f32[4,128]{1,0:T(4,128)S(1)}) custom-call(f32[3,8,32,256]{3,2,1,0:T(8,128)S(1)} %copy-done, f32[3,8,32,256]{3,2,1,0:T(8,128)S(1)} %copy-done.1, f32[8,32,256]{2,1,0:T(8,128)S(1)} %copy-done.2, f32[4,128]{1,0:T(4,128)S(1)} %copy-done.7), custom_call_target="tpu_custom_call" | custom-call | tf_op jit(solution)/shard_map/pallas_call | solution.py:258
  18.8 0.0 collective-permute-done.2.swap_in
  18.8 0.0 collective-permute-done.3.other_in
  18.8 0.0 collective-permute-done.near_in
  18.8 0.0 collective-permute-done.1.far_in
  18.9 0.0 copy-done.3
  18.9 0.9 %shard_map.88 = (f32[3,8,32,256]{3,2,1,0:T(8,128)S(1)}, f32[32,4,128]{2,1,0:T(4,128)}) custom-call(f32[3,8,32,256]{3,2,1,0:T(8,128)S(1)} %get-tuple-element.13.inside, f32[4,128]{1,0:T(4,128)S(1)} %get-tuple-element.14.moments, f32[7,32,256]{2,1,0:T(8,128)S(1)} %copy-done.3, f32[7,32,256]{2,1,0:T(8,128)S(1)} %copy-done.4, f32[7,8,256]{2,1,0:T(8,128)S(1)} %copy-done.5, ...), custom_call_target="tpu_custom_call" | custom-call | tf_op jit(solution)/shard_map/pallas_call | solution.py:313
  19.8 0.8 %all-to-all-done.load = f32[64,4,128]{2,1,0:T(4,128)S(1)} async-done(((f32[64,4,128]{2,1,0:T(4,128)}), f32[64,4,128]{2,1,0:T(4,128)S(1)}, u32[]{:S(2)}, u32[]{:S(2)}) %all-to-all-start) | async-done | bytes 131104 | tf_op jit(solution)/shard_map/all_to_all | solution.py:481
  20.6 5.7 %all-to-all-start.1 = ((f32[32,4,128]{2,1,0:T(4,128)}), f32[32,4,128]{2,1,0:T(4,128)S(1)}, u32[]{:S(2)}, u32[]{:S(2)}) async-start(f32[32,4,128]{2,1,0:T(4,128)} %get-tuple-element.21), calls=%async_computation.1 | async-start | bytes 131072 | tf_op jit(solution)/shard_map/all_to_all | solution.py:485
  26.4 4.8 %shard_map.89 = f32[3,8,32,256]{3,2,1,0:T(8,128)} custom-call(f32[3,8,32,256]{3,2,1,0:T(8,128)S(1)} %get-tuple-element.19.inside, f32[64,4,128]{2,1,0:T(4,128)S(1)} %all-to-all-done.load), custom_call_target="tpu_custom_call" | custom-call | tf_op jit(solution)/shard_map/pallas_call | solution.py:449
  31.2 2.3 %all-to-all-done.1.load = f32[32,4,128]{2,1,0:T(4,128)S(1)} async-done(((f32[32,4,128]{2,1,0:T(4,128)}), f32[32,4,128]{2,1,0:T(4,128)S(1)}, u32[]{:S(2)}, u32[]{:S(2)}) %all-to-all-start.1) | async-done | bytes 65568 | tf_op jit(solution)/shard_map/all_to_all | solution.py:485
  33.5 0.7 %shard_map.90 = f32[3,1,1,16]{3,2,1,0:T(1,128)} custom-call(f32[32,4,128]{2,1,0:T(4,128)S(1)} %all-to-all-done.1.load), custom_call_target="tpu_custom_call" | custom-call | tf_op jit(solution)/shard_map/pallas_call | solution.py:365
  (9 shorter events, 0.0 us)
Async XLA Ops:
  1.3 15.4 %copy-start = (f32[3,8,32,256]{3,2,1,0:T(8,128)S(1)}, f32[3,8,32,256]{3,2,1,0:T(8,128)}, u32[]{:S(2)}) copy-start(f32[3,8,32,256]{3,2,1,0:T(8,128)} %vort.3) | copy-start | bytes 2359300
  1.3 15.4 %copy-start.1 = (f32[3,8,32,256]{3,2,1,0:T(8,128)S(1)}, f32[3,8,32,256]{3,2,1,0:T(8,128)}, u32[]{:S(2)}) copy-start(f32[3,8,32,256]{3,2,1,0:T(8,128)} %velo.3) | copy-start | bytes 2359300
  4.2 12.5 %copy-start.2 = (f32[8,32,256]{2,1,0:T(8,128)S(1)}, f32[8,32,256]{2,1,0:T(8,128)}, u32[]{:S(2)}) copy-start(f32[8,32,256]{2,1,0:T(8,128)} %visc.3) | copy-start | bytes 786436
  4.2 14.7 %collective-permute-start = (f32[7,32,256]{2,1,0:T(8,128)}, f32[7,32,256]{2,1,0:T(8,128)S(1)}, u32[]{:S(2)}, u32[]{:S(2)}) collective-permute-start(f32[7,32,256]{2,1,0:T(8,128)} %get-tuple-element.15.near), channel_id=1, source_target_pairs={{0,4},{8,12},{16,20},{24,28},{4,0},{12,8},{20,16},{28,24},{1,5},{9... | collective-permute-start | bytes 688136 | tf_op jit(solution)/shard_map/ppermute | solution.py:465
  7.2 11.7 %collective-permute-start.1 = (f32[7,32,256]{2,1,0:T(8,128)}, f32[7,32,256]{2,1,0:T(8,128)S(1)}, u32[]{:S(2)}, u32[]{:S(2)}) collective-permute-start(f32[7,32,256]{2,1,0:T(8,128)} %get-tuple-element.16.far), channel_id=1, source_target_pairs={{4,8},{12,16},{20,24},{8,4},{16,12},{24,20},{5,9},{13,17},{21,25},... | collective-permute-start | bytes 688136 | tf_op jit(solution)/shard_map/ppermute | solution.py:465
  7.8 12.8 %all-to-all-start = ((f32[64,4,128]{2,1,0:T(4,128)}), f32[64,4,128]{2,1,0:T(4,128)S(1)}, u32[]{:S(2)}, u32[]{:S(2)}) async-start(f32[64,4,128]{2,1,0:T(4,128)} %get-tuple-element.20), calls=%async_computation | async-start | bytes 262144 | tf_op jit(solution)/shard_map/all_to_all | solution.py:481
  16.0 0.7 %copy-start.7 = (f32[4,128]{1,0:T(4,128)S(1)}, f32[4,128]{1,0:T(4,128)}, u32[]{:S(2)}) copy-start(f32[4,128]{1,0:T(4,128)} %get-tuple-element.12.tiles_in) | copy-start | bytes 6148
  16.0 2.8 %collective-permute-start.2 = (f32[7,8,256]{2,1,0:T(8,128)}, f32[7,8,256]{2,1,0:T(8,128)S(1)}, u32[]{:S(2)}, u32[]{:S(2)}) collective-permute-start(f32[7,8,256]{2,1,0:T(8,128)} %get-tuple-element.17.swap), channel_id=1, source_target_pairs={{0,1},{2,3},{1,0},{3,2},{4,5},{6,7},{5,4},{7,6},{8,9},{10,11},{9,8... | collective-permute-start | bytes 172040 | tf_op jit(solution)/shard_map/ppermute | solution.py:465
  16.0 2.8 %collective-permute-start.3 = (f32[7,8,256]{2,1,0:T(8,128)}, f32[7,8,256]{2,1,0:T(8,128)S(1)}, u32[]{:S(2)}, u32[]{:S(2)}) collective-permute-start(f32[7,8,256]{2,1,0:T(8,128)} %get-tuple-element.18.other), channel_id=1, source_target_pairs={{1,2},{2,1},{5,6},{6,5},{9,10},{10,9},{13,14},{14,13},{17,18},{18,... | collective-permute-start | bytes 172040 | tf_op jit(solution)/shard_map/ppermute | solution.py:465
  16.7 2.1 %copy-start.3 = (f32[7,32,256]{2,1,0:T(8,128)S(1)}, f32[7,32,256]{2,1,0:T(8,128)}, u32[]{:S(2)}) copy-start(f32[7,32,256]{2,1,0:T(8,128)} %get-tuple-element.15.near) | copy-start | bytes 688132
  16.7 2.1 %copy-start.4 = (f32[7,32,256]{2,1,0:T(8,128)S(1)}, f32[7,32,256]{2,1,0:T(8,128)}, u32[]{:S(2)}) copy-start(f32[7,32,256]{2,1,0:T(8,128)} %get-tuple-element.16.far) | copy-start | bytes 688132
  16.7 2.1 %copy-start.5 = (f32[7,8,256]{2,1,0:T(8,128)S(1)}, f32[7,8,256]{2,1,0:T(8,128)}, u32[]{:S(2)}) copy-start(f32[7,8,256]{2,1,0:T(8,128)} %get-tuple-element.17.swap) | copy-start | bytes 172036
  16.7 2.1 %copy-start.6 = (f32[7,8,256]{2,1,0:T(8,128)S(1)}, f32[7,8,256]{2,1,0:T(8,128)}, u32[]{:S(2)}) copy-start(f32[7,8,256]{2,1,0:T(8,128)} %get-tuple-element.18.other) | copy-start | bytes 172036
  20.6 12.9 %all-to-all-start.1 = ((f32[32,4,128]{2,1,0:T(4,128)}), f32[32,4,128]{2,1,0:T(4,128)S(1)}, u32[]{:S(2)}, u32[]{:S(2)}) async-start(f32[32,4,128]{2,1,0:T(4,128)} %get-tuple-element.21), calls=%async_computation.1 | async-start | bytes 131072 | tf_op jit(solution)/shard_map/all_to_all | solution.py:485

commit v19 on v16

--- a/solution.py
+++ b/solution.py
@@ -92,9 +92,9 @@
         self.sems = sems
         self.made = []
 
-    def start(self, source, target):
+    def start(self, source, target, priority=0):
         self.made.append(pltpu.make_async_copy(source, target, self.sems.at[len(self.made)]))
-        self.made[-1].start()
+        self.made[-1].start(priority)
 
     def wait(self, first, last):
         for k in range(first, last):
@@ -136,9 +136,9 @@
     copies.start(count_in, count)
     even = lax.axis_index("slab") % 2 == 0
     for face, at in ((near, jnp.where(even, cx - 1, 0)), (far, jnp.where(even, 0, cx - 1))):
-        copies.start(vort.at[:, at], face.at[0:3])
-        copies.start(velo.at[:, at], face.at[3:6])
-        copies.start(visc.at[at], face.at[6])
+        copies.start(vort.at[:, at], face.at[0:3], 1)
+        copies.start(velo.at[:, at], face.at[3:6], 1)
+        copies.start(visc.at[at], face.at[6], 1)
     even = lax.axis_index("pencil") % 2 == 0
     for face, at in ((swap, jnp.where(even, cy - 1, 0)), (other, jnp.where(even, 0, cy - 1))):
         copies.start(vort.at[:, :, at], face.at[0:3])
@@ -148,8 +148,8 @@
     pack_tiles(cap, cx * cy * nz, weights, cells, dest, count, packets)
     copies.start(packets, packets_out)
     copies.wait(4, 10)
-    copies.start(near, near_out)
-    copies.start(far, far_out)
+    copies.start(near, near_out, 1)
+    copies.start(far, far_out, 1)
     tile_moments(cap, nz, packets, moments)
     copies.start(moments, moments_out)
     copies.wait(10, 16)

time: 34.5 us -> 34.5 us (level)
  Pallas kernels: 10.5 us -> 9.41 us
  waiting for transfers between devices: 3.95 us -> 4.99 us
    pallas_call x1, Pallas kernels: 4.04 us -> 2.99 us  [deposit(): pl.pallas_call(functools.partial(deposit_kernel, cap), out_shape=shaped(*...]
    all_to_all x1, waiting for transfers between devices: 3.12 us -> 4.17 us  [per_device(): lax.all_to_all(load, ('slab', 'pencil'), 0, 0, axis_index_groups=[everyon...]
  transfers between devices with their start and end apart: 6 -> 6, of which waited for: 2 -> 2; matrix products, arithmetic and copies ran while one was open for 0% -> 0% of each run, Pallas kernels for 21% -> 17%
where the time goes in v19:
time: 34.5 us; the launch traced here: 34.2 us
  starting transfers between devices  18.2 us (53%)
  Pallas kernels  9.41 us (27%)
  waiting for transfers between devices  4.99 us (14%)
  between operations  1.49 us (4%)
    all_to_all x1, starting transfers between devices, per_device(): lax.all_to_all(packets, 'slab', 0, 0, axis_index_groups=[order], tiled=True)  8.15 us
    all_to_all x1, starting transfers between devices, per_device(): lax.all_to_all(load, ('slab', 'pencil'), 0, 0, axis_index_groups=[everyon...  5.74 us
    ppermute x4, starting transfers between devices, swapped(): return lax.ppermute(array, axis, up + [(j, i) for i, j in up])  4.33 us
    all_to_all x1, waiting for transfers between devices, per_device(): lax.all_to_all(load, ('slab', 'pencil'), 0, 0, axis_index_groups=[everyon...  4.17 us
    pallas_call x1, Pallas kernels, deposit(): pl.pallas_call(functools.partial(deposit_kernel, cap), out_shape=shaped(*...  2.99 us
    pallas_call x1, Pallas kernels, to_send(): pl.pallas_call(functools.partial(send_kernel, cap), out_shape=made, in_sp...  2.72 us
    pallas_call x1, Pallas kernels, inner(): pl.pallas_call(inner_kernel, out_shape=(shaped(*vort.shape), shaped(*tile...  2.05 us
    pallas_call x1, Pallas kernels, edges(): pl.pallas_call(edge_kernel, out_shape=(shaped(*inside.shape), load), in_s...  0.91 us
  transfers between devices with their start and end apart: 6, of which 2 were waited for; matrix products, arithmetic and copies ran while one was open for 0% of the time, Pallas kernels for 17%

profile of v19, /device:TPU:0, one launch (start us, length us, event | category | flops | bytes accessed | tf_op | source)
XLA Modules:
  0.0 34.2 jit_solution(7276003247492873317)
XLA Ops:
  1.3 2.7 %shard_map.86 = (f32[7,32,256]{2,1,0:T(8,128)}, f32[7,32,256]{2,1,0:T(8,128)}, f32[7,8,256]{2,1,0:T(8,128)}, f32[7,8,256]{2,1,0:T(8,128)}, f32[64,4,128]{2,1,0:T(4,128)}, /*index=5*/f32[4,128]{1,0:T(4,128)}) custom-call(f32[3,8,32,256]{3,2,1,0:T(8,128)} %vort.3, f32[3,8,32,256]{3,2,1,0:T(8,128)} %velo.3, f32[8,32,256]{2,1,0:T(8,128)} %visc.3, ...), custom_call_target="tpu_custom_call" | custom-call | tf_op jit(solution)/shard_map/pallas_call | solution.py:171
  4.0 0.0 copy-start.2
  4.0 3.0 %collective-permute-start = (f32[7,32,256]{2,1,0:T(8,128)}, f32[7,32,256]{2,1,0:T(8,128)S(1)}, u32[]{:S(2)}, u32[]{:S(2)}) collective-permute-start(f32[7,32,256]{2,1,0:T(8,128)} %get-tuple-element.15.near), channel_id=1, source_target_pairs={{0,4},{8,12},{16,20},{24,28},{4,0},{12,8},{20,16},{28,24},{1,5},{9... | collective-permute-start | bytes 688136 | tf_op jit(solution)/shard_map/ppermute | solution.py:465
  7.0 0.7 %collective-permute-start.1 = (f32[7,32,256]{2,1,0:T(8,128)}, f32[7,32,256]{2,1,0:T(8,128)S(1)}, u32[]{:S(2)}, u32[]{:S(2)}) collective-permute-start(f32[7,32,256]{2,1,0:T(8,128)} %get-tuple-element.16.far), channel_id=1, source_target_pairs={{4,8},{12,16},{20,24},{8,4},{16,12},{24,20},{5,9},{13,17},{21,25},... | collective-permute-start | bytes 688136 | tf_op jit(solution)/shard_map/ppermute | solution.py:465
  7.7 8.1 %all-to-all-start = ((f32[64,4,128]{2,1,0:T(4,128)}), f32[64,4,128]{2,1,0:T(4,128)S(1)}, u32[]{:S(2)}, u32[]{:S(2)}) async-start(f32[64,4,128]{2,1,0:T(4,128)} %get-tuple-element.20), calls=%async_computation | async-start | bytes 262144 | tf_op jit(solution)/shard_map/all_to_all | solution.py:481
  15.9 0.0 collective-permute-start.2
  15.9 0.7 %collective-permute-start.3 = (f32[7,8,256]{2,1,0:T(8,128)}, f32[7,8,256]{2,1,0:T(8,128)S(1)}, u32[]{:S(2)}, u32[]{:S(2)}) collective-permute-start(f32[7,8,256]{2,1,0:T(8,128)} %get-tuple-element.18.other), channel_id=1, source_target_pairs={{1,2},{2,1},{5,6},{6,5},{9,10},{10,9},{13,14},{14,13},{17,18},{18,... | collective-permute-start | bytes 172040 | tf_op jit(solution)/shard_map/ppermute | solution.py:465
  16.5 0.0 copy-done
  16.5 0.0 copy-done.1
  16.6 0.0 copy-done.2
  16.6 0.0 copy-done.7
  16.6 0.0 copy-start.3
  16.6 2.0 %shard_map.87 = (f32[3,8,32,256]{3,2,1,0:T(8,128)S(1)}, f32[4,128]{1,0:T(4,128)S(1)}) custom-call(f32[3,8,32,256]{3,2,1,0:T(8,128)S(1)} %copy-done, f32[3,8,32,256]{3,2,1,0:T(8,128)S(1)} %copy-done.1, f32[8,32,256]{2,1,0:T(8,128)S(1)} %copy-done.2, f32[4,128]{1,0:T(4,128)S(1)} %copy-done.7), custom_call_target="tpu_custom_call" | custom-call | tf_op jit(solution)/shard_map/pallas_call | solution.py:258
  18.7 0.0 collective-permute-done.2.swap_in
  18.7 0.0 collective-permute-done.3.other_in
  18.7 0.0 collective-permute-done.near_in
  18.7 0.0 collective-permute-done.1.far_in
  18.7 0.0 copy-done.3
  18.8 0.9 %shard_map.88 = (f32[3,8,32,256]{3,2,1,0:T(8,128)S(1)}, f32[32,4,128]{2,1,0:T(4,128)}) custom-call(f32[3,8,32,256]{3,2,1,0:T(8,128)S(1)} %get-tuple-element.13.inside, f32[4,128]{1,0:T(4,128)S(1)} %get-tuple-element.14.moments, f32[7,32,256]{2,1,0:T(8,128)S(1)} %copy-done.3, f32[7,32,256]{2,1,0:T(8,128)S(1)} %copy-done.4, f32[7,8,256]{2,1,0:T(8,128)S(1)} %copy-done.5, ...), custom_call_target="tpu_custom_call" | custom-call | tf_op jit(solution)/shard_map/pallas_call | solution.py:313
  19.7 0.8 %all-to-all-done.load = f32[64,4,128]{2,1,0:T(4,128)S(1)} async-done(((f32[64,4,128]{2,1,0:T(4,128)}), f32[64,4,128]{2,1,0:T(4,128)S(1)}, u32[]{:S(2)}, u32[]{:S(2)}) %all-to-all-start) | async-done | bytes 131104 | tf_op jit(solution)/shard_map/all_to_all | solution.py:481
  20.5 5.7 %all-to-all-start.1 = ((f32[32,4,128]{2,1,0:T(4,128)}), f32[32,4,128]{2,1,0:T(4,128)S(1)}, u32[]{:S(2)}, u32[]{:S(2)}) async-start(f32[32,4,128]{2,1,0:T(4,128)} %get-tuple-element.21), calls=%async_computation.1 | async-start | bytes 131072 | tf_op jit(solution)/shard_map/all_to_all | solution.py:485
  26.2 3.0 %shard_map.89 = f32[3,8,32,256]{3,2,1,0:T(8,128)} custom-call(f32[3,8,32,256]{3,2,1,0:T(8,128)S(1)} %get-tuple-element.19.inside, f32[64,4,128]{2,1,0:T(4,128)S(1)} %all-to-all-done.load), custom_call_target="tpu_custom_call" | custom-call | tf_op jit(solution)/shard_map/pallas_call | solution.py:449
  29.2 4.2 %all-to-all-done.1.load = f32[32,4,128]{2,1,0:T(4,128)S(1)} async-done(((f32[32,4,128]{2,1,0:T(4,128)}), f32[32,4,128]{2,1,0:T(4,128)S(1)}, u32[]{:S(2)}, u32[]{:S(2)}) %all-to-all-start.1) | async-done | bytes 65568 | tf_op jit(solution)/shard_map/all_to_all | solution.py:485
  33.4 0.7 %shard_map.90 = f32[3,1,1,16]{3,2,1,0:T(1,128)} custom-call(f32[32,4,128]{2,1,0:T(4,128)S(1)} %all-to-all-done.1.load), custom_call_target="tpu_custom_call" | custom-call | tf_op jit(solution)/shard_map/pallas_call | solution.py:365
  (9 shorter events, 0.0 us)
Async XLA Ops:
  1.3 15.3 %copy-start = (f32[3,8,32,256]{3,2,1,0:T(8,128)S(1)}, f32[3,8,32,256]{3,2,1,0:T(8,128)}, u32[]{:S(2)}) copy-start(f32[3,8,32,256]{3,2,1,0:T(8,128)} %vort.3) | copy-start | bytes 2359300
  1.3 15.3 %copy-start.1 = (f32[3,8,32,256]{3,2,1,0:T(8,128)S(1)}, f32[3,8,32,256]{3,2,1,0:T(8,128)}, u32[]{:S(2)}) copy-start(f32[3,8,32,256]{3,2,1,0:T(8,128)} %velo.3) | copy-start | bytes 2359300
  4.0 12.5 %copy-start.2 = (f32[8,32,256]{2,1,0:T(8,128)S(1)}, f32[8,32,256]{2,1,0:T(8,128)}, u32[]{:S(2)}) copy-start(f32[8,32,256]{2,1,0:T(8,128)} %visc.3) | copy-start | bytes 786436
  4.0 14.7 %collective-permute-start = (f32[7,32,256]{2,1,0:T(8,128)}, f32[7,32,256]{2,1,0:T(8,128)S(1)}, u32[]{:S(2)}, u32[]{:S(2)}) collective-permute-start(f32[7,32,256]{2,1,0:T(8,128)} %get-tuple-element.15.near), channel_id=1, source_target_pairs={{0,4},{8,12},{16,20},{24,28},{4,0},{12,8},{20,16},{28,24},{1,5},{9... | collective-permute-start | bytes 688136 | tf_op jit(solution)/shard_map/ppermute | solution.py:465
  7.0 11.7 %collective-permute-start.1 = (f32[7,32,256]{2,1,0:T(8,128)}, f32[7,32,256]{2,1,0:T(8,128)S(1)}, u32[]{:S(2)}, u32[]{:S(2)}) collective-permute-start(f32[7,32,256]{2,1,0:T(8,128)} %get-tuple-element.16.far), channel_id=1, source_target_pairs={{4,8},{12,16},{20,24},{8,4},{16,12},{24,20},{5,9},{13,17},{21,25},... | collective-permute-start | bytes 688136 | tf_op jit(solution)/shard_map/ppermute | solution.py:465
  7.7 12.8 %all-to-all-start = ((f32[64,4,128]{2,1,0:T(4,128)}), f32[64,4,128]{2,1,0:T(4,128)S(1)}, u32[]{:S(2)}, u32[]{:S(2)}) async-start(f32[64,4,128]{2,1,0:T(4,128)} %get-tuple-element.20), calls=%async_computation | async-start | bytes 262144 | tf_op jit(solution)/shard_map/all_to_all | solution.py:481
  15.9 0.7 %copy-start.7 = (f32[4,128]{1,0:T(4,128)S(1)}, f32[4,128]{1,0:T(4,128)}, u32[]{:S(2)}) copy-start(f32[4,128]{1,0:T(4,128)} %get-tuple-element.12.tiles_in) | copy-start | bytes 6148
  15.9 2.8 %collective-permute-start.2 = (f32[7,8,256]{2,1,0:T(8,128)}, f32[7,8,256]{2,1,0:T(8,128)S(1)}, u32[]{:S(2)}, u32[]{:S(2)}) collective-permute-start(f32[7,8,256]{2,1,0:T(8,128)} %get-tuple-element.17.swap), channel_id=1, source_target_pairs={{0,1},{2,3},{1,0},{3,2},{4,5},{6,7},{5,4},{7,6},{8,9},{10,11},{9,8... | collective-permute-start | bytes 172040 | tf_op jit(solution)/shard_map/ppermute | solution.py:465
  15.9 2.8 %collective-permute-start.3 = (f32[7,8,256]{2,1,0:T(8,128)}, f32[7,8,256]{2,1,0:T(8,128)S(1)}, u32[]{:S(2)}, u32[]{:S(2)}) collective-permute-start(f32[7,8,256]{2,1,0:T(8,128)} %get-tuple-element.18.other), channel_id=1, source_target_pairs={{1,2},{2,1},{5,6},{6,5},{9,10},{10,9},{13,14},{14,13},{17,18},{18,... | collective-permute-start | bytes 172040 | tf_op jit(solution)/shard_map/ppermute | solution.py:465
  16.6 2.1 %copy-start.3 = (f32[7,32,256]{2,1,0:T(8,128)S(1)}, f32[7,32,256]{2,1,0:T(8,128)}, u32[]{:S(2)}) copy-start(f32[7,32,256]{2,1,0:T(8,128)} %get-tuple-element.15.near) | copy-start | bytes 688132
  16.6 2.1 %copy-start.4 = (f32[7,32,256]{2,1,0:T(8,128)S(1)}, f32[7,32,256]{2,1,0:T(8,128)}, u32[]{:S(2)}) copy-start(f32[7,32,256]{2,1,0:T(8,128)} %get-tuple-element.16.far) | copy-start | bytes 688132
  16.6 2.1 %copy-start.5 = (f32[7,8,256]{2,1,0:T(8,128)S(1)}, f32[7,8,256]{2,1,0:T(8,128)}, u32[]{:S(2)}) copy-start(f32[7,8,256]{2,1,0:T(8,128)} %get-tuple-element.17.swap) | copy-start | bytes 172036
  16.6 2.1 %copy-start.6 = (f32[7,8,256]{2,1,0:T(8,128)S(1)}, f32[7,8,256]{2,1,0:T(8,128)}, u32[]{:S(2)}) copy-start(f32[7,8,256]{2,1,0:T(8,128)} %get-tuple-element.18.other) | copy-start | bytes 172036
  20.5 12.9 %all-to-all-start.1 = ((f32[32,4,128]{2,1,0:T(4,128)}), f32[32,4,128]{2,1,0:T(4,128)S(1)}, u32[]{:S(2)}, u32[]{:S(2)}) async-start(f32[32,4,128]{2,1,0:T(4,128)} %get-tuple-element.21), calls=%async_computation.1 | async-start | bytes 131072 | tf_op jit(solution)/shard_map/all_to_all | solution.py:485

commit v20 on v16

--- a/solution.py
+++ b/solution.py
@@ -134,25 +134,25 @@
     copies.start(cells_in, cells)
     copies.start(dest_in, dest)
     copies.start(count_in, count)
+    even = lax.axis_index("pencil") % 2 == 0
+    for face, at in ((swap, jnp.where(even, cy - 1, 0)), (other, jnp.where(even, 0, cy - 1))):
+        copies.start(vort.at[:, :, at], face.at[0:3])
+        copies.start(velo.at[:, :, at], face.at[3:6])
+        copies.start(visc.at[:, at], face.at[6])
     even = lax.axis_index("slab") % 2 == 0
     for face, at in ((near, jnp.where(even, cx - 1, 0)), (far, jnp.where(even, 0, cx - 1))):
         copies.start(vort.at[:, at], face.at[0:3])
         copies.start(velo.at[:, at], face.at[3:6])
         copies.start(visc.at[at], face.at[6])
-    even = lax.axis_index("pencil") % 2 == 0
-    for face, at in ((swap, jnp.where(even, cy - 1, 0)), (other, jnp.where(even, 0, cy - 1))):
-        copies.start(vort.at[:, :, at], face.at[0:3])
-        copies.start(velo.at[:, :, at], face.at[3:6])
-        copies.start(visc.at[:, at], face.at[6])
     copies.wait(0, 4)
     pack_tiles(cap, cx * cy * nz, weights, cells, dest, count, packets)
     copies.start(packets, packets_out)
-    copies.wait(4, 10)
+    copies.wait(10, 16)
     copies.start(near, near_out)
     copies.start(far, far_out)
     tile_moments(cap, nz, packets, moments)
     copies.start(moments, moments_out)
-    copies.wait(10, 16)
+    copies.wait(4, 10)
     copies.start(swap, swap_out)
     copies.start(other, other_out)
     copies.wait(16, 22)

time: 34.5 us -> 34.5 us (level)
  no operation moved by 1% of the time
where the time goes in v20:
time: 34.5 us; the launch traced here: 34.1 us
  starting transfers between devices  18.2 us (53%)
  Pallas kernels  10.5 us (30%)
  waiting for transfers between devices  3.95 us (11%)
  between operations  1.49 us (4%)
    all_to_all x1, starting transfers between devices, per_device(): lax.all_to_all(packets, 'slab', 0, 0, axis_index_groups=[order], tiled=True)  8.15 us
    all_to_all x1, starting transfers between devices, per_device(): lax.all_to_all(load, ('slab', 'pencil'), 0, 0, axis_index_groups=[everyon...  5.74 us
    ppermute x4, starting transfers between devices, swapped(): return lax.ppermute(array, axis, up + [(j, i) for i, j in up])  4.33 us
    pallas_call x1, Pallas kernels, deposit(): pl.pallas_call(functools.partial(deposit_kernel, cap), out_shape=shaped(*...  4.04 us
    all_to_all x1, waiting for transfers between devices, per_device(): lax.all_to_all(load, ('slab', 'pencil'), 0, 0, axis_index_groups=[everyon...  3.12 us
    pallas_call x1, Pallas kernels, to_send(): pl.pallas_call(functools.partial(send_kernel, cap), out_shape=made, in_sp...  2.71 us
    pallas_call x1, Pallas kernels, inner(): pl.pallas_call(inner_kernel, out_shape=(shaped(*vort.shape), shaped(*tile...  2.05 us
    pallas_call x1, Pallas kernels, edges(): pl.pallas_call(edge_kernel, out_shape=(shaped(*inside.shape), load), in_s...  0.91 us
  transfers between devices with their start and end apart: 6, of which 2 were waited for; matrix products, arithmetic and copies ran while one was open for 0% of the time, Pallas kernels for 21%

profile of v20, /device:TPU:0, one launch (start us, length us, event | category | flops | bytes accessed | tf_op | source)
XLA Modules:
  0.0 34.1 jit_solution(1319276955320157525)
XLA Ops:
  1.3 0.0 copy-start
  1.3 0.0 copy-start.1
  1.3 2.7 %shard_map.86 = (f32[7,32,256]{2,1,0:T(8,128)}, f32[7,32,256]{2,1,0:T(8,128)}, f32[7,8,256]{2,1,0:T(8,128)}, f32[7,8,256]{2,1,0:T(8,128)}, f32[64,4,128]{2,1,0:T(4,128)}, /*index=5*/f32[4,128]{1,0:T(4,128)}) custom-call(f32[3,8,32,256]{3,2,1,0:T(8,128)} %vort.3, f32[3,8,32,256]{3,2,1,0:T(8,128)} %velo.3, f32[8,32,256]{2,1,0:T(8,128)} %visc.3, ...), custom_call_target="tpu_custom_call" | custom-call | tf_op jit(solution)/shard_map/pallas_call | solution.py:171
  4.0 0.0 copy-start.2
  4.0 3.0 %collective-permute-start = (f32[7,32,256]{2,1,0:T(8,128)}, f32[7,32,256]{2,1,0:T(8,128)S(1)}, u32[]{:S(2)}, u32[]{:S(2)}) collective-permute-start(f32[7,32,256]{2,1,0:T(8,128)} %get-tuple-element.15.near), channel_id=1, source_target_pairs={{0,4},{8,12},{16,20},{24,28},{4,0},{12,8},{20,16},{28,24},{1,5},{9... | collective-permute-start | bytes 688136 | tf_op jit(solution)/shard_map/ppermute | solution.py:465
  7.0 0.7 %collective-permute-start.1 = (f32[7,32,256]{2,1,0:T(8,128)}, f32[7,32,256]{2,1,0:T(8,128)S(1)}, u32[]{:S(2)}, u32[]{:S(2)}) collective-permute-start(f32[7,32,256]{2,1,0:T(8,128)} %get-tuple-element.16.far), channel_id=1, source_target_pairs={{4,8},{12,16},{20,24},{8,4},{16,12},{24,20},{5,9},{13,17},{21,25},... | collective-permute-start | bytes 688136 | tf_op jit(solution)/shard_map/ppermute | solution.py:465
  7.7 8.1 %all-to-all-start = ((f32[64,4,128]{2,1,0:T(4,128)}), f32[64,4,128]{2,1,0:T(4,128)S(1)}, u32[]{:S(2)}, u32[]{:S(2)}) async-start(f32[64,4,128]{2,1,0:T(4,128)} %get-tuple-element.20), calls=%async_computation | async-start | bytes 262144 | tf_op jit(solution)/shard_map/all_to_all | solution.py:481
  15.9 0.0 collective-permute-start.2
  15.9 0.7 %collective-permute-start.3 = (f32[7,8,256]{2,1,0:T(8,128)}, f32[7,8,256]{2,1,0:T(8,128)S(1)}, u32[]{:S(2)}, u32[]{:S(2)}) collective-permute-start(f32[7,8,256]{2,1,0:T(8,128)} %get-tuple-element.18.other), channel_id=1, source_target_pairs={{1,2},{2,1},{5,6},{6,5},{9,10},{10,9},{13,14},{14,13},{17,18},{18,... | collective-permute-start | bytes 172040 | tf_op jit(solution)/shard_map/ppermute | solution.py:465
  16.5 0.0 copy-done
  16.5 0.0 copy-done.1
  16.6 0.0 copy-done.2
  16.6 0.0 copy-start.3
  16.6 2.0 %shard_map.87 = (f32[3,8,32,256]{3,2,1,0:T(8,128)S(1)}, f32[4,128]{1,0:T(4,128)S(1)}) custom-call(f32[3,8,32,256]{3,2,1,0:T(8,128)S(1)} %copy-done, f32[3,8,32,256]{3,2,1,0:T(8,128)S(1)} %copy-done.1, f32[8,32,256]{2,1,0:T(8,128)S(1)} %copy-done.2, f32[4,128]{1,0:T(4,128)S(1)} %copy-done.7), custom_call_target="tpu_custom_call" | custom-call | tf_op jit(solution)/shard_map/pallas_call | solution.py:258
  18.7 0.0 collective-permute-done.2.swap_in
  18.7 0.0 collective-permute-done.3.other_in
  18.7 0.0 collective-permute-done.near_in
  18.7 0.0 collective-permute-done.1.far_in
  18.8 0.9 %shard_map.88 = (f32[3,8,32,256]{3,2,1,0:T(8,128)S(1)}, f32[32,4,128]{2,1,0:T(4,128)}) custom-call(f32[3,8,32,256]{3,2,1,0:T(8,128)S(1)} %get-tuple-element.13.inside, f32[4,128]{1,0:T(4,128)S(1)} %get-tuple-element.14.moments, f32[7,32,256]{2,1,0:T(8,128)S(1)} %copy-done.3, f32[7,32,256]{2,1,0:T(8,128)S(1)} %copy-done.4, f32[7,8,256]{2,1,0:T(8,128)S(1)} %copy-done.5, ...), custom_call_target="tpu_custom_call" | custom-call | tf_op jit(solution)/shard_map/pallas_call | solution.py:313
  19.7 0.8 %all-to-all-done.load = f32[64,4,128]{2,1,0:T(4,128)S(1)} async-done(((f32[64,4,128]{2,1,0:T(4,128)}), f32[64,4,128]{2,1,0:T(4,128)S(1)}, u32[]{:S(2)}, u32[]{:S(2)}) %all-to-all-start) | async-done | bytes 131104 | tf_op jit(solution)/shard_map/all_to_all | solution.py:481
  20.5 5.7 %all-to-all-start.1 = ((f32[32,4,128]{2,1,0:T(4,128)}), f32[32,4,128]{2,1,0:T(4,128)S(1)}, u32[]{:S(2)}, u32[]{:S(2)}) async-start(f32[32,4,128]{2,1,0:T(4,128)} %get-tuple-element.21), calls=%async_computation.1 | async-start | bytes 131072 | tf_op jit(solution)/shard_map/all_to_all | solution.py:485
  26.2 4.0 %shard_map.89 = f32[3,8,32,256]{3,2,1,0:T(8,128)} custom-call(f32[3,8,32,256]{3,2,1,0:T(8,128)S(1)} %get-tuple-element.19.inside, f32[64,4,128]{2,1,0:T(4,128)S(1)} %all-to-all-done.load), custom_call_target="tpu_custom_call" | custom-call | tf_op jit(solution)/shard_map/pallas_call | solution.py:449
  30.3 3.1 %all-to-all-done.1.load = f32[32,4,128]{2,1,0:T(4,128)S(1)} async-done(((f32[32,4,128]{2,1,0:T(4,128)}), f32[32,4,128]{2,1,0:T(4,128)S(1)}, u32[]{:S(2)}, u32[]{:S(2)}) %all-to-all-start.1) | async-done | bytes 65568 | tf_op jit(solution)/shard_map/all_to_all | solution.py:485
  33.4 0.7 %shard_map.90 = f32[3,1,1,16]{3,2,1,0:T(1,128)} custom-call(f32[32,4,128]{2,1,0:T(4,128)S(1)} %all-to-all-done.1.load), custom_call_target="tpu_custom_call" | custom-call | tf_op jit(solution)/shard_map/pallas_call | solution.py:365
  (9 shorter events, 0.0 us)
Async XLA Ops:
  1.3 15.3 %copy-start = (f32[3,8,32,256]{3,2,1,0:T(8,128)S(1)}, f32[3,8,32,256]{3,2,1,0:T(8,128)}, u32[]{:S(2)}) copy-start(f32[3,8,32,256]{3,2,1,0:T(8,128)} %vort.3) | copy-start | bytes 2359300
  1.3 15.3 %copy-start.1 = (f32[3,8,32,256]{3,2,1,0:T(8,128)S(1)}, f32[3,8,32,256]{3,2,1,0:T(8,128)}, u32[]{:S(2)}) copy-start(f32[3,8,32,256]{3,2,1,0:T(8,128)} %velo.3) | copy-start | bytes 2359300
  4.0 12.5 %copy-start.2 = (f32[8,32,256]{2,1,0:T(8,128)S(1)}, f32[8,32,256]{2,1,0:T(8,128)}, u32[]{:S(2)}) copy-start(f32[8,32,256]{2,1,0:T(8,128)} %visc.3) | copy-start | bytes 786436
  4.0 14.7 %collective-permute-start = (f32[7,32,256]{2,1,0:T(8,128)}, f32[7,32,256]{2,1,0:T(8,128)S(1)}, u32[]{:S(2)}, u32[]{:S(2)}) collective-permute-start(f32[7,32,256]{2,1,0:T(8,128)} %get-tuple-element.15.near), channel_id=1, source_target_pairs={{0,4},{8,12},{16,20},{24,28},{4,0},{12,8},{20,16},{28,24},{1,5},{9... | collective-permute-start | bytes 688136 | tf_op jit(solution)/shard_map/ppermute | solution.py:465
  7.0 11.7 %collective-permute-start.1 = (f32[7,32,256]{2,1,0:T(8,128)}, f32[7,32,256]{2,1,0:T(8,128)S(1)}, u32[]{:S(2)}, u32[]{:S(2)}) collective-permute-start(f32[7,32,256]{2,1,0:T(8,128)} %get-tuple-element.16.far), channel_id=1, source_target_pairs={{4,8},{12,16},{20,24},{8,4},{16,12},{24,20},{5,9},{13,17},{21,25},... | collective-permute-start | bytes 688136 | tf_op jit(solution)/shard_map/ppermute | solution.py:465
  7.7 12.8 %all-to-all-start = ((f32[64,4,128]{2,1,0:T(4,128)}), f32[64,4,128]{2,1,0:T(4,128)S(1)}, u32[]{:S(2)}, u32[]{:S(2)}) async-start(f32[64,4,128]{2,1,0:T(4,128)} %get-tuple-element.20), calls=%async_computation | async-start | bytes 262144 | tf_op jit(solution)/shard_map/all_to_all | solution.py:481
  15.9 0.7 %copy-start.7 = (f32[4,128]{1,0:T(4,128)S(1)}, f32[4,128]{1,0:T(4,128)}, u32[]{:S(2)}) copy-start(f32[4,128]{1,0:T(4,128)} %get-tuple-element.12.tiles_in) | copy-start | bytes 6148
  15.9 2.8 %collective-permute-start.2 = (f32[7,8,256]{2,1,0:T(8,128)}, f32[7,8,256]{2,1,0:T(8,128)S(1)}, u32[]{:S(2)}, u32[]{:S(2)}) collective-permute-start(f32[7,8,256]{2,1,0:T(8,128)} %get-tuple-element.17.swap), channel_id=1, source_target_pairs={{0,1},{2,3},{1,0},{3,2},{4,5},{6,7},{5,4},{7,6},{8,9},{10,11},{9,8... | collective-permute-start | bytes 172040 | tf_op jit(solution)/shard_map/ppermute | solution.py:465
  15.9 2.8 %collective-permute-start.3 = (f32[7,8,256]{2,1,0:T(8,128)}, f32[7,8,256]{2,1,0:T(8,128)S(1)}, u32[]{:S(2)}, u32[]{:S(2)}) collective-permute-start(f32[7,8,256]{2,1,0:T(8,128)} %get-tuple-element.18.other), channel_id=1, source_target_pairs={{1,2},{2,1},{5,6},{6,5},{9,10},{10,9},{13,14},{14,13},{17,18},{18,... | collective-permute-start | bytes 172040 | tf_op jit(solution)/shard_map/ppermute | solution.py:465
  16.6 2.1 %copy-start.3 = (f32[7,32,256]{2,1,0:T(8,128)S(1)}, f32[7,32,256]{2,1,0:T(8,128)}, u32[]{:S(2)}) copy-start(f32[7,32,256]{2,1,0:T(8,128)} %get-tuple-element.15.near) | copy-start | bytes 688132
  16.6 2.1 %copy-start.4 = (f32[7,32,256]{2,1,0:T(8,128)S(1)}, f32[7,32,256]{2,1,0:T(8,128)}, u32[]{:S(2)}) copy-start(f32[7,32,256]{2,1,0:T(8,128)} %get-tuple-element.16.far) | copy-start | bytes 688132
  16.6 2.1 %copy-start.5 = (f32[7,8,256]{2,1,0:T(8,128)S(1)}, f32[7,8,256]{2,1,0:T(8,128)}, u32[]{:S(2)}) copy-start(f32[7,8,256]{2,1,0:T(8,128)} %get-tuple-element.17.swap) | copy-start | bytes 172036
  16.6 2.1 %copy-start.6 = (f32[7,8,256]{2,1,0:T(8,128)S(1)}, f32[7,8,256]{2,1,0:T(8,128)}, u32[]{:S(2)}) copy-start(f32[7,8,256]{2,1,0:T(8,128)} %get-tuple-element.18.other) | copy-start | bytes 172036
  20.5 12.9 %all-to-all-start.1 = ((f32[32,4,128]{2,1,0:T(4,128)}), f32[32,4,128]{2,1,0:T(4,128)S(1)}, u32[]{:S(2)}, u32[]{:S(2)}) async-start(f32[32,4,128]{2,1,0:T(4,128)} %get-tuple-element.21), calls=%async_computation.1 | async-start | bytes 131072 | tf_op jit(solution)/shard_map/all_to_all | solution.py:485

commit v21 on v18

--- a/solution.py
+++ b/solution.py
@@ -33,7 +33,7 @@
 def thirds(w):
     high, rest = split(w)
     middle, low = split(rest)
-    return [piece.astype(jnp.bfloat16) for piece in (high, middle, low)]
+    return [high, middle, low]
 
 
 def outward(count):
@@ -60,7 +60,7 @@
     rows = [weights[0], weights[1], weights[2], cells[...].astype(jnp.float32)]
     found = jnp.dot(
         jnp.concatenate([placed] * 3, axis=1).astype(jnp.bfloat16),
-        jnp.concatenate(thirds(jnp.concatenate(rows, axis=1)), axis=0),
+        jnp.concatenate(thirds(jnp.concatenate(rows, axis=1)), axis=0).astype(jnp.bfloat16),
         preferred_element_type=jnp.float32,
     )
     length = cells.shape[1]
@@ -242,7 +242,8 @@
     lane = lax.broadcasted_iota(jnp.int32, shape, 1)
     pick = (lane == lax.axis_index("slab") * (nz // CB) + level).astype(jnp.float32).astype(jnp.bfloat16)
     rows = jnp.concatenate(totals + [jnp.zeros_like(totals[0])], axis=0)
-    found = jnp.dot(jnp.concatenate(thirds(rows), axis=0), pick, preferred_element_type=jnp.float32)
+    pieces = jnp.concatenate(thirds(rows), axis=0).astype(jnp.bfloat16)
+    found = jnp.dot(pieces, pick, preferred_element_type=jnp.float32)
     return found[0:4] + (found[4:8] + found[8:12])
 
 

time: 34.6 us -> 34.6 us (level)
  waiting for transfers between devices: 3.14 us -> 4.99 us
  Pallas kernels: 11.4 us -> 9.55 us
    all_to_all x1, waiting for transfers between devices: 2.31 us -> 4.16 us  [per_device(): lax.all_to_all(load, ('slab', 'pencil'), 0, 0, axis_index_groups=[everyon...]
    pallas_call x1, Pallas kernels: 4.85 us -> 2.99 us  [deposit(): pl.pallas_call(functools.partial(deposit_kernel, cap), out_shape=shaped(*...]
  transfers between devices with their start and end apart: 6 -> 6, of which waited for: 2 -> 2; matrix products, arithmetic and copies ran while one was open for 0% -> 0% of each run, Pallas kernels for 23% -> 17%
where the time goes in v21:
time: 34.6 us; the launch traced here: 34.3 us
  starting transfers between devices  18.2 us (53%)
  Pallas kernels  9.55 us (28%)
  waiting for transfers between devices  4.99 us (14%)
  between operations  1.49 us (4%)
    all_to_all x1, starting transfers between devices, per_device(): lax.all_to_all(packets, 'slab', 0, 0, axis_index_groups=[order], tiled=True)  8.15 us
    all_to_all x1, starting transfers between devices, per_device(): lax.all_to_all(load, ('slab', 'pencil'), 0, 0, axis_index_groups=[everyon...  5.74 us
    ppermute x4, starting transfers between devices, swapped(): return lax.ppermute(array, axis, up + [(j, i) for i, j in up])  4.33 us
    all_to_all x1, waiting for transfers between devices, per_device(): lax.all_to_all(load, ('slab', 'pencil'), 0, 0, axis_index_groups=[everyon...  4.16 us
    pallas_call x1, Pallas kernels, deposit(): pl.pallas_call(functools.partial(deposit_kernel, cap), out_shape=shaped(*...  2.99 us
    pallas_call x1, Pallas kernels, to_send(): pl.pallas_call(functools.partial(send_kernel, cap), out_shape=made, in_sp...  2.85 us
    pallas_call x1, Pallas kernels, inner(): pl.pallas_call(inner_kernel, out_shape=(shaped(*vort.shape), shaped(*tile...  2.05 us
    pallas_call x1, Pallas kernels, edges(): pl.pallas_call(edge_kernel, out_shape=(shaped(*inside.shape), load), in_s...  0.91 us
  transfers between devices with their start and end apart: 6, of which 2 were waited for; matrix products, arithmetic and copies ran while one was open for 0% of the time, Pallas kernels for 17%

profile of v21, /device:TPU:0, one launch (start us, length us, event | category | flops | bytes accessed | tf_op | source)
XLA Modules:
  0.0 34.3 jit_solution(4644789938010351758)
XLA Ops:
  1.3 0.0 copy-start
  1.3 2.9 %shard_map.86 = (f32[7,32,256]{2,1,0:T(8,128)}, f32[7,32,256]{2,1,0:T(8,128)}, f32[7,8,256]{2,1,0:T(8,128)}, f32[7,8,256]{2,1,0:T(8,128)}, f32[64,4,128]{2,1,0:T(4,128)}, /*index=5*/f32[4,128]{1,0:T(4,128)}) custom-call(f32[3,8,32,256]{3,2,1,0:T(8,128)} %vort.3, f32[3,8,32,256]{3,2,1,0:T(8,128)} %velo.3, f32[8,32,256]{2,1,0:T(8,128)} %visc.3, ...), custom_call_target="tpu_custom_call" | custom-call | tf_op jit(solution)/shard_map/pallas_call | solution.py:171
  4.2 0.0 copy-start.2
  4.2 3.0 %collective-permute-start = (f32[7,32,256]{2,1,0:T(8,128)}, f32[7,32,256]{2,1,0:T(8,128)S(1)}, u32[]{:S(2)}, u32[]{:S(2)}) collective-permute-start(f32[7,32,256]{2,1,0:T(8,128)} %get-tuple-element.15.near), channel_id=1, source_target_pairs={{0,4},{8,12},{16,20},{24,28},{4,0},{12,8},{20,16},{28,24},{1,5},{9... | collective-permute-start | bytes 688136 | tf_op jit(solution)/shard_map/ppermute | solution.py:466
  7.2 0.7 %collective-permute-start.1 = (f32[7,32,256]{2,1,0:T(8,128)}, f32[7,32,256]{2,1,0:T(8,128)S(1)}, u32[]{:S(2)}, u32[]{:S(2)}) collective-permute-start(f32[7,32,256]{2,1,0:T(8,128)} %get-tuple-element.16.far), channel_id=1, source_target_pairs={{4,8},{12,16},{20,24},{8,4},{16,12},{24,20},{5,9},{13,17},{21,25},... | collective-permute-start | bytes 688136 | tf_op jit(solution)/shard_map/ppermute | solution.py:466
  7.8 8.1 %all-to-all-start = ((f32[64,4,128]{2,1,0:T(4,128)}), f32[64,4,128]{2,1,0:T(4,128)S(1)}, u32[]{:S(2)}, u32[]{:S(2)}) async-start(f32[64,4,128]{2,1,0:T(4,128)} %get-tuple-element.20), calls=%async_computation | async-start | bytes 262144 | tf_op jit(solution)/shard_map/all_to_all | solution.py:482
  16.0 0.0 collective-permute-start.2
  16.0 0.7 %collective-permute-start.3 = (f32[7,8,256]{2,1,0:T(8,128)}, f32[7,8,256]{2,1,0:T(8,128)S(1)}, u32[]{:S(2)}, u32[]{:S(2)}) collective-permute-start(f32[7,8,256]{2,1,0:T(8,128)} %get-tuple-element.18.other), channel_id=1, source_target_pairs={{1,2},{2,1},{5,6},{6,5},{9,10},{10,9},{13,14},{14,13},{17,18},{18,... | collective-permute-start | bytes 172040 | tf_op jit(solution)/shard_map/ppermute | solution.py:466
  16.7 0.0 copy-done
  16.7 0.0 copy-done.1
  16.7 0.0 copy-done.2
  16.7 0.0 copy-done.7
  16.7 0.0 copy-start.3
  16.8 2.0 %shard_map.87 = (f32[3,8,32,256]{3,2,1,0:T(8,128)S(1)}, f32[4,128]{1,0:T(4,128)S(1)}) custom-call(f32[3,8,32,256]{3,2,1,0:T(8,128)S(1)} %copy-done, f32[3,8,32,256]{3,2,1,0:T(8,128)S(1)} %copy-done.1, f32[8,32,256]{2,1,0:T(8,128)S(1)} %copy-done.2, f32[4,128]{1,0:T(4,128)S(1)} %copy-done.7), custom_call_target="tpu_custom_call" | custom-call | tf_op jit(solution)/shard_map/pallas_call | solution.py:259
  18.8 0.0 collective-permute-done.2.swap_in
  18.8 0.0 collective-permute-done.3.other_in
  18.8 0.0 collective-permute-done.near_in
  18.8 0.0 collective-permute-done.1.far_in
  18.9 0.9 %shard_map.88 = (f32[3,8,32,256]{3,2,1,0:T(8,128)S(1)}, f32[32,4,128]{2,1,0:T(4,128)}) custom-call(f32[3,8,32,256]{3,2,1,0:T(8,128)S(1)} %get-tuple-element.13.inside, f32[4,128]{1,0:T(4,128)S(1)} %get-tuple-element.14.moments, f32[7,32,256]{2,1,0:T(8,128)S(1)} %copy-done.3, f32[7,32,256]{2,1,0:T(8,128)S(1)} %copy-done.4, f32[7,8,256]{2,1,0:T(8,128)S(1)} %copy-done.5, ...), custom_call_target="tpu_custom_call" | custom-call | tf_op jit(solution)/shard_map/pallas_call | solution.py:314
  19.8 0.8 %all-to-all-done.load = f32[64,4,128]{2,1,0:T(4,128)S(1)} async-done(((f32[64,4,128]{2,1,0:T(4,128)}), f32[64,4,128]{2,1,0:T(4,128)S(1)}, u32[]{:S(2)}, u32[]{:S(2)}) %all-to-all-start) | async-done | bytes 131104 | tf_op jit(solution)/shard_map/all_to_all | solution.py:482
  20.6 5.7 %all-to-all-start.1 = ((f32[32,4,128]{2,1,0:T(4,128)}), f32[32,4,128]{2,1,0:T(4,128)S(1)}, u32[]{:S(2)}, u32[]{:S(2)}) async-start(f32[32,4,128]{2,1,0:T(4,128)} %get-tuple-element.21), calls=%async_computation.1 | async-start | bytes 131072 | tf_op jit(solution)/shard_map/all_to_all | solution.py:486
  26.4 3.0 %shard_map.89 = f32[3,8,32,256]{3,2,1,0:T(8,128)} custom-call(f32[3,8,32,256]{3,2,1,0:T(8,128)S(1)} %get-tuple-element.19.inside, f32[64,4,128]{2,1,0:T(4,128)S(1)} %all-to-all-done.load), custom_call_target="tpu_custom_call" | custom-call | tf_op jit(solution)/shard_map/pallas_call | solution.py:450
  29.4 4.2 %all-to-all-done.1.load = f32[32,4,128]{2,1,0:T(4,128)S(1)} async-done(((f32[32,4,128]{2,1,0:T(4,128)}), f32[32,4,128]{2,1,0:T(4,128)S(1)}, u32[]{:S(2)}, u32[]{:S(2)}) %all-to-all-start.1) | async-done | bytes 65568 | tf_op jit(solution)/shard_map/all_to_all | solution.py:486
  33.5 0.7 %shard_map.90 = f32[3,1,1,16]{3,2,1,0:T(1,128)} custom-call(f32[32,4,128]{2,1,0:T(4,128)S(1)} %all-to-all-done.1.load), custom_call_target="tpu_custom_call" | custom-call | tf_op jit(solution)/shard_map/pallas_call | solution.py:366
  (9 shorter events, 0.0 us)
Async XLA Ops:
  1.3 15.4 %copy-start = (f32[3,8,32,256]{3,2,1,0:T(8,128)S(1)}, f32[3,8,32,256]{3,2,1,0:T(8,128)}, u32[]{:S(2)}) copy-start(f32[3,8,32,256]{3,2,1,0:T(8,128)} %vort.3) | copy-start | bytes 2359300
  1.3 15.4 %copy-start.1 = (f32[3,8,32,256]{3,2,1,0:T(8,128)S(1)}, f32[3,8,32,256]{3,2,1,0:T(8,128)}, u32[]{:S(2)}) copy-start(f32[3,8,32,256]{3,2,1,0:T(8,128)} %velo.3) | copy-start | bytes 2359300
  4.2 12.5 %copy-start.2 = (f32[8,32,256]{2,1,0:T(8,128)S(1)}, f32[8,32,256]{2,1,0:T(8,128)}, u32[]{:S(2)}) copy-start(f32[8,32,256]{2,1,0:T(8,128)} %visc.3) | copy-start | bytes 786436
  4.2 14.7 %collective-permute-start = (f32[7,32,256]{2,1,0:T(8,128)}, f32[7,32,256]{2,1,0:T(8,128)S(1)}, u32[]{:S(2)}, u32[]{:S(2)}) collective-permute-start(f32[7,32,256]{2,1,0:T(8,128)} %get-tuple-element.15.near), channel_id=1, source_target_pairs={{0,4},{8,12},{16,20},{24,28},{4,0},{12,8},{20,16},{28,24},{1,5},{9... | collective-permute-start | bytes 688136 | tf_op jit(solution)/shard_map/ppermute | solution.py:466
  7.2 11.7 %collective-permute-start.1 = (f32[7,32,256]{2,1,0:T(8,128)}, f32[7,32,256]{2,1,0:T(8,128)S(1)}, u32[]{:S(2)}, u32[]{:S(2)}) collective-permute-start(f32[7,32,256]{2,1,0:T(8,128)} %get-tuple-element.16.far), channel_id=1, source_target_pairs={{4,8},{12,16},{20,24},{8,4},{16,12},{24,20},{5,9},{13,17},{21,25},... | collective-permute-start | bytes 688136 | tf_op jit(solution)/shard_map/ppermute | solution.py:466
  7.8 12.8 %all-to-all-start = ((f32[64,4,128]{2,1,0:T(4,128)}), f32[64,4,128]{2,1,0:T(4,128)S(1)}, u32[]{:S(2)}, u32[]{:S(2)}) async-start(f32[64,4,128]{2,1,0:T(4,128)} %get-tuple-element.20), calls=%async_computation | async-start | bytes 262144 | tf_op jit(solution)/shard_map/all_to_all | solution.py:482
  16.0 0.7 %copy-start.7 = (f32[4,128]{1,0:T(4,128)S(1)}, f32[4,128]{1,0:T(4,128)}, u32[]{:S(2)}) copy-start(f32[4,128]{1,0:T(4,128)} %get-tuple-element.12.tiles_in) | copy-start | bytes 6148
  16.0 2.8 %collective-permute-start.2 = (f32[7,8,256]{2,1,0:T(8,128)}, f32[7,8,256]{2,1,0:T(8,128)S(1)}, u32[]{:S(2)}, u32[]{:S(2)}) collective-permute-start(f32[7,8,256]{2,1,0:T(8,128)} %get-tuple-element.17.swap), channel_id=1, source_target_pairs={{0,1},{2,3},{1,0},{3,2},{4,5},{6,7},{5,4},{7,6},{8,9},{10,11},{9,8... | collective-permute-start | bytes 172040 | tf_op jit(solution)/shard_map/ppermute | solution.py:466
  16.0 2.8 %collective-permute-start.3 = (f32[7,8,256]{2,1,0:T(8,128)}, f32[7,8,256]{2,1,0:T(8,128)S(1)}, u32[]{:S(2)}, u32[]{:S(2)}) collective-permute-start(f32[7,8,256]{2,1,0:T(8,128)} %get-tuple-element.18.other), channel_id=1, source_target_pairs={{1,2},{2,1},{5,6},{6,5},{9,10},{10,9},{13,14},{14,13},{17,18},{18,... | collective-permute-start | bytes 172040 | tf_op jit(solution)/shard_map/ppermute | solution.py:466
  16.7 2.1 %copy-start.3 = (f32[7,32,256]{2,1,0:T(8,128)S(1)}, f32[7,32,256]{2,1,0:T(8,128)}, u32[]{:S(2)}) copy-start(f32[7,32,256]{2,1,0:T(8,128)} %get-tuple-element.15.near) | copy-start | bytes 688132
  16.7 2.1 %copy-start.4 = (f32[7,32,256]{2,1,0:T(8,128)S(1)}, f32[7,32,256]{2,1,0:T(8,128)}, u32[]{:S(2)}) copy-start(f32[7,32,256]{2,1,0:T(8,128)} %get-tuple-element.16.far) | copy-start | bytes 688132
  16.7 2.1 %copy-start.5 = (f32[7,8,256]{2,1,0:T(8,128)S(1)}, f32[7,8,256]{2,1,0:T(8,128)}, u32[]{:S(2)}) copy-start(f32[7,8,256]{2,1,0:T(8,128)} %get-tuple-element.17.swap) | copy-start | bytes 172036
  16.7 2.1 %copy-start.6 = (f32[7,8,256]{2,1,0:T(8,128)S(1)}, f32[7,8,256]{2,1,0:T(8,128)}, u32[]{:S(2)}) copy-start(f32[7,8,256]{2,1,0:T(8,128)} %get-tuple-element.18.other) | copy-start | bytes 172036
  20.6 12.9 %all-to-all-start.1 = ((f32[32,4,128]{2,1,0:T(4,128)}), f32[32,4,128]{2,1,0:T(4,128)S(1)}, u32[]{:S(2)}, u32[]{:S(2)}) async-start(f32[32,4,128]{2,1,0:T(4,128)} %get-tuple-element.21), calls=%async_computation.1 | async-start | bytes 131072 | tf_op jit(solution)/shard_map/all_to_all | solution.py:486

commit v22 on v21

--- a/solution.py
+++ b/solution.py
@@ -147,11 +147,11 @@
     copies.wait(0, 4)
     pack_tiles(cap, cx * cy * nz, weights, cells, dest, count, packets)
     copies.start(packets, packets_out)
-    tile_moments(cap, nz, packets, moments)
-    copies.start(moments, moments_out)
     copies.wait(4, 10)
     copies.start(near, near_out)
     copies.start(far, far_out)
+    tile_moments(cap, nz, packets, moments)
+    copies.start(moments, moments_out)
     copies.wait(10, 16)
     copies.start(swap, swap_out)
     copies.start(other, other_out)

time: 34.6 us -> 34.5 us (level)
  waiting for transfers between devices: 4.99 us -> 3.13 us
  Pallas kernels: 9.55 us -> 11.3 us
    all_to_all x1, waiting for transfers between devices: 4.16 us -> 2.3 us  [per_device(): lax.all_to_all(load, ('slab', 'pencil'), 0, 0, axis_index_groups=[everyon...]
    pallas_call x1, Pallas kernels: 2.99 us -> 4.86 us  [deposit(): pl.pallas_call(functools.partial(deposit_kernel, cap), out_shape=shaped(*...]
  transfers between devices with their start and end apart: 6 -> 6, of which waited for: 2 -> 2; matrix products, arithmetic and copies ran while one was open for 0% -> 0% of each run, Pallas kernels for 17% -> 23%
where the time goes in v22:
time: 34.5 us; the launch traced here: 34.1 us
  starting transfers between devices  18.2 us (53%)
  Pallas kernels  11.3 us (33%)
  waiting for transfers between devices  3.13 us (9%)
  between operations  1.49 us (4%)
    all_to_all x1, starting transfers between devices, per_device(): lax.all_to_all(packets, 'slab', 0, 0, axis_index_groups=[order], tiled=True)  8.15 us
    all_to_all x1, starting transfers between devices, per_device(): lax.all_to_all(load, ('slab', 'pencil'), 0, 0, axis_index_groups=[everyon...  5.74 us
    pallas_call x1, Pallas kernels, deposit(): pl.pallas_call(functools.partial(deposit_kernel, cap), out_shape=shaped(*...  4.86 us
    ppermute x4, starting transfers between devices, swapped(): return lax.ppermute(array, axis, up + [(j, i) for i, j in up])  4.33 us
    pallas_call x1, Pallas kernels, to_send(): pl.pallas_call(functools.partial(send_kernel, cap), out_shape=made, in_sp...  2.71 us
    all_to_all x1, waiting for transfers between devices, per_device(): lax.all_to_all(load, ('slab', 'pencil'), 0, 0, axis_index_groups=[everyon...  2.3 us
    pallas_call x1, Pallas kernels, inner(): pl.pallas_call(inner_kernel, out_shape=(shaped(*vort.shape), shaped(*tile...  2.05 us
    pallas_call x1, Pallas kernels, edges(): pl.pallas_call(edge_kernel, out_shape=(shaped(*inside.shape), load), in_s...  0.91 us
  transfers between devices with their start and end apart: 6, of which 2 were waited for; matrix products, arithmetic and copies ran while one was open for 0% of the time, Pallas kernels for 23%

profile of v22, /device:TPU:0, one launch (start us, length us, event | category | flops | bytes accessed | tf_op | source)
XLA Modules:
  0.0 34.1 jit_solution(16054104906352140418)
XLA Ops:
  1.3 0.0 copy-start
  1.3 0.0 copy-start.1
  1.3 2.7 %shard_map.86 = (f32[7,32,256]{2,1,0:T(8,128)}, f32[7,32,256]{2,1,0:T(8,128)}, f32[7,8,256]{2,1,0:T(8,128)}, f32[7,8,256]{2,1,0:T(8,128)}, f32[64,4,128]{2,1,0:T(4,128)}, /*index=5*/f32[4,128]{1,0:T(4,128)}) custom-call(f32[3,8,32,256]{3,2,1,0:T(8,128)} %vort.3, f32[3,8,32,256]{3,2,1,0:T(8,128)} %velo.3, f32[8,32,256]{2,1,0:T(8,128)} %visc.3, ...), custom_call_target="tpu_custom_call" | custom-call | tf_op jit(solution)/shard_map/pallas_call | solution.py:171
  4.0 0.0 copy-start.2
  4.0 3.0 %collective-permute-start = (f32[7,32,256]{2,1,0:T(8,128)}, f32[7,32,256]{2,1,0:T(8,128)S(1)}, u32[]{:S(2)}, u32[]{:S(2)}) collective-permute-start(f32[7,32,256]{2,1,0:T(8,128)} %get-tuple-element.15.near), channel_id=1, source_target_pairs={{0,4},{8,12},{16,20},{24,28},{4,0},{12,8},{20,16},{28,24},{1,5},{9... | collective-permute-start | bytes 688136 | tf_op jit(solution)/shard_map/ppermute | solution.py:466
  7.0 0.7 %collective-permute-start.1 = (f32[7,32,256]{2,1,0:T(8,128)}, f32[7,32,256]{2,1,0:T(8,128)S(1)}, u32[]{:S(2)}, u32[]{:S(2)}) collective-permute-start(f32[7,32,256]{2,1,0:T(8,128)} %get-tuple-element.16.far), channel_id=1, source_target_pairs={{4,8},{12,16},{20,24},{8,4},{16,12},{24,20},{5,9},{13,17},{21,25},... | collective-permute-start | bytes 688136 | tf_op jit(solution)/shard_map/ppermute | solution.py:466
  7.7 8.1 %all-to-all-start = ((f32[64,4,128]{2,1,0:T(4,128)}), f32[64,4,128]{2,1,0:T(4,128)S(1)}, u32[]{:S(2)}, u32[]{:S(2)}) async-start(f32[64,4,128]{2,1,0:T(4,128)} %get-tuple-element.20), calls=%async_computation | async-start | bytes 262144 | tf_op jit(solution)/shard_map/all_to_all | solution.py:482
  15.9 0.0 collective-permute-start.2
  15.9 0.7 %collective-permute-start.3 = (f32[7,8,256]{2,1,0:T(8,128)}, f32[7,8,256]{2,1,0:T(8,128)S(1)}, u32[]{:S(2)}, u32[]{:S(2)}) collective-permute-start(f32[7,8,256]{2,1,0:T(8,128)} %get-tuple-element.18.other), channel_id=1, source_target_pairs={{1,2},{2,1},{5,6},{6,5},{9,10},{10,9},{13,14},{14,13},{17,18},{18,... | collective-permute-start | bytes 172040 | tf_op jit(solution)/shard_map/ppermute | solution.py:466
  16.5 0.0 copy-done
  16.5 0.0 copy-done.1
  16.6 0.0 copy-done.2
  16.6 0.0 copy-start.3
  16.6 2.0 %shard_map.87 = (f32[3,8,32,256]{3,2,1,0:T(8,128)S(1)}, f32[4,128]{1,0:T(4,128)S(1)}) custom-call(f32[3,8,32,256]{3,2,1,0:T(8,128)S(1)} %copy-done, f32[3,8,32,256]{3,2,1,0:T(8,128)S(1)} %copy-done.1, f32[8,32,256]{2,1,0:T(8,128)S(1)} %copy-done.2, f32[4,128]{1,0:T(4,128)S(1)} %copy-done.7), custom_call_target="tpu_custom_call" | custom-call | tf_op jit(solution)/shard_map/pallas_call | solution.py:259
  18.7 0.0 collective-permute-done.2.swap_in
  18.7 0.0 collective-permute-done.3.other_in
  18.7 0.0 collective-permute-done.near_in
  18.7 0.0 collective-permute-done.1.far_in
  18.8 0.9 %shard_map.88 = (f32[3,8,32,256]{3,2,1,0:T(8,128)S(1)}, f32[32,4,128]{2,1,0:T(4,128)}) custom-call(f32[3,8,32,256]{3,2,1,0:T(8,128)S(1)} %get-tuple-element.13.inside, f32[4,128]{1,0:T(4,128)S(1)} %get-tuple-element.14.moments, f32[7,32,256]{2,1,0:T(8,128)S(1)} %copy-done.3, f32[7,32,256]{2,1,0:T(8,128)S(1)} %copy-done.4, f32[7,8,256]{2,1,0:T(8,128)S(1)} %copy-done.5, ...), custom_call_target="tpu_custom_call" | custom-call | tf_op jit(solution)/shard_map/pallas_call | solution.py:314
  19.7 0.8 %all-to-all-done.load = f32[64,4,128]{2,1,0:T(4,128)S(1)} async-done(((f32[64,4,128]{2,1,0:T(4,128)}), f32[64,4,128]{2,1,0:T(4,128)S(1)}, u32[]{:S(2)}, u32[]{:S(2)}) %all-to-all-start) | async-done | bytes 131104 | tf_op jit(solution)/shard_map/all_to_all | solution.py:482
  20.5 5.7 %all-to-all-start.1 = ((f32[32,4,128]{2,1,0:T(4,128)}), f32[32,4,128]{2,1,0:T(4,128)S(1)}, u32[]{:S(2)}, u32[]{:S(2)}) async-start(f32[32,4,128]{2,1,0:T(4,128)} %get-tuple-element.21), calls=%async_computation.1 | async-start | bytes 131072 | tf_op jit(solution)/shard_map/all_to_all | solution.py:486
  26.2 4.9 %shard_map.89 = f32[3,8,32,256]{3,2,1,0:T(8,128)} custom-call(f32[3,8,32,256]{3,2,1,0:T(8,128)S(1)} %get-tuple-element.19.inside, f32[64,4,128]{2,1,0:T(4,128)S(1)} %all-to-all-done.load), custom_call_target="tpu_custom_call" | custom-call | tf_op jit(solution)/shard_map/pallas_call | solution.py:450
  31.1 2.3 %all-to-all-done.1.load = f32[32,4,128]{2,1,0:T(4,128)S(1)} async-done(((f32[32,4,128]{2,1,0:T(4,128)}), f32[32,4,128]{2,1,0:T(4,128)S(1)}, u32[]{:S(2)}, u32[]{:S(2)}) %all-to-all-start.1) | async-done | bytes 65568 | tf_op jit(solution)/shard_map/all_to_all | solution.py:486
  33.4 0.7 %shard_map.90 = f32[3,1,1,16]{3,2,1,0:T(1,128)} custom-call(f32[32,4,128]{2,1,0:T(4,128)S(1)} %all-to-all-done.1.load), custom_call_target="tpu_custom_call" | custom-call | tf_op jit(solution)/shard_map/pallas_call | solution.py:366
  (9 shorter events, 0.0 us)
Async XLA Ops:
  1.3 15.3 %copy-start = (f32[3,8,32,256]{3,2,1,0:T(8,128)S(1)}, f32[3,8,32,256]{3,2,1,0:T(8,128)}, u32[]{:S(2)}) copy-start(f32[3,8,32,256]{3,2,1,0:T(8,128)} %vort.3) | copy-start | bytes 2359300
  1.3 15.3 %copy-start.1 = (f32[3,8,32,256]{3,2,1,0:T(8,128)S(1)}, f32[3,8,32,256]{3,2,1,0:T(8,128)}, u32[]{:S(2)}) copy-start(f32[3,8,32,256]{3,2,1,0:T(8,128)} %velo.3) | copy-start | bytes 2359300
  4.0 12.5 %copy-start.2 = (f32[8,32,256]{2,1,0:T(8,128)S(1)}, f32[8,32,256]{2,1,0:T(8,128)}, u32[]{:S(2)}) copy-start(f32[8,32,256]{2,1,0:T(8,128)} %visc.3) | copy-start | bytes 786436
  4.0 14.7 %collective-permute-start = (f32[7,32,256]{2,1,0:T(8,128)}, f32[7,32,256]{2,1,0:T(8,128)S(1)}, u32[]{:S(2)}, u32[]{:S(2)}) collective-permute-start(f32[7,32,256]{2,1,0:T(8,128)} %get-tuple-element.15.near), channel_id=1, source_target_pairs={{0,4},{8,12},{16,20},{24,28},{4,0},{12,8},{20,16},{28,24},{1,5},{9... | collective-permute-start | bytes 688136 | tf_op jit(solution)/shard_map/ppermute | solution.py:466
  7.0 11.7 %collective-permute-start.1 = (f32[7,32,256]{2,1,0:T(8,128)}, f32[7,32,256]{2,1,0:T(8,128)S(1)}, u32[]{:S(2)}, u32[]{:S(2)}) collective-permute-start(f32[7,32,256]{2,1,0:T(8,128)} %get-tuple-element.16.far), channel_id=1, source_target_pairs={{4,8},{12,16},{20,24},{8,4},{16,12},{24,20},{5,9},{13,17},{21,25},... | collective-permute-start | bytes 688136 | tf_op jit(solution)/shard_map/ppermute | solution.py:466
  7.7 12.8 %all-to-all-start = ((f32[64,4,128]{2,1,0:T(4,128)}), f32[64,4,128]{2,1,0:T(4,128)S(1)}, u32[]{:S(2)}, u32[]{:S(2)}) async-start(f32[64,4,128]{2,1,0:T(4,128)} %get-tuple-element.20), calls=%async_computation | async-start | bytes 262144 | tf_op jit(solution)/shard_map/all_to_all | solution.py:482
  15.9 0.7 %copy-start.7 = (f32[4,128]{1,0:T(4,128)S(1)}, f32[4,128]{1,0:T(4,128)}, u32[]{:S(2)}) copy-start(f32[4,128]{1,0:T(4,128)} %get-tuple-element.12.tiles_in) | copy-start | bytes 6148
  15.9 2.8 %collective-permute-start.2 = (f32[7,8,256]{2,1,0:T(8,128)}, f32[7,8,256]{2,1,0:T(8,128)S(1)}, u32[]{:S(2)}, u32[]{:S(2)}) collective-permute-start(f32[7,8,256]{2,1,0:T(8,128)} %get-tuple-element.17.swap), channel_id=1, source_target_pairs={{0,1},{2,3},{1,0},{3,2},{4,5},{6,7},{5,4},{7,6},{8,9},{10,11},{9,8... | collective-permute-start | bytes 172040 | tf_op jit(solution)/shard_map/ppermute | solution.py:466
  15.9 2.8 %collective-permute-start.3 = (f32[7,8,256]{2,1,0:T(8,128)}, f32[7,8,256]{2,1,0:T(8,128)S(1)}, u32[]{:S(2)}, u32[]{:S(2)}) collective-permute-start(f32[7,8,256]{2,1,0:T(8,128)} %get-tuple-element.18.other), channel_id=1, source_target_pairs={{1,2},{2,1},{5,6},{6,5},{9,10},{10,9},{13,14},{14,13},{17,18},{18,... | collective-permute-start | bytes 172040 | tf_op jit(solution)/shard_map/ppermute | solution.py:466
  16.6 2.1 %copy-start.3 = (f32[7,32,256]{2,1,0:T(8,128)S(1)}, f32[7,32,256]{2,1,0:T(8,128)}, u32[]{:S(2)}) copy-start(f32[7,32,256]{2,1,0:T(8,128)} %get-tuple-element.15.near) | copy-start | bytes 688132
  16.6 2.1 %copy-start.4 = (f32[7,32,256]{2,1,0:T(8,128)S(1)}, f32[7,32,256]{2,1,0:T(8,128)}, u32[]{:S(2)}) copy-start(f32[7,32,256]{2,1,0:T(8,128)} %get-tuple-element.16.far) | copy-start | bytes 688132
  16.6 2.1 %copy-start.5 = (f32[7,8,256]{2,1,0:T(8,128)S(1)}, f32[7,8,256]{2,1,0:T(8,128)}, u32[]{:S(2)}) copy-start(f32[7,8,256]{2,1,0:T(8,128)} %get-tuple-element.17.swap) | copy-start | bytes 172036
  16.6 2.1 %copy-start.6 = (f32[7,8,256]{2,1,0:T(8,128)S(1)}, f32[7,8,256]{2,1,0:T(8,128)}, u32[]{:S(2)}) copy-start(f32[7,8,256]{2,1,0:T(8,128)} %get-tuple-element.18.other) | copy-start | bytes 172036
  20.5 12.9 %all-to-all-start.1 = ((f32[32,4,128]{2,1,0:T(4,128)}), f32[32,4,128]{2,1,0:T(4,128)S(1)}, u32[]{:S(2)}, u32[]{:S(2)}) async-start(f32[32,4,128]{2,1,0:T(4,128)} %get-tuple-element.21), calls=%async_computation.1 | async-start | bytes 131072 | tf_op jit(solution)/shard_map/all_to_all | solution.py:486
